TPU v7x, 256 devices: a whole 4x4x8 slice. The times are simulated.
256 devices in a mesh: lat: 4 (over x_hi, core), lon: 64 (over x_lo, z, y).
Axes of the slice: x: 4 (x_hi: 2, x_lo: 2; x = x_hi * 2 + x_lo), y: 4, z: 8, core: 2. Of those that a mesh axis runs over, the one named last changes fastest.
Arguments:
- inputs: bfloat16 [32, 2048, 1024], P(None, 'lon', 'lat'), may hold values from -6 to 6
- kernel_one: bfloat16 [3, 3, 32, 32], replicated, may hold values from -0.375 to 0.375
- kernel_two: bfloat16 [3, 3, 32, 32], replicated, may hold values from -0.375 to 0.375
- cotangent: bfloat16 [32, 2048, 1024], P(None, 'lon', 'lat'), may hold values from -6 to 6
Outputs:
- input_grad: bfloat16 [32, 2048, 1024], P(None, 'lon', 'lat')
- kernel_one_grad: float32 [3, 3, 32, 32], replicated
- kernel_two_grad: float32 [3, 3, 32, 32], replicated
All inputs are finite; a program needn't handle non-finite values.
Results may differ from a plain program's by a relative error of at most 0.0032.
Values may be sent and summed in bfloat16 or wider, within the bound.
No kernel may reach another device: no remote copies, remote signals or barrier semaphores. Data moves between devices by JAX's collectives and lax.ppermute only.
A program may use at most 128 MiB of HBM per device.

v0:
```python
import math

import jax
import jax.numpy as jnp
from jax import lax
from jax.sharding import PartitionSpec as P


def with_halo(block, sides, width, periodic):
    for axis, dim in sides:
        count = lax.axis_size(axis)
        forward = [(i, i + 1) for i in range(count - 1)]
        if periodic:
            forward.append((count - 1, 0))
        backward = [(target, source) for source, target in forward]
        low = lax.ppermute(
            lax.slice_in_dim(block, block.shape[dim] - width, None, axis=dim), axis, forward
        )
        high = lax.ppermute(lax.slice_in_dim(block, 0, width, axis=dim), axis, backward)
        block = jnp.concatenate([low, block, high], axis=dim)
    return block


def convolve(source, kernel):
    summed = lax.conv_general_dilated(
        source[None],
        kernel,
        (1, 1),
        "VALID",
        dimension_numbers=("NCHW", "HWOI", "NCHW"),
        preferred_element_type=jnp.float32,
    )
    return summed[0]


def kernel_terms(upstream, source):
    lhs_batch = source[:, None]
    rhs_taps = upstream[:, None]
    summed = lax.conv_general_dilated(
        lhs_batch,
        rhs_taps,
        (1, 1),
        "VALID",
        dimension_numbers=("NCHW", "OIHW", "NCHW"),
        preferred_element_type=jnp.float32,
    )
    return jnp.transpose(summed, (2, 3, 1, 0))


def flipped(kernel):
    return jnp.transpose(jnp.flip(kernel, (0, 1)), (0, 1, 3, 2))


def silu_slope(pre_act):
    sigmoid_value = jax.nn.sigmoid(pre_act)
    return sigmoid_value * (1.0 + pre_act * (1.0 - sigmoid_value))


def on_device(inputs, kernel_one, kernel_two, cotangent):
    channels = inputs.shape[0]
    lon_cells = inputs.shape[1]
    lat_cells = inputs.shape[2]
    grad_scale = 1.0 / math.sqrt(
        lon_cells * lat_cells * lax.axis_size("lat") * lax.axis_size("lon")
    )
    stacked = jnp.concatenate([inputs, cotangent], 0)
    back_one = flipped(kernel_one)
    back_two = flipped(kernel_two)
    lon_wide = with_halo(stacked, (("lon", 1),), 1, True)
    extended = with_halo(lon_wide, (("lat", 2),), 1, False)
    in_cycle = extended[:channels]
    cot_cycle = extended[channels:]
    pre_act = convolve(in_cycle, kernel_one)
    activation = jax.nn.silu(pre_act).astype(jnp.bfloat16)
    act_lon = with_halo(activation, (("lon", 1),), 1, True)
    act_cycle = with_halo(act_lon, (("lat", 2),), 1, False)
    back_grad = convolve(cot_cycle, back_two)
    pre_local = (back_grad * silu_slope(pre_act)).astype(jnp.bfloat16)
    grad_lon = with_halo(pre_local, (("lon", 1),), 1, True)
    grad_cycle = with_halo(grad_lon, (("lat", 2),), 1, False)
    grad_two = kernel_terms(cotangent, act_cycle) * grad_scale
    input_grad = (cotangent.astype(jnp.float32) + convolve(grad_cycle, back_one)).astype(
        jnp.bfloat16
    )
    grad_one = kernel_terms(pre_local, in_cycle) * grad_scale
    grad_one, grad_two = lax.psum((grad_one, grad_two), ("lat", "lon"))
    return (input_grad, grad_one, grad_two)


def solution(mesh):
    placed = (P(None, "lon", "lat"), P(), P(), P(None, "lon", "lat"))
    return jax.shard_map(
        on_device,
        mesh=mesh,
        in_specs=placed,
        out_specs=(P(None, "lon", "lat"), P(), P()),
        check_vma=False,
    )
```

profile of v0, /device:TPU:1, one launch (start us, length us, event | category | flops | bytes accessed | tf_op | source)
XLA Modules:
  0.0 476.4 jit_solution(1986543042868271021)
XLA Ops:
  7.2 1.3 copy_dynamic-update-slice_fusion
  8.6 1.3 copy_dynamic-update-slice_fusion.1
  9.9 9.9 %collective-permute-start.1 = (bf16[64,1,256]{2,0,1:T(8,128)(2,1)S(1)}, bf16[64,1,256]{2,0,1:T(8,128)(2,1)S(1)}, u32[]{:S(2)}, u32[]{:S(2)}) collective-permute-start(bf16[64,1,256]{2,0,1:T(8,128)(2,1)S(1)} %get-tuple-element.22), channel_id=1, source_target_pairs={{1,0},{2,1},{3,2},{4,3},{5,4},{6,5},{7,6},{8,7},{9,8},{10,9},{11,1... | collective-permute-start | bytes 98312 | tf_op jit(solution)/shard_map/ppermute | solution.py:19
  19.8 1.0 collective-permute-done.1
  20.8 6.0 %collective-permute-done = bf16[64,1,256]{2,0,1:T(8,128)(2,1)S(1)} collective-permute-done((bf16[64,1,256]{2,0,1:T(8,128)(2,1)S(1)}, bf16[64,1,256]{2,0,1:T(8,128)(2,1)S(1)}, u32[]{:S(2)}, u32[]{:S(2)}) %collective-permute-start) | collective-permute-done | bytes 32800 | tf_op jit(solution)/shard_map/ppermute | solution.py:16
  27.5 4.0 collective-permute-start.3
  31.9 4.7 collective-permute-start.2
  36.6 4.7 copy.51
  42.1 1.1 pad_maximum_fusion
  43.2 1.4 slice_bitcast_fusion.2
  44.8 1.9 reshape.65
  46.7 4.4 copy.43
  51.0 0.9 slice.70
  52.0 5.9 %broadcast_select_fusion.1 = f32[32,8,33,32]{3,1,2,0:T(8,128)} fusion(pred[8,33]{0,1:T(8,128)(4,1)S(1)} %copy-done.12, bf16[3,3,32,32]{3,2,1,0:T(8,128)(2,1)S(1)} %copy-done, bf16[32,34,1,7,2]{0,3,4,1,2:T(8,128)(2,1)S(1)} %slice.70, bf16[32,34,1,8,33]{0,3,4,1,2:T(8,128)(2,1)} %copy.43), kind=kOutput, calls=%fused_computation.23 | convolution fusion | flops 157811712 | bytes 1704968 | tf_op jit(solution)/shard_map/conv_general_dilated | solution.py:25
  58.0 6.1 %copy.44 = f32[32,8,33,32]{2,1,3,0:T(8,128)} copy(f32[32,8,33,32]{3,1,2,0:T(8,128)} %broadcast_select_fusion.1) | data formatting | bytes 2162688 | tf_op jit(solution)/shard_map/conv_general_dilated | solution.py:25
  64.1 4.6 reshape.69
  68.8 1.9 reshape.58
  70.7 4.4 copy.40
  75.1 0.9 slice.67
  76.1 6.8 %broadcast_select_fusion.2 = f32[32,8,33,32]{3,1,2,0:T(8,128)} fusion(pred[8,33]{0,1:T(8,128)(4,1)S(1)} %copy-done.12, bf16[3,3,32,32]{3,2,1,0:T(8,128)(2,1)S(1)} %copy-done.11, bf16[32,34,1,7,2]{0,3,4,1,2:T(8,128)(2,1)S(1)} %slice.67, bf16[32,34,1,8,33]{0,3,4,1,2:T(8,128)(2,1)} %copy.40), kind=kOutput, calls=%fused_computation.24 | convolution fusion | flops 157811712 | bytes 1704968 | tf_op jit(solution)/shard_map/conv_general_dilated | solution.py:25
  82.9 6.1 %copy.41 = f32[32,8,33,32]{2,1,3,0:T(8,128)} copy(f32[32,8,33,32]{3,1,2,0:T(8,128)} %broadcast_select_fusion.2) | data formatting | bytes 2162688 | tf_op jit(solution)/shard_map/conv_general_dilated | solution.py:25
  89.0 3.7 reshape.62
  92.7 1.2 fusion.47
  93.9 1.2 fusion.35
  95.7 1.5 collective-permute-start.4
  97.2 11.0 %copy.48 = bf16[32,1,34,258]{0,1,3,2:T(2,128)(2,1)} copy(bf16[32,1,34,258]{3,0,2,1:T(8,128)(2,1)} %get-tuple-element.14) | data formatting | bytes 1122816 | tf_op jit(solution)/shard_map/broadcast_in_dim | solution.py:37
  108.2 7.0 %copy.49 = bf16[32,1,32,256]{0,1,3,2:T(2,128)(2,1)} copy(bf16[32,1,32,256]{3,0,2,1:T(8,128)(2,1)S(1)} %copy-done.10) | data formatting | bytes 1048576 | tf_op jit(solution)/shard_map/convert_element_type | solution.py:78
  115.1 1.4 fusion.61
  116.5 4.2 collective-permute-start.9
  120.7 24.7 %convolution_multiply_fusion.1 = f32[3,3,32,32]{2,3,1,0:T(8,128)} fusion(bf16[32,1,34,258]{0,1,3,2:T(2,128)(2,1)} %copy.48, bf16[32,1,32,256]{0,1,3,2:T(2,128)(2,1)} %copy.49), kind=kOutput, calls=%fused_computation.30 | convolution fusion | flops 151004160 | bytes 1122560 | tf_op jit(solution)/shard_map/transpose | solution.py:47
  146.4 1.9 collective-permute-start.7
  148.3 5.1 %collective-permute-start.6 = (bf16[32,34,1]{2,0,1:T(8,128)(2,1)S(1)}, bf16[32,34,1]{2,0,1:T(8,128)(2,1)S(1)}, u32[]{:S(2)}, u32[]{:S(2)}) collective-permute-start(bf16[32,34,1]{2,0,1:T(8,128)(2,1)S(1)} %get-tuple-element.25), channel_id=1, source_target_pairs={{0,64},{64,128},{128,192},{1,65},{65,129},{129,193},{2,66},{66,130... | collective-permute-start | bytes 6536 | tf_op jit(solution)/shard_map/ppermute | solution.py:16
  154.5 1.9 collective-permute-start.11
  156.4 5.1 %collective-permute-start.10 = (bf16[32,34,1]{2,0,1:T(8,128)(2,1)S(1)}, bf16[32,34,1]{2,0,1:T(8,128)(2,1)}, u32[]{:S(2)}, u32[]{:S(2)}) collective-permute-start(bf16[32,34,1]{2,0,1:T(8,128)(2,1)S(1)} %get-tuple-element.23), channel_id=1, source_target_pairs={{0,64},{64,128},{128,192},{1,65},{65,129},{129,193},{2,66},{66,130... | collective-permute-start | bytes 6536 | tf_op jit(solution)/shard_map/ppermute | solution.py:16
  161.6 1.3 maximum_bitcast_fusion
  162.9 1.0 pad.4
  163.9 3.5 reshape.72
  167.4 4.4 copy.46
  172.8 6.7 %broadcast_select_fusion = f32[32,8,33,32]{3,1,2,0:T(8,128)} fusion(pred[8,33]{0,1:T(8,128)(4,1)S(1)} %copy-done.13, bf16[3,3,32,32]{3,2,1,0:T(8,128)(2,1)S(1)} %copy-done, bf16[32,34,1,7,2]{0,3,4,1,2:T(8,128)(2,1)S(1)} %slice.76, bf16[32,34,1,8,33]{0,3,4,1,2:T(8,128)(2,1)} %copy.46), kind=kOutput, calls=%fused_computation.22 | convolution fusion | flops 157811712 | bytes 1704968 | tf_op jit(solution)/shard_map/conv_general_dilated | solution.py:25
  179.5 6.2 %copy.47 = f32[32,8,33,32]{2,1,3,0:T(8,128)} copy(f32[32,8,33,32]{3,1,2,0:T(8,128)} %broadcast_select_fusion) | data formatting | bytes 2162688 | tf_op jit(solution)/shard_map/conv_general_dilated | solution.py:25
  185.7 4.6 reshape.76
  190.2 1.6 maximum_bitcast_fusion.1
  191.8 8.4 %copy.50 = bf16[32,1,34,258]{0,1,3,2:T(2,128)(2,1)} copy(bf16[32,1,34,258]{3,0,2,1:T(8,128)(2,1)S(1)} %maximum_bitcast_fusion.1) | data formatting | bytes 1122816 | tf_op jit(solution)/shard_map/broadcast_in_dim | solution.py:37
  200.3 24.7 %convolution_multiply_fusion = f32[3,3,32,32]{2,3,1,0:T(8,128)} fusion(bf16[32,1,34,258]{0,1,3,2:T(2,128)(2,1)} %copy.50, bf16[32,1,32,256]{0,1,3,2:T(2,128)(2,1)} %copy.51), kind=kOutput, calls=%fused_computation.29 | convolution fusion | flops 151004160 | bytes 1122560 | tf_op jit(solution)/shard_map/transpose | solution.py:47
  225.5 1.1 copy.52
  226.6 239.4 %all-reduce.3.cloned.1.call-done = (f32[3,3,32,32]{2,3,1,0:T(8,128)}, f32[3,3,32,32]{2,3,1,0:T(8,128)}) async-done(((f32[3,3,32,32]{2,3,1,0:T(8,128)}, f32[3,3,32,32]{2,3,1,0:T(8,128)}), (f32[3,3,32,32]{2,3,1,0:T(8,128)}, f32[3,3,32,32]{2,3,1,0:T(8,128)})) %all-reduce.3.cloned.1.call-update) | async-done | bytes 73744 | tf_op jit(solution)/shard_map/psum | solution.py:86
  466.0 1.7 copy.53
  467.7 1.7 copy.54
  (59 shorter events, 6.1 us)
Async XLA Ops:
  7.2 44.8 %copy-start = (bf16[3,3,32,32]{3,2,1,0:T(8,128)(2,1)S(1)}, bf16[3,3,32,32]{3,2,1,0:T(8,128)(2,1)}, u32[]{:S(2)}) copy-start(bf16[3,3,32,32]{3,2,1,0:T(8,128)(2,1)} %param.5) | copy-start | bytes 55300
  7.2 458.8 %all-reduce.3.cloned.1.call-start = ((), (), s32[]{:S(2)}) async-start(), calls=%async_computation | async-start | bytes 589824 | tf_op jit(solution)/shard_map/psum | solution.py:86
  9.9 10.9 %collective-permute-start.1 = (bf16[64,1,256]{2,0,1:T(8,128)(2,1)S(1)}, bf16[64,1,256]{2,0,1:T(8,128)(2,1)S(1)}, u32[]{:S(2)}, u32[]{:S(2)}) collective-permute-start(bf16[64,1,256]{2,0,1:T(8,128)(2,1)S(1)} %get-tuple-element.22), channel_id=1, source_target_pairs={{1,0},{2,1},{3,2},{4,3},{5,4},{6,5},{7,6},{8,7},{9,8},{10,9},{11,1... | collective-permute-start | bytes 98312 | tf_op jit(solution)/shard_map/ppermute | solution.py:19
  19.8 16.8 %copy-start.6 = (bf16[32,32,256]{2,1,0:T(8,128)(2,1)S(1)}, bf16[32,32,256]{2,1,0:T(8,128)(2,1)}, u32[]{:S(2)}) copy-start(bf16[32,32,256]{2,1,0:T(8,128)(2,1)} %param.7) | copy-start | bytes 1572868
  19.8 7.0 %collective-permute-start = (bf16[64,1,256]{2,0,1:T(8,128)(2,1)S(1)}, bf16[64,1,256]{2,0,1:T(8,128)(2,1)S(1)}, u32[]{:S(2)}, u32[]{:S(2)}) collective-permute-start(bf16[64,1,256]{2,0,1:T(8,128)(2,1)S(1)} %get-tuple-element.21), channel_id=1, source_target_pairs={{0,1},{1,2},{2,3},{3,4},{4,5},{5,6},{6,7},{7,8},{8,9},{9,10},{10,1... | collective-permute-start | bytes 98312 | tf_op jit(solution)/shard_map/ppermute | solution.py:16
  27.5 13.8 %collective-permute-start.3 = (bf16[64,34,1]{0,1,2:T(8,128)(2,1)S(1)}, bf16[64,34,1]{0,1,2:T(8,128)(2,1)S(1)}, u32[]{:S(2)}, u32[]{:S(2)}) collective-permute-start(bf16[64,34,1]{0,1,2:T(8,128)(2,1)S(1)} %copy.36), channel_id=1, source_target_pairs={{64,0},{128,64},{192,128},{65,1},{129,65},{193,129},{66,2},{130,66... | collective-permute-start | bytes 13064 | tf_op jit(solution)/shard_map/ppermute | solution.py:19
  31.9 9.9 %collective-permute-start.2 = (bf16[64,34,1]{0,1,2:T(8,128)(2,1)S(1)}, bf16[64,34,1]{0,1,2:T(8,128)(2,1)S(1)}, u32[]{:S(2)}, u32[]{:S(2)}) collective-permute-start(bf16[64,34,1]{0,1,2:T(8,128)(2,1)S(1)} %copy.35), channel_id=1, source_target_pairs={{0,64},{64,128},{128,192},{1,65},{65,129},{129,193},{2,66},{66,130... | collective-permute-start | bytes 13064 | tf_op jit(solution)/shard_map/ppermute | solution.py:16
  46.6 5.4 %copy-start.12 = (pred[8,33]{0,1:T(8,128)(4,1)S(1)}, pred[8,33]{0,1:T(8,128)(4,1)}, u32[]{:S(2)}) copy-start(pred[8,33]{0,1:T(8,128)(4,1)} %constant.20) | copy-start | bytes 796
  64.1 4.6 copy-start.9
  70.7 5.4 %copy-start.11 = (bf16[3,3,32,32]{3,2,1,0:T(8,128)(2,1)S(1)}, bf16[3,3,32,32]{3,2,1,0:T(8,128)(2,1)}, u32[]{:S(2)}) copy-start(bf16[3,3,32,32]{3,2,1,0:T(8,128)(2,1)} %param.6) | copy-start | bytes 55300
  89.0 3.7 copy-start.2
  93.9 1.2 copy-start.4
  95.7 49.7 %collective-permute-start.5 = (bf16[32,1,256]{2,0,1:T(8,128)(2,1)}, bf16[32,1,256]{2,0,1:T(8,128)(2,1)}, u32[]{:S(2)}, u32[]{:S(2)}) collective-permute-start(bf16[32,1,256]{2,0,1:T(8,128)(2,1)} %get-tuple-element.30), channel_id=1, source_target_pairs={{1,0},{2,1},{3,2},{4,3},{5,4},{6,5},{7,6},{8,7},{9,8},{10,9},{11,1... | collective-permute-start | bytes 49160 | tf_op jit(solution)/shard_map/ppermute | solution.py:19
  95.7 49.7 %collective-permute-start.4 = (bf16[32,1,256]{2,0,1:T(8,128)(2,1)}, bf16[32,1,256]{2,0,1:T(8,128)(2,1)}, u32[]{:S(2)}, u32[]{:S(2)}) collective-permute-start(bf16[32,1,256]{2,0,1:T(8,128)(2,1)} %get-tuple-element.29), channel_id=1, source_target_pairs={{0,1},{1,2},{2,3},{3,4},{4,5},{5,6},{6,7},{7,8},{8,9},{9,10},{10,1... | collective-permute-start | bytes 49160 | tf_op jit(solution)/shard_map/ppermute | solution.py:16
  97.2 11.0 %copy-start.10 = (bf16[32,1,32,256]{3,0,2,1:T(8,128)(2,1)S(1)}, bf16[32,1,32,256]{3,0,2,1:T(8,128)(2,1)}, u32[]{:S(2)}) copy-start(bf16[32,1,32,256]{3,0,2,1:T(8,128)(2,1)} %fusion.35) | copy-start | bytes 1572868
  116.5 37.0 %collective-permute-start.9 = (bf16[32,1,256]{2,0,1:T(8,128)(2,1)}, bf16[32,1,256]{2,0,1:T(8,128)(2,1)}, u32[]{:S(2)}, u32[]{:S(2)}) collective-permute-start(bf16[32,1,256]{2,0,1:T(8,128)(2,1)} %get-tuple-element.28), channel_id=1, source_target_pairs={{1,0},{2,1},{3,2},{4,3},{5,4},{6,5},{7,6},{8,7},{9,8},{10,9},{11,1... | collective-permute-start | bytes 49160 | tf_op jit(solution)/shard_map/ppermute | solution.py:19
  120.7 32.8 %collective-permute-start.8 = (bf16[32,1,256]{2,0,1:T(8,128)(2,1)}, bf16[32,1,256]{2,0,1:T(8,128)(2,1)}, u32[]{:S(2)}, u32[]{:S(2)}) collective-permute-start(bf16[32,1,256]{2,0,1:T(8,128)(2,1)} %get-tuple-element.27), channel_id=1, source_target_pairs={{0,1},{1,2},{2,3},{3,4},{4,5},{5,6},{6,7},{7,8},{8,9},{9,10},{10,1... | collective-permute-start | bytes 49160 | tf_op jit(solution)/shard_map/ppermute | solution.py:16
  120.7 24.7 %copy-start.5 = (bf16[32,32,256]{2,0,1:T(8,128)(2,1)S(1)}, bf16[32,32,256]{2,0,1:T(8,128)(2,1)}, u32[]{:S(2)}) copy-start(bf16[32,32,256]{2,0,1:T(8,128)(2,1)} %copy-done.4) | copy-start | bytes 1572868
  145.4 8.1 %copy-start.3 = (bf16[32,32,256]{2,0,1:T(8,128)(2,1)S(1)}, bf16[32,32,256]{2,0,1:T(8,128)(2,1)}, u32[]{:S(2)}) copy-start(bf16[32,32,256]{2,0,1:T(8,128)(2,1)} %get-tuple-element.17) | copy-start | bytes 1572868
  146.4 15.2 %collective-permute-start.7 = (bf16[32,34,1]{2,0,1:T(8,128)(2,1)S(1)}, bf16[32,34,1]{2,0,1:T(8,128)(2,1)S(1)}, u32[]{:S(2)}, u32[]{:S(2)}) collective-permute-start(bf16[32,34,1]{2,0,1:T(8,128)(2,1)S(1)} %get-tuple-element.26), channel_id=1, source_target_pairs={{64,0},{128,64},{192,128},{65,1},{129,65},{193,129},{66,2},{130,66... | collective-permute-start | bytes 6536 | tf_op jit(solution)/shard_map/ppermute | solution.py:19
  148.3 13.2 %collective-permute-start.6 = (bf16[32,34,1]{2,0,1:T(8,128)(2,1)S(1)}, bf16[32,34,1]{2,0,1:T(8,128)(2,1)S(1)}, u32[]{:S(2)}, u32[]{:S(2)}) collective-permute-start(bf16[32,34,1]{2,0,1:T(8,128)(2,1)S(1)} %get-tuple-element.25), channel_id=1, source_target_pairs={{0,64},{64,128},{128,192},{1,65},{65,129},{129,193},{2,66},{66,130... | collective-permute-start | bytes 6536 | tf_op jit(solution)/shard_map/ppermute | solution.py:16
  154.5 35.7 %collective-permute-start.11 = (bf16[32,34,1]{2,0,1:T(8,128)(2,1)S(1)}, bf16[32,34,1]{2,0,1:T(8,128)(2,1)}, u32[]{:S(2)}, u32[]{:S(2)}) collective-permute-start(bf16[32,34,1]{2,0,1:T(8,128)(2,1)S(1)} %get-tuple-element.24), channel_id=1, source_target_pairs={{64,0},{128,64},{192,128},{65,1},{129,65},{193,129},{66,2},{130,66... | collective-permute-start | bytes 6536 | tf_op jit(solution)/shard_map/ppermute | solution.py:19
  156.4 33.8 %collective-permute-start.10 = (bf16[32,34,1]{2,0,1:T(8,128)(2,1)S(1)}, bf16[32,34,1]{2,0,1:T(8,128)(2,1)}, u32[]{:S(2)}, u32[]{:S(2)}) collective-permute-start(bf16[32,34,1]{2,0,1:T(8,128)(2,1)S(1)} %get-tuple-element.23), channel_id=1, source_target_pairs={{0,64},{64,128},{128,192},{1,65},{65,129},{129,193},{2,66},{66,130... | collective-permute-start | bytes 6536 | tf_op jit(solution)/shard_map/ppermute | solution.py:16
  167.4 5.4 %copy-start.13 = (pred[8,33]{0,1:T(8,128)(4,1)S(1)}, pred[8,33]{0,1:T(8,128)(4,1)}, u32[]{:S(2)}) copy-start(pred[8,33]{0,1:T(8,128)(4,1)} %constant.20) | copy-start | bytes 796
  200.3 24.8 %copy-start.7 = (bf16[32,32,256]{2,1,0:T(8,128)(2,1)S(1)}, bf16[32,32,256]{2,1,0:T(8,128)(2,1)}, u32[]{:S(2)}) copy-start(bf16[32,32,256]{2,1,0:T(8,128)(2,1)} %param.7) | copy-start | bytes 1572868
  200.3 24.8 %copy-start.8 = (f32[32,1,264,32]{2,3,0,1:T(8,128)S(1)}, f32[32,1,264,32]{2,3,0,1:T(8,128)}, u32[]{:S(2)}) copy-start(f32[32,1,264,32]{2,3,0,1:T(8,128)} %reshape.76) | copy-start | bytes 3244036
  200.3 269.1 %copy-start.1 = (bf16[3,3,32,32]{3,2,1,0:T(8,128)(2,1)S(1)}, bf16[3,3,32,32]{3,2,1,0:T(8,128)(2,1)}, u32[]{:S(2)}) copy-start(bf16[3,3,32,32]{3,2,1,0:T(8,128)(2,1)} %param.5) | copy-start | bytes 55300
Sparse Core Ops, SparseCore 0:
  225.2 240.7 all-reduce.2
where the time goes:
time: 481 us; the launch traced here: 476 us
  waiting for transfers between devices  246 us (51%)
  local copies, waits for them, and re-layouts  99.4 us (21%)
  matrix products  68.9 us (14%)
  starting transfers between devices  38.4 us (8%)
  between operations  14.6 us (3%)
  other arithmetic  8.59 us (2%)
    psum x1, waiting for transfers between devices, on_device(): grad_one, grad_two = lax.psum((grad_one, grad_two), ('lat', 'lon'))  239 us
    conv_general_dilated x15, local copies, waits for them, and re-layouts, convolve(): lax.conv_general_dilated(source[None], kernel, (1, 1), 'VALID', dimension...  54.6 us
    transpose x2, matrix products, kernel_terms(): return jnp.transpose(summed, (2, 3, 1, 0))  49.4 us
    ppermute x6, starting transfers between devices, with_halo(): lax.ppermute(lax.slice_in_dim(block, 0, width, axis=dim), axis, backward)  21.9 us
    broadcast_in_dim x3, local copies, waits for them, and re-layouts, kernel_terms(): lhs_batch = source[:, None]  20.8 us
    conv_general_dilated x3, matrix products, convolve(): lax.conv_general_dilated(source[None], kernel, (1, 1), 'VALID', dimension...  19.5 us
    ppermute x6, starting transfers between devices, with_halo(): lax.ppermute(lax.slice_in_dim(block, block.shape[dim] - width, None, axis...  16.5 us
  transfers between devices with their start and end apart: 13, of which 3 were waited for; matrix products, arithmetic and copies ran while one was open for 17% of the time, Pallas kernels for 0%

commit v1 on v0

--- a/solution.py
+++ b/solution.py
@@ -56,6 +56,66 @@
     return sigmoid_value * (1.0 + pre_act * (1.0 - sigmoid_value))
 
 
+def pairs(counts, partner):
+    lat_count, lon_count = counts
+    listed = []
+    for lat in range(lat_count):
+        for lon in range(lon_count):
+            to_lat, to_lon = partner(lat, lon)
+            listed.append((lat * lon_count + lon, to_lat * lon_count + to_lon))
+    return listed
+
+
+def x_partner(mask):
+    def partner(lat, lon):
+        place = ((lat >> 1) * 2 + (lon >> 5)) ^ mask
+        return (place >> 1) * 2 + (lat & 1), (place & 1) * 32 + (lon & 31)
+
+    return partner
+
+
+def y_partner(mask):
+    return lambda lat, lon: (lat, lon ^ mask)
+
+
+def z_partner(mask):
+    def partner(lat, lon):
+        place = (lon >> 2) & 7
+        if mask == 3:
+            place = (place + (1 if place % 2 else -1)) % 8
+        else:
+            place ^= mask
+        return lat, (lon & 35) | (place << 2)
+
+    return partner
+
+
+def exchange(value, partner):
+    counts = (lax.axis_size("lat"), lax.axis_size("lon"))
+    return lax.ppermute(value, ("lat", "lon"), pairs(counts, partner))
+
+
+def sum_of_four(value, partner):
+    near, far, wrap = [exchange(value, partner(mask)) for mask in (1, 2, 3)]
+    return (value + near) + (far + wrap)
+
+
+def sum_everywhere(halves):
+    core = lax.axis_index("lat") % 2
+    other_core = lambda lat, lon: (lat ^ 1, lon)
+    mine = lax.dynamic_index_in_dim(halves, core, 0, False)
+    theirs = lax.dynamic_index_in_dim(halves, 1 - core, 0, False)
+    total = mine + exchange(theirs, other_core)
+    total = sum_of_four(total, x_partner)
+    total = sum_of_four(total, y_partner)
+    total = total + exchange(total, z_partner(4))
+    total = sum_of_four(total, z_partner)
+    other = exchange(total, other_core)
+    first = jnp.where(core == 0, total, other)
+    second = jnp.where(core == 0, other, total)
+    return jnp.stack([first, second])
+
+
 def on_device(inputs, kernel_one, kernel_two, cotangent):
     channels = inputs.shape[0]
     lon_cells = inputs.shape[1]
@@ -83,8 +143,13 @@
         jnp.bfloat16
     )
     grad_one = kernel_terms(pre_local, in_cycle) * grad_scale
-    grad_one, grad_two = lax.psum((grad_one, grad_two), ("lat", "lon"))
-    return (input_grad, grad_one, grad_two)
+    halves = jnp.stack([grad_one.reshape(-1, 128), grad_two.reshape(-1, 128)])
+    summed = sum_everywhere(halves)
+    return (
+        input_grad,
+        summed[0].reshape(grad_one.shape),
+        summed[1].reshape(grad_two.shape),
+    )
 
 
 def solution(mesh):

time: 481 us -> 245 us (0.51)
  the two profiles are of different devices: /device:TPU:1 before, /device:TPU:5 now
where the time goes in v1:
time: 245 us; the launch traced here: 240 us
  local copies, waits for them, and re-layouts  95.2 us (39%)
  matrix products  67.5 us (28%)
  starting transfers between devices  54.2 us (22%)
  waiting for transfers between devices  15.1 us (6%)
  other arithmetic  6.97 us (3%)
    conv_general_dilated x15, local copies, waits for them, and re-layouts, convolve(): lax.conv_general_dilated(source[None], kernel, (1, 1), 'VALID', dimension...  52.2 us
    transpose x2, matrix products, kernel_terms(): return jnp.transpose(summed, (2, 3, 1, 0))  48.1 us
    ppermute x6, starting transfers between devices, with_halo(): lax.ppermute(lax.slice_in_dim(block, 0, width, axis=dim), axis, backward)  25.5 us
    ppermute x12, starting transfers between devices, exchange(): return lax.ppermute(value, ('lat', 'lon'), pairs(counts, partner))  22.8 us
    broadcast_in_dim x3, local copies, waits for them, and re-layouts, kernel_terms(): lhs_batch = source[:, None]  21.1 us
    conv_general_dilated x3, matrix products, convolve(): lax.conv_general_dilated(source[None], kernel, (1, 1), 'VALID', dimension...  19.4 us
    ppermute x6, waiting for transfers between devices, with_halo(): lax.ppermute(lax.slice_in_dim(block, block.shape[dim] - width, None, axis...  14 us
    convert_element_type x1, local copies, waits for them, and re-layouts, on_device(): pre_local = (back_grad * silu_slope(pre_act)).astype(jnp.bfloat16)  7.06 us
  transfers between devices with their start and end apart: 24, of which 5 were waited for; matrix products, arithmetic and copies ran while one was open for 24% of the time, Pallas kernels for 0%

profile of v1, /device:TPU:5, one launch (start us, length us, event | category | flops | bytes accessed | tf_op | source)
XLA Modules:
  0.0 240.3 jit_solution(9517449513876424098)
XLA Ops:
  0.6 1.4 copy_dynamic-update-slice_fusion
  2.0 1.3 copy_dynamic-update-slice_fusion.1
  3.4 8.7 %collective-permute-start.1 = (bf16[64,1,256]{2,0,1:T(8,128)(2,1)S(1)}, bf16[64,1,256]{2,0,1:T(8,128)(2,1)S(1)}, u32[]{:S(2)}, u32[]{:S(2)}) collective-permute-start(bf16[64,1,256]{2,0,1:T(8,128)(2,1)S(1)} %get-tuple-element.17), channel_id=1, source_target_pairs={{1,0},{2,1},{3,2},{4,3},{5,4},{6,5},{7,6},{8,7},{9,8},{10,9},{11,1... | collective-permute-start | bytes 98312 | tf_op jit(solution)/shard_map/ppermute | solution.py:19
  13.1 6.0 %collective-permute-done = bf16[64,1,256]{2,0,1:T(8,128)(2,1)S(1)} collective-permute-done((bf16[64,1,256]{2,0,1:T(8,128)(2,1)S(1)}, bf16[64,1,256]{2,0,1:T(8,128)(2,1)S(1)}, u32[]{:S(2)}, u32[]{:S(2)}) %collective-permute-start) | collective-permute-done | bytes 32800 | tf_op jit(solution)/shard_map/ppermute | solution.py:16
  19.9 4.0 %collective-permute-start.3 = (bf16[64,34,1]{0,1,2:T(8,128)(2,1)S(1)}, bf16[64,34,1]{0,1,2:T(8,128)(2,1)S(1)}, u32[]{:S(2)}, u32[]{:S(2)}) collective-permute-start(bf16[64,34,1]{0,1,2:T(8,128)(2,1)S(1)} %copy.34), channel_id=1, source_target_pairs={{64,0},{128,64},{192,128},{65,1},{129,65},{193,129},{66,2},{130,66... | collective-permute-start | bytes 13064 | tf_op jit(solution)/shard_map/ppermute | solution.py:19
  24.2 1.8 collective-permute-start.2
  26.1 4.7 %copy.50 = bf16[32,1,32,256]{0,1,3,2:T(2,128)(2,1)} copy(bf16[32,1,32,256]{3,2,0,1:T(8,128)(2,1)S(1)} %bitcast.126) | data formatting | bytes 1048576 | tf_op jit(solution)/shard_map/broadcast_in_dim | solution.py:38
  31.6 1.1 pad_maximum_fusion
  32.7 1.4 slice_bitcast_fusion.2
  34.2 1.9 reshape.65
  36.1 4.4 %copy.41 = bf16[32,34,1,8,33]{0,3,4,1,2:T(8,128)(2,1)} copy(bf16[32,34,1,8,33]{4,3,0,1,2:T(8,128)(2,1)S(1)} %reshape.65) | data formatting | bytes 1148928 | tf_op jit(solution)/shard_map/conv_general_dilated | solution.py:25
  41.5 5.9 %broadcast_select_fusion.1 = f32[32,8,33,32]{3,1,2,0:T(8,128)} fusion(pred[8,33]{0,1:T(8,128)(4,1)S(1)} %copy-done.10, bf16[3,3,32,32]{3,2,1,0:T(8,128)(2,1)S(1)} %copy-done, bf16[32,34,1,7,2]{0,3,4,1,2:T(8,128)(2,1)S(1)} %slice.70, bf16[32,34,1,8,33]{0,3,4,1,2:T(8,128)(2,1)} %copy.41), kind=kOutput, calls=%fused_computation.23 | convolution fusion | flops 157811712 | bytes 1704968 | tf_op jit(solution)/shard_map/conv_general_dilated | solution.py:25
  47.4 6.1 %copy.42 = f32[32,8,33,32]{2,1,3,0:T(8,128)} copy(f32[32,8,33,32]{3,1,2,0:T(8,128)} %broadcast_select_fusion.1) | data formatting | bytes 2162688 | tf_op jit(solution)/shard_map/conv_general_dilated | solution.py:25
  53.5 4.7 %reshape.69 = f32[32,1,264,32]{2,3,0,1:T(8,128)} reshape(f32[32,8,33,32]{2,1,3,0:T(8,128)} %copy.42) | data formatting | bytes 2162688 | tf_op jit(solution)/shard_map/conv_general_dilated | solution.py:25
  58.3 1.9 reshape.58
  60.2 4.4 %copy.38 = bf16[32,34,1,8,33]{0,3,4,1,2:T(8,128)(2,1)} copy(bf16[32,34,1,8,33]{4,3,0,1,2:T(8,128)(2,1)S(1)} %reshape.58) | data formatting | bytes 1148928 | tf_op jit(solution)/shard_map/conv_general_dilated | solution.py:25
  65.5 6.8 %broadcast_select_fusion.2 = f32[32,8,33,32]{3,1,2,0:T(8,128)} fusion(pred[8,33]{0,1:T(8,128)(4,1)S(1)} %copy-done.10, bf16[3,3,32,32]{3,2,1,0:T(8,128)(2,1)S(1)} %copy-done.9, bf16[32,34,1,7,2]{0,3,4,1,2:T(8,128)(2,1)S(1)} %slice.67, bf16[32,34,1,8,33]{0,3,4,1,2:T(8,128)(2,1)} %copy.38), kind=kOutput, calls=%fused_computation.24 | convolution fusion | flops 157811712 | bytes 1704968 | tf_op jit(solution)/shard_map/conv_general_dilated | solution.py:25
  72.3 6.1 %copy.39 = f32[32,8,33,32]{2,1,3,0:T(8,128)} copy(f32[32,8,33,32]{3,1,2,0:T(8,128)} %broadcast_select_fusion.2) | data formatting | bytes 2162688 | tf_op jit(solution)/shard_map/conv_general_dilated | solution.py:25
  78.4 3.7 %reshape.62 = f32[32,1,264,32]{2,3,0,1:T(8,128)S(1)} reshape(f32[32,8,33,32]{2,1,3,0:T(8,128)} %copy.39) | data formatting | bytes 2162688 | tf_op jit(solution)/shard_map/conv_general_dilated | solution.py:25
  82.2 1.4 fusion.47
  83.6 1.2 fusion.35
  84.7 11.0 %copy.46 = bf16[32,1,34,258]{0,1,3,2:T(2,128)(2,1)} copy(bf16[32,1,34,258]{3,0,2,1:T(8,128)(2,1)} %get-tuple-element.9) | data formatting | bytes 1122816 | tf_op jit(solution)/shard_map/broadcast_in_dim | solution.py:37
  95.8 7.1 %copy.47 = bf16[32,1,32,256]{0,1,3,2:T(2,128)(2,1)} copy(bf16[32,1,32,256]{3,0,2,1:T(8,128)(2,1)S(1)} %copy-done.7) | data formatting | bytes 1048576 | tf_op jit(solution)/shard_map/convert_element_type | solution.py:138
  102.8 1.3 fusion.61
  104.2 1.5 collective-permute-start.8
  105.6 24.0 %convolution_multiply_fusion.1 = f32[3,3,32,32]{2,3,1,0:T(8,128)S(1)} fusion(bf16[32,1,34,258]{0,1,3,2:T(2,128)(2,1)} %copy.46, bf16[32,1,32,256]{0,1,3,2:T(2,128)(2,1)} %copy.47), kind=kOutput, calls=%fused_computation.30 | convolution fusion | flops 151004160 | bytes 1122560 | tf_op jit(solution)/shard_map/transpose | solution.py:47
  130.9 3.6 %collective-permute-start.11 = (bf16[32,34,1]{2,0,1:T(8,128)(2,1)S(1)}, bf16[32,34,1]{2,0,1:T(8,128)(2,1)S(1)}, u32[]{:S(2)}, u32[]{:S(2)}) collective-permute-start(bf16[32,34,1]{2,0,1:T(8,128)(2,1)S(1)} %get-tuple-element.19), channel_id=1, source_target_pairs={{64,0},{128,64},{192,128},{65,1},{129,65},{193,129},{66,2},{130,66... | collective-permute-start | bytes 6536 | tf_op jit(solution)/shard_map/ppermute | solution.py:19
  134.5 1.3 collective-permute-start.10
  136.4 3.2 %collective-permute-done.10 = bf16[32,34,1]{2,0,1:T(8,128)(2,1)S(1)} collective-permute-done((bf16[32,34,1]{2,0,1:T(8,128)(2,1)S(1)}, bf16[32,34,1]{2,0,1:T(8,128)(2,1)S(1)}, u32[]{:S(2)}, u32[]{:S(2)}) %collective-permute-start.10) | collective-permute-done | bytes 2208 | tf_op jit(solution)/shard_map/ppermute | solution.py:16
  139.7 1.3 maximum_bitcast_fusion.1
  140.9 8.7 %copy.49 = bf16[32,1,34,258]{0,1,3,2:T(2,128)(2,1)} copy(bf16[32,1,34,258]{3,0,2,1:T(8,128)(2,1)S(1)} %maximum_bitcast_fusion.1) | data formatting | bytes 1122816 | tf_op jit(solution)/shard_map/broadcast_in_dim | solution.py:37
  149.6 24.0 %convolution_multiply_fusion = f32[3,3,32,32]{2,3,1,0:T(8,128)S(1)} fusion(bf16[32,1,34,258]{0,1,3,2:T(2,128)(2,1)} %copy.49, bf16[32,1,32,256]{0,1,3,2:T(2,128)(2,1)} %copy.50), kind=kOutput, calls=%fused_computation.29 | convolution fusion | flops 151004160 | bytes 1122560 | tf_op jit(solution)/shard_map/transpose | solution.py:47
  173.9 6.5 %collective-permute-start.12 = (f32[72,128]{1,0:T(8,128)S(1)}, f32[72,128]{1,0:T(8,128)S(1)}, u32[]{:S(2)}, u32[]{:S(2)}) collective-permute-start(f32[72,128]{1,0:T(8,128)S(1)} %dynamic-slice_bitcast_fusion), channel_id=1, source_target_pairs={{0,64},{1,65},{2,66},{3,67},{4,68},{5,69},{6,70},{7,71},{8,72},{9,... | collective-permute-start | bytes 110600 | tf_op jit(solution)/shard_map/ppermute | solution.py:95
  180.4 4.8 %collective-permute-start.5 = (bf16[32,1,256]{2,0,1:T(8,128)(2,1)S(1)}, bf16[32,1,256]{2,0,1:T(8,128)(2,1)S(1)}, u32[]{:S(2)}, u32[]{:S(2)}) collective-permute-start(bf16[32,1,256]{2,0,1:T(8,128)(2,1)S(1)} %get-tuple-element.25), channel_id=1, source_target_pairs={{1,0},{2,1},{3,2},{4,3},{5,4},{6,5},{7,6},{8,7},{9,8},{10,9},{11,1... | collective-permute-start | bytes 49160 | tf_op jit(solution)/shard_map/ppermute | solution.py:19
  186.2 3.0 %collective-permute-start.13 = (f32[72,128]{1,0:T(8,128)S(1)}, f32[72,128]{1,0:T(8,128)S(1)}, u32[]{:S(2)}, u32[]{:S(2)}) collective-permute-start(f32[72,128]{1,0:T(8,128)S(1)} %bitcast_add_fusion), channel_id=1, source_target_pairs={{0,32},{1,33},{2,34},{3,35},{4,36},{5,37},{6,38},{7,39},{8,40},{9,... | collective-permute-start | bytes 110600 | tf_op jit(solution)/shard_map/ppermute | solution.py:95
  189.2 2.8 %collective-permute-done.4 = bf16[32,1,256]{2,0,1:T(8,128)(2,1)S(1)} collective-permute-done((bf16[32,1,256]{2,0,1:T(8,128)(2,1)S(1)}, bf16[32,1,256]{2,0,1:T(8,128)(2,1)S(1)}, u32[]{:S(2)}, u32[]{:S(2)}) %collective-permute-start.4) | collective-permute-done | bytes 16416 | tf_op jit(solution)/shard_map/ppermute | solution.py:16
  192.4 2.5 %collective-permute-start.16 = (f32[72,128]{1,0:T(8,128)S(1)}, f32[72,128]{1,0:T(8,128)S(1)}, u32[]{:S(2)}, u32[]{:S(2)}) collective-permute-start(f32[72,128]{1,0:T(8,128)S(1)} %add_add_fusion.2), channel_id=1, source_target_pairs={{0,1},{1,0},{2,3},{3,2},{4,5},{5,4},{6,7},{7,6},{8,9},{9,8},{10,11... | collective-permute-start | bytes 110600 | tf_op jit(solution)/shard_map/ppermute | solution.py:95
  195.1 4.3 %collective-permute-start.7 = (bf16[32,34,1]{2,0,1:T(8,128)(2,1)S(1)}, bf16[32,34,1]{2,0,1:T(8,128)(2,1)S(1)}, u32[]{:S(2)}, u32[]{:S(2)}) collective-permute-start(bf16[32,34,1]{2,0,1:T(8,128)(2,1)S(1)} %get-tuple-element.21), channel_id=1, source_target_pairs={{64,0},{128,64},{192,128},{65,1},{129,65},{193,129},{66,2},{130,66... | collective-permute-start | bytes 6536 | tf_op jit(solution)/shard_map/ppermute | solution.py:19
  199.4 1.3 collective-permute-start.6
  200.8 2.0 collective-permute-done.6
  203.5 2.1 reshape.72
  205.6 4.4 %copy.44 = bf16[32,34,1,8,33]{0,3,4,1,2:T(8,128)(2,1)} copy(bf16[32,34,1,8,33]{4,3,0,1,2:T(8,128)(2,1)S(1)} %reshape.72) | data formatting | bytes 1148928 | tf_op jit(solution)/shard_map/conv_general_dilated | solution.py:25
  211.1 2.0 collective-permute-start.22
  213.1 1.2 collective-permute-start.20
  214.3 6.7 %broadcast_select_fusion = f32[32,8,33,32]{3,1,2,0:T(8,128)} fusion(pred[8,33]{0,1:T(8,128)(4,1)S(1)} %copy-done.11, bf16[3,3,32,32]{3,2,1,0:T(8,128)(2,1)S(1)} %copy-done, bf16[32,34,1,7,2]{0,3,4,1,2:T(8,128)(2,1)S(1)} %slice.76, bf16[32,34,1,8,33]{0,3,4,1,2:T(8,128)(2,1)} %copy.44), kind=kOutput, calls=%fused_computation.22 | convolution fusion | flops 157811712 | bytes 1704968 | tf_op jit(solution)/shard_map/conv_general_dilated | solution.py:25
  220.9 6.2 %copy.45 = f32[32,8,33,32]{2,1,3,0:T(8,128)} copy(f32[32,8,33,32]{3,1,2,0:T(8,128)} %broadcast_select_fusion) | data formatting | bytes 2162688 | tf_op jit(solution)/shard_map/conv_general_dilated | solution.py:25
  227.1 3.5 %reshape.76 = f32[32,1,264,32]{2,3,0,1:T(8,128)S(1)} reshape(f32[32,8,33,32]{2,1,3,0:T(8,128)} %copy.45) | data formatting | bytes 2162688 | tf_op jit(solution)/shard_map/conv_general_dilated | solution.py:25
  230.7 6.3 %collective-permute-start.23 = (f32[72,128]{1,0:T(8,128)S(1)}, f32[72,128]{1,0:T(8,128)S(1)}, u32[]{:S(2)}, u32[]{:S(2)}) collective-permute-start(f32[72,128]{1,0:T(8,128)S(1)} %add_add_fusion), channel_id=1, source_target_pairs={{0,64},{1,65},{2,66},{3,67},{4,68},{5,69},{6,70},{7,71},{8,72},{9,... | collective-permute-start | bytes 110600 | tf_op jit(solution)/shard_map/ppermute | solution.py:95
  (89 shorter events, 13.2 us)
Async XLA Ops:
  0.6 40.8 %copy-start = (bf16[3,3,32,32]{3,2,1,0:T(8,128)(2,1)S(1)}, bf16[3,3,32,32]{3,2,1,0:T(8,128)(2,1)}, u32[]{:S(2)}) copy-start(bf16[3,3,32,32]{3,2,1,0:T(8,128)(2,1)} %param.5) | copy-start | bytes 55300
  3.4 9.8 %collective-permute-start.1 = (bf16[64,1,256]{2,0,1:T(8,128)(2,1)S(1)}, bf16[64,1,256]{2,0,1:T(8,128)(2,1)S(1)}, u32[]{:S(2)}, u32[]{:S(2)}) collective-permute-start(bf16[64,1,256]{2,0,1:T(8,128)(2,1)S(1)} %get-tuple-element.17), channel_id=1, source_target_pairs={{1,0},{2,1},{3,2},{4,3},{5,4},{6,5},{7,6},{8,7},{9,8},{10,9},{11,1... | collective-permute-start | bytes 98312 | tf_op jit(solution)/shard_map/ppermute | solution.py:19
  12.1 13.9 %copy-start.4 = (bf16[32,32,256]{2,1,0:T(8,128)(2,1)S(1)}, bf16[32,32,256]{2,1,0:T(8,128)(2,1)}, u32[]{:S(2)}) copy-start(bf16[32,32,256]{2,1,0:T(8,128)(2,1)} %param.7) | copy-start | bytes 1572868
  12.1 7.0 %collective-permute-start = (bf16[64,1,256]{2,0,1:T(8,128)(2,1)S(1)}, bf16[64,1,256]{2,0,1:T(8,128)(2,1)S(1)}, u32[]{:S(2)}, u32[]{:S(2)}) collective-permute-start(bf16[64,1,256]{2,0,1:T(8,128)(2,1)S(1)} %get-tuple-element.16), channel_id=1, source_target_pairs={{0,1},{1,2},{2,3},{3,4},{4,5},{5,6},{6,7},{7,8},{8,9},{9,10},{10,1... | collective-permute-start | bytes 98312 | tf_op jit(solution)/shard_map/ppermute | solution.py:16
  19.9 10.9 %collective-permute-start.3 = (bf16[64,34,1]{0,1,2:T(8,128)(2,1)S(1)}, bf16[64,34,1]{0,1,2:T(8,128)(2,1)S(1)}, u32[]{:S(2)}, u32[]{:S(2)}) collective-permute-start(bf16[64,34,1]{0,1,2:T(8,128)(2,1)S(1)} %copy.34), channel_id=1, source_target_pairs={{64,0},{128,64},{192,128},{65,1},{129,65},{193,129},{66,2},{130,66... | collective-permute-start | bytes 13064 | tf_op jit(solution)/shard_map/ppermute | solution.py:19
  24.2 7.0 %collective-permute-start.2 = (bf16[64,34,1]{0,1,2:T(8,128)(2,1)S(1)}, bf16[64,34,1]{0,1,2:T(8,128)(2,1)S(1)}, u32[]{:S(2)}, u32[]{:S(2)}) collective-permute-start(bf16[64,34,1]{0,1,2:T(8,128)(2,1)S(1)} %copy.33), channel_id=1, source_target_pairs={{0,64},{64,128},{128,192},{1,65},{65,129},{129,193},{2,66},{66,130... | collective-permute-start | bytes 13064 | tf_op jit(solution)/shard_map/ppermute | solution.py:16
  36.1 5.4 %copy-start.10 = (pred[8,33]{0,1:T(8,128)(4,1)S(1)}, pred[8,33]{0,1:T(8,128)(4,1)}, u32[]{:S(2)}) copy-start(pred[8,33]{0,1:T(8,128)(4,1)} %constant.49) | copy-start | bytes 796
  53.5 4.7 %copy-start.6 = (bf16[32,34,1,258]{3,0,1,2:T(8,128)(2,1)S(1)}, bf16[32,34,1,258]{3,0,1,2:T(8,128)(2,1)}, u32[]{:S(2)}) copy-start(bf16[32,34,1,258]{3,0,1,2:T(8,128)(2,1)} %get-tuple-element.11) | copy-start | bytes 1684228
  60.2 5.4 %copy-start.9 = (bf16[3,3,32,32]{3,2,1,0:T(8,128)(2,1)S(1)}, bf16[3,3,32,32]{3,2,1,0:T(8,128)(2,1)}, u32[]{:S(2)}) copy-start(bf16[3,3,32,32]{3,2,1,0:T(8,128)(2,1)} %param.6) | copy-start | bytes 55300
  78.4 3.7 %copy-start.1 = (f32[32,1,264,32]{2,3,0,1:T(8,128)S(1)}, f32[32,1,264,32]{2,3,0,1:T(8,128)}, u32[]{:S(2)}) copy-start(f32[32,1,264,32]{2,3,0,1:T(8,128)} %reshape.69) | copy-start | bytes 3244036
  84.7 11.0 %copy-start.7 = (bf16[32,1,32,256]{3,0,2,1:T(8,128)(2,1)S(1)}, bf16[32,1,32,256]{3,0,2,1:T(8,128)(2,1)}, u32[]{:S(2)}) copy-start(bf16[32,1,32,256]{3,0,2,1:T(8,128)(2,1)} %fusion.35) | copy-start | bytes 1572868
  104.2 25.7 %collective-permute-start.9 = (bf16[32,1,256]{2,0,1:T(8,128)(2,1)}, bf16[32,1,256]{2,0,1:T(8,128)(2,1)}, u32[]{:S(2)}, u32[]{:S(2)}) collective-permute-start(bf16[32,1,256]{2,0,1:T(8,128)(2,1)} %get-tuple-element.23), channel_id=1, source_target_pairs={{1,0},{2,1},{3,2},{4,3},{5,4},{6,5},{7,6},{8,7},{9,8},{10,9},{11,1... | collective-permute-start | bytes 49160 | tf_op jit(solution)/shard_map/ppermute | solution.py:19
  104.2 25.7 %collective-permute-start.8 = (bf16[32,1,256]{2,0,1:T(8,128)(2,1)}, bf16[32,1,256]{2,0,1:T(8,128)(2,1)}, u32[]{:S(2)}, u32[]{:S(2)}) collective-permute-start(bf16[32,1,256]{2,0,1:T(8,128)(2,1)} %get-tuple-element.22), channel_id=1, source_target_pairs={{0,1},{1,2},{2,3},{3,4},{4,5},{5,6},{6,7},{7,8},{8,9},{9,10},{10,1... | collective-permute-start | bytes 49160 | tf_op jit(solution)/shard_map/ppermute | solution.py:16
  105.6 24.3 %copy-start.3 = (bf16[32,32,256]{2,0,1:T(8,128)(2,1)S(1)}, bf16[32,32,256]{2,0,1:T(8,128)(2,1)}, u32[]{:S(2)}) copy-start(bf16[32,32,256]{2,0,1:T(8,128)(2,1)} %get-tuple-element.12) | copy-start | bytes 1572868
  130.9 5.5 %collective-permute-start.11 = (bf16[32,34,1]{2,0,1:T(8,128)(2,1)S(1)}, bf16[32,34,1]{2,0,1:T(8,128)(2,1)S(1)}, u32[]{:S(2)}, u32[]{:S(2)}) collective-permute-start(bf16[32,34,1]{2,0,1:T(8,128)(2,1)S(1)} %get-tuple-element.19), channel_id=1, source_target_pairs={{64,0},{128,64},{192,128},{65,1},{129,65},{193,129},{66,2},{130,66... | collective-permute-start | bytes 6536 | tf_op jit(solution)/shard_map/ppermute | solution.py:19
  134.5 5.1 %collective-permute-start.10 = (bf16[32,34,1]{2,0,1:T(8,128)(2,1)S(1)}, bf16[32,34,1]{2,0,1:T(8,128)(2,1)S(1)}, u32[]{:S(2)}, u32[]{:S(2)}) collective-permute-start(bf16[32,34,1]{2,0,1:T(8,128)(2,1)S(1)} %get-tuple-element.18), channel_id=1, source_target_pairs={{0,64},{64,128},{128,192},{1,65},{65,129},{129,193},{2,66},{66,130... | collective-permute-start | bytes 6536 | tf_op jit(solution)/shard_map/ppermute | solution.py:16
  149.6 24.2 %copy-start.8 = (f32[2,72,128]{2,1,0:T(8,128)S(1)}, f32[2,72,128]{2,1,0:T(8,128)}, u32[]{:S(2)}) copy-start(f32[2,72,128]{2,1,0:T(8,128)} %constant_dynamic-update-slice_fusion.1) | copy-start | bytes 221188
  149.6 30.8 %copy-start.2 = (bf16[32,32,256]{2,0,1:T(8,128)(2,1)S(1)}, bf16[32,32,256]{2,0,1:T(8,128)(2,1)}, u32[]{:S(2)}) copy-start(bf16[32,32,256]{2,0,1:T(8,128)(2,1)} %get-tuple-element.13) | copy-start | bytes 1572868
  173.9 11.4 %collective-permute-start.12 = (f32[72,128]{1,0:T(8,128)S(1)}, f32[72,128]{1,0:T(8,128)S(1)}, u32[]{:S(2)}, u32[]{:S(2)}) collective-permute-start(f32[72,128]{1,0:T(8,128)S(1)} %dynamic-slice_bitcast_fusion), channel_id=1, source_target_pairs={{0,64},{1,65},{2,66},{3,67},{4,68},{5,69},{6,70},{7,71},{8,72},{9,... | collective-permute-start | bytes 110600 | tf_op jit(solution)/shard_map/ppermute | solution.py:95
  180.4 8.8 %collective-permute-start.5 = (bf16[32,1,256]{2,0,1:T(8,128)(2,1)S(1)}, bf16[32,1,256]{2,0,1:T(8,128)(2,1)S(1)}, u32[]{:S(2)}, u32[]{:S(2)}) collective-permute-start(bf16[32,1,256]{2,0,1:T(8,128)(2,1)S(1)} %get-tuple-element.25), channel_id=1, source_target_pairs={{1,0},{2,1},{3,2},{4,3},{5,4},{6,5},{7,6},{8,7},{9,8},{10,9},{11,1... | collective-permute-start | bytes 49160 | tf_op jit(solution)/shard_map/ppermute | solution.py:19
  185.3 6.8 %collective-permute-start.4 = (bf16[32,1,256]{2,0,1:T(8,128)(2,1)S(1)}, bf16[32,1,256]{2,0,1:T(8,128)(2,1)S(1)}, u32[]{:S(2)}, u32[]{:S(2)}) collective-permute-start(bf16[32,1,256]{2,0,1:T(8,128)(2,1)S(1)} %get-tuple-element.24), channel_id=1, source_target_pairs={{0,1},{1,2},{2,3},{3,4},{4,5},{5,6},{6,7},{7,8},{8,9},{9,10},{10,1... | collective-permute-start | bytes 49160 | tf_op jit(solution)/shard_map/ppermute | solution.py:16
  185.3 6.9 %collective-permute-start.14 = (f32[72,128]{1,0:T(8,128)S(1)}, f32[72,128]{1,0:T(8,128)S(1)}, u32[]{:S(2)}, u32[]{:S(2)}) collective-permute-start(f32[72,128]{1,0:T(8,128)S(1)} %bitcast_add_fusion), channel_id=1, source_target_pairs={{0,128},{1,129},{2,130},{3,131},{4,132},{5,133},{6,134},{7,135},{8... | collective-permute-start | bytes 110600 | tf_op jit(solution)/shard_map/ppermute | solution.py:95
  185.4 6.8 %collective-permute-start.15 = (f32[72,128]{1,0:T(8,128)S(1)}, f32[72,128]{1,0:T(8,128)S(1)}, u32[]{:S(2)}, u32[]{:S(2)}) collective-permute-start(f32[72,128]{1,0:T(8,128)S(1)} %bitcast_add_fusion), channel_id=1, source_target_pairs={{0,160},{1,161},{2,162},{3,163},{4,164},{5,165},{6,166},{7,167},{8... | collective-permute-start | bytes 110600 | tf_op jit(solution)/shard_map/ppermute | solution.py:95
  186.2 6.0 %collective-permute-start.13 = (f32[72,128]{1,0:T(8,128)S(1)}, f32[72,128]{1,0:T(8,128)S(1)}, u32[]{:S(2)}, u32[]{:S(2)}) collective-permute-start(f32[72,128]{1,0:T(8,128)S(1)} %bitcast_add_fusion), channel_id=1, source_target_pairs={{0,32},{1,33},{2,34},{3,35},{4,36},{5,37},{6,38},{7,39},{8,40},{9,... | collective-permute-start | bytes 110600 | tf_op jit(solution)/shard_map/ppermute | solution.py:95
  192.2 8.5 %collective-permute-start.17 = (f32[72,128]{1,0:T(8,128)S(1)}, f32[72,128]{1,0:T(8,128)S(1)}, u32[]{:S(2)}, u32[]{:S(2)}) collective-permute-start(f32[72,128]{1,0:T(8,128)S(1)} %add_add_fusion.2), channel_id=1, source_target_pairs={{0,2},{1,3},{2,0},{3,1},{4,6},{5,7},{6,4},{7,5},{8,10},{9,11},{10,... | collective-permute-start | bytes 110600 | tf_op jit(solution)/shard_map/ppermute | solution.py:95
  192.3 8.4 %collective-permute-start.18 = (f32[72,128]{1,0:T(8,128)S(1)}, f32[72,128]{1,0:T(8,128)S(1)}, u32[]{:S(2)}, u32[]{:S(2)}) collective-permute-start(f32[72,128]{1,0:T(8,128)S(1)} %add_add_fusion.2), channel_id=1, source_target_pairs={{0,3},{1,2},{2,1},{3,0},{4,7},{5,6},{6,5},{7,4},{8,11},{9,10},{10,... | collective-permute-start | bytes 110600 | tf_op jit(solution)/shard_map/ppermute | solution.py:95
  192.4 8.3 %collective-permute-start.16 = (f32[72,128]{1,0:T(8,128)S(1)}, f32[72,128]{1,0:T(8,128)S(1)}, u32[]{:S(2)}, u32[]{:S(2)}) collective-permute-start(f32[72,128]{1,0:T(8,128)S(1)} %add_add_fusion.2), channel_id=1, source_target_pairs={{0,1},{1,0},{2,3},{3,2},{4,5},{5,4},{6,7},{7,6},{8,9},{9,8},{10,11... | collective-permute-start | bytes 110600 | tf_op jit(solution)/shard_map/ppermute | solution.py:95
  195.1 5.7 %collective-permute-start.7 = (bf16[32,34,1]{2,0,1:T(8,128)(2,1)S(1)}, bf16[32,34,1]{2,0,1:T(8,128)(2,1)S(1)}, u32[]{:S(2)}, u32[]{:S(2)}) collective-permute-start(bf16[32,34,1]{2,0,1:T(8,128)(2,1)S(1)} %get-tuple-element.21), channel_id=1, source_target_pairs={{64,0},{128,64},{192,128},{65,1},{129,65},{193,129},{66,2},{130,66... | collective-permute-start | bytes 6536 | tf_op jit(solution)/shard_map/ppermute | solution.py:19
  199.4 3.5 %collective-permute-start.6 = (bf16[32,34,1]{2,0,1:T(8,128)(2,1)S(1)}, bf16[32,34,1]{2,0,1:T(8,128)(2,1)S(1)}, u32[]{:S(2)}, u32[]{:S(2)}) collective-permute-start(bf16[32,34,1]{2,0,1:T(8,128)(2,1)S(1)} %get-tuple-element.20), channel_id=1, source_target_pairs={{0,64},{64,128},{128,192},{1,65},{65,129},{129,193},{2,66},{66,130... | collective-permute-start | bytes 6536 | tf_op jit(solution)/shard_map/ppermute | solution.py:16
  200.7 10.2 %collective-permute-start.19 = (f32[72,128]{1,0:T(8,128)S(1)}, f32[72,128]{1,0:T(8,128)S(1)}, u32[]{:S(2)}, u32[]{:S(2)}) collective-permute-start(f32[72,128]{1,0:T(8,128)S(1)} %add_add_fusion.1), channel_id=1, source_target_pairs={{0,16},{1,17},{2,18},{3,19},{4,20},{5,21},{6,22},{7,23},{8,24},{9,... | collective-permute-start | bytes 110600 | tf_op jit(solution)/shard_map/ppermute | solution.py:95
  205.6 8.7 %copy-start.11 = (pred[8,33]{0,1:T(8,128)(4,1)S(1)}, pred[8,33]{0,1:T(8,128)(4,1)}, u32[]{:S(2)}) copy-start(pred[8,33]{0,1:T(8,128)(4,1)} %constant.49) | copy-start | bytes 796
  211.0 19.7 %collective-permute-start.21 = (f32[72,128]{1,0:T(8,128)S(1)}, f32[72,128]{1,0:T(8,128)S(1)}, u32[]{:S(2)}, u32[]{:S(2)}) collective-permute-start(f32[72,128]{1,0:T(8,128)S(1)} %add.89), channel_id=1, source_target_pairs={{0,8},{1,9},{2,10},{3,11},{4,12},{5,13},{6,14},{7,15},{8,0},{9,1},... | collective-permute-start | bytes 110600 | tf_op jit(solution)/shard_map/ppermute | solution.py:95
  211.1 19.6 %collective-permute-start.22 = (f32[72,128]{1,0:T(8,128)S(1)}, f32[72,128]{1,0:T(8,128)S(1)}, u32[]{:S(2)}, u32[]{:S(2)}) collective-permute-start(f32[72,128]{1,0:T(8,128)S(1)} %add.89), channel_id=1, source_target_pairs={{0,28},{1,29},{2,30},{3,31},{4,8},{5,9},{6,10},{7,11},{8,4},{9,5},... | collective-permute-start | bytes 110600 | tf_op jit(solution)/shard_map/ppermute | solution.py:95
  213.1 17.6 %collective-permute-start.20 = (f32[72,128]{1,0:T(8,128)S(1)}, f32[72,128]{1,0:T(8,128)S(1)}, u32[]{:S(2)}, u32[]{:S(2)}) collective-permute-start(f32[72,128]{1,0:T(8,128)S(1)} %add.89), channel_id=1, source_target_pairs={{0,4},{1,5},{2,6},{3,7},{4,0},{5,1},{6,2},{7,3},{8,12},{9,13},{10,... | collective-permute-start | bytes 110600 | tf_op jit(solution)/shard_map/ppermute | solution.py:95
  227.1 9.9 %copy-start.5 = (bf16[32,32,256]{2,1,0:T(8,128)(2,1)S(1)}, bf16[32,32,256]{2,1,0:T(8,128)(2,1)}, u32[]{:S(2)}) copy-start(bf16[32,32,256]{2,1,0:T(8,128)(2,1)} %param.7) | copy-start | bytes 1572868
  230.7 7.8 %collective-permute-start.23 = (f32[72,128]{1,0:T(8,128)S(1)}, f32[72,128]{1,0:T(8,128)S(1)}, u32[]{:S(2)}, u32[]{:S(2)}) collective-permute-start(f32[72,128]{1,0:T(8,128)S(1)} %add_add_fusion), channel_id=1, source_target_pairs={{0,64},{1,65},{2,66},{3,67},{4,68},{5,69},{6,70},{7,71},{8,72},{9,... | collective-permute-start | bytes 110600 | tf_op jit(solution)/shard_map/ppermute | solution.py:95

commit v2 on v1

v2 whole, which is shorter than its diff:
```python
import functools
import math

import jax
import jax.numpy as jnp
import numpy as np
from jax import lax
from jax.experimental import pallas as pl
from jax.experimental.pallas import tpu as pltpu
from jax.sharding import PartitionSpec as P

BF = jnp.bfloat16
F32 = jnp.float32
GROUP = 6
WINDOW = GROUP + 2
HALF = 16
PARAMS = pltpu.CompilerParams(vmem_limit_bytes=40 * 2**20)


def dot(left, right):
    return lax.dot_general(left, right, (((1,), (0,)), ((), ())), preferred_element_type=F32)


def dot_lanes(left, right):
    return lax.dot_general(left, right, (((1,), (1,)), ((), ())), preferred_element_type=F32)


def dot_rows(left, right):
    return lax.dot_general(left, right, (((0,), (0,)), ((), ())), preferred_element_type=F32)


def iota(shape, dim):
    return lax.broadcasted_iota(jnp.int32, shape, dim)


def call(kernel, outs, scratch, flops, *operands):
    bytes_moved = sum(o.size * o.dtype.itemsize for o in (*operands, *outs))
    return pl.pallas_call(
        kernel,
        out_shape=outs,
        in_specs=[pl.BlockSpec(memory_space=pltpu.VMEM)] * len(operands),
        out_specs=[pl.BlockSpec(memory_space=pltpu.VMEM)] * len(outs),
        scratch_shapes=scratch,
        compiler_params=PARAMS,
        cost_estimate=pl.CostEstimate(flops=flops, bytes_accessed=bytes_moved, transcendentals=0),
    )(*operands)


def shape(*dims, dtype=BF):
    return jax.ShapeDtypeStruct(dims, dtype)


def is_odd():
    return lax.axis_index("lat") % 2


def pack_kernel(x_ref, cot_ref, perm_ref, xl_ref, cl_ref, core_ref, mid_ref):
    lat_cells = x_ref.shape[2]
    odd = is_odd()
    row = iota((2 * HALF, lat_cells), 0)
    lane = iota((2 * HALF, lat_cells), 1)
    high = jnp.where(row < HALF, 1 - odd, odd)
    cell = jnp.where(high == 1, lat_cells - 2, 0) + row % 2
    edges = jnp.zeros((2 * HALF, xl_ref.shape[0]), F32)
    for place, (source, target) in enumerate(((x_ref, xl_ref), (cot_ref, cl_ref))):
        for part in range(source.shape[1] // HALF):
            block = source[:, part * HALF : (part + 1) * HALF, :].reshape(-1, lat_cells)
            rows = block.shape[0]
            target[part * rows : (part + 1) * rows, :] = dot(perm_ref[...], block).astype(BF)
        chosen = ((row % HALF) // 2 == place) & (lane == cell)
        edges = edges + dot_lanes(chosen.astype(F32).astype(BF), target[...])
    core_ref[...] = edges[:HALF].astype(BF)
    mid_ref[...] = edges[HALF:].astype(BF)


def weight_kernel(one_ref, two_ref, first_ref, back_ref):
    channels = one_ref.shape[2]
    lanes = WINDOW * channels
    tiled = (iota((channels, lanes), 1) % channels == iota((channels, lanes), 0)).astype(F32).astype(BF)
    block = iota((channels, lanes), 1) // channels
    for q in range(3):
        firsts = [dot(one_ref[p, q], tiled) for p in range(3)]
        backs = [dot_rows(two_ref[2 - p, 2 - q], tiled) for p in range(3)]
        for bases, target in ((firsts, first_ref), (backs, back_ref)):
            for a in range(GROUP):
                band = jnp.zeros((channels, lanes), F32)
                for p in range(3):
                    band = jnp.where(block == a + p, bases[p], band)
                target[q, a * channels : (a + 1) * channels, :] = band.astype(BF)


def last_weight_kernel(one_ref, last_ref):
    channels = one_ref.shape[2]
    rows, lanes = last_ref.shape[1:]
    tiled = (iota((channels, lanes), 1) % channels == iota((channels, lanes), 0)).astype(F32).astype(BF)
    spread = (iota((rows, channels), 0) // HALF == iota((rows, channels), 1)).astype(F32).astype(BF)
    step = iota((rows, lanes), 1) // channels - iota((rows, lanes), 0) % HALF
    for q in range(3):
        total = jnp.zeros((rows, lanes), F32)
        for p in range(3):
            base = dot_rows(one_ref[2 - p, 2 - q], tiled).astype(BF)
            total = jnp.where(step == p, dot(spread, base), total)
        last_ref[q] = total.astype(BF)


def halo_place(odd, place, lat_cells):
    row = iota((2 * HALF, lat_cells), 0)
    lane = iota((2 * HALF, lat_cells), 1)
    from_low = jnp.where(row < HALF, odd, 1 - odd) == 1
    wanted_row = 2 * place + jnp.where(from_low, 1, 0)
    wanted_lane = jnp.where(from_low, 0, lat_cells - 1)
    return ((row % HALF == wanted_row) & (lane == wanted_lane)).astype(F32).astype(BF)


def write_shifted(values, edge_columns, target, rows):
    lat_cells = values.shape[1]
    lane = iota(values.shape, 1)
    wide = values.astype(F32)
    below = jnp.where(lane == 0, edge_columns, pltpu.roll(wide, 1, 1))
    above = jnp.where(lane == lat_cells - 1, edge_columns, pltpu.roll(wide, lat_cells - 1, 1))
    target[0, rows, :] = below.astype(BF)
    target[1, rows, :] = values
    target[2, rows, :] = above.astype(BF)


def activate(pre_act, back_grad):
    sigmoid_value = 0.5 * jnp.tanh(0.5 * pre_act) + 0.5
    activation = pre_act * sigmoid_value
    slope = sigmoid_value + activation * (1.0 - sigmoid_value)
    return activation, back_grad * slope


def conv_rows(weight_ref, shifted, rows, out_rows):
    count = rows.stop - rows.start
    return sum(dot(weight_ref[q, :out_rows, :count], shifted[q, rows, :]) for q in range(3))


def inner_kernel(x_ref, cot_ref, core_ref, mid_ref, first_ref, back_ref, pre_ref, grads_ref, xs, cs, total):
    lat_cells = x_ref.shape[1]
    channels = grads_ref.shape[2]
    odd = is_odd()
    halos = jnp.concatenate([core_ref[...], mid_ref[...]], 0)
    everything = slice(0, x_ref.shape[0])
    for place, (source, target) in enumerate(((x_ref, xs), (cot_ref, cs))):
        columns = dot_rows(halos, halo_place(odd, place, lat_cells))
        write_shifted(source[...], columns, target, everything)
    group_rows = GROUP * channels
    for k in range(pre_ref.shape[0] // group_rows):
        rows = slice(k * group_rows, k * group_rows + WINDOW * channels)
        pre_act = conv_rows(first_ref, xs, rows, group_rows)
        back_grad = conv_rows(back_ref, cs, rows, group_rows)
        activation, pre_grad = activate(pre_act, back_grad)
        activation = activation.astype(BF)
        pre_grad = pre_grad.astype(BF)
        pre_ref[k * group_rows : (k + 1) * group_rows, :] = pre_grad
        for q in range(3):
            for place, (own, raw) in enumerate(((pre_grad, xs), (activation, cs))):
                term = dot_lanes(own, raw[q, rows, :])
                if k == 0:
                    total[place, q] = term
                else:
                    total[place, q] += term
    for place in range(2):
        for q in range(3):
            summed = jnp.zeros((channels, WINDOW * channels), F32)
            for a in range(GROUP):
                band = total[place, q, a * channels : (a + 1) * channels, :]
                if a:
                    band = pltpu.roll(band, WINDOW * channels - a * channels, 1)
                summed = summed + band
            grads_ref[place, q] = summed[:, :128]


def edge_kernel(x_ref, cot_ref, core_ref, mid_ref, left_ref, right_ref, first_ref, back_ref, grads_ref,
                low_ref, high_ref, out_ref, xs, cs):
    lat_cells = x_ref.shape[1]
    channels = grads_ref.shape[2]
    odd = is_odd()
    two = 2 * channels
    own_rows = x_ref.shape[0]
    sums = [[grads_ref[place, q][:, : 3 * channels] for q in range(3)] for place in range(2)]
    for side, (message, target) in enumerate(((left_ref, low_ref), (right_ref, high_ref))):
        own = slice(0, two) if side == 0 else slice(own_rows - two, own_rows)
        sent = message[2 * two : 2 * two + HALF, :]
        sent_halos = jnp.concatenate([sent[:, :two], sent[:, two : 2 * two]], 0).astype(F32)
        own_halos = jnp.concatenate([core_ref[:, own], mid_ref[:, own]], 0).astype(F32)
        order = (sent_halos, own_halos) if side == 0 else (own_halos, sent_halos)
        halos = jnp.concatenate(order, 1).astype(BF)
        for place, (source, shifted) in enumerate(((x_ref, xs), (cot_ref, cs))):
            sent_rows = message[place * two : (place + 1) * two, :]
            order = (sent_rows, source[own, :]) if side == 0 else (source[own, :], sent_rows)
            columns = dot_rows(halos, halo_place(odd, place, lat_cells))
            write_shifted(jnp.concatenate(order, 0), columns, shifted, slice(0, 2 * two))
        rows = slice(0, 2 * two)
        pre_act = conv_rows(first_ref, xs, rows, two)
        back_grad = conv_rows(back_ref, cs, rows, two)
        activation, pre_grad = activate(pre_act, back_grad)
        pre_grad = pre_grad.astype(BF)
        target[...] = pre_grad
        mine = slice(channels, two) if side == 0 else slice(0, channels)
        near = slice(channels, 2 * two) if side == 0 else slice(0, 3 * channels)
        activation = activation[mine].astype(BF)
        pre_grad = pre_grad[mine]
        for q in range(3):
            sums[0][q] = sums[0][q] + dot_lanes(pre_grad, xs[q, near, :])
            sums[1][q] = sums[1][q] + dot_lanes(activation, cs[q, near, :])
    for place in range(2):
        for q in range(3):
            out_ref[place, q, :, : 3 * channels] = sums[place][q]
            out_ref[place, q, :, 3 * channels :] = jnp.zeros((channels, 128 - 3 * channels), F32)


def last_kernel(x_ref, cot_ref, core_ref, mid_ref, left_ref, right_ref, first_ref, back_ref, low_ref, pre_ref,
                high_ref, last_ref, raw_ref, out_ref, rows_buffer, strips, ps):
    lat_cells = x_ref.shape[1]
    channels = out_ref.shape[0]
    two = 2 * channels
    own_rows = x_ref.shape[0]
    wide_rows = own_rows + 2 * two
    odd = is_odd()
    core, mid = core_ref[...].astype(F32), mid_ref[...].astype(F32)
    lat = lax.axis_index("lat")
    lat_count = lax.axis_size("lat")

    def halo_lanes(value, first):
        parts = [left_ref[2 * two : 2 * two + HALF, first : first + two].astype(F32), value,
                 right_ref[2 * two : 2 * two + HALF, first : first + two].astype(F32)]
        return parts

    def put(target, parts):
        target[:, 0:two] = parts[0]
        target[:, two : two + own_rows] = parts[1]
        target[:, two + own_rows : wide_rows] = parts[2]

    put(strips.at[0], halo_lanes(core, 0))
    put(strips.at[1], halo_lanes(mid, two))
    core_wide, mid_wide = strips[0], strips[1]
    low = jnp.where(odd == 1, core_wide, mid_wide)
    high = jnp.where(odd == 1, mid_wide, core_wide)
    row = iota((HALF, lat_cells), 0)
    lane = iota((HALF, lat_cells), 1)
    ends = ((row < 2) & (lane == row * (lat_cells - 1))).astype(F32).astype(BF)
    values = []
    span = 4 * channels
    window = 6 * channels
    for place, (source, weight_ref) in enumerate(((x_ref, first_ref), (cot_ref, back_ref))):
        rows_buffer[0:two, :] = left_ref[place * two : (place + 1) * two, :]
        rows_buffer[two : two + own_rows, :] = source[...]
        rows_buffer[two + own_rows : wide_rows, :] = right_ref[place * two : (place + 1) * two, :]
        own = dot_lanes(ends, rows_buffer[...])
        low_rows = [low[2 * place : 2 * place + 1], low[2 * place + 1 : 2 * place + 2], own[0:1]]
        high_rows = [own[1:2], high[2 * place : 2 * place + 1], high[2 * place + 1 : 2 * place + 2]]
        total = None
        for q in range(3):
            which = iota((HALF, wide_rows), 0)
            strip = jnp.where(which == 0, low_rows[q], jnp.where(which == 1, high_rows[q], 0.0))
            strip = jnp.concatenate([strip, jnp.zeros((HALF, 128), F32)], 1)
            stacked = jnp.concatenate(
                [strip[:, k : k + window] for k in range(0, wide_rows, span)], 0
            ).astype(BF)
            term = dot_lanes(stacked, weight_ref[q, :span, :window])
            total = term if total is None else total + term
        values.append(total)
    _, pre_grad = activate(*values)
    beyond = jnp.where(iota(pre_grad.shape, 0) % HALF == 0, lat, lat_count - 1 - lat)
    pre_grad = jnp.where(beyond > 0, pre_grad, 0.0)
    pre_strip = jnp.concatenate(
        [pre_grad[k : k + HALF] for k in range(0, pre_grad.shape[0], HALF)], 1
    ).astype(BF)
    wide = pre_ref.shape[0] + 2 * two
    columns = dot_rows(pre_strip, ends)[:wide]
    rows_buffer[0:two, :] = low_ref[...]
    rows_buffer[two : wide - two, :] = pre_ref[...]
    rows_buffer[wide - two : wide, :] = high_ref[...]
    write_shifted(rows_buffer[0:wide, :], columns, ps, slice(0, wide))
    count = last_ref.shape[2]
    for part in range(out_ref.shape[1] // HALF):
        start = part * HALF * channels
        total = sum(dot(last_ref[q], ps[q, start : start + count, :]) for q in range(3))
        lons = slice(part * HALF, (part + 1) * HALF)
        total = total.reshape(channels, HALF, lat_cells) + raw_ref[:, lons, :].astype(F32)
        out_ref[:, lons, :] = total.astype(BF)


def result_kernel(scale, mine_ref, other_ref, one_ref, two_ref):
    channels = one_ref.shape[2]
    odd = is_odd()
    first = jnp.where(odd == 0, mine_ref[...], other_ref[...]) * scale
    second = jnp.where(odd == 0, other_ref[...], mine_ref[...]) * scale
    for q in range(3):
        for p in range(3):
            lanes = slice(p * channels, (p + 1) * channels)
            one_ref[p, q] = first[q][:, lanes]
            two_ref[2 - p, 2 - q] = second[q][:, lanes].T


def pairs(counts, partner):
    lat_count, lon_count = counts
    listed = []
    for lat in range(lat_count):
        for lon in range(lon_count):
            to_lat, to_lon = partner(lat, lon)
            listed.append((lat * lon_count + lon, to_lat * lon_count + to_lon))
    return listed


def x_partner(mask):
    def partner(lat, lon):
        place = ((lat >> 1) * 2 + (lon >> 5)) ^ mask
        return (place >> 1) * 2 + (lat & 1), (place & 1) * 32 + (lon & 31)

    return partner


def y_partner(mask):
    return lambda lat, lon: (lat, lon ^ mask)


def z_partner(mask):
    def partner(lat, lon):
        place = (lon >> 2) & 7
        if mask == 3:
            place = (place + (1 if place % 2 else -1)) % 8
        else:
            place ^= mask
        return lat, (lon & 35) | (place << 2)

    return partner


def exchange(value, partner):
    counts = (lax.axis_size("lat"), lax.axis_size("lon"))
    return lax.ppermute(value, ("lat", "lon"), pairs(counts, partner))


def sum_of_four(value, partner):
    near, far, wrap = [exchange(value, partner(mask)) for mask in (1, 2, 3)]
    return (value + near) + (far + wrap)


def sum_everywhere(halves):
    core = lax.axis_index("lat") % 2
    other_core = lambda lat, lon: (lat ^ 1, lon)
    mine = lax.dynamic_index_in_dim(halves, core, 0, False)
    theirs = lax.dynamic_index_in_dim(halves, 1 - core, 0, False)
    total = mine + exchange(theirs, other_core)
    total = sum_of_four(total, x_partner)
    total = sum_of_four(total, y_partner)
    total = total + exchange(total, z_partner(4))
    total = sum_of_four(total, z_partner)
    other = exchange(total, other_core)
    return total, other


def lat_exchange(core, mid):
    count = lax.axis_size("lat")
    inner = [pair for low in range(1, count - 1, 2) for pair in ((low, low + 1), (low + 1, low))]
    return lax.ppermute(core, "lat", [(i, i ^ 1) for i in range(count)]), lax.ppermute(mid, "lat", inner)


def on_device(inputs, kernel_one, kernel_two, cotangent):
    channels, lon_cells, lat_cells = inputs.shape
    cells = lon_cells * lat_cells * lax.axis_size("lat") * lax.axis_size("lon")
    rows = channels * lon_cells
    two = 2 * channels
    place = np.arange(HALF * channels)
    perm = np.zeros((HALF * channels, HALF * channels), np.float32)
    perm[place, (place % channels) * HALF + place // channels] = 1.0
    perm = jnp.asarray(perm, BF)

    x_rows, cot_rows, core_out, mid_out = call(
        pack_kernel,
        [shape(rows, lat_cells), shape(rows, lat_cells), shape(HALF, rows), shape(HALF, rows)],
        [],
        10**9,
        inputs,
        cotangent,
        perm,
    )
    core_in, mid_in = lat_exchange(core_out, mid_out)

    def message(part):
        pieces = jnp.concatenate([core_in[:, part], mid_in[:, part]], 1)
        pieces = jnp.pad(pieces, ((0, 0), (0, lat_cells - 2 * two)))
        return jnp.concatenate([x_rows[part], cot_rows[part], pieces], 0)

    count = lax.axis_size("lon")
    to_left = message(slice(0, two))
    to_right = message(slice(rows - two, rows))
    from_left = lax.ppermute(to_right, "lon", [(i, (i + 1) % count) for i in range(count)])
    from_right = lax.ppermute(to_left, "lon", [((i + 1) % count, i) for i in range(count)])

    first, back = call(
        weight_kernel,
        [shape(3, GROUP * channels, WINDOW * channels)] * 2,
        [],
        10**8,
        kernel_one,
        kernel_two,
    )
    inner_rows = rows - two
    shifted = pltpu.VMEM((3, rows, lat_cells), BF)
    pre_inner, inner_grads = call(
        inner_kernel,
        [shape(inner_rows, lat_cells), shape(2, 3, channels, 128, dtype=F32)],
        [shifted, shifted, pltpu.VMEM((2, 3, GROUP * channels, WINDOW * channels), F32)],
        4 * 10**9,
        x_rows, cot_rows, core_in, mid_in, first, back,
    )
    edge_shifted = pltpu.VMEM((3, 2 * two, lat_cells), BF)
    pre_low, pre_high, grads = call(
        edge_kernel,
        [shape(two, lat_cells), shape(two, lat_cells), shape(2, 3, channels, 128, dtype=F32)],
        [edge_shifted, edge_shifted],
        10**9,
        x_rows, cot_rows, core_in, mid_in, from_left, from_right, first, back, inner_grads,
    )
    (last_weights,) = call(
        last_weight_kernel,
        [shape(3, HALF * channels, (HALF + 2) * channels)],
        [],
        10**9,
        kernel_one,
    )
    (input_grad,) = call(
        last_kernel,
        [shape(channels, lon_cells, lat_cells)],
        [
            pltpu.VMEM((rows + 2 * two, lat_cells), BF),
            pltpu.VMEM((2, HALF, rows + 2 * two), F32),
            pltpu.VMEM((3, rows + two, lat_cells), BF),
        ],
        2 * 10**9,
        x_rows, cot_rows, core_in, mid_in, from_left, from_right, first, back,
        pre_low, pre_inner, pre_high, last_weights, cotangent,
    )
    mine, other = sum_everywhere(grads.reshape(2, 3 * channels, 128))
    grad_one, grad_two = call(
        functools.partial(result_kernel, 1.0 / math.sqrt(cells)),
        [shape(3, 3, channels, channels, dtype=F32)] * 2,
        [],
        10**6,
        mine.reshape(3, channels, 128),
        other.reshape(3, channels, 128),
    )
    return (input_grad, grad_one, grad_two)


def solution(mesh):
    placed = (P(None, "lon", "lat"), P(), P(), P(None, "lon", "lat"))
    return jax.shard_map(
        on_device,
        mesh=mesh,
        in_specs=placed,
        out_specs=(P(None, "lon", "lat"), P(), P()),
        check_vma=False,
    )
```

time: 245 us -> 63.5 us (0.26)
  the two profiles are of different devices: /device:TPU:5 before, /device:TPU:1 now
where the time goes in v2:
time: 63.5 us; the launch traced here: 63.3 us
  starting transfers between devices  32.4 us (51%)
  waiting for transfers between devices  14.3 us (23%)
  Pallas kernels  12.2 us (19%)
  local copies, waits for them, and re-layouts  3.3 us (5%)
  between operations  0.85 us (1%)
    ppermute x12, starting transfers between devices, exchange(): return lax.ppermute(value, ('lat', 'lon'), pairs(counts, partner))  19 us
    pallas_call x7, Pallas kernels, call(): pl.pallas_call(kernel, out_shape=outs, in_specs=[pl.BlockSpec(memory_spac...  12.2 us
    ppermute x12, waiting for transfers between devices, exchange(): return lax.ppermute(value, ('lat', 'lon'), pairs(counts, partner))  10.7 us
    ppermute x1, starting transfers between devices, on_device(): lax.ppermute(to_left, 'lon', [((i + 1) % count, i) for i in range(count)])  7.28 us
    ppermute x1, waiting for transfers between devices, lat_exchange(): lax.ppermute(mid, 'lat', inner)  3.56 us
    ppermute x1, starting transfers between devices, lat_exchange(): lax.ppermute(core, 'lat', [(i, i ^ 1) for i in range(count)])  3.29 us
    unnamed x12, local copies, waits for them, and re-layouts  3.13 us
    ppermute x1, starting transfers between devices, lat_exchange(): lax.ppermute(mid, 'lat', inner)  2.82 us
  transfers between devices with their start and end apart: 16, of which 7 were waited for; matrix products, arithmetic and copies ran while one was open for 0% of the time, Pallas kernels for 15%

profile of v2, /device:TPU:1, one launch (start us, length us, event | category | flops | bytes accessed | tf_op | source)
XLA Modules:
  0.0 63.3 jit_solution(18220336710611766672)
XLA Ops:
  0.6 0.0 copy-start
  0.6 1.0 %copy-done = bf16[32,32,256]{2,1,0:T(8,128)(2,1)S(1)} copy-done((bf16[32,32,256]{2,1,0:T(8,128)(2,1)S(1)}, bf16[32,32,256]{2,1,0:T(8,128)(2,1)}, u32[]{:S(2)}) %copy-start) | copy-done | bytes 524312
  1.7 1.0 %copy-done.1 = bf16[32,32,256]{2,1,0:T(8,128)(2,1)S(1)} copy-done((bf16[32,32,256]{2,1,0:T(8,128)(2,1)S(1)}, bf16[32,32,256]{2,1,0:T(8,128)(2,1)}, u32[]{:S(2)}) %copy-start.1) | copy-done | bytes 524312
  2.7 1.0 %copy-done.5 = bf16[512,512]{1,0:T(8,128)(2,1)S(1)} copy-done((bf16[512,512]{1,0:T(8,128)(2,1)S(1)}, bf16[512,512]{1,0:T(8,128)(2,1)}, u32[]{:S(2)}) %copy-start.5) | copy-done | bytes 524312
  3.8 1.0 %shard_map.76 = (bf16[1024,256]{1,0:T(8,128)(2,1)S(1)}, bf16[1024,256]{1,0:T(8,128)(2,1)S(1)}, bf16[16,1024]{1,0:T(8,128)(2,1)S(1)}, bf16[16,1024]{1,0:T(8,128)(2,1)S(1)}) custom-call(bf16[32,32,256]{2,1,0:T(8,128)(2,1)S(1)} %copy-done, bf16[32,32,256]{2,1,0:T(8,128)(2,1)S(1)} %copy-done.1, bf16[512,512]{1,0:T(8,128)(2,1)S(1)} %copy-done.5), custom_call_target="tpu_custom_call" | custom-call | flops 1000000000 | bytes 2686976 | tf_op jit(solution)/shard_map/pallas_call | solution.py:38
  4.8 3.3 %collective-permute-start = (bf16[16,1024]{1,0:T(8,128)(2,1)S(1)}, bf16[16,1024]{1,0:T(8,128)(2,1)S(1)}, u32[]{:S(2)}, u32[]{:S(2)}) collective-permute-start(bf16[16,1024]{1,0:T(8,128)(2,1)S(1)} %get-tuple-element.18), channel_id=1, source_target_pairs={{0,64},{64,0},{128,192},{192,128},{1,65},{65,1},{129,193},{193,129... | collective-permute-start | bytes 98312 | tf_op jit(solution)/shard_map/ppermute | solution.py:358
  8.1 2.8 %collective-permute-start.1 = (bf16[16,1024]{1,0:T(8,128)(2,1)S(1)}, bf16[16,1024]{1,0:T(8,128)(2,1)S(1)}, u32[]{:S(2)}, u32[]{:S(2)}) collective-permute-start(bf16[16,1024]{1,0:T(8,128)(2,1)S(1)} %get-tuple-element.19), channel_id=1, source_target_pairs={{64,128},{128,64},{65,129},{129,65},{66,130},{130,66},{67,131},{13... | collective-permute-start | bytes 98312 | tf_op jit(solution)/shard_map/ppermute | solution.py:358
  10.9 0.0 copy-done.3
  11.0 0.3 shard_map.77
  11.3 3.6 %collective-permute-done.1.mid_ref = bf16[16,1024]{1,0:T(8,128)(2,1)S(1)} collective-permute-done((bf16[16,1024]{1,0:T(8,128)(2,1)S(1)}, bf16[16,1024]{1,0:T(8,128)(2,1)S(1)}, u32[]{:S(2)}, u32[]{:S(2)}) %collective-permute-start.1) | collective-permute-done | bytes 32800 | tf_op jit(solution)/shard_map/ppermute | solution.py:358
  14.8 0.1 fusion.9
  14.9 0.0 collective-permute-done.core_ref
  14.9 0.1 fusion.8
  15.0 0.1 fusion.4
  15.1 0.1 collective-permute-start.2
  15.1 0.1 fusion.5
  15.2 7.3 %collective-permute-start.3 = (bf16[144,256]{1,0:T(8,128)(2,1)S(1)}, bf16[144,256]{1,0:T(8,128)(2,1)S(1)}, u32[]{:S(2)}, u32[]{:S(2)}) collective-permute-start(bf16[144,256]{1,0:T(8,128)(2,1)S(1)} %pad_maximum_fusion.1), channel_id=1, source_target_pairs={{1,0},{2,1},{3,2},{4,3},{5,4},{6,5},{7,6},{8,7},{9,8},{10,9},{11,1... | collective-permute-start | bytes 221192 | tf_op jit(solution)/shard_map/ppermute | solution.py:391
  22.5 3.1 %shard_map.78 = (bf16[960,256]{1,0:T(8,128)(2,1)S(1)}, f32[2,3,32,128]{3,2,1,0:T(8,128)S(1)}) custom-call(bf16[1024,256]{1,0:T(8,128)(2,1)S(1)} %get-tuple-element.16.x_ref, bf16[1024,256]{1,0:T(8,128)(2,1)S(1)} %get-tuple-element.17.cot_ref, bf16[16,1024]{1,0:T(8,128)(2,1)S(1)} %collective-permute-done.core_ref, ...), custom_call_target="tpu_custom_call" | custom-call | flops 4000000000 | bytes 2293760 | tf_op jit(solution)/shard_map/pallas_call | solution.py:38
  25.6 0.0 collective-permute-done.2.left_ref
  25.6 0.0 collective-permute-done.3.right_ref
  25.6 1.0 %shard_map.79 = (bf16[64,256]{1,0:T(8,128)(2,1)S(1)}, bf16[64,256]{1,0:T(8,128)(2,1)S(1)}, f32[2,3,32,128]{3,2,1,0:T(8,128)S(1)}) custom-call(bf16[1024,256]{1,0:T(8,128)(2,1)S(1)} %get-tuple-element.16.x_ref, bf16[1024,256]{1,0:T(8,128)(2,1)S(1)} %get-tuple-element.17.cot_ref, bf16[16,1024]{1,0:T(8,128)(2,1)S(1)} %collective-permute-done.core_ref, ...), custom_call_target="tpu_custom_call" | custom-call | flops 1000000000 | bytes 2113536 | tf_op jit(solution)/shard_map/pallas_call | solution.py:38
  26.7 0.1 collective-permute-start.4
  26.8 1.2 %collective-permute-done.4 = f32[96,128]{1,0:T(8,128)S(1)} collective-permute-done((f32[96,128]{1,0:T(8,128)S(1)}, f32[96,128]{1,0:T(8,128)S(1)}, u32[]{:S(2)}, u32[]{:S(2)}) %collective-permute-start.4) | collective-permute-done | bytes 49184 | tf_op jit(solution)/shard_map/ppermute | solution.py:333
  28.0 2.4 %collective-permute-start.6 = (f32[96,128]{1,0:T(8,128)S(1)}, f32[96,128]{1,0:T(8,128)S(1)}, u32[]{:S(2)}, u32[]{:S(2)}) collective-permute-start(f32[96,128]{1,0:T(8,128)S(1)} %bitcast_add_fusion), channel_id=1, source_target_pairs={{0,128},{1,129},{2,130},{3,131},{4,132},{5,133},{6,134},{7,135},{8... | collective-permute-start | bytes 147464 | tf_op jit(solution)/shard_map/ppermute | solution.py:333
  30.5 0.3 collective-permute-start.7
  30.8 0.0 collective-permute-start.5
  30.8 1.8 %collective-permute-done.6 = f32[96,128]{1,0:T(8,128)S(1)} collective-permute-done((f32[96,128]{1,0:T(8,128)S(1)}, f32[96,128]{1,0:T(8,128)S(1)}, u32[]{:S(2)}, u32[]{:S(2)}) %collective-permute-start.6) | collective-permute-done | bytes 49184 | tf_op jit(solution)/shard_map/ppermute | solution.py:333
  32.6 2.0 %collective-permute-done.7 = f32[96,128]{1,0:T(8,128)S(1)} collective-permute-done((f32[96,128]{1,0:T(8,128)S(1)}, f32[96,128]{1,0:T(8,128)S(1)}, u32[]{:S(2)}, u32[]{:S(2)}) %collective-permute-start.7) | collective-permute-done | bytes 49184 | tf_op jit(solution)/shard_map/ppermute | solution.py:333
  34.6 0.0 collective-permute-done.5
  34.6 0.1 collective-permute-start.9
  34.7 0.1 collective-permute-start.10
  34.8 2.5 %collective-permute-start.8 = (f32[96,128]{1,0:T(8,128)S(1)}, f32[96,128]{1,0:T(8,128)S(1)}, u32[]{:S(2)}, u32[]{:S(2)}) collective-permute-start(f32[96,128]{1,0:T(8,128)S(1)} %add_add_fusion.2), channel_id=1, source_target_pairs={{0,1},{1,0},{2,3},{3,2},{4,5},{5,4},{6,7},{7,6},{8,9},{9,8},{10,11... | collective-permute-start | bytes 147464 | tf_op jit(solution)/shard_map/ppermute | solution.py:333
  37.4 1.9 %collective-permute-done.9 = f32[96,128]{1,0:T(8,128)S(1)} collective-permute-done((f32[96,128]{1,0:T(8,128)S(1)}, f32[96,128]{1,0:T(8,128)S(1)}, u32[]{:S(2)}, u32[]{:S(2)}) %collective-permute-start.9) | collective-permute-done | bytes 49184 | tf_op jit(solution)/shard_map/ppermute | solution.py:333
  39.3 0.2 collective-permute-done.10
  39.5 0.0 collective-permute-done.8
  39.5 3.4 %collective-permute-start.11 = (f32[96,128]{1,0:T(8,128)S(1)}, f32[96,128]{1,0:T(8,128)S(1)}, u32[]{:S(2)}, u32[]{:S(2)}) collective-permute-start(f32[96,128]{1,0:T(8,128)S(1)} %add_add_fusion.1), channel_id=1, source_target_pairs={{0,16},{1,17},{2,18},{3,19},{4,20},{5,21},{6,22},{7,23},{8,24},{9,... | collective-permute-start | bytes 147464 | tf_op jit(solution)/shard_map/ppermute | solution.py:333
  42.9 3.6 %collective-permute-done.11 = f32[96,128]{1,0:T(8,128)S(1)} collective-permute-done((f32[96,128]{1,0:T(8,128)S(1)}, f32[96,128]{1,0:T(8,128)S(1)}, u32[]{:S(2)}, u32[]{:S(2)}) %collective-permute-start.11) | collective-permute-done | bytes 49184 | tf_op jit(solution)/shard_map/ppermute | solution.py:333
  46.5 0.4 collective-permute-start.13
  46.8 2.9 %collective-permute-start.14 = (f32[96,128]{1,0:T(8,128)S(1)}, f32[96,128]{1,0:T(8,128)S(1)}, u32[]{:S(2)}, u32[]{:S(2)}) collective-permute-start(f32[96,128]{1,0:T(8,128)S(1)} %add.59), channel_id=1, source_target_pairs={{0,28},{1,29},{2,30},{3,31},{4,8},{5,9},{6,10},{7,11},{8,4},{9,5},... | collective-permute-start | bytes 147464 | tf_op jit(solution)/shard_map/ppermute | solution.py:333
  49.7 1.1 %collective-permute-start.12 = (f32[96,128]{1,0:T(8,128)S(1)}, f32[96,128]{1,0:T(8,128)S(1)}, u32[]{:S(2)}, u32[]{:S(2)}) collective-permute-start(f32[96,128]{1,0:T(8,128)S(1)} %add.59), channel_id=1, source_target_pairs={{0,4},{1,5},{2,6},{3,7},{4,0},{5,1},{6,2},{7,3},{8,12},{9,13},{10,... | collective-permute-start | bytes 147464 | tf_op jit(solution)/shard_map/ppermute | solution.py:333
  50.9 2.8 %shard_map.80.last_ref = bf16[3,512,576]{2,1,0:T(8,128)(2,1)S(1)} custom-call(bf16[3,3,32,32]{3,2,1,0:T(8,128)(2,1)S(1)} %copy-done.4), custom_call_target="tpu_custom_call" | custom-call | flops 1000000000 | bytes 1787904 | tf_op jit(solution)/shard_map/pallas_call | solution.py:38
  53.7 0.0 collective-permute-done.13
  53.7 0.0 collective-permute-done.14
  53.7 0.0 collective-permute-done.12
  53.7 5.6 %collective-permute-start.15 = (f32[96,128]{1,0:T(8,128)S(1)}, f32[96,128]{1,0:T(8,128)S(1)}, u32[]{:S(2)}, u32[]{:S(2)}) collective-permute-start(f32[96,128]{1,0:T(8,128)S(1)} %add_add_fusion), channel_id=1, source_target_pairs={{0,64},{1,65},{2,66},{3,67},{4,68},{5,69},{6,70},{7,71},{8,72},{9,... | collective-permute-start | bytes 147464 | tf_op jit(solution)/shard_map/ppermute | solution.py:333
  59.3 3.1 %shard_map.81 = bf16[32,32,256]{2,1,0:T(8,128)(2,1)} custom-call(bf16[1024,256]{1,0:T(8,128)(2,1)S(1)} %get-tuple-element.16.x_ref, bf16[1024,256]{1,0:T(8,128)(2,1)S(1)} %get-tuple-element.17.cot_ref, bf16[16,1024]{1,0:T(8,128)(2,1)S(1)} %collective-permute-done.core_ref, bf16[16,1024]{1,0:T(8,128)(2,1)S(1)} %collective-permute-done.1.mid_ref, ...), custom_call_target="tpu_custom_call" | custom-call | flops 2000000000 | bytes 5226496 | tf_op jit(solution)/shard_map/pallas_call | solution.py:38
  62.4 0.0 collective-permute-done.15
  62.4 0.9 %shard_map.82 = (f32[3,3,32,32]{3,2,1,0:T(8,128)}, f32[3,3,32,32]{3,2,1,0:T(8,128)}) custom-call(f32[3,32,128]{2,1,0:T(8,128)S(1)} %bitcast.7, f32[3,32,128]{2,1,0:T(8,128)S(1)} %bitcast.10), custom_call_target="tpu_custom_call" | custom-call | flops 1000000 | bytes 172032 | tf_op jit(solution)/shard_map/pallas_call | solution.py:38
  (16 shorter events, 0.1 us)
Async XLA Ops:
  0.6 1.0 %copy-start = (bf16[32,32,256]{2,1,0:T(8,128)(2,1)S(1)}, bf16[32,32,256]{2,1,0:T(8,128)(2,1)}, u32[]{:S(2)}) copy-start(bf16[32,32,256]{2,1,0:T(8,128)(2,1)} %x_ref.1) | copy-start | bytes 1572868
  1.7 1.0 %copy-start.1 = (bf16[32,32,256]{2,1,0:T(8,128)(2,1)S(1)}, bf16[32,32,256]{2,1,0:T(8,128)(2,1)}, u32[]{:S(2)}) copy-start(bf16[32,32,256]{2,1,0:T(8,128)(2,1)} %raw_ref.1) | copy-start | bytes 1572868
  2.7 1.0 %copy-start.5 = (bf16[512,512]{1,0:T(8,128)(2,1)S(1)}, bf16[512,512]{1,0:T(8,128)(2,1)}, u32[]{:S(2)}) copy-start(bf16[512,512]{1,0:T(8,128)(2,1)} %constant.33.clone.perm_ref) | copy-start | bytes 1572868
  3.8 7.2 %copy-start.3 = (bf16[3,3,32,32]{3,2,1,0:T(8,128)(2,1)S(1)}, bf16[3,3,32,32]{3,2,1,0:T(8,128)(2,1)}, u32[]{:S(2)}) copy-start(bf16[3,3,32,32]{3,2,1,0:T(8,128)(2,1)} %two_ref.1) | copy-start | bytes 55300
  3.8 7.2 %copy-start.4 = (bf16[3,3,32,32]{3,2,1,0:T(8,128)(2,1)S(1)}, bf16[3,3,32,32]{3,2,1,0:T(8,128)(2,1)}, u32[]{:S(2)}) copy-start(bf16[3,3,32,32]{3,2,1,0:T(8,128)(2,1)} %one_ref.3) | copy-start | bytes 55300
  4.8 10.1 %collective-permute-start = (bf16[16,1024]{1,0:T(8,128)(2,1)S(1)}, bf16[16,1024]{1,0:T(8,128)(2,1)S(1)}, u32[]{:S(2)}, u32[]{:S(2)}) collective-permute-start(bf16[16,1024]{1,0:T(8,128)(2,1)S(1)} %get-tuple-element.18), channel_id=1, source_target_pairs={{0,64},{64,0},{128,192},{192,128},{1,65},{65,1},{129,193},{193,129... | collective-permute-start | bytes 98312 | tf_op jit(solution)/shard_map/ppermute | solution.py:358
  8.1 6.7 %collective-permute-start.1 = (bf16[16,1024]{1,0:T(8,128)(2,1)S(1)}, bf16[16,1024]{1,0:T(8,128)(2,1)S(1)}, u32[]{:S(2)}, u32[]{:S(2)}) collective-permute-start(bf16[16,1024]{1,0:T(8,128)(2,1)S(1)} %get-tuple-element.19), channel_id=1, source_target_pairs={{64,128},{128,64},{65,129},{129,65},{66,130},{130,66},{67,131},{13... | collective-permute-start | bytes 98312 | tf_op jit(solution)/shard_map/ppermute | solution.py:358
  15.1 10.5 %collective-permute-start.2 = (bf16[144,256]{1,0:T(8,128)(2,1)S(1)}, bf16[144,256]{1,0:T(8,128)(2,1)S(1)}, u32[]{:S(2)}, u32[]{:S(2)}) collective-permute-start(bf16[144,256]{1,0:T(8,128)(2,1)S(1)} %pad_maximum_fusion), channel_id=1, source_target_pairs={{0,1},{1,2},{2,3},{3,4},{4,5},{5,6},{6,7},{7,8},{8,9},{9,10},{10,1... | collective-permute-start | bytes 221192 | tf_op jit(solution)/shard_map/ppermute | solution.py:390
  15.2 10.4 %collective-permute-start.3 = (bf16[144,256]{1,0:T(8,128)(2,1)S(1)}, bf16[144,256]{1,0:T(8,128)(2,1)S(1)}, u32[]{:S(2)}, u32[]{:S(2)}) collective-permute-start(bf16[144,256]{1,0:T(8,128)(2,1)S(1)} %pad_maximum_fusion.1), channel_id=1, source_target_pairs={{1,0},{2,1},{3,2},{4,3},{5,4},{6,5},{7,6},{8,7},{9,8},{10,9},{11,1... | collective-permute-start | bytes 221192 | tf_op jit(solution)/shard_map/ppermute | solution.py:391
  26.7 1.3 %collective-permute-start.4 = (f32[96,128]{1,0:T(8,128)S(1)}, f32[96,128]{1,0:T(8,128)S(1)}, u32[]{:S(2)}, u32[]{:S(2)}) collective-permute-start(f32[96,128]{1,0:T(8,128)S(1)} %dynamic-slice_bitcast_fusion), channel_id=1, source_target_pairs={{0,64},{1,65},{2,66},{3,67},{4,68},{5,69},{6,70},{7,71},{8,72},{9,... | collective-permute-start | bytes 147464 | tf_op jit(solution)/shard_map/ppermute | solution.py:333
  28.0 4.6 %collective-permute-start.6 = (f32[96,128]{1,0:T(8,128)S(1)}, f32[96,128]{1,0:T(8,128)S(1)}, u32[]{:S(2)}, u32[]{:S(2)}) collective-permute-start(f32[96,128]{1,0:T(8,128)S(1)} %bitcast_add_fusion), channel_id=1, source_target_pairs={{0,128},{1,129},{2,130},{3,131},{4,132},{5,133},{6,134},{7,135},{8... | collective-permute-start | bytes 147464 | tf_op jit(solution)/shard_map/ppermute | solution.py:333
  30.5 4.2 %collective-permute-start.7 = (f32[96,128]{1,0:T(8,128)S(1)}, f32[96,128]{1,0:T(8,128)S(1)}, u32[]{:S(2)}, u32[]{:S(2)}) collective-permute-start(f32[96,128]{1,0:T(8,128)S(1)} %bitcast_add_fusion), channel_id=1, source_target_pairs={{0,160},{1,161},{2,162},{3,163},{4,164},{5,165},{6,166},{7,167},{8... | collective-permute-start | bytes 147464 | tf_op jit(solution)/shard_map/ppermute | solution.py:333
  30.8 3.8 %collective-permute-start.5 = (f32[96,128]{1,0:T(8,128)S(1)}, f32[96,128]{1,0:T(8,128)S(1)}, u32[]{:S(2)}, u32[]{:S(2)}) collective-permute-start(f32[96,128]{1,0:T(8,128)S(1)} %bitcast_add_fusion), channel_id=1, source_target_pairs={{0,32},{1,33},{2,34},{3,35},{4,36},{5,37},{6,38},{7,39},{8,40},{9,... | collective-permute-start | bytes 147464 | tf_op jit(solution)/shard_map/ppermute | solution.py:333
  34.6 4.6 %collective-permute-start.9 = (f32[96,128]{1,0:T(8,128)S(1)}, f32[96,128]{1,0:T(8,128)S(1)}, u32[]{:S(2)}, u32[]{:S(2)}) collective-permute-start(f32[96,128]{1,0:T(8,128)S(1)} %add_add_fusion.2), channel_id=1, source_target_pairs={{0,2},{1,3},{2,0},{3,1},{4,6},{5,7},{6,4},{7,5},{8,10},{9,11},{10,... | collective-permute-start | bytes 147464 | tf_op jit(solution)/shard_map/ppermute | solution.py:333
  34.7 4.8 %collective-permute-start.10 = (f32[96,128]{1,0:T(8,128)S(1)}, f32[96,128]{1,0:T(8,128)S(1)}, u32[]{:S(2)}, u32[]{:S(2)}) collective-permute-start(f32[96,128]{1,0:T(8,128)S(1)} %add_add_fusion.2), channel_id=1, source_target_pairs={{0,3},{1,2},{2,1},{3,0},{4,7},{5,6},{6,5},{7,4},{8,11},{9,10},{10,... | collective-permute-start | bytes 147464 | tf_op jit(solution)/shard_map/ppermute | solution.py:333
  34.8 4.7 %collective-permute-start.8 = (f32[96,128]{1,0:T(8,128)S(1)}, f32[96,128]{1,0:T(8,128)S(1)}, u32[]{:S(2)}, u32[]{:S(2)}) collective-permute-start(f32[96,128]{1,0:T(8,128)S(1)} %add_add_fusion.2), channel_id=1, source_target_pairs={{0,1},{1,0},{2,3},{3,2},{4,5},{5,4},{6,7},{7,6},{8,9},{9,8},{10,11... | collective-permute-start | bytes 147464 | tf_op jit(solution)/shard_map/ppermute | solution.py:333
  39.5 6.9 %collective-permute-start.11 = (f32[96,128]{1,0:T(8,128)S(1)}, f32[96,128]{1,0:T(8,128)S(1)}, u32[]{:S(2)}, u32[]{:S(2)}) collective-permute-start(f32[96,128]{1,0:T(8,128)S(1)} %add_add_fusion.1), channel_id=1, source_target_pairs={{0,16},{1,17},{2,18},{3,19},{4,20},{5,21},{6,22},{7,23},{8,24},{9,... | collective-permute-start | bytes 147464 | tf_op jit(solution)/shard_map/ppermute | solution.py:333
  46.5 12.9 %copy-start.2 = (bf16[32,32,256]{2,1,0:T(8,128)(2,1)S(1)}, bf16[32,32,256]{2,1,0:T(8,128)(2,1)}, u32[]{:S(2)}) copy-start(bf16[32,32,256]{2,1,0:T(8,128)(2,1)} %raw_ref.1) | copy-start | bytes 1572868
  46.5 7.2 %collective-permute-start.13 = (f32[96,128]{1,0:T(8,128)S(1)}, f32[96,128]{1,0:T(8,128)S(1)}, u32[]{:S(2)}, u32[]{:S(2)}) collective-permute-start(f32[96,128]{1,0:T(8,128)S(1)} %add.59), channel_id=1, source_target_pairs={{0,8},{1,9},{2,10},{3,11},{4,12},{5,13},{6,14},{7,15},{8,0},{9,1},... | collective-permute-start | bytes 147464 | tf_op jit(solution)/shard_map/ppermute | solution.py:333
  46.8 6.9 %collective-permute-start.14 = (f32[96,128]{1,0:T(8,128)S(1)}, f32[96,128]{1,0:T(8,128)S(1)}, u32[]{:S(2)}, u32[]{:S(2)}) collective-permute-start(f32[96,128]{1,0:T(8,128)S(1)} %add.59), channel_id=1, source_target_pairs={{0,28},{1,29},{2,30},{3,31},{4,8},{5,9},{6,10},{7,11},{8,4},{9,5},... | collective-permute-start | bytes 147464 | tf_op jit(solution)/shard_map/ppermute | solution.py:333
  49.7 4.0 %collective-permute-start.12 = (f32[96,128]{1,0:T(8,128)S(1)}, f32[96,128]{1,0:T(8,128)S(1)}, u32[]{:S(2)}, u32[]{:S(2)}) collective-permute-start(f32[96,128]{1,0:T(8,128)S(1)} %add.59), channel_id=1, source_target_pairs={{0,4},{1,5},{2,6},{3,7},{4,0},{5,1},{6,2},{7,3},{8,12},{9,13},{10,... | collective-permute-start | bytes 147464 | tf_op jit(solution)/shard_map/ppermute | solution.py:333
  53.7 8.7 %collective-permute-start.15 = (f32[96,128]{1,0:T(8,128)S(1)}, f32[96,128]{1,0:T(8,128)S(1)}, u32[]{:S(2)}, u32[]{:S(2)}) collective-permute-start(f32[96,128]{1,0:T(8,128)S(1)} %add_add_fusion), channel_id=1, source_target_pairs={{0,64},{1,65},{2,66},{3,67},{4,68},{5,69},{6,70},{7,71},{8,72},{9,... | collective-permute-start | bytes 147464 | tf_op jit(solution)/shard_map/ppermute | solution.py:333

commit v3 on v2

--- a/solution.py
+++ b/solution.py
@@ -3,7 +3,6 @@
 
 import jax
 import jax.numpy as jnp
-import numpy as np
 from jax import lax
 from jax.experimental import pallas as pl
 from jax.experimental.pallas import tpu as pltpu
@@ -33,13 +32,16 @@
     return lax.broadcasted_iota(jnp.int32, shape, dim)
 
 
-def call(kernel, outs, scratch, flops, *operands):
+def call(kernel, outs, scratch, flops, *operands, hbm_in=(), hbm_out=()):
+    spaces = [pltpu.HBM if i in hbm_in else pltpu.VMEM for i in range(len(operands))]
+    out_spaces = [pltpu.HBM if i in hbm_out else pltpu.VMEM for i in range(len(outs))]
     bytes_moved = sum(o.size * o.dtype.itemsize for o in (*operands, *outs))
+    operands = [pltpu.with_memory_space_constraint(o, pltpu.HBM) if i in hbm_in else o for i, o in enumerate(operands)]
     return pl.pallas_call(
         kernel,
         out_shape=outs,
-        in_specs=[pl.BlockSpec(memory_space=pltpu.VMEM)] * len(operands),
-        out_specs=[pl.BlockSpec(memory_space=pltpu.VMEM)] * len(outs),
+        in_specs=[pl.BlockSpec(memory_space=space) for space in spaces],
+        out_specs=[pl.BlockSpec(memory_space=space) for space in out_spaces],
         scratch_shapes=scratch,
         compiler_params=PARAMS,
         cost_estimate=pl.CostEstimate(flops=flops, bytes_accessed=bytes_moved, transcendentals=0),
@@ -54,26 +56,59 @@
     return lax.axis_index("lat") % 2
 
 
-def pack_kernel(x_ref, cot_ref, perm_ref, xl_ref, cl_ref, core_ref, mid_ref):
-    lat_cells = x_ref.shape[2]
+def pack_kernel(x_ref, cot_ref, one_hbm, two_hbm, xl_ref, cl_ref, core_ref, mid_ref, first_ref, back_ref, last_ref,
+                raw, one_ref, two_ref, perm, sems):
+    channels, lon_cells, lat_cells = x_ref.shape
+    parts = lon_cells // HALF
+    pieces = 2
+    span = channels // pieces
+    kernels = [
+        pltpu.make_async_copy(source, target, sems.at[place])
+        for place, (source, target) in enumerate(((one_hbm, one_ref), (two_hbm, two_ref)))
+    ]
+    copies = []
+    for place, source in enumerate((x_ref, cot_ref)):
+        for part in range(parts):
+            for piece in range(pieces):
+                number = (place * parts + part) * pieces + piece
+                some = pl.ds(piece * span, span)
+                copies.append(
+                    pltpu.make_async_copy(
+                        source.at[some, pl.ds(part * HALF, HALF), :],
+                        raw.at[place * parts + part, some],
+                        sems.at[2 + number],
+                    )
+                )
+    for copy in (*kernels, *copies):
+        copy.start()
+    to_row = iota(perm.shape, 0)
+    from_row = iota(perm.shape, 1)
+    moved = (to_row % channels) * HALF + to_row // channels
+    perm[...] = jnp.where(from_row == moved, 1.0, 0.0).astype(BF)
+    for copy in kernels:
+        copy.wait()
+    write_weights(one_ref, two_ref, first_ref, back_ref, last_ref)
     odd = is_odd()
     row = iota((2 * HALF, lat_cells), 0)
     lane = iota((2 * HALF, lat_cells), 1)
     high = jnp.where(row < HALF, 1 - odd, odd)
     cell = jnp.where(high == 1, lat_cells - 2, 0) + row % 2
     edges = jnp.zeros((2 * HALF, xl_ref.shape[0]), F32)
-    for place, (source, target) in enumerate(((x_ref, xl_ref), (cot_ref, cl_ref))):
-        for part in range(source.shape[1] // HALF):
-            block = source[:, part * HALF : (part + 1) * HALF, :].reshape(-1, lat_cells)
-            rows = block.shape[0]
-            target[part * rows : (part + 1) * rows, :] = dot(perm_ref[...], block).astype(BF)
+    rows = HALF * channels
+    for place, target in enumerate((xl_ref, cl_ref)):
+        for part in range(parts):
+            number = place * parts + part
+            for copy in copies[number * pieces : (number + 1) * pieces]:
+                copy.wait()
+            block = raw[number].reshape(rows, lat_cells)
+            target[part * rows : (part + 1) * rows, :] = dot(perm[...], block).astype(BF)
         chosen = ((row % HALF) // 2 == place) & (lane == cell)
         edges = edges + dot_lanes(chosen.astype(F32).astype(BF), target[...])
     core_ref[...] = edges[:HALF].astype(BF)
     mid_ref[...] = edges[HALF:].astype(BF)
 
 
-def weight_kernel(one_ref, two_ref, first_ref, back_ref):
+def write_weights(one_ref, two_ref, first_ref, back_ref, last_ref):
     channels = one_ref.shape[2]
     lanes = WINDOW * channels
     tiled = (iota((channels, lanes), 1) % channels == iota((channels, lanes), 0)).astype(F32).astype(BF)
@@ -81,26 +116,13 @@
     for q in range(3):
         firsts = [dot(one_ref[p, q], tiled) for p in range(3)]
         backs = [dot_rows(two_ref[2 - p, 2 - q], tiled) for p in range(3)]
-        for bases, target in ((firsts, first_ref), (backs, back_ref)):
+        lasts = [dot_rows(one_ref[2 - p, 2 - q], tiled) for p in range(3)]
+        for bases, target in ((firsts, first_ref), (backs, back_ref), (lasts, last_ref)):
             for a in range(GROUP):
                 band = jnp.zeros((channels, lanes), F32)
                 for p in range(3):
                     band = jnp.where(block == a + p, bases[p], band)
                 target[q, a * channels : (a + 1) * channels, :] = band.astype(BF)
-
-
-def last_weight_kernel(one_ref, last_ref):
-    channels = one_ref.shape[2]
-    rows, lanes = last_ref.shape[1:]
-    tiled = (iota((channels, lanes), 1) % channels == iota((channels, lanes), 0)).astype(F32).astype(BF)
-    spread = (iota((rows, channels), 0) // HALF == iota((rows, channels), 1)).astype(F32).astype(BF)
-    step = iota((rows, lanes), 1) // channels - iota((rows, lanes), 0) % HALF
-    for q in range(3):
-        total = jnp.zeros((rows, lanes), F32)
-        for p in range(3):
-            base = dot_rows(one_ref[2 - p, 2 - q], tiled).astype(BF)
-            total = jnp.where(step == p, dot(spread, base), total)
-        last_ref[q] = total.astype(BF)
 
 
 def halo_place(odd, place, lat_cells):
@@ -205,13 +227,37 @@
             sums[0][q] = sums[0][q] + dot_lanes(pre_grad, xs[q, near, :])
             sums[1][q] = sums[1][q] + dot_lanes(activation, cs[q, near, :])
     for place in range(2):
-        for q in range(3):
-            out_ref[place, q, :, : 3 * channels] = sums[place][q]
-            out_ref[place, q, :, 3 * channels :] = jnp.zeros((channels, 128 - 3 * channels), F32)
+        pack_taps(sums[place], out_ref.at[place])
+
+
+def pack_taps(taps, out_ref):
+    channels = taps[0].shape[0]
+    used = 3 * channels
+    for q in range(2):
+        out_ref[q * channels : (q + 1) * channels, :] = jnp.concatenate(
+            [taps[q], taps[2][:, q * channels : (q + 1) * channels]], 1
+        )
+    rest = taps[2][:, 2 * channels : used]
+    count = 128 // channels
+    rows = channels // count
+    out_ref[2 * channels :, :] = jnp.concatenate(
+        [rest[i * rows : (i + 1) * rows] for i in range(count)], 1
+    )
+
+
+def unpack_taps(packed, channels):
+    used = 3 * channels
+    count = 128 // channels
+    main = [packed[q * channels : (q + 1) * channels] for q in range(2)]
+    rest = packed[2 * channels :]
+    last = jnp.concatenate([rest[:, i * channels : (i + 1) * channels] for i in range(count)], 0)
+    third = jnp.concatenate([main[0][:, used:], main[1][:, used:], last], 1)
+    return [main[0], main[1], third]
 
 
 def last_kernel(x_ref, cot_ref, core_ref, mid_ref, left_ref, right_ref, first_ref, back_ref, low_ref, pre_ref,
-                high_ref, last_ref, raw_ref, out_ref, rows_buffer, strips, ps):
+                high_ref, last_ref, raw_ref, partial_ref, out_ref, passed_ref, rows_buffer, strips, ps, placed, result, sems):
+    passed_ref[...] = partial_ref[...]
     lat_cells = x_ref.shape[1]
     channels = out_ref.shape[0]
     two = 2 * channels
@@ -273,13 +319,33 @@
     rows_buffer[two : wide - two, :] = pre_ref[...]
     rows_buffer[wide - two : wide, :] = high_ref[...]
     write_shifted(rows_buffer[0:wide, :], columns, ps, slice(0, wide))
-    count = last_ref.shape[2]
-    for part in range(out_ref.shape[1] // HALF):
-        start = part * HALF * channels
-        total = sum(dot(last_ref[q], ps[q, start : start + count, :]) for q in range(3))
-        lons = slice(part * HALF, (part + 1) * HALF)
-        total = total.reshape(channels, HALF, lat_cells) + raw_ref[:, lons, :].astype(F32)
-        out_ref[:, lons, :] = total.astype(BF)
+    lon_cells = out_ref.shape[1]
+    copies = []
+    done = 0
+    for first in range(0, lon_cells, GROUP):
+        lons = min(GROUP, lon_cells - first)
+        rows = slice(first * channels, (first + lons + 2) * channels)
+        total = conv_rows(last_ref, ps, rows, lons * channels)
+        for a in range(lons):
+            lon_rows = total[a * channels : (a + 1) * channels]
+            for tile in range(lat_cells // 128):
+                lanes = slice(tile * 128, (tile + 1) * 128)
+                placed[tile, pl.ds(first + a, channels, stride=lon_cells), :] = lon_rows[:, lanes]
+        if first + lons >= done + HALF:
+            part = slice(done, done + HALF)
+            for tile in range(lat_cells // 128):
+                lanes = slice(tile * 128, (tile + 1) * 128)
+                block = placed[tile].reshape(channels, lon_cells, 128)[:, part, :]
+                block = block + raw_ref[:, part, lanes].astype(F32)
+                result[:, part, lanes] = block.astype(BF)
+            copy = pltpu.make_async_copy(
+                result.at[:, pl.ds(done, HALF), :], out_ref.at[:, pl.ds(done, HALF), :], sems.at[done // HALF]
+            )
+            copy.start()
+            copies.append(copy)
+            done += HALF
+    for copy in copies:
+        copy.wait()
 
 
 def result_kernel(scale, mine_ref, other_ref, one_ref, two_ref):
@@ -287,6 +353,8 @@
     odd = is_odd()
     first = jnp.where(odd == 0, mine_ref[...], other_ref[...]) * scale
     second = jnp.where(odd == 0, other_ref[...], mine_ref[...]) * scale
+    first = unpack_taps(first, channels)
+    second = unpack_taps(second, channels)
     for q in range(3):
         for p in range(3):
             lanes = slice(p * channels, (p + 1) * channels)
@@ -317,15 +385,7 @@
 
 
 def z_partner(mask):
-    def partner(lat, lon):
-        place = (lon >> 2) & 7
-        if mask == 3:
-            place = (place + (1 if place % 2 else -1)) % 8
-        else:
-            place ^= mask
-        return lat, (lon & 35) | (place << 2)
-
-    return partner
+    return lambda lat, lon: (lat, lon ^ (mask << 2))
 
 
 def exchange(value, partner):
@@ -338,7 +398,7 @@
     return (value + near) + (far + wrap)
 
 
-def sum_everywhere(halves):
+def sum_everywhere(halves, between):
     core = lax.axis_index("lat") % 2
     other_core = lambda lat, lon: (lat ^ 1, lon)
     mine = lax.dynamic_index_in_dim(halves, core, 0, False)
@@ -346,10 +406,12 @@
     total = mine + exchange(theirs, other_core)
     total = sum_of_four(total, x_partner)
     total = sum_of_four(total, y_partner)
-    total = total + exchange(total, z_partner(4))
     total = sum_of_four(total, z_partner)
+    far = exchange(total, z_partner(7))
+    input_grad, total = between(total)
+    total = total + far
     other = exchange(total, other_core)
-    return total, other
+    return total, other, input_grad
 
 
 def lat_exchange(core, mid):
@@ -363,19 +425,23 @@
     cells = lon_cells * lat_cells * lax.axis_size("lat") * lax.axis_size("lon")
     rows = channels * lon_cells
     two = 2 * channels
-    place = np.arange(HALF * channels)
-    perm = np.zeros((HALF * channels, HALF * channels), np.float32)
-    perm[place, (place % channels) * HALF + place // channels] = 1.0
-    perm = jnp.asarray(perm, BF)
-
-    x_rows, cot_rows, core_out, mid_out = call(
+    weights = [shape(3, GROUP * channels, WINDOW * channels)] * 3
+    x_rows, cot_rows, core_out, mid_out, first, back, last = call(
         pack_kernel,
-        [shape(rows, lat_cells), shape(rows, lat_cells), shape(HALF, rows), shape(HALF, rows)],
-        [],
+        [shape(rows, lat_cells), shape(rows, lat_cells), shape(HALF, rows), shape(HALF, rows), *weights],
+        [
+            pltpu.VMEM((2 * lon_cells // HALF, channels, HALF, lat_cells), BF),
+            pltpu.VMEM(kernel_one.shape, BF),
+            pltpu.VMEM(kernel_two.shape, BF),
+            pltpu.VMEM((HALF * channels, HALF * channels), BF),
+            pltpu.SemaphoreType.DMA((2 + 4 * lon_cells // HALF,)),
+        ],
         10**9,
         inputs,
         cotangent,
-        perm,
+        kernel_one,
+        kernel_two,
+        hbm_in=(0, 1, 2, 3),
     )
     core_in, mid_in = lat_exchange(core_out, mid_out)
 
@@ -390,14 +456,6 @@
     from_left = lax.ppermute(to_right, "lon", [(i, (i + 1) % count) for i in range(count)])
     from_right = lax.ppermute(to_left, "lon", [((i + 1) % count, i) for i in range(count)])
 
-    first, back = call(
-        weight_kernel,
-        [shape(3, GROUP * channels, WINDOW * channels)] * 2,
-        [],
-        10**8,
-        kernel_one,
-        kernel_two,
-    )
     inner_rows = rows - two
     shifted = pltpu.VMEM((3, rows, lat_cells), BF)
     pre_inner, inner_grads = call(
@@ -410,38 +468,37 @@
     edge_shifted = pltpu.VMEM((3, 2 * two, lat_cells), BF)
     pre_low, pre_high, grads = call(
         edge_kernel,
-        [shape(two, lat_cells), shape(two, lat_cells), shape(2, 3, channels, 128, dtype=F32)],
+        [shape(two, lat_cells), shape(two, lat_cells), shape(2, 9 * channels * channels // 128, 128, dtype=F32)],
         [edge_shifted, edge_shifted],
         10**9,
         x_rows, cot_rows, core_in, mid_in, from_left, from_right, first, back, inner_grads,
     )
-    (last_weights,) = call(
-        last_weight_kernel,
-        [shape(3, HALF * channels, (HALF + 2) * channels)],
-        [],
-        10**9,
-        kernel_one,
-    )
-    (input_grad,) = call(
-        last_kernel,
-        [shape(channels, lon_cells, lat_cells)],
-        [
-            pltpu.VMEM((rows + 2 * two, lat_cells), BF),
-            pltpu.VMEM((2, HALF, rows + 2 * two), F32),
-            pltpu.VMEM((3, rows + two, lat_cells), BF),
-        ],
-        2 * 10**9,
-        x_rows, cot_rows, core_in, mid_in, from_left, from_right, first, back,
-        pre_low, pre_inner, pre_high, last_weights, cotangent,
-    )
-    mine, other = sum_everywhere(grads.reshape(2, 3 * channels, 128))
+    def finish(partial):
+        return call(
+            last_kernel,
+            [shape(channels, lon_cells, lat_cells), shape(*partial.shape, dtype=F32)],
+            [
+                pltpu.VMEM((rows + 2 * two, lat_cells), BF),
+                pltpu.VMEM((2, HALF, rows + 2 * two), F32),
+                pltpu.VMEM((3, rows + two, lat_cells), BF),
+                pltpu.VMEM((lat_cells // 128, rows, 128), F32),
+                pltpu.VMEM((channels, lon_cells, lat_cells), BF),
+                pltpu.SemaphoreType.DMA((lon_cells // HALF,)),
+            ],
+            2 * 10**9,
+            x_rows, cot_rows, core_in, mid_in, from_left, from_right, first, back,
+            pre_low, pre_inner, pre_high, last, cotangent, partial,
+            hbm_out=(0,),
+        )
+
+    mine, other, input_grad = sum_everywhere(grads, finish)
     grad_one, grad_two = call(
         functools.partial(result_kernel, 1.0 / math.sqrt(cells)),
         [shape(3, 3, channels, channels, dtype=F32)] * 2,
         [],
         10**6,
-        mine.reshape(3, channels, 128),
-        other.reshape(3, channels, 128),
+        mine,
+        other,
     )
     return (input_grad, grad_one, grad_two)
 

time: 63.5 us -> 59.7 us (0.940)
  local copies, waits for them, and re-layouts: 3.3 us -> 0.18 us
    unnamed x12 -> x2, local copies, waits for them, and re-layouts: 3.13 us -> 0.01 us
    pallas_call x7 -> x5, Pallas kernels: 12.2 us -> 11.7 us  [call(): pl.pallas_call(kernel, out_shape=outs, in_specs=[pl.BlockSpec(memory_spac...]
  transfers between devices with their start and end apart: 16 -> 16, of which waited for: 7 -> 11; matrix products, arithmetic and copies ran while one was open for 0% -> 0% of each run, Pallas kernels for 15% -> 10%
where the time goes in v3:
time: 59.7 us; the launch traced here: 59.6 us
  starting transfers between devices  32.6 us (55%)
  waiting for transfers between devices  14.1 us (24%)
  Pallas kernels  11.7 us (20%)
  between operations  0.8 us (1%)
    ppermute x12, starting transfers between devices, exchange(): return lax.ppermute(value, ('lat', 'lon'), pairs(counts, partner))  19.1 us
    pallas_call x5, Pallas kernels, call(): pl.pallas_call(kernel, out_shape=outs, in_specs=[pl.BlockSpec(memory_spac...  11.7 us
    ppermute x12, waiting for transfers between devices, exchange(): return lax.ppermute(value, ('lat', 'lon'), pairs(counts, partner))  10.3 us
    ppermute x1, starting transfers between devices, on_device(): lax.ppermute(to_left, 'lon', [((i + 1) % count, i) for i in range(count)])  7.27 us
    ppermute x1, waiting for transfers between devices, lat_exchange(): lax.ppermute(mid, 'lat', inner)  3.78 us
    ppermute x1, starting transfers between devices, lat_exchange(): lax.ppermute(core, 'lat', [(i, i ^ 1) for i in range(count)])  3.33 us
    ppermute x1, starting transfers between devices, lat_exchange(): lax.ppermute(mid, 'lat', inner)  2.81 us
  transfers between devices with their start and end apart: 16, of which 11 were waited for; matrix products, arithmetic and copies ran while one was open for 0% of the time, Pallas kernels for 10%

profile of v3, /device:TPU:1, one launch (start us, length us, event | category | flops | bytes accessed | tf_op | source)
XLA Modules:
  0.0 59.6 jit_solution(902205736255278073)
XLA Ops:
  0.6 3.4 %shard_map.67 = (bf16[1024,256]{1,0:T(8,128)(2,1)S(1)}, bf16[1024,256]{1,0:T(8,128)(2,1)S(1)}, bf16[16,1024]{1,0:T(8,128)(2,1)S(1)}, bf16[16,1024]{1,0:T(8,128)(...) custom-call(bf16[32,32,256]{2,1,0:T(8,128)(2,1)} %x_ref.1, ...), custom_call_target="tpu_custom_call" | custom-call | flops 1000000000 | bytes 3084288 | tf_op jit(solution)/shard_map/pallas_call | solution.py:40
  4.0 3.3 %collective-permute-start = (bf16[16,1024]{1,0:T(8,128)(2,1)S(1)}, bf16[16,1024]{1,0:T(8,128)(2,1)S(1)}, u32[]{:S(2)}, u32[]{:S(2)}) collective-permute-start(bf16[16,1024]{1,0:T(8,128)(2,1)S(1)} %get-tuple-element.21), channel_id=1, source_target_pairs={{0,64},{64,0},{128,192},{192,128},{1,65},{65,1},{129,193},{193,129... | collective-permute-start | bytes 98312 | tf_op jit(solution)/shard_map/ppermute | solution.py:420
  7.4 2.8 %collective-permute-start.1 = (bf16[16,1024]{1,0:T(8,128)(2,1)S(1)}, bf16[16,1024]{1,0:T(8,128)(2,1)S(1)}, u32[]{:S(2)}, u32[]{:S(2)}) collective-permute-start(bf16[16,1024]{1,0:T(8,128)(2,1)S(1)} %get-tuple-element.22), channel_id=1, source_target_pairs={{64,128},{128,64},{65,129},{129,65},{66,130},{130,66},{67,131},{13... | collective-permute-start | bytes 98312 | tf_op jit(solution)/shard_map/ppermute | solution.py:420
  10.2 0.0 collective-permute-done.core_ref
  10.2 0.1 fusion.8
  10.3 3.8 %collective-permute-done.1.mid_ref = bf16[16,1024]{1,0:T(8,128)(2,1)S(1)} collective-permute-done((bf16[16,1024]{1,0:T(8,128)(2,1)S(1)}, bf16[16,1024]{1,0:T(8,128)(2,1)S(1)}, u32[]{:S(2)}, u32[]{:S(2)}) %collective-permute-start.1) | collective-permute-done | bytes 32800 | tf_op jit(solution)/shard_map/ppermute | solution.py:420
  14.1 0.1 fusion.9
  14.2 0.1 fusion.4
  14.3 0.1 collective-permute-start.2
  14.3 0.1 fusion.5
  14.4 7.3 %collective-permute-start.3 = (bf16[144,256]{1,0:T(8,128)(2,1)S(1)}, bf16[144,256]{1,0:T(8,128)(2,1)S(1)}, u32[]{:S(2)}, u32[]{:S(2)}) collective-permute-start(bf16[144,256]{1,0:T(8,128)(2,1)S(1)} %pad_maximum_fusion.1), channel_id=1, source_target_pairs={{1,0},{2,1},{3,2},{4,3},{5,4},{6,5},{7,6},{8,7},{9,8},{10,9},{11,1... | collective-permute-start | bytes 221192 | tf_op jit(solution)/shard_map/ppermute | solution.py:457
  21.7 3.1 %shard_map.68 = (bf16[960,256]{1,0:T(8,128)(2,1)S(1)}, f32[2,3,32,128]{3,2,1,0:T(8,128)S(1)}) custom-call(bf16[1024,256]{1,0:T(8,128)(2,1)S(1)} %get-tuple-element.19.x_ref, bf16[1024,256]{1,0:T(8,128)(2,1)S(1)} %get-tuple-element.20.cot_ref, bf16[16,1024]{1,0:T(8,128)(2,1)S(1)} %collective-permute-done.core_ref, ...), custom_call_target="tpu_custom_call" | custom-call | flops 4000000000 | bytes 2293760 | tf_op jit(solution)/shard_map/pallas_call | solution.py:40
  24.8 0.0 collective-permute-done.2.left_ref
  24.8 0.0 collective-permute-done.3.right_ref
  24.8 1.1 %shard_map.69 = (bf16[64,256]{1,0:T(8,128)(2,1)S(1)}, bf16[64,256]{1,0:T(8,128)(2,1)S(1)}, f32[2,72,128]{2,1,0:T(8,128)S(1)}) custom-call(bf16[1024,256]{1,0:T(8,128)(2,1)S(1)} %get-tuple-element.19.x_ref, bf16[1024,256]{1,0:T(8,128)(2,1)S(1)} %get-tuple-element.20.cot_ref, bf16[16,1024]{1,0:T(8,128)(2,1)S(1)} %collective-permute-done.core_ref, ...), custom_call_target="tpu_custom_call" | custom-call | flops 1000000000 | bytes 2088960 | tf_op jit(solution)/shard_map/pallas_call | solution.py:40
  25.9 0.0 copy-start
  26.0 0.1 collective-permute-start.4
  26.1 1.2 %collective-permute-done.4 = f32[72,128]{1,0:T(8,128)S(1)} collective-permute-done((f32[72,128]{1,0:T(8,128)S(1)}, f32[72,128]{1,0:T(8,128)S(1)}, u32[]{:S(2)}, u32[]{:S(2)}) %collective-permute-start.4) | collective-permute-done | bytes 36896 | tf_op jit(solution)/shard_map/ppermute | solution.py:393
  27.3 1.8 %collective-permute-start.7 = (f32[72,128]{1,0:T(8,128)S(1)}, f32[72,128]{1,0:T(8,128)S(1)}, u32[]{:S(2)}, u32[]{:S(2)}) collective-permute-start(f32[72,128]{1,0:T(8,128)S(1)} %bitcast_add_fusion), channel_id=1, source_target_pairs={{0,160},{1,161},{2,162},{3,163},{4,164},{5,165},{6,166},{7,167},{8... | collective-permute-start | bytes 110600 | tf_op jit(solution)/shard_map/ppermute | solution.py:393
  29.1 0.7 %collective-permute-start.6 = (f32[72,128]{1,0:T(8,128)S(1)}, f32[72,128]{1,0:T(8,128)S(1)}, u32[]{:S(2)}, u32[]{:S(2)}) collective-permute-start(f32[72,128]{1,0:T(8,128)S(1)} %bitcast_add_fusion), channel_id=1, source_target_pairs={{0,128},{1,129},{2,130},{3,131},{4,132},{5,133},{6,134},{7,135},{8... | collective-permute-start | bytes 110600 | tf_op jit(solution)/shard_map/ppermute | solution.py:393
  29.8 0.7 %collective-permute-start.5 = (f32[72,128]{1,0:T(8,128)S(1)}, f32[72,128]{1,0:T(8,128)S(1)}, u32[]{:S(2)}, u32[]{:S(2)}) collective-permute-start(f32[72,128]{1,0:T(8,128)S(1)} %bitcast_add_fusion), channel_id=1, source_target_pairs={{0,32},{1,33},{2,34},{3,35},{4,36},{5,37},{6,38},{7,39},{8,40},{9,... | collective-permute-start | bytes 110600 | tf_op jit(solution)/shard_map/ppermute | solution.py:393
  30.5 0.8 %collective-permute-done.7 = f32[72,128]{1,0:T(8,128)S(1)} collective-permute-done((f32[72,128]{1,0:T(8,128)S(1)}, f32[72,128]{1,0:T(8,128)S(1)}, u32[]{:S(2)}, u32[]{:S(2)}) %collective-permute-start.7) | collective-permute-done | bytes 36896 | tf_op jit(solution)/shard_map/ppermute | solution.py:393
  31.3 2.1 %collective-permute-done.6 = f32[72,128]{1,0:T(8,128)S(1)} collective-permute-done((f32[72,128]{1,0:T(8,128)S(1)}, f32[72,128]{1,0:T(8,128)S(1)}, u32[]{:S(2)}, u32[]{:S(2)}) %collective-permute-start.6) | collective-permute-done | bytes 36896 | tf_op jit(solution)/shard_map/ppermute | solution.py:393
  33.4 0.0 collective-permute-done.5
  33.4 0.1 collective-permute-start.10
  33.5 0.1 collective-permute-start.9
  33.6 3.1 %collective-permute-start.8 = (f32[72,128]{1,0:T(8,128)S(1)}, f32[72,128]{1,0:T(8,128)S(1)}, u32[]{:S(2)}, u32[]{:S(2)}) collective-permute-start(f32[72,128]{1,0:T(8,128)S(1)} %add_add_fusion.2), channel_id=1, source_target_pairs={{0,1},{1,0},{2,3},{3,2},{4,5},{5,4},{6,7},{7,6},{8,9},{9,8},{10,11... | collective-permute-start | bytes 110600 | tf_op jit(solution)/shard_map/ppermute | solution.py:393
  36.7 0.8 %collective-permute-done.10 = f32[72,128]{1,0:T(8,128)S(1)} collective-permute-done((f32[72,128]{1,0:T(8,128)S(1)}, f32[72,128]{1,0:T(8,128)S(1)}, u32[]{:S(2)}, u32[]{:S(2)}) %collective-permute-start.10) | collective-permute-done | bytes 36896 | tf_op jit(solution)/shard_map/ppermute | solution.py:393
  37.5 0.4 collective-permute-done.9
  37.9 0.6 collective-permute-done.8
  38.5 5.2 %collective-permute-start.13 = (f32[72,128]{1,0:T(8,128)S(1)}, f32[72,128]{1,0:T(8,128)S(1)}, u32[]{:S(2)}, u32[]{:S(2)}) collective-permute-start(f32[72,128]{1,0:T(8,128)S(1)} %add_add_fusion.1), channel_id=1, source_target_pairs={{0,12},{1,13},{2,14},{3,15},{4,8},{5,9},{6,10},{7,11},{8,4},{9,5},... | collective-permute-start | bytes 110600 | tf_op jit(solution)/shard_map/ppermute | solution.py:393
  43.7 0.0 collective-permute-start.12
  43.7 0.4 collective-permute-start.11
  44.1 1.1 %collective-permute-done.13 = f32[72,128]{1,0:T(8,128)S(1)} collective-permute-done((f32[72,128]{1,0:T(8,128)S(1)}, f32[72,128]{1,0:T(8,128)S(1)}, u32[]{:S(2)}, u32[]{:S(2)}) %collective-permute-start.13) | collective-permute-done | bytes 36896 | tf_op jit(solution)/shard_map/ppermute | solution.py:393
  45.2 2.3 %collective-permute-done.12 = f32[72,128]{1,0:T(8,128)S(1)} collective-permute-done((f32[72,128]{1,0:T(8,128)S(1)}, f32[72,128]{1,0:T(8,128)S(1)}, u32[]{:S(2)}, u32[]{:S(2)}) %collective-permute-start.12) | collective-permute-done | bytes 36896 | tf_op jit(solution)/shard_map/ppermute | solution.py:393
  47.4 0.0 collective-permute-done.11
  47.4 0.7 %collective-permute-start.14 = (f32[72,128]{1,0:T(8,128)S(1)}, f32[72,128]{1,0:T(8,128)S(1)}, u32[]{:S(2)}, u32[]{:S(2)}) collective-permute-start(f32[72,128]{1,0:T(8,128)S(1)} %add_add_fusion.partial_ref), channel_id=1, source_target_pairs={{0,28},{1,29},{2,30},{3,31},{4,24},{5,25},{6,26},{7,27},{8,20},{9,... | collective-permute-start | bytes 110600 | tf_op jit(solution)/shard_map/ppermute | solution.py:393
  48.2 0.0 copy-done
  48.2 3.1 %shard_map.70 = (bf16[32,32,256]{2,1,0:T(8,128)(2,1)}, f32[72,128]{1,0:T(8,128)S(1)}) custom-call(bf16[1024,256]{1,0:T(8,128)(2,1)S(1)} %get-tuple-element.19.x_ref, bf16[1024,256]{1,0:T(8,128)(2,1)S(1)} %get-tuple-element.20.cot_ref, bf16[16,1024]{1,0:T(8,128)(2,1)S(1)} %collective-permute-done.core_ref, ...), custom_call_target="tpu_custom_call" | custom-call | flops 2000000000 | bytes 3825664 | tf_op jit(solution)/shard_map/pallas_call | solution.py:40
  51.3 0.3 collective-permute-done.14
  51.7 6.1 %collective-permute-start.15 = (f32[72,128]{1,0:T(8,128)S(1)}, f32[72,128]{1,0:T(8,128)S(1)}, u32[]{:S(2)}, u32[]{:S(2)}) collective-permute-start(f32[72,128]{1,0:T(8,128)S(1)} %add.62.mine_ref), channel_id=1, source_target_pairs={{0,64},{1,65},{2,66},{3,67},{4,68},{5,69},{6,70},{7,71},{8,72},{9,... | collective-permute-start | bytes 110600 | tf_op jit(solution)/shard_map/ppermute | solution.py:393
  57.7 0.9 %collective-permute-done.15.other_ref = f32[72,128]{1,0:T(8,128)S(1)} collective-permute-done((f32[72,128]{1,0:T(8,128)S(1)}, f32[72,128]{1,0:T(8,128)S(1)}, u32[]{:S(2)}, u32[]{:S(2)}) %collective-permute-start.15) | collective-permute-done | bytes 36896 | tf_op jit(solution)/shard_map/ppermute | solution.py:393
  58.6 1.0 %shard_map.71 = (f32[3,3,32,32]{3,2,1,0:T(8,128)}, f32[3,3,32,32]{3,2,1,0:T(8,128)}) custom-call(f32[72,128]{1,0:T(8,128)S(1)} %add.62.mine_ref, f32[72,128]{1,0:T(8,128)S(1)} %collective-permute-done.15.other_ref), custom_call_target="tpu_custom_call" | custom-call | flops 1000000 | bytes 147456 | tf_op jit(solution)/shard_map/pallas_call | solution.py:40
  (9 shorter events, 0.1 us)
Async XLA Ops:
  4.0 6.2 %collective-permute-start = (bf16[16,1024]{1,0:T(8,128)(2,1)S(1)}, bf16[16,1024]{1,0:T(8,128)(2,1)S(1)}, u32[]{:S(2)}, u32[]{:S(2)}) collective-permute-start(bf16[16,1024]{1,0:T(8,128)(2,1)S(1)} %get-tuple-element.21), channel_id=1, source_target_pairs={{0,64},{64,0},{128,192},{192,128},{1,65},{65,1},{129,193},{193,129... | collective-permute-start | bytes 98312 | tf_op jit(solution)/shard_map/ppermute | solution.py:420
  7.4 6.7 %collective-permute-start.1 = (bf16[16,1024]{1,0:T(8,128)(2,1)S(1)}, bf16[16,1024]{1,0:T(8,128)(2,1)S(1)}, u32[]{:S(2)}, u32[]{:S(2)}) collective-permute-start(bf16[16,1024]{1,0:T(8,128)(2,1)S(1)} %get-tuple-element.22), channel_id=1, source_target_pairs={{64,128},{128,64},{65,129},{129,65},{66,130},{130,66},{67,131},{13... | collective-permute-start | bytes 98312 | tf_op jit(solution)/shard_map/ppermute | solution.py:420
  14.3 10.5 %collective-permute-start.2 = (bf16[144,256]{1,0:T(8,128)(2,1)S(1)}, bf16[144,256]{1,0:T(8,128)(2,1)S(1)}, u32[]{:S(2)}, u32[]{:S(2)}) collective-permute-start(bf16[144,256]{1,0:T(8,128)(2,1)S(1)} %pad_maximum_fusion), channel_id=1, source_target_pairs={{0,1},{1,2},{2,3},{3,4},{4,5},{5,6},{6,7},{7,8},{8,9},{9,10},{10,1... | collective-permute-start | bytes 221192 | tf_op jit(solution)/shard_map/ppermute | solution.py:456
  14.4 10.4 %collective-permute-start.3 = (bf16[144,256]{1,0:T(8,128)(2,1)S(1)}, bf16[144,256]{1,0:T(8,128)(2,1)S(1)}, u32[]{:S(2)}, u32[]{:S(2)}) collective-permute-start(bf16[144,256]{1,0:T(8,128)(2,1)S(1)} %pad_maximum_fusion.1), channel_id=1, source_target_pairs={{1,0},{2,1},{3,2},{4,3},{5,4},{6,5},{7,6},{8,7},{9,8},{10,9},{11,1... | collective-permute-start | bytes 221192 | tf_op jit(solution)/shard_map/ppermute | solution.py:457
  25.9 22.2 %copy-start = (bf16[32,32,256]{2,1,0:T(8,128)(2,1)S(1)}, bf16[32,32,256]{2,1,0:T(8,128)(2,1)}, u32[]{:S(2)}) copy-start(bf16[32,32,256]{2,1,0:T(8,128)(2,1)} %raw_ref.1) | copy-start | bytes 1572868
  26.0 1.3 %collective-permute-start.4 = (f32[72,128]{1,0:T(8,128)S(1)}, f32[72,128]{1,0:T(8,128)S(1)}, u32[]{:S(2)}, u32[]{:S(2)}) collective-permute-start(f32[72,128]{1,0:T(8,128)S(1)} %dynamic-slice_bitcast_fusion), channel_id=1, source_target_pairs={{0,64},{1,65},{2,66},{3,67},{4,68},{5,69},{6,70},{7,71},{8,72},{9,... | collective-permute-start | bytes 110600 | tf_op jit(solution)/shard_map/ppermute | solution.py:393
  27.3 4.0 %collective-permute-start.7 = (f32[72,128]{1,0:T(8,128)S(1)}, f32[72,128]{1,0:T(8,128)S(1)}, u32[]{:S(2)}, u32[]{:S(2)}) collective-permute-start(f32[72,128]{1,0:T(8,128)S(1)} %bitcast_add_fusion), channel_id=1, source_target_pairs={{0,160},{1,161},{2,162},{3,163},{4,164},{5,165},{6,166},{7,167},{8... | collective-permute-start | bytes 110600 | tf_op jit(solution)/shard_map/ppermute | solution.py:393
  29.1 4.3 %collective-permute-start.6 = (f32[72,128]{1,0:T(8,128)S(1)}, f32[72,128]{1,0:T(8,128)S(1)}, u32[]{:S(2)}, u32[]{:S(2)}) collective-permute-start(f32[72,128]{1,0:T(8,128)S(1)} %bitcast_add_fusion), channel_id=1, source_target_pairs={{0,128},{1,129},{2,130},{3,131},{4,132},{5,133},{6,134},{7,135},{8... | collective-permute-start | bytes 110600 | tf_op jit(solution)/shard_map/ppermute | solution.py:393
  29.8 3.6 %collective-permute-start.5 = (f32[72,128]{1,0:T(8,128)S(1)}, f32[72,128]{1,0:T(8,128)S(1)}, u32[]{:S(2)}, u32[]{:S(2)}) collective-permute-start(f32[72,128]{1,0:T(8,128)S(1)} %bitcast_add_fusion), channel_id=1, source_target_pairs={{0,32},{1,33},{2,34},{3,35},{4,36},{5,37},{6,38},{7,39},{8,40},{9,... | collective-permute-start | bytes 110600 | tf_op jit(solution)/shard_map/ppermute | solution.py:393
  33.4 4.1 %collective-permute-start.10 = (f32[72,128]{1,0:T(8,128)S(1)}, f32[72,128]{1,0:T(8,128)S(1)}, u32[]{:S(2)}, u32[]{:S(2)}) collective-permute-start(f32[72,128]{1,0:T(8,128)S(1)} %add_add_fusion.2), channel_id=1, source_target_pairs={{0,3},{1,2},{2,1},{3,0},{4,7},{5,6},{6,5},{7,4},{8,11},{9,10},{10,... | collective-permute-start | bytes 110600 | tf_op jit(solution)/shard_map/ppermute | solution.py:393
  33.5 4.4 %collective-permute-start.9 = (f32[72,128]{1,0:T(8,128)S(1)}, f32[72,128]{1,0:T(8,128)S(1)}, u32[]{:S(2)}, u32[]{:S(2)}) collective-permute-start(f32[72,128]{1,0:T(8,128)S(1)} %add_add_fusion.2), channel_id=1, source_target_pairs={{0,2},{1,3},{2,0},{3,1},{4,6},{5,7},{6,4},{7,5},{8,10},{9,11},{10,... | collective-permute-start | bytes 110600 | tf_op jit(solution)/shard_map/ppermute | solution.py:393
  33.6 4.9 %collective-permute-start.8 = (f32[72,128]{1,0:T(8,128)S(1)}, f32[72,128]{1,0:T(8,128)S(1)}, u32[]{:S(2)}, u32[]{:S(2)}) collective-permute-start(f32[72,128]{1,0:T(8,128)S(1)} %add_add_fusion.2), channel_id=1, source_target_pairs={{0,1},{1,0},{2,3},{3,2},{4,5},{5,4},{6,7},{7,6},{8,9},{9,8},{10,11... | collective-permute-start | bytes 110600 | tf_op jit(solution)/shard_map/ppermute | solution.py:393
  38.5 6.7 %collective-permute-start.13 = (f32[72,128]{1,0:T(8,128)S(1)}, f32[72,128]{1,0:T(8,128)S(1)}, u32[]{:S(2)}, u32[]{:S(2)}) collective-permute-start(f32[72,128]{1,0:T(8,128)S(1)} %add_add_fusion.1), channel_id=1, source_target_pairs={{0,12},{1,13},{2,14},{3,15},{4,8},{5,9},{6,10},{7,11},{8,4},{9,5},... | collective-permute-start | bytes 110600 | tf_op jit(solution)/shard_map/ppermute | solution.py:393
  43.7 3.7 %collective-permute-start.12 = (f32[72,128]{1,0:T(8,128)S(1)}, f32[72,128]{1,0:T(8,128)S(1)}, u32[]{:S(2)}, u32[]{:S(2)}) collective-permute-start(f32[72,128]{1,0:T(8,128)S(1)} %add_add_fusion.1), channel_id=1, source_target_pairs={{0,8},{1,9},{2,10},{3,11},{4,12},{5,13},{6,14},{7,15},{8,0},{9,1},... | collective-permute-start | bytes 110600 | tf_op jit(solution)/shard_map/ppermute | solution.py:393
  43.7 3.7 %collective-permute-start.11 = (f32[72,128]{1,0:T(8,128)S(1)}, f32[72,128]{1,0:T(8,128)S(1)}, u32[]{:S(2)}, u32[]{:S(2)}) collective-permute-start(f32[72,128]{1,0:T(8,128)S(1)} %add_add_fusion.1), channel_id=1, source_target_pairs={{0,4},{1,5},{2,6},{3,7},{4,0},{5,1},{6,2},{7,3},{8,12},{9,13},{10,... | collective-permute-start | bytes 110600 | tf_op jit(solution)/shard_map/ppermute | solution.py:393
  47.4 4.2 %collective-permute-start.14 = (f32[72,128]{1,0:T(8,128)S(1)}, f32[72,128]{1,0:T(8,128)S(1)}, u32[]{:S(2)}, u32[]{:S(2)}) collective-permute-start(f32[72,128]{1,0:T(8,128)S(1)} %add_add_fusion.partial_ref), channel_id=1, source_target_pairs={{0,28},{1,29},{2,30},{3,31},{4,24},{5,25},{6,26},{7,27},{8,20},{9,... | collective-permute-start | bytes 110600 | tf_op jit(solution)/shard_map/ppermute | solution.py:393
  51.7 6.9 %collective-permute-start.15 = (f32[72,128]{1,0:T(8,128)S(1)}, f32[72,128]{1,0:T(8,128)S(1)}, u32[]{:S(2)}, u32[]{:S(2)}) collective-permute-start(f32[72,128]{1,0:T(8,128)S(1)} %add.62.mine_ref), channel_id=1, source_target_pairs={{0,64},{1,65},{2,66},{3,67},{4,68},{5,69},{6,70},{7,71},{8,72},{9,... | collective-permute-start | bytes 110600 | tf_op jit(solution)/shard_map/ppermute | solution.py:393

commit v4 on v3

--- a/solution.py
+++ b/solution.py
@@ -13,7 +13,7 @@
 GROUP = 6
 WINDOW = GROUP + 2
 HALF = 16
-PARAMS = pltpu.CompilerParams(vmem_limit_bytes=40 * 2**20)
+PARAMS = pltpu.CompilerParams(vmem_limit_bytes=16 * 2**20)
 
 
 def dot(left, right):
@@ -56,56 +56,48 @@
     return lax.axis_index("lat") % 2
 
 
-def pack_kernel(x_ref, cot_ref, one_hbm, two_hbm, xl_ref, cl_ref, core_ref, mid_ref, first_ref, back_ref, last_ref,
-                raw, one_ref, two_ref, perm, sems):
-    channels, lon_cells, lat_cells = x_ref.shape
+def border_kernel(x_hbm, cot_hbm, one_hbm, two_hbm, raw_ref, one_ref, two_ref, perm_ref, core_ref, mid_ref, sems):
+    channels, lon_cells, lat_cells = x_hbm.shape
     parts = lon_cells // HALF
-    pieces = 2
-    span = channels // pieces
-    kernels = [
-        pltpu.make_async_copy(source, target, sems.at[place])
-        for place, (source, target) in enumerate(((one_hbm, one_ref), (two_hbm, two_ref)))
-    ]
-    copies = []
-    for place, source in enumerate((x_ref, cot_ref)):
+    pieces = [(one_hbm, one_ref), (two_hbm, two_ref)]
+    for place, source in enumerate((x_hbm, cot_hbm)):
         for part in range(parts):
-            for piece in range(pieces):
-                number = (place * parts + part) * pieces + piece
-                some = pl.ds(piece * span, span)
-                copies.append(
-                    pltpu.make_async_copy(
-                        source.at[some, pl.ds(part * HALF, HALF), :],
-                        raw.at[place * parts + part, some],
-                        sems.at[2 + number],
-                    )
-                )
-    for copy in (*kernels, *copies):
+            pieces.append((source.at[:, pl.ds(part * HALF, HALF), :], raw_ref.at[place * parts + part]))
+    copies = [pltpu.make_async_copy(*piece, sems.at[number]) for number, piece in enumerate(pieces)]
+    for copy in copies:
         copy.start()
-    to_row = iota(perm.shape, 0)
-    from_row = iota(perm.shape, 1)
+    to_row = iota(perm_ref.shape, 0)
+    from_row = iota(perm_ref.shape, 1)
     moved = (to_row % channels) * HALF + to_row // channels
-    perm[...] = jnp.where(from_row == moved, 1.0, 0.0).astype(BF)
-    for copy in kernels:
-        copy.wait()
-    write_weights(one_ref, two_ref, first_ref, back_ref, last_ref)
+    perm_ref[...] = jnp.where(from_row == moved, 1.0, 0.0).astype(BF)
     odd = is_odd()
     row = iota((2 * HALF, lat_cells), 0)
     lane = iota((2 * HALF, lat_cells), 1)
     high = jnp.where(row < HALF, 1 - odd, odd)
     cell = jnp.where(high == 1, lat_cells - 2, 0) + row % 2
-    edges = jnp.zeros((2 * HALF, xl_ref.shape[0]), F32)
+    chosen = [
+        (((row % HALF) // 2 == place) & (lane == cell)).astype(F32).astype(BF) for place in range(2)
+    ]
     rows = HALF * channels
+    for copy in copies:
+        copy.wait()
+    for part in range(parts):
+        edges = sum(
+            dot_lanes(chosen[place], raw_ref[place * parts + part].reshape(rows, lat_cells)) for place in range(2)
+        )
+        edges = dot_lanes(edges.astype(BF), perm_ref[...]).astype(BF)
+        core_ref[:, part * rows : (part + 1) * rows] = edges[:HALF]
+        mid_ref[:, part * rows : (part + 1) * rows] = edges[HALF:]
+
+
+def row_kernel(raw_ref, perm_ref, one_ref, two_ref, xl_ref, cl_ref, first_ref, back_ref, last_ref):
+    rows = perm_ref.shape[0]
+    parts = xl_ref.shape[0] // rows
     for place, target in enumerate((xl_ref, cl_ref)):
         for part in range(parts):
-            number = place * parts + part
-            for copy in copies[number * pieces : (number + 1) * pieces]:
-                copy.wait()
-            block = raw[number].reshape(rows, lat_cells)
-            target[part * rows : (part + 1) * rows, :] = dot(perm[...], block).astype(BF)
-        chosen = ((row % HALF) // 2 == place) & (lane == cell)
-        edges = edges + dot_lanes(chosen.astype(F32).astype(BF), target[...])
-    core_ref[...] = edges[:HALF].astype(BF)
-    mid_ref[...] = edges[HALF:].astype(BF)
+            block = raw_ref[place * parts + part].reshape(rows, target.shape[1])
+            target[part * rows : (part + 1) * rows, :] = dot(perm_ref[...], block).astype(BF)
+    write_weights(one_ref, two_ref, first_ref, back_ref, last_ref)
 
 
 def write_weights(one_ref, two_ref, first_ref, back_ref, last_ref):
@@ -255,11 +247,11 @@
     return [main[0], main[1], third]
 
 
-def last_kernel(x_ref, cot_ref, core_ref, mid_ref, left_ref, right_ref, first_ref, back_ref, low_ref, pre_ref,
-                high_ref, last_ref, raw_ref, partial_ref, out_ref, passed_ref, rows_buffer, strips, ps, placed, result, sems):
+def outer_kernel(x_ref, cot_ref, core_ref, mid_ref, left_ref, right_ref, first_ref, back_ref, low_ref, pre_ref,
+                 high_ref, partial_ref, ps, passed_ref, rows_buffer, strips):
     passed_ref[...] = partial_ref[...]
     lat_cells = x_ref.shape[1]
-    channels = out_ref.shape[0]
+    channels = low_ref.shape[0] // 2
     two = 2 * channels
     own_rows = x_ref.shape[0]
     wide_rows = own_rows + 2 * two
@@ -319,7 +311,12 @@
     rows_buffer[two : wide - two, :] = pre_ref[...]
     rows_buffer[wide - two : wide, :] = high_ref[...]
     write_shifted(rows_buffer[0:wide, :], columns, ps, slice(0, wide))
-    lon_cells = out_ref.shape[1]
+
+
+def last_kernel(ps, last_ref, raw_ref, partial_ref, out_ref, passed_ref, placed, result, sems):
+    passed_ref[...] = partial_ref[...]
+    channels, lon_cells, lat_cells = out_ref.shape
+    parts = lon_cells // HALF
     copies = []
     done = 0
     for first in range(0, lon_cells, GROUP):
@@ -336,7 +333,7 @@
             for tile in range(lat_cells // 128):
                 lanes = slice(tile * 128, (tile + 1) * 128)
                 block = placed[tile].reshape(channels, lon_cells, 128)[:, part, :]
-                block = block + raw_ref[:, part, lanes].astype(F32)
+                block = block + raw_ref[parts + done // HALF, :, :, lanes].astype(F32)
                 result[:, part, lanes] = block.astype(BF)
             copy = pltpu.make_async_copy(
                 result.at[:, pl.ds(done, HALF), :], out_ref.at[:, pl.ds(done, HALF), :], sems.at[done // HALF]
@@ -393,22 +390,25 @@
     return lax.ppermute(value, ("lat", "lon"), pairs(counts, partner))
 
 
-def sum_of_four(value, partner):
-    near, far, wrap = [exchange(value, partner(mask)) for mask in (1, 2, 3)]
-    return (value + near) + (far + wrap)
-
-
-def sum_everywhere(halves, between):
+def sum_of_four(value, partner, masks, beside=None):
+    first, second, third = [exchange(value, partner(mask)) for mask in masks]
+    result = None
+    if beside is not None:
+        result, value = beside(value)
+    return (value + first) + (second + third), result
+
+
+def sum_everywhere(halves, widen, finish):
     core = lax.axis_index("lat") % 2
     other_core = lambda lat, lon: (lat ^ 1, lon)
     mine = lax.dynamic_index_in_dim(halves, core, 0, False)
     theirs = lax.dynamic_index_in_dim(halves, 1 - core, 0, False)
     total = mine + exchange(theirs, other_core)
-    total = sum_of_four(total, x_partner)
-    total = sum_of_four(total, y_partner)
-    total = sum_of_four(total, z_partner)
+    total, _ = sum_of_four(total, x_partner, (1, 3, 2))
+    total, shifted = sum_of_four(total, y_partner, (1, 3, 2), widen)
+    total, _ = sum_of_four(total, z_partner, (1, 2, 3))
     far = exchange(total, z_partner(7))
-    input_grad, total = between(total)
+    input_grad, total = finish(shifted, total)
     total = total + far
     other = exchange(total, other_core)
     return total, other, input_grad
@@ -417,7 +417,8 @@
 def lat_exchange(core, mid):
     count = lax.axis_size("lat")
     inner = [pair for low in range(1, count - 1, 2) for pair in ((low, low + 1), (low + 1, low))]
-    return lax.ppermute(core, "lat", [(i, i ^ 1) for i in range(count)]), lax.ppermute(mid, "lat", inner)
+    mid = lax.ppermute(mid, "lat", inner)
+    return lax.ppermute(core, "lat", [(i, i ^ 1) for i in range(count)]), mid
 
 
 def on_device(inputs, kernel_one, kernel_two, cotangent):
@@ -425,18 +426,20 @@
     cells = lon_cells * lat_cells * lax.axis_size("lat") * lax.axis_size("lon")
     rows = channels * lon_cells
     two = 2 * channels
+    parts = lon_cells // HALF
     weights = [shape(3, GROUP * channels, WINDOW * channels)] * 3
-    x_rows, cot_rows, core_out, mid_out, first, back, last = call(
-        pack_kernel,
-        [shape(rows, lat_cells), shape(rows, lat_cells), shape(HALF, rows), shape(HALF, rows), *weights],
+    raw, one, two_kernel, perm, core_out, mid_out = call(
+        border_kernel,
         [
-            pltpu.VMEM((2 * lon_cells // HALF, channels, HALF, lat_cells), BF),
-            pltpu.VMEM(kernel_one.shape, BF),
-            pltpu.VMEM(kernel_two.shape, BF),
-            pltpu.VMEM((HALF * channels, HALF * channels), BF),
-            pltpu.SemaphoreType.DMA((2 + 4 * lon_cells // HALF,)),
+            shape(2 * parts, channels, HALF, lat_cells),
+            shape(*kernel_one.shape),
+            shape(*kernel_two.shape),
+            shape(HALF * channels, HALF * channels),
+            shape(HALF, rows),
+            shape(HALF, rows),
         ],
-        10**9,
+        [pltpu.SemaphoreType.DMA((2 + 2 * parts,))],
+        10**8,
         inputs,
         cotangent,
         kernel_one,
@@ -444,6 +447,16 @@
         hbm_in=(0, 1, 2, 3),
     )
     core_in, mid_in = lat_exchange(core_out, mid_out)
+    x_rows, cot_rows, first, back, last = call(
+        row_kernel,
+        [shape(rows, lat_cells), shape(rows, lat_cells), *weights],
+        [],
+        10**9,
+        raw,
+        perm,
+        one,
+        two_kernel,
+    )
 
     def message(part):
         pieces = jnp.concatenate([core_in[:, part], mid_in[:, part]], 1)
@@ -473,25 +486,34 @@
         10**9,
         x_rows, cot_rows, core_in, mid_in, from_left, from_right, first, back, inner_grads,
     )
-    def finish(partial):
+    def widen(partial):
+        return call(
+            outer_kernel,
+            [shape(3, rows + two, lat_cells), shape(*partial.shape, dtype=F32)],
+            [
+                pltpu.VMEM((rows + 2 * two, lat_cells), BF),
+                pltpu.VMEM((2, HALF, rows + 2 * two), F32),
+            ],
+            10**9,
+            x_rows, cot_rows, core_in, mid_in, from_left, from_right, first, back,
+            pre_low, pre_inner, pre_high, partial,
+        )
+
+    def finish(shifted, partial):
         return call(
             last_kernel,
             [shape(channels, lon_cells, lat_cells), shape(*partial.shape, dtype=F32)],
             [
-                pltpu.VMEM((rows + 2 * two, lat_cells), BF),
-                pltpu.VMEM((2, HALF, rows + 2 * two), F32),
-                pltpu.VMEM((3, rows + two, lat_cells), BF),
                 pltpu.VMEM((lat_cells // 128, rows, 128), F32),
                 pltpu.VMEM((channels, lon_cells, lat_cells), BF),
                 pltpu.SemaphoreType.DMA((lon_cells // HALF,)),
             ],
             2 * 10**9,
-            x_rows, cot_rows, core_in, mid_in, from_left, from_right, first, back,
-            pre_low, pre_inner, pre_high, last, cotangent, partial,
+            shifted, last, raw, partial,
             hbm_out=(0,),
         )
 
-    mine, other, input_grad = sum_everywhere(grads, finish)
+    mine, other, input_grad = sum_everywhere(grads, widen, finish)
     grad_one, grad_two = call(
         functools.partial(result_kernel, 1.0 / math.sqrt(cells)),
         [shape(3, 3, channels, channels, dtype=F32)] * 2,

time: 59.7 us -> 58.7 us (0.983)
  starting transfers between devices: 32.6 us -> 30 us
  other arithmetic: 0.21 us -> 0.98 us
  local copies, waits for them, and re-layouts: 0.18 us -> 0.8 us
    ppermute x12, starting transfers between devices: 19.1 us -> 16.5 us  [exchange(): return lax.ppermute(value, ('lat', 'lon'), pairs(counts, partner))]
    ppermute x12, waiting for transfers between devices: 10.3 us -> 11.5 us  [exchange(): return lax.ppermute(value, ('lat', 'lon'), pairs(counts, partner))]
    ppermute x2, waiting for transfers between devices: 3.78 us -> 2.88 us  [the longest x1 2.88 us: lat_exchange(): mid = lax.ppermute(mid, 'lat', inner)]
    add x1, other arithmetic: 0.01 us -> 0.77 us  [sum_everywhere(): total = mine + exchange(theirs, other_core)]
    squeeze x1, local copies, waits for them, and re-layouts: 0.01 us -> 0.63 us  [sum_everywhere(): theirs = lax.dynamic_index_in_dim(halves, 1 - core, 0, False)]
    pallas_call x5 -> x7, Pallas kernels: 11.7 us -> 11.6 us  [call(): pl.pallas_call(kernel, out_shape=outs, in_specs=[pl.BlockSpec(memory_spac...]
  transfers between devices with their start and end apart: 16 -> 16, of which waited for: 11 -> 10; matrix products, arithmetic and copies ran while one was open for 0% -> 0% of each run, Pallas kernels for 10% -> 13%
where the time goes in v4:
time: 58.7 us; the launch traced here: 58.5 us
  starting transfers between devices  30 us (51%)
  waiting for transfers between devices  14.4 us (25%)
  Pallas kernels  11.6 us (20%)
  other arithmetic  0.98 us (2%)
  local copies, waits for them, and re-layouts  0.8 us (1%)
  between operations  0.8 us (1%)
    ppermute x12, starting transfers between devices, exchange(): return lax.ppermute(value, ('lat', 'lon'), pairs(counts, partner))  16.5 us
    pallas_call x7, Pallas kernels, call(): pl.pallas_call(kernel, out_shape=outs, in_specs=[pl.BlockSpec(memory_spac...  11.6 us
    ppermute x12, waiting for transfers between devices, exchange(): return lax.ppermute(value, ('lat', 'lon'), pairs(counts, partner))  11.5 us
    ppermute x1, starting transfers between devices, on_device(): lax.ppermute(to_left, 'lon', [((i + 1) % count, i) for i in range(count)])  7.27 us
    ppermute x1, starting transfers between devices, lat_exchange(): return (lax.ppermute(core, 'lat', [(i, i ^ 1) for i in range(count)]), mid)  3.32 us
    ppermute x1, waiting for transfers between devices, lat_exchange(): mid = lax.ppermute(mid, 'lat', inner)  2.88 us
    ppermute x1, starting transfers between devices, lat_exchange(): mid = lax.ppermute(mid, 'lat', inner)  2.82 us
  transfers between devices with their start and end apart: 16, of which 10 were waited for; matrix products, arithmetic and copies ran while one was open for 0% of the time, Pallas kernels for 13%

profile of v4, /device:TPU:1, one launch (start us, length us, event | category | flops | bytes accessed | tf_op | source)
XLA Modules:
  0.0 58.5 jit_solution(13562904126268306834)
XLA Ops:
  0.6 2.1 %shard_map.67 = (bf16[4,32,16,256]{3,2,1,0:T(8,128)(2,1)S(1)}, bf16[3,3,32,32]{3,2,1,0:T(8,128)(2,1)S(1)}, bf16[3,3,32,32]{3,2,1,0:T(8,128)(2,1)S(1)}, bf16[512,...) custom-call(bf16[32,32,256]{2,1,0:T(8,128)(2,1)} %x_hbm.1, ...), custom_call_target="tpu_custom_call" | custom-call | flops 100000000 | bytes 2760704 | tf_op jit(solution)/shard_map/pallas_call | solution.py:40
  2.8 3.3 %collective-permute-start = (bf16[16,1024]{1,0:T(8,128)(2,1)S(1)}, bf16[16,1024]{1,0:T(8,128)(2,1)S(1)}, u32[]{:S(2)}, u32[]{:S(2)}) collective-permute-start(bf16[16,1024]{1,0:T(8,128)(2,1)S(1)} %get-tuple-element.31), channel_id=1, source_target_pairs={{0,64},{64,0},{128,192},{192,128},{1,65},{65,1},{129,193},{193,129... | collective-permute-start | bytes 98312 | tf_op jit(solution)/shard_map/ppermute | solution.py:421
  6.1 2.8 %collective-permute-start.1 = (bf16[16,1024]{1,0:T(8,128)(2,1)S(1)}, bf16[16,1024]{1,0:T(8,128)(2,1)S(1)}, u32[]{:S(2)}, u32[]{:S(2)}) collective-permute-start(bf16[16,1024]{1,0:T(8,128)(2,1)S(1)} %get-tuple-element.32), channel_id=1, source_target_pairs={{64,128},{128,64},{65,129},{129,65},{66,130},{130,66},{67,131},{13... | collective-permute-start | bytes 98312 | tf_op jit(solution)/shard_map/ppermute | solution.py:420
  8.9 0.9 %shard_map.68 = (bf16[1024,256]{1,0:T(8,128)(2,1)S(1)}, bf16[1024,256]{1,0:T(8,128)(2,1)S(1)}, bf16[3,192,256]{2,1,0:T(8,128)(2,1)S(1)}, bf16[3,192,256]{2,1,0:T(8,128)(2,1)S(1)}, bf16[3,192,256]{2,1,0:T(8,128)(2,1)S(1)}) custom-call(bf16[4,32,16,256]{3,2,1,0:T(8,128)(2,1)S(1)} %get-tuple-element.25.raw_ref, ...), custom_call_target="tpu_custom_call" | custom-call | flops 1000000000 | bytes 3543040 | tf_op jit(solution)/shard_map/pallas_call | solution.py:40
  9.8 0.0 copy-start
  9.8 0.0 collective-permute-done.core_ref
  9.9 0.1 fusion.8
  9.9 2.9 %collective-permute-done.1.mid_ref = bf16[16,1024]{1,0:T(8,128)(2,1)S(1)} collective-permute-done((bf16[16,1024]{1,0:T(8,128)(2,1)S(1)}, bf16[16,1024]{1,0:T(8,128)(2,1)S(1)}, u32[]{:S(2)}, u32[]{:S(2)}) %collective-permute-start.1) | collective-permute-done | bytes 32800 | tf_op jit(solution)/shard_map/ppermute | solution.py:420
  12.8 0.1 fusion.9
  12.9 0.1 fusion.4
  13.0 0.0 copy-done
  13.0 0.1 collective-permute-start.2
  13.1 0.1 fusion.5
  13.1 7.3 %collective-permute-start.3 = (bf16[144,256]{1,0:T(8,128)(2,1)S(1)}, bf16[144,256]{1,0:T(8,128)(2,1)S(1)}, u32[]{:S(2)}, u32[]{:S(2)}) collective-permute-start(bf16[144,256]{1,0:T(8,128)(2,1)S(1)} %pad_maximum_fusion.1), channel_id=1, source_target_pairs={{1,0},{2,1},{3,2},{4,3},{5,4},{6,5},{7,6},{8,7},{9,8},{10,9},{11,1... | collective-permute-start | bytes 221192 | tf_op jit(solution)/shard_map/ppermute | solution.py:470
  20.4 3.1 %shard_map.69 = (bf16[960,256]{1,0:T(8,128)(2,1)S(1)}, f32[2,3,32,128]{3,2,1,0:T(8,128)S(1)}) custom-call(bf16[1024,256]{1,0:T(8,128)(2,1)S(1)} %get-tuple-element.29.x_ref, bf16[1024,256]{1,0:T(8,128)(2,1)S(1)} %get-tuple-element.30.cot_ref, bf16[16,1024]{1,0:T(8,128)(2,1)S(1)} %collective-permute-done.core_ref, ...), custom_call_target="tpu_custom_call" | custom-call | flops 4000000000 | bytes 2293760 | tf_op jit(solution)/shard_map/pallas_call | solution.py:40
  23.5 0.0 collective-permute-done.2.left_ref
  23.6 0.0 collective-permute-done.3.right_ref
  23.6 1.1 %shard_map.70 = (bf16[64,256]{1,0:T(8,128)(2,1)S(1)}, bf16[64,256]{1,0:T(8,128)(2,1)S(1)}, f32[2,72,128]{2,1,0:T(8,128)S(1)}) custom-call(bf16[1024,256]{1,0:T(8,128)(2,1)S(1)} %get-tuple-element.29.x_ref, bf16[1024,256]{1,0:T(8,128)(2,1)S(1)} %get-tuple-element.30.cot_ref, bf16[16,1024]{1,0:T(8,128)(2,1)S(1)} %collective-permute-done.core_ref, ...), custom_call_target="tpu_custom_call" | custom-call | flops 1000000000 | bytes 2088960 | tf_op jit(solution)/shard_map/pallas_call | solution.py:40
  24.7 0.6 %dynamic-slice_bitcast_fusion = f32[72,128]{1,0:T(8,128)} fusion(f32[2,72,128]{2,1,0:T(8,128)S(1)} %get-tuple-element.39, s32[]{:T(128)S(6)} %select_n.16), kind=kLoop, calls=%fused_computation.6 | loop fusion | bytes 73732 | tf_op jit(solution)/shard_map/jit(dynamic_index_in_dim)/squeeze | solution.py:405
  25.3 0.0 collective-permute-start.4
  25.3 1.6 %collective-permute-done.4 = f32[72,128]{1,0:T(8,128)} collective-permute-done((f32[72,128]{1,0:T(8,128)}, f32[72,128]{1,0:T(8,128)}, u32[]{:S(2)}, u32[]{:S(2)}) %collective-permute-start.4) | collective-permute-done | bytes 36896 | tf_op jit(solution)/shard_map/ppermute | solution.py:390
  26.9 0.8 %bitcast_add_fusion = f32[72,128]{1,0:T(8,128)S(1)} fusion(f32[72,128]{1,0:T(8,128)} %collective-permute-done.4, f32[2,72,128]{2,1,0:T(8,128)S(1)} %get-tuple-element.39, s32[]{:T(128)S(6)} %select_n.15), kind=kLoop, calls=%fused_computation.2 | loop fusion | flops 9216 | bytes 110596 | tf_op jit(solution)/shard_map/add | solution.py:406
  27.6 2.4 %collective-permute-start.7 = (f32[72,128]{1,0:T(8,128)S(1)}, f32[72,128]{1,0:T(8,128)S(1)}, u32[]{:S(2)}, u32[]{:S(2)}) collective-permute-start(f32[72,128]{1,0:T(8,128)S(1)} %bitcast_add_fusion), channel_id=1, source_target_pairs={{0,128},{1,129},{2,130},{3,131},{4,132},{5,133},{6,134},{7,135},{8... | collective-permute-start | bytes 110600 | tf_op jit(solution)/shard_map/ppermute | solution.py:390
  30.1 0.2 collective-permute-start.6
  30.3 0.0 collective-permute-start.5
  30.3 1.7 %collective-permute-done.7 = f32[72,128]{1,0:T(8,128)S(1)} collective-permute-done((f32[72,128]{1,0:T(8,128)S(1)}, f32[72,128]{1,0:T(8,128)S(1)}, u32[]{:S(2)}, u32[]{:S(2)}) %collective-permute-start.7) | collective-permute-done | bytes 36896 | tf_op jit(solution)/shard_map/ppermute | solution.py:390
  32.0 2.1 %collective-permute-done.6 = f32[72,128]{1,0:T(8,128)S(1)} collective-permute-done((f32[72,128]{1,0:T(8,128)S(1)}, f32[72,128]{1,0:T(8,128)S(1)}, u32[]{:S(2)}, u32[]{:S(2)}) %collective-permute-start.6) | collective-permute-done | bytes 36896 | tf_op jit(solution)/shard_map/ppermute | solution.py:390
  34.1 0.0 collective-permute-done.5
  34.1 0.1 collective-permute-start.10
  34.2 0.1 collective-permute-start.9
  34.3 2.5 %collective-permute-start.8 = (f32[72,128]{1,0:T(8,128)S(1)}, f32[72,128]{1,0:T(8,128)S(1)}, u32[]{:S(2)}, u32[]{:S(2)}) collective-permute-start(f32[72,128]{1,0:T(8,128)S(1)} %add_add_fusion.2.partial_ref), channel_id=1, source_target_pairs={{0,1},{1,0},{2,3},{3,2},{4,5},{5,4},{6,7},{7,6},{8,9},{9,8},{10,11... | collective-permute-start | bytes 110600 | tf_op jit(solution)/shard_map/ppermute | solution.py:390
  36.8 1.2 %shard_map.71 = (bf16[3,1088,256]{2,1,0:T(8,128)(2,1)S(1)}, f32[72,128]{1,0:T(8,128)S(1)}) custom-call(bf16[1024,256]{1,0:T(8,128)(2,1)S(1)} %get-tuple-element.29.x_ref, bf16[1024,256]{1,0:T(8,128)(2,1)S(1)} %get-tuple-element.30.cot_ref, bf16[16,1024]{1,0:T(8,128)(2,1)S(1)} %collective-permute-done.core_ref, ...), custom_call_target="tpu_custom_call" | custom-call | flops 1000000000 | bytes 4153344 | tf_op jit(solution)/shard_map/pallas_call | solution.py:40
  38.0 0.6 %collective-permute-done.10 = f32[72,128]{1,0:T(8,128)S(1)} collective-permute-done((f32[72,128]{1,0:T(8,128)S(1)}, f32[72,128]{1,0:T(8,128)S(1)}, u32[]{:S(2)}, u32[]{:S(2)}) %collective-permute-start.10) | collective-permute-done | bytes 36896 | tf_op jit(solution)/shard_map/ppermute | solution.py:390
  38.6 0.1 collective-permute-done.9
  38.7 0.0 collective-permute-done.8
  38.7 4.2 %collective-permute-start.13 = (f32[72,128]{1,0:T(8,128)S(1)}, f32[72,128]{1,0:T(8,128)S(1)}, u32[]{:S(2)}, u32[]{:S(2)}) collective-permute-start(f32[72,128]{1,0:T(8,128)S(1)} %add_add_fusion.1), channel_id=1, source_target_pairs={{0,12},{1,13},{2,14},{3,15},{4,8},{5,9},{6,10},{7,11},{8,4},{9,5},... | collective-permute-start | bytes 110600 | tf_op jit(solution)/shard_map/ppermute | solution.py:390
  42.9 0.0 collective-permute-start.12
  42.9 0.6 collective-permute-start.11
  43.5 0.8 %collective-permute-done.13 = f32[72,128]{1,0:T(8,128)S(1)} collective-permute-done((f32[72,128]{1,0:T(8,128)S(1)}, f32[72,128]{1,0:T(8,128)S(1)}, u32[]{:S(2)}, u32[]{:S(2)}) %collective-permute-start.13) | collective-permute-done | bytes 36896 | tf_op jit(solution)/shard_map/ppermute | solution.py:390
  44.3 2.4 %collective-permute-done.12 = f32[72,128]{1,0:T(8,128)S(1)} collective-permute-done((f32[72,128]{1,0:T(8,128)S(1)}, f32[72,128]{1,0:T(8,128)S(1)}, u32[]{:S(2)}, u32[]{:S(2)}) %collective-permute-start.12) | collective-permute-done | bytes 36896 | tf_op jit(solution)/shard_map/ppermute | solution.py:390
  46.6 0.0 collective-permute-done.11
  46.7 0.4 collective-permute-start.14
  47.1 0.0 copy-done.1
  47.1 2.2 %shard_map.72 = (bf16[32,32,256]{2,1,0:T(8,128)(2,1)}, f32[72,128]{1,0:T(8,128)S(1)}) custom-call(bf16[3,1088,256]{2,1,0:T(8,128)(2,1)S(1)} %get-tuple-element.40.ps, bf16[3,192,256]{2,1,0:T(8,128)(2,1)S(1)} %copy-done.1, bf16[4,32,16,256]{3,2,1,0:T(8,128)(2,1)S(1)} %get-tuple-element.25.raw_ref, f32[72,128]{1,0:T(8,128)S(1)} %add_add_fusion.partial_ref), custom_call_target="tpu_custom_call" | custom-call | flops 2000000000 | bytes 3612672 | tf_op jit(solution)/shard_map/pallas_call | solution.py:40
  49.3 1.5 %collective-permute-done.14 = f32[72,128]{1,0:T(8,128)S(1)} collective-permute-done((f32[72,128]{1,0:T(8,128)S(1)}, f32[72,128]{1,0:T(8,128)S(1)}, u32[]{:S(2)}, u32[]{:S(2)}) %collective-permute-start.14) | collective-permute-done | bytes 36896 | tf_op jit(solution)/shard_map/ppermute | solution.py:390
  50.8 5.9 %collective-permute-start.15 = (f32[72,128]{1,0:T(8,128)S(1)}, f32[72,128]{1,0:T(8,128)S(1)}, u32[]{:S(2)}, u32[]{:S(2)}) collective-permute-start(f32[72,128]{1,0:T(8,128)S(1)} %add.62.mine_ref), channel_id=1, source_target_pairs={{0,64},{1,65},{2,66},{3,67},{4,68},{5,69},{6,70},{7,71},{8,72},{9,... | collective-permute-start | bytes 110600 | tf_op jit(solution)/shard_map/ppermute | solution.py:390
  56.7 0.9 %collective-permute-done.15.other_ref = f32[72,128]{1,0:T(8,128)S(1)} collective-permute-done((f32[72,128]{1,0:T(8,128)S(1)}, f32[72,128]{1,0:T(8,128)S(1)}, u32[]{:S(2)}, u32[]{:S(2)}) %collective-permute-start.15) | collective-permute-done | bytes 36896 | tf_op jit(solution)/shard_map/ppermute | solution.py:390
  57.5 1.0 %shard_map.73 = (f32[3,3,32,32]{3,2,1,0:T(8,128)}, f32[3,3,32,32]{3,2,1,0:T(8,128)}) custom-call(f32[72,128]{1,0:T(8,128)S(1)} %add.62.mine_ref, f32[72,128]{1,0:T(8,128)S(1)} %collective-permute-done.15.other_ref), custom_call_target="tpu_custom_call" | custom-call | flops 1000000 | bytes 147456 | tf_op jit(solution)/shard_map/pallas_call | solution.py:40
  (8 shorter events, 0.1 us)
Async XLA Ops:
  2.8 7.1 %collective-permute-start = (bf16[16,1024]{1,0:T(8,128)(2,1)S(1)}, bf16[16,1024]{1,0:T(8,128)(2,1)S(1)}, u32[]{:S(2)}, u32[]{:S(2)}) collective-permute-start(bf16[16,1024]{1,0:T(8,128)(2,1)S(1)} %get-tuple-element.31), channel_id=1, source_target_pairs={{0,64},{64,0},{128,192},{192,128},{1,65},{65,1},{129,193},{193,129... | collective-permute-start | bytes 98312 | tf_op jit(solution)/shard_map/ppermute | solution.py:421
  6.1 6.7 %collective-permute-start.1 = (bf16[16,1024]{1,0:T(8,128)(2,1)S(1)}, bf16[16,1024]{1,0:T(8,128)(2,1)S(1)}, u32[]{:S(2)}, u32[]{:S(2)}) collective-permute-start(bf16[16,1024]{1,0:T(8,128)(2,1)S(1)} %get-tuple-element.32), channel_id=1, source_target_pairs={{64,128},{128,64},{65,129},{129,65},{66,130},{130,66},{67,131},{13... | collective-permute-start | bytes 98312 | tf_op jit(solution)/shard_map/ppermute | solution.py:420
  9.8 3.2 %copy-start = (bf16[3,192,256]{2,1,0:T(8,128)(2,1)}, bf16[3,192,256]{2,1,0:T(8,128)(2,1)S(1)}, u32[]{:S(2)}) copy-start(bf16[3,192,256]{2,1,0:T(8,128)(2,1)S(1)} %get-tuple-element.41.last_ref) | copy-start | bytes 884740
  13.0 10.6 %collective-permute-start.2 = (bf16[144,256]{1,0:T(8,128)(2,1)S(1)}, bf16[144,256]{1,0:T(8,128)(2,1)S(1)}, u32[]{:S(2)}, u32[]{:S(2)}) collective-permute-start(bf16[144,256]{1,0:T(8,128)(2,1)S(1)} %pad_maximum_fusion), channel_id=1, source_target_pairs={{0,1},{1,2},{2,3},{3,4},{4,5},{5,6},{6,7},{7,8},{8,9},{9,10},{10,1... | collective-permute-start | bytes 221192 | tf_op jit(solution)/shard_map/ppermute | solution.py:469
  13.1 10.4 %collective-permute-start.3 = (bf16[144,256]{1,0:T(8,128)(2,1)S(1)}, bf16[144,256]{1,0:T(8,128)(2,1)S(1)}, u32[]{:S(2)}, u32[]{:S(2)}) collective-permute-start(bf16[144,256]{1,0:T(8,128)(2,1)S(1)} %pad_maximum_fusion.1), channel_id=1, source_target_pairs={{1,0},{2,1},{3,2},{4,3},{5,4},{6,5},{7,6},{8,7},{9,8},{10,9},{11,1... | collective-permute-start | bytes 221192 | tf_op jit(solution)/shard_map/ppermute | solution.py:470
  25.3 1.6 %collective-permute-start.4 = (f32[72,128]{1,0:T(8,128)}, f32[72,128]{1,0:T(8,128)}, u32[]{:S(2)}, u32[]{:S(2)}) collective-permute-start(f32[72,128]{1,0:T(8,128)} %dynamic-slice_bitcast_fusion), channel_id=1, source_target_pairs={{0,64},{1,65},{2,66},{3,67},{4,68},{5,69},{6,70},{7,71},{8,72},{9,... | collective-permute-start | bytes 110600 | tf_op jit(solution)/shard_map/ppermute | solution.py:390
  27.6 4.3 %collective-permute-start.7 = (f32[72,128]{1,0:T(8,128)S(1)}, f32[72,128]{1,0:T(8,128)S(1)}, u32[]{:S(2)}, u32[]{:S(2)}) collective-permute-start(f32[72,128]{1,0:T(8,128)S(1)} %bitcast_add_fusion), channel_id=1, source_target_pairs={{0,128},{1,129},{2,130},{3,131},{4,132},{5,133},{6,134},{7,135},{8... | collective-permute-start | bytes 110600 | tf_op jit(solution)/shard_map/ppermute | solution.py:390
  30.1 4.0 %collective-permute-start.6 = (f32[72,128]{1,0:T(8,128)S(1)}, f32[72,128]{1,0:T(8,128)S(1)}, u32[]{:S(2)}, u32[]{:S(2)}) collective-permute-start(f32[72,128]{1,0:T(8,128)S(1)} %bitcast_add_fusion), channel_id=1, source_target_pairs={{0,160},{1,161},{2,162},{3,163},{4,164},{5,165},{6,166},{7,167},{8... | collective-permute-start | bytes 110600 | tf_op jit(solution)/shard_map/ppermute | solution.py:390
  30.3 3.8 %collective-permute-start.5 = (f32[72,128]{1,0:T(8,128)S(1)}, f32[72,128]{1,0:T(8,128)S(1)}, u32[]{:S(2)}, u32[]{:S(2)}) collective-permute-start(f32[72,128]{1,0:T(8,128)S(1)} %bitcast_add_fusion), channel_id=1, source_target_pairs={{0,32},{1,33},{2,34},{3,35},{4,36},{5,37},{6,38},{7,39},{8,40},{9,... | collective-permute-start | bytes 110600 | tf_op jit(solution)/shard_map/ppermute | solution.py:390
  34.1 4.5 %collective-permute-start.10 = (f32[72,128]{1,0:T(8,128)S(1)}, f32[72,128]{1,0:T(8,128)S(1)}, u32[]{:S(2)}, u32[]{:S(2)}) collective-permute-start(f32[72,128]{1,0:T(8,128)S(1)} %add_add_fusion.2.partial_ref), channel_id=1, source_target_pairs={{0,2},{1,3},{2,0},{3,1},{4,6},{5,7},{6,4},{7,5},{8,10},{9,11},{10,... | collective-permute-start | bytes 110600 | tf_op jit(solution)/shard_map/ppermute | solution.py:390
  34.2 4.5 %collective-permute-start.9 = (f32[72,128]{1,0:T(8,128)S(1)}, f32[72,128]{1,0:T(8,128)S(1)}, u32[]{:S(2)}, u32[]{:S(2)}) collective-permute-start(f32[72,128]{1,0:T(8,128)S(1)} %add_add_fusion.2.partial_ref), channel_id=1, source_target_pairs={{0,3},{1,2},{2,1},{3,0},{4,7},{5,6},{6,5},{7,4},{8,11},{9,10},{10,... | collective-permute-start | bytes 110600 | tf_op jit(solution)/shard_map/ppermute | solution.py:390
  34.3 4.4 %collective-permute-start.8 = (f32[72,128]{1,0:T(8,128)S(1)}, f32[72,128]{1,0:T(8,128)S(1)}, u32[]{:S(2)}, u32[]{:S(2)}) collective-permute-start(f32[72,128]{1,0:T(8,128)S(1)} %add_add_fusion.2.partial_ref), channel_id=1, source_target_pairs={{0,1},{1,0},{2,3},{3,2},{4,5},{5,4},{6,7},{7,6},{8,9},{9,8},{10,11... | collective-permute-start | bytes 110600 | tf_op jit(solution)/shard_map/ppermute | solution.py:390
  36.8 10.3 %copy-start.1 = (bf16[3,192,256]{2,1,0:T(8,128)(2,1)S(1)}, bf16[3,192,256]{2,1,0:T(8,128)(2,1)}, u32[]{:S(2)}) copy-start(bf16[3,192,256]{2,1,0:T(8,128)(2,1)} %copy-done) | copy-start | bytes 884740
  38.7 5.6 %collective-permute-start.13 = (f32[72,128]{1,0:T(8,128)S(1)}, f32[72,128]{1,0:T(8,128)S(1)}, u32[]{:S(2)}, u32[]{:S(2)}) collective-permute-start(f32[72,128]{1,0:T(8,128)S(1)} %add_add_fusion.1), channel_id=1, source_target_pairs={{0,12},{1,13},{2,14},{3,15},{4,8},{5,9},{6,10},{7,11},{8,4},{9,5},... | collective-permute-start | bytes 110600 | tf_op jit(solution)/shard_map/ppermute | solution.py:390
  42.9 3.7 %collective-permute-start.12 = (f32[72,128]{1,0:T(8,128)S(1)}, f32[72,128]{1,0:T(8,128)S(1)}, u32[]{:S(2)}, u32[]{:S(2)}) collective-permute-start(f32[72,128]{1,0:T(8,128)S(1)} %add_add_fusion.1), channel_id=1, source_target_pairs={{0,8},{1,9},{2,10},{3,11},{4,12},{5,13},{6,14},{7,15},{8,0},{9,1},... | collective-permute-start | bytes 110600 | tf_op jit(solution)/shard_map/ppermute | solution.py:390
  42.9 3.7 %collective-permute-start.11 = (f32[72,128]{1,0:T(8,128)S(1)}, f32[72,128]{1,0:T(8,128)S(1)}, u32[]{:S(2)}, u32[]{:S(2)}) collective-permute-start(f32[72,128]{1,0:T(8,128)S(1)} %add_add_fusion.1), channel_id=1, source_target_pairs={{0,4},{1,5},{2,6},{3,7},{4,0},{5,1},{6,2},{7,3},{8,12},{9,13},{10,... | collective-permute-start | bytes 110600 | tf_op jit(solution)/shard_map/ppermute | solution.py:390
  46.7 4.1 %collective-permute-start.14 = (f32[72,128]{1,0:T(8,128)S(1)}, f32[72,128]{1,0:T(8,128)S(1)}, u32[]{:S(2)}, u32[]{:S(2)}) collective-permute-start(f32[72,128]{1,0:T(8,128)S(1)} %add_add_fusion.partial_ref), channel_id=1, source_target_pairs={{0,28},{1,29},{2,30},{3,31},{4,24},{5,25},{6,26},{7,27},{8,20},{9,... | collective-permute-start | bytes 110600 | tf_op jit(solution)/shard_map/ppermute | solution.py:390
  50.8 6.8 %collective-permute-start.15 = (f32[72,128]{1,0:T(8,128)S(1)}, f32[72,128]{1,0:T(8,128)S(1)}, u32[]{:S(2)}, u32[]{:S(2)}) collective-permute-start(f32[72,128]{1,0:T(8,128)S(1)} %add.62.mine_ref), channel_id=1, source_target_pairs={{0,64},{1,65},{2,66},{3,67},{4,68},{5,69},{6,70},{7,71},{8,72},{9,... | collective-permute-start | bytes 110600 | tf_op jit(solution)/shard_map/ppermute | solution.py:390

commit v5 on v4

--- a/solution.py
+++ b/solution.py
@@ -90,31 +90,32 @@
         mid_ref[:, part * rows : (part + 1) * rows] = edges[HALF:]
 
 
-def row_kernel(raw_ref, perm_ref, one_ref, two_ref, xl_ref, cl_ref, first_ref, back_ref, last_ref):
+def row_kernel(raw_ref, perm_ref, one_ref, two_ref, xl_ref, cl_ref, first_ref, back_ref):
     rows = perm_ref.shape[0]
     parts = xl_ref.shape[0] // rows
     for place, target in enumerate((xl_ref, cl_ref)):
         for part in range(parts):
             block = raw_ref[place * parts + part].reshape(rows, target.shape[1])
             target[part * rows : (part + 1) * rows, :] = dot(perm_ref[...], block).astype(BF)
-    write_weights(one_ref, two_ref, first_ref, back_ref, last_ref)
-
-
-def write_weights(one_ref, two_ref, first_ref, back_ref, last_ref):
-    channels = one_ref.shape[2]
+    write_band(one_ref, False, first_ref)
+    write_band(two_ref, True, back_ref)
+
+
+def write_band(kernel, transposed, target):
+    channels = kernel.shape[2]
     lanes = WINDOW * channels
     tiled = (iota((channels, lanes), 1) % channels == iota((channels, lanes), 0)).astype(F32).astype(BF)
     block = iota((channels, lanes), 1) // channels
     for q in range(3):
-        firsts = [dot(one_ref[p, q], tiled) for p in range(3)]
-        backs = [dot_rows(two_ref[2 - p, 2 - q], tiled) for p in range(3)]
-        lasts = [dot_rows(one_ref[2 - p, 2 - q], tiled) for p in range(3)]
-        for bases, target in ((firsts, first_ref), (backs, back_ref), (lasts, last_ref)):
-            for a in range(GROUP):
-                band = jnp.zeros((channels, lanes), F32)
-                for p in range(3):
-                    band = jnp.where(block == a + p, bases[p], band)
-                target[q, a * channels : (a + 1) * channels, :] = band.astype(BF)
+        if transposed:
+            bases = [dot_rows(kernel[2 - p, 2 - q], tiled) for p in range(3)]
+        else:
+            bases = [dot(kernel[p, q], tiled) for p in range(3)]
+        for a in range(GROUP):
+            band = jnp.zeros((channels, lanes), F32)
+            for p in range(3):
+                band = jnp.where(block == a + p, bases[p], band)
+            target[q, a * channels : (a + 1) * channels, :] = band.astype(BF)
 
 
 def halo_place(odd, place, lat_cells):
@@ -123,18 +124,18 @@
     from_low = jnp.where(row < HALF, odd, 1 - odd) == 1
     wanted_row = 2 * place + jnp.where(from_low, 1, 0)
     wanted_lane = jnp.where(from_low, 0, lat_cells - 1)
-    return ((row % HALF == wanted_row) & (lane == wanted_lane)).astype(F32).astype(BF)
+    lat = lax.axis_index("lat")
+    inside = jnp.where(row < HALF, 1, lat * (lax.axis_size("lat") - 1 - lat))
+    return ((row % HALF == wanted_row) & (lane == wanted_lane) & (inside > 0)).astype(F32).astype(BF)
 
 
 def write_shifted(values, edge_columns, target, rows):
     lat_cells = values.shape[1]
     lane = iota(values.shape, 1)
-    wide = values.astype(F32)
-    below = jnp.where(lane == 0, edge_columns, pltpu.roll(wide, 1, 1))
-    above = jnp.where(lane == lat_cells - 1, edge_columns, pltpu.roll(wide, lat_cells - 1, 1))
-    target[0, rows, :] = below.astype(BF)
+    columns = edge_columns.astype(BF)
+    target[0, rows, :] = jnp.where(lane == 0, columns, pltpu.roll(values, 1, 1))
     target[1, rows, :] = values
-    target[2, rows, :] = above.astype(BF)
+    target[2, rows, :] = jnp.where(lane == lat_cells - 1, columns, pltpu.roll(values, lat_cells - 1, 1))
 
 
 def activate(pre_act, back_grad):
@@ -186,7 +187,7 @@
 
 
 def edge_kernel(x_ref, cot_ref, core_ref, mid_ref, left_ref, right_ref, first_ref, back_ref, grads_ref,
-                low_ref, high_ref, out_ref, xs, cs):
+                low_ref, high_ref, out_ref, xs_sides, cs_sides):
     lat_cells = x_ref.shape[1]
     channels = grads_ref.shape[2]
     odd = is_odd()
@@ -194,6 +195,7 @@
     own_rows = x_ref.shape[0]
     sums = [[grads_ref[place, q][:, : 3 * channels] for q in range(3)] for place in range(2)]
     for side, (message, target) in enumerate(((left_ref, low_ref), (right_ref, high_ref))):
+        xs, cs = xs_sides.at[side], cs_sides.at[side]
         own = slice(0, two) if side == 0 else slice(own_rows - two, own_rows)
         sent = message[2 * two : 2 * two + HALF, :]
         sent_halos = jnp.concatenate([sent[:, :two], sent[:, two : 2 * two]], 0).astype(F32)
@@ -218,23 +220,19 @@
         for q in range(3):
             sums[0][q] = sums[0][q] + dot_lanes(pre_grad, xs[q, near, :])
             sums[1][q] = sums[1][q] + dot_lanes(activation, cs[q, near, :])
-    for place in range(2):
-        pack_taps(sums[place], out_ref.at[place])
-
-
-def pack_taps(taps, out_ref):
+    out_ref[...] = jnp.concatenate([pack_taps(taps) for taps in sums], 0)
+
+
+def pack_taps(taps):
     channels = taps[0].shape[0]
-    used = 3 * channels
-    for q in range(2):
-        out_ref[q * channels : (q + 1) * channels, :] = jnp.concatenate(
-            [taps[q], taps[2][:, q * channels : (q + 1) * channels]], 1
-        )
-    rest = taps[2][:, 2 * channels : used]
+    main = [
+        jnp.concatenate([taps[q], taps[2][:, q * channels : (q + 1) * channels]], 1) for q in range(2)
+    ]
+    rest = taps[2][:, 2 * channels :]
     count = 128 // channels
     rows = channels // count
-    out_ref[2 * channels :, :] = jnp.concatenate(
-        [rest[i * rows : (i + 1) * rows] for i in range(count)], 1
-    )
+    last = jnp.concatenate([rest[i * rows : (i + 1) * rows] for i in range(count)], 1)
+    return jnp.concatenate([*main, last], 0)
 
 
 def unpack_taps(packed, channels):
@@ -248,8 +246,9 @@
 
 
 def outer_kernel(x_ref, cot_ref, core_ref, mid_ref, left_ref, right_ref, first_ref, back_ref, low_ref, pre_ref,
-                 high_ref, partial_ref, ps, passed_ref, rows_buffer, strips):
+                 high_ref, one_ref, partial_ref, ps, last_ref, passed_ref, rows_buffer, strips):
     passed_ref[...] = partial_ref[...]
+    write_band(one_ref, True, last_ref)
     lat_cells = x_ref.shape[1]
     channels = low_ref.shape[0] // 2
     two = 2 * channels
@@ -345,11 +344,11 @@
         copy.wait()
 
 
-def result_kernel(scale, mine_ref, other_ref, one_ref, two_ref):
+def result_kernel(scale, total_ref, given_ref, one_ref, two_ref):
     channels = one_ref.shape[2]
-    odd = is_odd()
-    first = jnp.where(odd == 0, mine_ref[...], other_ref[...]) * scale
-    second = jnp.where(odd == 0, other_ref[...], mine_ref[...]) * scale
+    rows = total_ref.shape[0] // 2
+    sums = jnp.where(is_odd() == 1, total_ref[...], given_ref[...]) * scale
+    first, second = sums[:rows], sums[rows:]
     first = unpack_taps(first, channels)
     second = unpack_taps(second, channels)
     for q in range(3):
@@ -364,7 +363,7 @@
     listed = []
     for lat in range(lat_count):
         for lon in range(lon_count):
-            to_lat, to_lon = partner(lat, lon)
+            to_lat, to_lon = partner(lat, lon) if lat % 2 else (lat, lon ^ 32)
             listed.append((lat * lon_count + lon, to_lat * lon_count + to_lon))
     return listed
 
@@ -394,30 +393,26 @@
     first, second, third = [exchange(value, partner(mask)) for mask in masks]
     result = None
     if beside is not None:
-        result, value = beside(value)
+        *result, value = beside(value)
     return (value + first) + (second + third), result
 
 
-def sum_everywhere(halves, widen, finish):
-    core = lax.axis_index("lat") % 2
-    other_core = lambda lat, lon: (lat ^ 1, lon)
-    mine = lax.dynamic_index_in_dim(halves, core, 0, False)
-    theirs = lax.dynamic_index_in_dim(halves, 1 - core, 0, False)
-    total = mine + exchange(theirs, other_core)
+def sum_everywhere(mine, widen, finish):
+    swap = [(lat, lat ^ 1) for lat in range(lax.axis_size("lat"))]
+    total = mine + lax.ppermute(mine, "lat", swap)
     total, _ = sum_of_four(total, x_partner, (1, 3, 2))
     total, shifted = sum_of_four(total, y_partner, (1, 3, 2), widen)
     total, _ = sum_of_four(total, z_partner, (1, 2, 3))
-    far = exchange(total, z_partner(7))
-    input_grad, total = finish(shifted, total)
+    far = exchange(total, z_partner(6))
+    input_grad, total = finish(*shifted, total)
     total = total + far
-    other = exchange(total, other_core)
-    return total, other, input_grad
+    given = lax.ppermute(total, "lat", swap)
+    return total, given, input_grad
 
 
 def lat_exchange(core, mid):
     count = lax.axis_size("lat")
-    inner = [pair for low in range(1, count - 1, 2) for pair in ((low, low + 1), (low + 1, low))]
-    mid = lax.ppermute(mid, "lat", inner)
+    mid = lax.ppermute(mid, "lat", [(i, (i - 1 if i % 2 == 0 else i + 1) % count) for i in range(count)])
     return lax.ppermute(core, "lat", [(i, i ^ 1) for i in range(count)]), mid
 
 
@@ -427,7 +422,7 @@
     rows = channels * lon_cells
     two = 2 * channels
     parts = lon_cells // HALF
-    weights = [shape(3, GROUP * channels, WINDOW * channels)] * 3
+    weights = shape(3, GROUP * channels, WINDOW * channels)
     raw, one, two_kernel, perm, core_out, mid_out = call(
         border_kernel,
         [
@@ -447,9 +442,9 @@
         hbm_in=(0, 1, 2, 3),
     )
     core_in, mid_in = lat_exchange(core_out, mid_out)
-    x_rows, cot_rows, first, back, last = call(
+    x_rows, cot_rows, first, back = call(
         row_kernel,
-        [shape(rows, lat_cells), shape(rows, lat_cells), *weights],
+        [shape(rows, lat_cells), shape(rows, lat_cells), weights, weights],
         [],
         10**9,
         raw,
@@ -478,10 +473,11 @@
         4 * 10**9,
         x_rows, cot_rows, core_in, mid_in, first, back,
     )
-    edge_shifted = pltpu.VMEM((3, 2 * two, lat_cells), BF)
+    edge_shifted = pltpu.VMEM((2, 3, 2 * two, lat_cells), BF)
+    partial = shape(2 * 9 * channels * channels // 128, 128, dtype=F32)
     pre_low, pre_high, grads = call(
         edge_kernel,
-        [shape(two, lat_cells), shape(two, lat_cells), shape(2, 9 * channels * channels // 128, 128, dtype=F32)],
+        [shape(two, lat_cells), shape(two, lat_cells), partial],
         [edge_shifted, edge_shifted],
         10**9,
         x_rows, cot_rows, core_in, mid_in, from_left, from_right, first, back, inner_grads,
@@ -489,17 +485,17 @@
     def widen(partial):
         return call(
             outer_kernel,
-            [shape(3, rows + two, lat_cells), shape(*partial.shape, dtype=F32)],
+            [shape(3, rows + two, lat_cells), weights, shape(*partial.shape, dtype=F32)],
             [
                 pltpu.VMEM((rows + 2 * two, lat_cells), BF),
                 pltpu.VMEM((2, HALF, rows + 2 * two), F32),
             ],
             10**9,
             x_rows, cot_rows, core_in, mid_in, from_left, from_right, first, back,
-            pre_low, pre_inner, pre_high, partial,
+            pre_low, pre_inner, pre_high, one, partial,
         )
 
-    def finish(shifted, partial):
+    def finish(shifted, last, partial):
         return call(
             last_kernel,
             [shape(channels, lon_cells, lat_cells), shape(*partial.shape, dtype=F32)],
@@ -513,14 +509,14 @@
             hbm_out=(0,),
         )
 
-    mine, other, input_grad = sum_everywhere(grads, widen, finish)
+    total, given, input_grad = sum_everywhere(grads, widen, finish)
     grad_one, grad_two = call(
         functools.partial(result_kernel, 1.0 / math.sqrt(cells)),
         [shape(3, 3, channels, channels, dtype=F32)] * 2,
         [],
         10**6,
-        mine,
-        other,
+        total,
+        given,
     )
     return (input_grad, grad_one, grad_two)
 

time: 58.7 us -> 52.2 us (0.89)
  starting transfers between devices: 30 us -> 23.9 us
  waiting for transfers between devices: 14.4 us -> 15.7 us
  other arithmetic: 0.98 us -> 0.25 us
  local copies, waits for them, and re-layouts: 0.8 us -> 0.16 us
    ppermute x12 -> x10, starting transfers between devices: 16.5 us -> 11.7 us  [exchange(): return lax.ppermute(value, ('lat', 'lon'), pairs(counts, partner))]
    ppermute x1 -> x3, waiting for transfers between devices: 2.88 us -> 5.1 us  [the longest x1 2.93 us: lat_exchange(): lax.ppermute(mid, 'lat', [(i, (i - 1 if i % 2 == 0 else i + 1) % count) f...]
    ppermute x1 -> x3, starting transfers between devices: 2.82 us -> 1.52 us  [the longest x1 1 us: lat_exchange(): lax.ppermute(mid, 'lat', [(i, (i - 1 if i % 2 == 0 else i + 1) % count) f...]
    ppermute x12 -> x10, waiting for transfers between devices: 11.5 us -> 10.6 us  [exchange(): return lax.ppermute(value, ('lat', 'lon'), pairs(counts, partner))]
    add x1, other arithmetic: 0.77 us -> 0.01 us  [sum_everywhere(): total = mine + lax.ppermute(mine, 'lat', swap)]
    squeeze x1 -> x0, local copies, waits for them, and re-layouts: 0.63 us -> none  [sum_everywhere(): theirs = lax.dynamic_index_in_dim(halves, 1 - core, 0, False)]
  transfers between devices with their start and end apart: 16 -> 16, of which waited for: 10 -> 11; matrix products, arithmetic and copies ran while one was open for 0% -> 0% of each run, Pallas kernels for 13% -> 14%
where the time goes in v5:
time: 52.2 us; the launch traced here: 52.1 us
  starting transfers between devices  23.9 us (46%)
  waiting for transfers between devices  15.7 us (30%)
  Pallas kernels  11.3 us (22%)
  between operations  0.77 us (1%)
    ppermute x10, starting transfers between devices, exchange(): return lax.ppermute(value, ('lat', 'lon'), pairs(counts, partner))  11.7 us
    pallas_call x7, Pallas kernels, call(): pl.pallas_call(kernel, out_shape=outs, in_specs=[pl.BlockSpec(memory_spac...  11.3 us
    ppermute x10, waiting for transfers between devices, exchange(): return lax.ppermute(value, ('lat', 'lon'), pairs(counts, partner))  10.6 us
    ppermute x1, starting transfers between devices, on_device(): lax.ppermute(to_left, 'lon', [((i + 1) % count, i) for i in range(count)])  7.29 us
    ppermute x1, starting transfers between devices, lat_exchange(): return (lax.ppermute(core, 'lat', [(i, i ^ 1) for i in range(count)]), mid)  3.32 us
    ppermute x1, waiting for transfers between devices, lat_exchange(): lax.ppermute(mid, 'lat', [(i, (i - 1 if i % 2 == 0 else i + 1) % count) f...  2.93 us
    ppermute x1, waiting for transfers between devices, sum_everywhere(): given = lax.ppermute(total, 'lat', swap)  1.25 us
  transfers between devices with their start and end apart: 16, of which 11 were waited for; matrix products, arithmetic and copies ran while one was open for 0% of the time, Pallas kernels for 14%

profile of v5, /device:TPU:1, one launch (start us, length us, event | category | flops | bytes accessed | tf_op | source)
XLA Modules:
  0.0 52.1 jit_solution(4244198662885478027)
XLA Ops:
  0.6 2.1 %shard_map.67 = (bf16[4,32,16,256]{3,2,1,0:T(8,128)(2,1)S(1)}, bf16[3,3,32,32]{3,2,1,0:T(8,128)(2,1)S(1)}, bf16[3,3,32,32]{3,2,1,0:T(8,128)(2,1)S(1)}, bf16[512,...) custom-call(bf16[32,32,256]{2,1,0:T(8,128)(2,1)} %x_hbm.1, ...), custom_call_target="tpu_custom_call" | custom-call | flops 100000000 | bytes 2760704 | tf_op jit(solution)/shard_map/pallas_call | solution.py:40
  2.8 3.3 %collective-permute-start = (bf16[16,1024]{1,0:T(8,128)(2,1)S(1)}, bf16[16,1024]{1,0:T(8,128)(2,1)S(1)}, u32[]{:S(2)}, u32[]{:S(2)}) collective-permute-start(bf16[16,1024]{1,0:T(8,128)(2,1)S(1)} %get-tuple-element.31), channel_id=1, source_target_pairs={{0,64},{64,0},{128,192},{192,128},{1,65},{65,1},{129,193},{193,129... | collective-permute-start | bytes 98312 | tf_op jit(solution)/shard_map/ppermute | solution.py:416
  6.1 1.0 %collective-permute-start.1 = (bf16[16,1024]{1,0:T(8,128)(2,1)S(1)}, bf16[16,1024]{1,0:T(8,128)(2,1)S(1)}, u32[]{:S(2)}, u32[]{:S(2)}) collective-permute-start(bf16[16,1024]{1,0:T(8,128)(2,1)S(1)} %get-tuple-element.32), channel_id=1, source_target_pairs={{0,192},{64,128},{128,64},{192,0},{1,193},{65,129},{129,65},{193,1... | collective-permute-start | bytes 98312 | tf_op jit(solution)/shard_map/ppermute | solution.py:415
  7.1 0.8 %shard_map.68 = (bf16[1024,256]{1,0:T(8,128)(2,1)S(1)}, bf16[1024,256]{1,0:T(8,128)(2,1)S(1)}, bf16[3,192,256]{2,1,0:T(8,128)(2,1)S(1)}, bf16[3,192,256]{2,1,0:T(8,128)(2,1)S(1)}) custom-call(bf16[4,32,16,256]{3,2,1,0:T(8,128)(2,1)S(1)} %get-tuple-element.25.raw_ref, bf16[512,512]{1,0:T(8,128)(2,1)S(1)} %get-tuple-element.26.perm_ref, ...), custom_call_target="tpu_custom_call" | custom-call | flops 1000000000 | bytes 3248128 | tf_op jit(solution)/shard_map/pallas_call | solution.py:40
  7.9 0.0 collective-permute-done.core_ref
  7.9 0.1 fusion.8
  8.0 2.9 %collective-permute-done.1.mid_ref = bf16[16,1024]{1,0:T(8,128)(2,1)S(1)} collective-permute-done((bf16[16,1024]{1,0:T(8,128)(2,1)S(1)}, bf16[16,1024]{1,0:T(8,128)(2,1)S(1)}, u32[]{:S(2)}, u32[]{:S(2)}) %collective-permute-start.1) | collective-permute-done | bytes 32800 | tf_op jit(solution)/shard_map/ppermute | solution.py:415
  10.9 0.1 fusion.9
  11.0 0.1 fusion.4
  11.1 0.1 collective-permute-start.2
  11.2 0.1 fusion.5
  11.3 7.3 %collective-permute-start.3 = (bf16[144,256]{1,0:T(8,128)(2,1)S(1)}, bf16[144,256]{1,0:T(8,128)(2,1)S(1)}, u32[]{:S(2)}, u32[]{:S(2)}) collective-permute-start(bf16[144,256]{1,0:T(8,128)(2,1)S(1)} %pad_maximum_fusion.1), channel_id=1, source_target_pairs={{1,0},{2,1},{3,2},{4,3},{5,4},{6,5},{7,6},{8,7},{9,8},{10,9},{11,1... | collective-permute-start | bytes 221192 | tf_op jit(solution)/shard_map/ppermute | solution.py:465
  18.5 2.9 %shard_map.69 = (bf16[960,256]{1,0:T(8,128)(2,1)S(1)}, f32[2,3,32,128]{3,2,1,0:T(8,128)S(1)}) custom-call(bf16[1024,256]{1,0:T(8,128)(2,1)S(1)} %get-tuple-element.29.x_ref, bf16[1024,256]{1,0:T(8,128)(2,1)S(1)} %get-tuple-element.30.cot_ref, bf16[16,1024]{1,0:T(8,128)(2,1)S(1)} %collective-permute-done.core_ref, ...), custom_call_target="tpu_custom_call" | custom-call | flops 4000000000 | bytes 2293760 | tf_op jit(solution)/shard_map/pallas_call | solution.py:40
  21.5 0.0 collective-permute-done.2.left_ref
  21.5 0.0 collective-permute-done.3.right_ref
  21.5 1.1 %shard_map.70 = (bf16[64,256]{1,0:T(8,128)(2,1)S(1)}, bf16[64,256]{1,0:T(8,128)(2,1)S(1)}, f32[144,128]{1,0:T(8,128)S(1)}) custom-call(bf16[1024,256]{1,0:T(8,128)(2,1)S(1)} %get-tuple-element.29.x_ref, bf16[1024,256]{1,0:T(8,128)(2,1)S(1)} %get-tuple-element.30.cot_ref, bf16[16,1024]{1,0:T(8,128)(2,1)S(1)} %collective-permute-done.core_ref, ...), custom_call_target="tpu_custom_call" | custom-call | flops 1000000000 | bytes 2088960 | tf_op jit(solution)/shard_map/pallas_call | solution.py:40
  22.6 0.4 collective-permute-start.4
  23.0 0.9 %collective-permute-done.4 = f32[144,128]{1,0:T(8,128)S(1)} collective-permute-done((f32[144,128]{1,0:T(8,128)S(1)}, f32[144,128]{1,0:T(8,128)S(1)}, u32[]{:S(2)}, u32[]{:S(2)}) %collective-permute-start.4) | collective-permute-done | bytes 73760 | tf_op jit(solution)/shard_map/ppermute | solution.py:402
  24.0 2.5 %collective-permute-start.7 = (f32[144,128]{1,0:T(8,128)S(1)}, f32[144,128]{1,0:T(8,128)S(1)}, u32[]{:S(2)}, u32[]{:S(2)}) collective-permute-start(f32[144,128]{1,0:T(8,128)S(1)} %add.37), channel_id=1, source_target_pairs={{0,32},{1,33},{2,34},{3,35},{4,36},{5,37},{6,38},{7,39},{8,40},{9,... | collective-permute-start | bytes 221192 | tf_op jit(solution)/shard_map/ppermute | solution.py:389
  26.5 0.2 collective-permute-start.6
  26.7 0.0 collective-permute-start.5
  26.7 2.1 %collective-permute-done.7 = f32[144,128]{1,0:T(8,128)S(1)} collective-permute-done((f32[144,128]{1,0:T(8,128)S(1)}, f32[144,128]{1,0:T(8,128)S(1)}, u32[]{:S(2)}, u32[]{:S(2)}) %collective-permute-start.7) | collective-permute-done | bytes 73760 | tf_op jit(solution)/shard_map/ppermute | solution.py:389
  28.8 2.2 %collective-permute-done.6 = f32[144,128]{1,0:T(8,128)S(1)} collective-permute-done((f32[144,128]{1,0:T(8,128)S(1)}, f32[144,128]{1,0:T(8,128)S(1)}, u32[]{:S(2)}, u32[]{:S(2)}) %collective-permute-start.6) | collective-permute-done | bytes 73760 | tf_op jit(solution)/shard_map/ppermute | solution.py:389
  30.9 0.1 collective-permute-done.5
  31.1 0.1 collective-permute-start.10
  31.2 0.1 collective-permute-start.9
  31.3 2.5 %collective-permute-start.8 = (f32[144,128]{1,0:T(8,128)S(1)}, f32[144,128]{1,0:T(8,128)S(1)}, u32[]{:S(2)}, u32[]{:S(2)}) collective-permute-start(f32[144,128]{1,0:T(8,128)S(1)} %add_add_fusion.2.partial_ref), channel_id=1, source_target_pairs={{0,32},{1,33},{2,34},{3,35},{4,36},{5,37},{6,38},{7,39},{8,40},{9,... | collective-permute-start | bytes 221192 | tf_op jit(solution)/shard_map/ppermute | solution.py:389
  33.8 1.2 %shard_map.71 = (bf16[3,1088,256]{2,1,0:T(8,128)(2,1)S(1)}, bf16[3,192,256]{2,1,0:T(8,128)(2,1)S(1)}, f32[144,128]{1,0:T(8,128)S(1)}) custom-call(bf16[1024,256]{1,0:T(8,128)(2,1)S(1)} %get-tuple-element.29.x_ref, bf16[1024,256]{1,0:T(8,128)(2,1)S(1)} %get-tuple-element.30.cot_ref, bf16[16,1024]{1,0:T(8,128)(2,1)S(1)} %collective-permute-done.core_ref, ...), custom_call_target="tpu_custom_call" | custom-call | flops 1000000000 | bytes 4540416 | tf_op jit(solution)/shard_map/pallas_call | solution.py:40
  35.0 1.0 %collective-permute-done.10 = f32[144,128]{1,0:T(8,128)S(1)} collective-permute-done((f32[144,128]{1,0:T(8,128)S(1)}, f32[144,128]{1,0:T(8,128)S(1)}, u32[]{:S(2)}, u32[]{:S(2)}) %collective-permute-start.10) | collective-permute-done | bytes 73760 | tf_op jit(solution)/shard_map/ppermute | solution.py:389
  36.0 0.5 collective-permute-done.9
  36.5 0.0 collective-permute-done.8
  36.5 3.6 %collective-permute-start.13 = (f32[144,128]{1,0:T(8,128)S(1)}, f32[144,128]{1,0:T(8,128)S(1)}, u32[]{:S(2)}, u32[]{:S(2)}) collective-permute-start(f32[144,128]{1,0:T(8,128)S(1)} %add_add_fusion.1), channel_id=1, source_target_pairs={{0,32},{1,33},{2,34},{3,35},{4,36},{5,37},{6,38},{7,39},{8,40},{9,... | collective-permute-start | bytes 221192 | tf_op jit(solution)/shard_map/ppermute | solution.py:389
  40.1 0.0 collective-permute-start.12
  40.1 0.6 %collective-permute-start.11 = (f32[144,128]{1,0:T(8,128)S(1)}, f32[144,128]{1,0:T(8,128)S(1)}, u32[]{:S(2)}, u32[]{:S(2)}) collective-permute-start(f32[144,128]{1,0:T(8,128)S(1)} %add_add_fusion.1), channel_id=1, source_target_pairs={{0,32},{1,33},{2,34},{3,35},{4,36},{5,37},{6,38},{7,39},{8,40},{9,... | collective-permute-start | bytes 221192 | tf_op jit(solution)/shard_map/ppermute | solution.py:389
  40.7 1.2 %collective-permute-done.13 = f32[144,128]{1,0:T(8,128)S(1)} collective-permute-done((f32[144,128]{1,0:T(8,128)S(1)}, f32[144,128]{1,0:T(8,128)S(1)}, u32[]{:S(2)}, u32[]{:S(2)}) %collective-permute-start.13) | collective-permute-done | bytes 73760 | tf_op jit(solution)/shard_map/ppermute | solution.py:389
  41.9 2.4 %collective-permute-done.12 = f32[144,128]{1,0:T(8,128)S(1)} collective-permute-done((f32[144,128]{1,0:T(8,128)S(1)}, f32[144,128]{1,0:T(8,128)S(1)}, u32[]{:S(2)}, u32[]{:S(2)}) %collective-permute-start.12) | collective-permute-done | bytes 73760 | tf_op jit(solution)/shard_map/ppermute | solution.py:389
  44.2 0.0 collective-permute-done.11
  44.2 2.1 %collective-permute-start.14 = (f32[144,128]{1,0:T(8,128)S(1)}, f32[144,128]{1,0:T(8,128)S(1)}, u32[]{:S(2)}, u32[]{:S(2)}) collective-permute-start(f32[144,128]{1,0:T(8,128)S(1)} %add_add_fusion.partial_ref), channel_id=1, source_target_pairs={{0,32},{1,33},{2,34},{3,35},{4,36},{5,37},{6,38},{7,39},{8,40},{9,... | collective-permute-start | bytes 221192 | tf_op jit(solution)/shard_map/ppermute | solution.py:389
  46.3 2.2 %shard_map.72 = (bf16[32,32,256]{2,1,0:T(8,128)(2,1)}, f32[144,128]{1,0:T(8,128)S(1)}) custom-call(bf16[3,1088,256]{2,1,0:T(8,128)(2,1)S(1)} %get-tuple-element.40.ps, bf16[3,192,256]{2,1,0:T(8,128)(2,1)S(1)} %get-tuple-element.41.last_ref, bf16[4,32,16,256]{3,2,1,0:T(8,128)(2,1)S(1)} %get-tuple-element.25.raw_ref, f32[144,128]{1,0:T(8,128)S(1)} %add_add_fusion.partial_ref), custom_call_target="tpu_custom_call" | custom-call | flops 2000000000 | bytes 3686400 | tf_op jit(solution)/shard_map/pallas_call | solution.py:40
  48.5 1.2 %collective-permute-done.14 = f32[144,128]{1,0:T(8,128)S(1)} collective-permute-done((f32[144,128]{1,0:T(8,128)S(1)}, f32[144,128]{1,0:T(8,128)S(1)}, u32[]{:S(2)}, u32[]{:S(2)}) %collective-permute-start.14) | collective-permute-done | bytes 73760 | tf_op jit(solution)/shard_map/ppermute | solution.py:389
  49.8 0.1 collective-permute-start.15
  49.9 1.3 %collective-permute-done.15.given_ref = f32[144,128]{1,0:T(8,128)S(1)} collective-permute-done((f32[144,128]{1,0:T(8,128)S(1)}, f32[144,128]{1,0:T(8,128)S(1)}, u32[]{:S(2)}, u32[]{:S(2)}) %collective-permute-start.15) | collective-permute-done | bytes 73760 | tf_op jit(solution)/shard_map/ppermute | solution.py:409
  51.1 1.0 %shard_map.73 = (f32[3,3,32,32]{3,2,1,0:T(8,128)}, f32[3,3,32,32]{3,2,1,0:T(8,128)}) custom-call(f32[144,128]{1,0:T(8,128)S(1)} %add.47.total_ref, f32[144,128]{1,0:T(8,128)S(1)} %collective-permute-done.15.given_ref), custom_call_target="tpu_custom_call" | custom-call | flops 1000000 | bytes 221184 | tf_op jit(solution)/shard_map/pallas_call | solution.py:40
  (8 shorter events, 0.1 us)
Async XLA Ops:
  2.8 5.2 %collective-permute-start = (bf16[16,1024]{1,0:T(8,128)(2,1)S(1)}, bf16[16,1024]{1,0:T(8,128)(2,1)S(1)}, u32[]{:S(2)}, u32[]{:S(2)}) collective-permute-start(bf16[16,1024]{1,0:T(8,128)(2,1)S(1)} %get-tuple-element.31), channel_id=1, source_target_pairs={{0,64},{64,0},{128,192},{192,128},{1,65},{65,1},{129,193},{193,129... | collective-permute-start | bytes 98312 | tf_op jit(solution)/shard_map/ppermute | solution.py:416
  6.1 4.9 %collective-permute-start.1 = (bf16[16,1024]{1,0:T(8,128)(2,1)S(1)}, bf16[16,1024]{1,0:T(8,128)(2,1)S(1)}, u32[]{:S(2)}, u32[]{:S(2)}) collective-permute-start(bf16[16,1024]{1,0:T(8,128)(2,1)S(1)} %get-tuple-element.32), channel_id=1, source_target_pairs={{0,192},{64,128},{128,64},{192,0},{1,193},{65,129},{129,65},{193,1... | collective-permute-start | bytes 98312 | tf_op jit(solution)/shard_map/ppermute | solution.py:415
  11.1 10.4 %collective-permute-start.2 = (bf16[144,256]{1,0:T(8,128)(2,1)S(1)}, bf16[144,256]{1,0:T(8,128)(2,1)S(1)}, u32[]{:S(2)}, u32[]{:S(2)}) collective-permute-start(bf16[144,256]{1,0:T(8,128)(2,1)S(1)} %pad_maximum_fusion), channel_id=1, source_target_pairs={{0,1},{1,2},{2,3},{3,4},{4,5},{5,6},{6,7},{7,8},{8,9},{9,10},{10,1... | collective-permute-start | bytes 221192 | tf_op jit(solution)/shard_map/ppermute | solution.py:464
  11.3 10.2 %collective-permute-start.3 = (bf16[144,256]{1,0:T(8,128)(2,1)S(1)}, bf16[144,256]{1,0:T(8,128)(2,1)S(1)}, u32[]{:S(2)}, u32[]{:S(2)}) collective-permute-start(bf16[144,256]{1,0:T(8,128)(2,1)S(1)} %pad_maximum_fusion.1), channel_id=1, source_target_pairs={{1,0},{2,1},{3,2},{4,3},{5,4},{6,5},{7,6},{8,7},{9,8},{10,9},{11,1... | collective-permute-start | bytes 221192 | tf_op jit(solution)/shard_map/ppermute | solution.py:465
  22.6 1.4 %collective-permute-start.4 = (f32[144,128]{1,0:T(8,128)S(1)}, f32[144,128]{1,0:T(8,128)S(1)}, u32[]{:S(2)}, u32[]{:S(2)}) collective-permute-start(f32[144,128]{1,0:T(8,128)S(1)} %get-tuple-element.39), channel_id=1, source_target_pairs={{0,64},{64,0},{128,192},{192,128},{1,65},{65,1},{129,193},{193,129... | collective-permute-start | bytes 221192 | tf_op jit(solution)/shard_map/ppermute | solution.py:402
  24.0 4.8 %collective-permute-start.7 = (f32[144,128]{1,0:T(8,128)S(1)}, f32[144,128]{1,0:T(8,128)S(1)}, u32[]{:S(2)}, u32[]{:S(2)}) collective-permute-start(f32[144,128]{1,0:T(8,128)S(1)} %add.37), channel_id=1, source_target_pairs={{0,32},{1,33},{2,34},{3,35},{4,36},{5,37},{6,38},{7,39},{8,40},{9,... | collective-permute-start | bytes 221192 | tf_op jit(solution)/shard_map/ppermute | solution.py:389
  26.5 4.4 %collective-permute-start.6 = (f32[144,128]{1,0:T(8,128)S(1)}, f32[144,128]{1,0:T(8,128)S(1)}, u32[]{:S(2)}, u32[]{:S(2)}) collective-permute-start(f32[144,128]{1,0:T(8,128)S(1)} %add.37), channel_id=1, source_target_pairs={{0,32},{1,33},{2,34},{3,35},{4,36},{5,37},{6,38},{7,39},{8,40},{9,... | collective-permute-start | bytes 221192 | tf_op jit(solution)/shard_map/ppermute | solution.py:389
  26.7 4.4 %collective-permute-start.5 = (f32[144,128]{1,0:T(8,128)S(1)}, f32[144,128]{1,0:T(8,128)S(1)}, u32[]{:S(2)}, u32[]{:S(2)}) collective-permute-start(f32[144,128]{1,0:T(8,128)S(1)} %add.37), channel_id=1, source_target_pairs={{0,32},{1,33},{2,34},{3,35},{4,36},{5,37},{6,38},{7,39},{8,40},{9,... | collective-permute-start | bytes 221192 | tf_op jit(solution)/shard_map/ppermute | solution.py:389
  31.1 4.9 %collective-permute-start.10 = (f32[144,128]{1,0:T(8,128)S(1)}, f32[144,128]{1,0:T(8,128)S(1)}, u32[]{:S(2)}, u32[]{:S(2)}) collective-permute-start(f32[144,128]{1,0:T(8,128)S(1)} %add_add_fusion.2.partial_ref), channel_id=1, source_target_pairs={{0,32},{1,33},{2,34},{3,35},{4,36},{5,37},{6,38},{7,39},{8,40},{9,... | collective-permute-start | bytes 221192 | tf_op jit(solution)/shard_map/ppermute | solution.py:389
  31.2 5.3 %collective-permute-start.9 = (f32[144,128]{1,0:T(8,128)S(1)}, f32[144,128]{1,0:T(8,128)S(1)}, u32[]{:S(2)}, u32[]{:S(2)}) collective-permute-start(f32[144,128]{1,0:T(8,128)S(1)} %add_add_fusion.2.partial_ref), channel_id=1, source_target_pairs={{0,32},{1,33},{2,34},{3,35},{4,36},{5,37},{6,38},{7,39},{8,40},{9,... | collective-permute-start | bytes 221192 | tf_op jit(solution)/shard_map/ppermute | solution.py:389
  31.3 5.2 %collective-permute-start.8 = (f32[144,128]{1,0:T(8,128)S(1)}, f32[144,128]{1,0:T(8,128)S(1)}, u32[]{:S(2)}, u32[]{:S(2)}) collective-permute-start(f32[144,128]{1,0:T(8,128)S(1)} %add_add_fusion.2.partial_ref), channel_id=1, source_target_pairs={{0,32},{1,33},{2,34},{3,35},{4,36},{5,37},{6,38},{7,39},{8,40},{9,... | collective-permute-start | bytes 221192 | tf_op jit(solution)/shard_map/ppermute | solution.py:389
  36.5 5.4 %collective-permute-start.13 = (f32[144,128]{1,0:T(8,128)S(1)}, f32[144,128]{1,0:T(8,128)S(1)}, u32[]{:S(2)}, u32[]{:S(2)}) collective-permute-start(f32[144,128]{1,0:T(8,128)S(1)} %add_add_fusion.1), channel_id=1, source_target_pairs={{0,32},{1,33},{2,34},{3,35},{4,36},{5,37},{6,38},{7,39},{8,40},{9,... | collective-permute-start | bytes 221192 | tf_op jit(solution)/shard_map/ppermute | solution.py:389
  40.1 4.1 %collective-permute-start.12 = (f32[144,128]{1,0:T(8,128)S(1)}, f32[144,128]{1,0:T(8,128)S(1)}, u32[]{:S(2)}, u32[]{:S(2)}) collective-permute-start(f32[144,128]{1,0:T(8,128)S(1)} %add_add_fusion.1), channel_id=1, source_target_pairs={{0,32},{1,33},{2,34},{3,35},{4,36},{5,37},{6,38},{7,39},{8,40},{9,... | collective-permute-start | bytes 221192 | tf_op jit(solution)/shard_map/ppermute | solution.py:389
  40.1 4.1 %collective-permute-start.11 = (f32[144,128]{1,0:T(8,128)S(1)}, f32[144,128]{1,0:T(8,128)S(1)}, u32[]{:S(2)}, u32[]{:S(2)}) collective-permute-start(f32[144,128]{1,0:T(8,128)S(1)} %add_add_fusion.1), channel_id=1, source_target_pairs={{0,32},{1,33},{2,34},{3,35},{4,36},{5,37},{6,38},{7,39},{8,40},{9,... | collective-permute-start | bytes 221192 | tf_op jit(solution)/shard_map/ppermute | solution.py:389
  44.2 5.5 %collective-permute-start.14 = (f32[144,128]{1,0:T(8,128)S(1)}, f32[144,128]{1,0:T(8,128)S(1)}, u32[]{:S(2)}, u32[]{:S(2)}) collective-permute-start(f32[144,128]{1,0:T(8,128)S(1)} %add_add_fusion.partial_ref), channel_id=1, source_target_pairs={{0,32},{1,33},{2,34},{3,35},{4,36},{5,37},{6,38},{7,39},{8,40},{9,... | collective-permute-start | bytes 221192 | tf_op jit(solution)/shard_map/ppermute | solution.py:389
  49.8 1.4 %collective-permute-start.15 = (f32[144,128]{1,0:T(8,128)S(1)}, f32[144,128]{1,0:T(8,128)S(1)}, u32[]{:S(2)}, u32[]{:S(2)}) collective-permute-start(f32[144,128]{1,0:T(8,128)S(1)} %add.47.total_ref), channel_id=1, source_target_pairs={{0,64},{64,0},{128,192},{192,128},{1,65},{65,1},{129,193},{193,129... | collective-permute-start | bytes 221192 | tf_op jit(solution)/shard_map/ppermute | solution.py:409

commit v6 on v5

--- a/solution.py
+++ b/solution.py
@@ -81,16 +81,27 @@
     rows = HALF * channels
     for copy in copies:
         copy.wait()
+    folded = [[], []]
     for part in range(parts):
         edges = sum(
             dot_lanes(chosen[place], raw_ref[place * parts + part].reshape(rows, lat_cells)) for place in range(2)
         )
-        edges = dot_lanes(edges.astype(BF), perm_ref[...]).astype(BF)
-        core_ref[:, part * rows : (part + 1) * rows] = edges[:HALF]
-        mid_ref[:, part * rows : (part + 1) * rows] = edges[HALF:]
-
-
-def row_kernel(raw_ref, perm_ref, one_ref, two_ref, xl_ref, cl_ref, first_ref, back_ref):
+        edges = dot_lanes(edges.astype(BF), perm_ref[...])
+        for first in range(0, rows, lat_cells):
+            for half in range(2):
+                folded[half].append(edges[half * HALF : half * HALF + 4, first : first + lat_cells])
+    core_ref[...] = jnp.concatenate(folded[0], 0).astype(BF)
+    mid_ref[...] = jnp.concatenate(folded[1], 0).astype(BF)
+
+
+def unfold(edges):
+    wide = edges.astype(F32)
+    lanes = jnp.concatenate([wide[first : first + 4] for first in range(0, wide.shape[0], 4)], 1)
+    return jnp.concatenate([lanes, jnp.zeros((HALF - 4, lanes.shape[1]), F32)], 0)
+
+
+def row_kernel(raw_ref, perm_ref, one_ref, two_ref, core_ref, xl_ref, cl_ref, first_ref, back_ref, passed_ref):
+    passed_ref[...] = core_ref[...]
     rows = perm_ref.shape[0]
     parts = xl_ref.shape[0] // rows
     for place, target in enumerate((xl_ref, cl_ref)):
@@ -116,6 +127,28 @@
             for p in range(3):
                 band = jnp.where(block == a + p, bases[p], band)
             target[q, a * channels : (a + 1) * channels, :] = band.astype(BF)
+
+
+def lon_is_odd():
+    return lax.axis_index("lon") % 2
+
+
+def message_kernel(x_ref, cot_ref, core_in, mid_in, far_ref, near_ref, core_ref, mid_ref):
+    rows, lat_cells = x_ref.shape
+    two = (far_ref.shape[0] - HALF) // 2
+    core, mid = unfold(core_in[...]), unfold(mid_in[...])
+    core_ref[...] = core.astype(BF)
+    mid_ref[...] = mid.astype(BF)
+    odd = lon_is_odd()
+    for target, high in ((far_ref, odd), (near_ref, 1 - odd)):
+        part = pl.ds(pl.multiple_of(high * (rows - two), two), two)
+        target[0:two, :] = x_ref[part, :]
+        target[two : 2 * two, :] = cot_ref[part, :]
+        halos = [
+            jnp.where(high == 1, value[:, rows - two :], value[:, :two]).astype(BF) for value in (core, mid)
+        ]
+        target[2 * two :, : 2 * two] = jnp.concatenate(halos, 1)
+        target[2 * two :, 2 * two :] = jnp.zeros((HALF, lat_cells - 2 * two), BF)
 
 
 def halo_place(odd, place, lat_cells):
@@ -186,31 +219,35 @@
             grads_ref[place, q] = summed[:, :128]
 
 
-def edge_kernel(x_ref, cot_ref, core_ref, mid_ref, left_ref, right_ref, first_ref, back_ref, grads_ref,
-                low_ref, high_ref, out_ref, xs_sides, cs_sides):
+def edge_kernel(x_ref, cot_ref, core_ref, mid_ref, far_ref, near_ref, first_ref, back_ref, grads_ref,
+                low_ref, high_ref, out_ref, left_ref, right_ref, xs_sides, cs_sides):
     lat_cells = x_ref.shape[1]
     channels = grads_ref.shape[2]
     odd = is_odd()
     two = 2 * channels
     own_rows = x_ref.shape[0]
     sums = [[grads_ref[place, q][:, : 3 * channels] for q in range(3)] for place in range(2)]
-    for side, (message, target) in enumerate(((left_ref, low_ref), (right_ref, high_ref))):
-        xs, cs = xs_sides.at[side], cs_sides.at[side]
+    far, near = far_ref[...].astype(F32), near_ref[...].astype(F32)
+    left_ref[...] = jnp.where(lon_is_odd() == 1, near, far).astype(BF)
+    right_ref[...] = jnp.where(lon_is_odd() == 1, far, near).astype(BF)
+    sides = ((left_ref, low_ref), (right_ref, high_ref))
+    for side, (message, _) in enumerate(sides):
         own = slice(0, two) if side == 0 else slice(own_rows - two, own_rows)
         sent = message[2 * two : 2 * two + HALF, :]
         sent_halos = jnp.concatenate([sent[:, :two], sent[:, two : 2 * two]], 0).astype(F32)
         own_halos = jnp.concatenate([core_ref[:, own], mid_ref[:, own]], 0).astype(F32)
         order = (sent_halos, own_halos) if side == 0 else (own_halos, sent_halos)
         halos = jnp.concatenate(order, 1).astype(BF)
-        for place, (source, shifted) in enumerate(((x_ref, xs), (cot_ref, cs))):
+        for place, (source, shifted) in enumerate(((x_ref, xs_sides), (cot_ref, cs_sides))):
             sent_rows = message[place * two : (place + 1) * two, :]
             order = (sent_rows, source[own, :]) if side == 0 else (source[own, :], sent_rows)
             columns = dot_rows(halos, halo_place(odd, place, lat_cells))
-            write_shifted(jnp.concatenate(order, 0), columns, shifted, slice(0, 2 * two))
-        rows = slice(0, 2 * two)
-        pre_act = conv_rows(first_ref, xs, rows, two)
-        back_grad = conv_rows(back_ref, cs, rows, two)
-        activation, pre_grad = activate(pre_act, back_grad)
+            write_shifted(jnp.concatenate(order, 0), columns, shifted.at[side], slice(0, 2 * two))
+    rows = slice(0, 2 * two)
+    pre_acts = [conv_rows(first_ref, xs_sides.at[side], rows, two) for side in range(2)]
+    back_grads = [conv_rows(back_ref, cs_sides.at[side], rows, two) for side in range(2)]
+    for side, (_, target) in enumerate(sides):
+        activation, pre_grad = activate(pre_acts[side], back_grads[side])
         pre_grad = pre_grad.astype(BF)
         target[...] = pre_grad
         mine = slice(channels, two) if side == 0 else slice(0, channels)
@@ -218,8 +255,8 @@
         activation = activation[mine].astype(BF)
         pre_grad = pre_grad[mine]
         for q in range(3):
-            sums[0][q] = sums[0][q] + dot_lanes(pre_grad, xs[q, near, :])
-            sums[1][q] = sums[1][q] + dot_lanes(activation, cs[q, near, :])
+            sums[0][q] = sums[0][q] + dot_lanes(pre_grad, xs_sides[side, q, near, :])
+            sums[1][q] = sums[1][q] + dot_lanes(activation, cs_sides[side, q, near, :])
     out_ref[...] = jnp.concatenate([pack_taps(taps) for taps in sums], 0)
 
 
@@ -358,12 +395,15 @@
             two_ref[2 - p, 2 - q] = second[q][:, lanes].T
 
 
-def pairs(counts, partner):
+ALONG_X, ALONG_Y = 32, 1
+
+
+def pairs(counts, partner, idle):
     lat_count, lon_count = counts
     listed = []
     for lat in range(lat_count):
         for lon in range(lon_count):
-            to_lat, to_lon = partner(lat, lon) if lat % 2 else (lat, lon ^ 32)
+            to_lat, to_lon = partner(lat, lon) if lat % 2 else (lat, lon ^ idle)
             listed.append((lat * lon_count + lon, to_lat * lon_count + to_lon))
     return listed
 
@@ -384,13 +424,13 @@
     return lambda lat, lon: (lat, lon ^ (mask << 2))
 
 
-def exchange(value, partner):
+def exchange(value, partner, idle):
     counts = (lax.axis_size("lat"), lax.axis_size("lon"))
-    return lax.ppermute(value, ("lat", "lon"), pairs(counts, partner))
-
-
-def sum_of_four(value, partner, masks, beside=None):
-    first, second, third = [exchange(value, partner(mask)) for mask in masks]
+    return lax.ppermute(value, ("lat", "lon"), pairs(counts, partner, idle))
+
+
+def sum_of_four(value, partner, masks, idle, beside=None):
+    first, second, third = [exchange(value, partner(mask), idle) for mask in masks]
     result = None
     if beside is not None:
         *result, value = beside(value)
@@ -398,22 +438,24 @@
 
 
 def sum_everywhere(mine, widen, finish):
-    swap = [(lat, lat ^ 1) for lat in range(lax.axis_size("lat"))]
-    total = mine + lax.ppermute(mine, "lat", swap)
-    total, _ = sum_of_four(total, x_partner, (1, 3, 2))
-    total, shifted = sum_of_four(total, y_partner, (1, 3, 2), widen)
-    total, _ = sum_of_four(total, z_partner, (1, 2, 3))
-    far = exchange(total, z_partner(6))
-    input_grad, total = finish(*shifted, total)
-    total = total + far
-    given = lax.ppermute(total, "lat", swap)
+    total = mine + core_exchange(mine)
+    total, _ = sum_of_four(total, x_partner, (1, 3, 2), ALONG_Y)
+    total, shifted = sum_of_four(total, y_partner, (1, 3, 2), ALONG_X, widen)
+    total, (input_grad,) = sum_of_four(
+        total, z_partner, (1, 2, 3), ALONG_X, lambda value: finish(*shifted, value)
+    )
+    total = total + exchange(total, z_partner(6), ALONG_X)
+    given = core_exchange(total)
     return total, given, input_grad
 
 
-def lat_exchange(core, mid):
+def mid_exchange(edges):
     count = lax.axis_size("lat")
-    mid = lax.ppermute(mid, "lat", [(i, (i - 1 if i % 2 == 0 else i + 1) % count) for i in range(count)])
-    return lax.ppermute(core, "lat", [(i, i ^ 1) for i in range(count)]), mid
+    return lax.ppermute(edges, "lat", [(i, (i - 1 if i % 2 == 0 else i + 1) % count) for i in range(count)])
+
+
+def core_exchange(value):
+    return lax.ppermute(value, "lat", [(i, i ^ 1) for i in range(lax.axis_size("lat"))])
 
 
 def on_device(inputs, kernel_one, kernel_two, cotangent):
@@ -423,6 +465,7 @@
     two = 2 * channels
     parts = lon_cells // HALF
     weights = shape(3, GROUP * channels, WINDOW * channels)
+    folded = shape(4 * rows // lat_cells, lat_cells)
     raw, one, two_kernel, perm, core_out, mid_out = call(
         border_kernel,
         [
@@ -430,8 +473,8 @@
             shape(*kernel_one.shape),
             shape(*kernel_two.shape),
             shape(HALF * channels, HALF * channels),
-            shape(HALF, rows),
-            shape(HALF, rows),
+            folded,
+            folded,
         ],
         [pltpu.SemaphoreType.DMA((2 + 2 * parts,))],
         10**8,
@@ -441,28 +484,28 @@
         kernel_two,
         hbm_in=(0, 1, 2, 3),
     )
-    core_in, mid_in = lat_exchange(core_out, mid_out)
-    x_rows, cot_rows, first, back = call(
+    mid_in = mid_exchange(mid_out)
+    x_rows, cot_rows, first, back, core_out = call(
         row_kernel,
-        [shape(rows, lat_cells), shape(rows, lat_cells), weights, weights],
+        [shape(rows, lat_cells), shape(rows, lat_cells), weights, weights, folded],
         [],
         10**9,
         raw,
         perm,
         one,
         two_kernel,
-    )
-
-    def message(part):
-        pieces = jnp.concatenate([core_in[:, part], mid_in[:, part]], 1)
-        pieces = jnp.pad(pieces, ((0, 0), (0, lat_cells - 2 * two)))
-        return jnp.concatenate([x_rows[part], cot_rows[part], pieces], 0)
-
+        core_out,
+    )
+    core_in = core_exchange(core_out)
+
+    message = shape(2 * two + HALF, lat_cells)
+    edges = shape(HALF, rows)
+    far_out, near_out, core_in, mid_in = call(
+        message_kernel, [message, message, edges, edges], [], 10**6, x_rows, cot_rows, core_in, mid_in
+    )
     count = lax.axis_size("lon")
-    to_left = message(slice(0, two))
-    to_right = message(slice(rows - two, rows))
-    from_left = lax.ppermute(to_right, "lon", [(i, (i + 1) % count) for i in range(count)])
-    from_right = lax.ppermute(to_left, "lon", [((i + 1) % count, i) for i in range(count)])
+    far_in = lax.ppermute(far_out, "lon", [(i, (i + 1 if i % 2 else i - 1) % count) for i in range(count)])
+    near_in = lax.ppermute(near_out, "lon", [(i, i ^ 1) for i in range(count)])
 
     inner_rows = rows - two
     shifted = pltpu.VMEM((3, rows, lat_cells), BF)
@@ -475,12 +518,12 @@
     )
     edge_shifted = pltpu.VMEM((2, 3, 2 * two, lat_cells), BF)
     partial = shape(2 * 9 * channels * channels // 128, 128, dtype=F32)
-    pre_low, pre_high, grads = call(
+    pre_low, pre_high, grads, from_left, from_right = call(
         edge_kernel,
-        [shape(two, lat_cells), shape(two, lat_cells), partial],
+        [shape(two, lat_cells), shape(two, lat_cells), partial, message, message],
         [edge_shifted, edge_shifted],
         10**9,
-        x_rows, cot_rows, core_in, mid_in, from_left, from_right, first, back, inner_grads,
+        x_rows, cot_rows, core_in, mid_in, far_in, near_in, first, back, inner_grads,
     )
     def widen(partial):
         return call(

time: 52.2 us -> 51.8 us (level)
  starting transfers between devices: 23.9 us -> 25.6 us
  waiting for transfers between devices: 15.7 us -> 14 us
    ppermute x16, starting transfers between devices: 23.9 us -> 25.6 us  [the longest x10 10.8 us: exchange(): return lax.ppermute(value, ('lat', 'lon'), pairs(counts, partner, idle))]
    ppermute x16, waiting for transfers between devices: 15.7 us -> 14 us  [the longest x10 10.4 us: exchange(): return lax.ppermute(value, ('lat', 'lon'), pairs(counts, partner, idle))]
    pallas_call x7 -> x8, Pallas kernels: 11.3 us -> 11.1 us  [call(): pl.pallas_call(kernel, out_shape=outs, in_specs=[pl.BlockSpec(memory_spac...]
  transfers between devices with their start and end apart: 16 -> 16, of which waited for: 11 -> 12; matrix products, arithmetic and copies ran while one was open for 0% -> 0% of each run, Pallas kernels for 14% -> 14%
where the time goes in v6:
time: 51.8 us; the launch traced here: 51.7 us
  starting transfers between devices  25.6 us (49%)
  waiting for transfers between devices  14 us (27%)
  Pallas kernels  11.1 us (21%)
  between operations  0.78 us (2%)
    pallas_call x8, Pallas kernels, call(): pl.pallas_call(kernel, out_shape=outs, in_specs=[pl.BlockSpec(memory_spac...  11.1 us
    ppermute x10, starting transfers between devices, exchange(): return lax.ppermute(value, ('lat', 'lon'), pairs(counts, partner, idle))  10.8 us
    ppermute x10, waiting for transfers between devices, exchange(): return lax.ppermute(value, ('lat', 'lon'), pairs(counts, partner, idle))  10.4 us
    ppermute x1, starting transfers between devices, on_device(): lax.ppermute(far_out, 'lon', [(i, (i + 1 if i % 2 else i - 1) % count) fo...  8.5 us
    ppermute x1, starting transfers between devices, mid_exchange(): lax.ppermute(edges, 'lat', [(i, (i - 1 if i % 2 == 0 else i + 1) % count)...  4.22 us
    ppermute x3, waiting for transfers between devices, core_exchange(): lax.ppermute(value, 'lat', [(i, i ^ 1) for i in range(lax.axis_size('lat'...  2.92 us
    ppermute x3, starting transfers between devices, core_exchange(): lax.ppermute(value, 'lat', [(i, i ^ 1) for i in range(lax.axis_size('lat'...  2.09 us
  transfers between devices with their start and end apart: 16, of which 12 were waited for; matrix products, arithmetic and copies ran while one was open for 0% of the time, Pallas kernels for 14%

profile of v6, /device:TPU:1, one launch (start us, length us, event | category | flops | bytes accessed | tf_op | source)
XLA Modules:
  0.0 51.7 jit_solution(16132807736001147059)
XLA Ops:
  0.6 2.1 %shard_map.67 = (bf16[4,32,16,256]{3,2,1,0:T(8,128)(2,1)S(1)}, bf16[3,3,32,32]{3,2,1,0:T(8,128)(2,1)S(1)}, bf16[3,3,32,32]{3,2,1,0:T(8,128)(2,1)S(1)}, bf16[512,...) custom-call(bf16[32,32,256]{2,1,0:T(8,128)(2,1)} %x_hbm.1, ...), custom_call_target="tpu_custom_call" | custom-call | flops 100000000 | bytes 2711552 | tf_op jit(solution)/shard_map/pallas_call | solution.py:40
  2.8 4.2 %collective-permute-start.1 = (bf16[16,256]{1,0:T(8,128)(2,1)S(1)}, bf16[16,256]{1,0:T(8,128)(2,1)S(1)}, u32[]{:S(2)}, u32[]{:S(2)}) collective-permute-start(bf16[16,256]{1,0:T(8,128)(2,1)S(1)} %get-tuple-element.40), channel_id=1, source_target_pairs={{0,192},{64,128},{128,64},{192,0},{1,193},{65,129},{129,65},{193,1... | collective-permute-start | bytes 24584 | tf_op jit(solution)/shard_map/ppermute | solution.py:454
  7.0 0.8 %shard_map.68 = (bf16[1024,256]{1,0:T(8,128)(2,1)S(1)}, bf16[1024,256]{1,0:T(8,128)(2,1)S(1)}, bf16[3,192,256]{2,1,0:T(8,128)(2,1)S(1)}, bf16[3,192,256]{2,1,0:T(8,128)(2,1)S(1)}, bf16[16,256]{1,0:T(8,128)(2,1)S(1)}) custom-call(bf16[4,32,16,256]{3,2,1,0:T(8,128)(2,1)S(1)} %get-tuple-element.32.raw_ref, bf16[512,512]{1,0:T(8,128)(2,1)S(1)} %get-tuple-element.33.perm_ref, ...), custom_call_target="tpu_custom_call" | custom-call | flops 1000000000 | bytes 3264512 | tf_op jit(solution)/shard_map/pallas_call | solution.py:40
  7.8 0.1 collective-permute-start
  7.9 0.4 collective-permute-done.1.mid_in
  8.3 0.8 %collective-permute-done.core_in = bf16[16,256]{1,0:T(8,128)(2,1)S(1)} collective-permute-done((bf16[16,256]{1,0:T(8,128)(2,1)S(1)}, bf16[16,256]{1,0:T(8,128)(2,1)S(1)}, u32[]{:S(2)}, u32[]{:S(2)}) %collective-permute-start) | collective-permute-done | bytes 8224 | tf_op jit(solution)/shard_map/ppermute | solution.py:458
  9.1 0.1 shard_map.69
  9.2 8.5 %collective-permute-start.2 = (bf16[144,256]{1,0:T(8,128)(2,1)S(1)}, bf16[144,256]{1,0:T(8,128)(2,1)S(1)}, u32[]{:S(2)}, u32[]{:S(2)}) collective-permute-start(bf16[144,256]{1,0:T(8,128)(2,1)S(1)} %get-tuple-element.43), channel_id=1, source_target_pairs={{0,63},{1,2},{2,1},{3,4},{4,3},{5,6},{6,5},{7,8},{8,7},{9,10},{10,... | collective-permute-start | bytes 221192 | tf_op jit(solution)/shard_map/ppermute | solution.py:507
  17.7 0.0 collective-permute-start.3
  17.7 2.9 %shard_map.70 = (bf16[960,256]{1,0:T(8,128)(2,1)S(1)}, f32[2,3,32,128]{3,2,1,0:T(8,128)S(1)}) custom-call(bf16[1024,256]{1,0:T(8,128)(2,1)S(1)} %get-tuple-element.37.x_ref, bf16[1024,256]{1,0:T(8,128)(2,1)S(1)} %get-tuple-element.38.cot_ref, bf16[16,1024]{1,0:T(8,128)(2,1)S(1)} %get-tuple-element.41.core_ref, ...), custom_call_target="tpu_custom_call" | custom-call | flops 4000000000 | bytes 2293760 | tf_op jit(solution)/shard_map/pallas_call | solution.py:40
  20.6 0.0 collective-permute-done.2.far_ref
  20.6 0.3 collective-permute-done.3.near_ref
  20.9 0.9 %shard_map.71 = (bf16[64,256]{1,0:T(8,128)(2,1)S(1)}, bf16[64,256]{1,0:T(8,128)(2,1)S(1)}, f32[144,128]{1,0:T(8,128)S(1)}, bf16[144,256]{1,0:T(8,128)(2,1)S(1)}, bf16[144,256]{1,0:T(8,128)(2,1)S(1)}) custom-call(bf16[1024,256]{1,0:T(8,128)(2,1)S(1)} %get-tuple-element.37.x_ref, bf16[1024,256]{1,0:T(8,128)(2,1)S(1)} %get-tuple-element.38.cot_ref, ...), custom_call_target="tpu_custom_call" | custom-call | flops 1000000000 | bytes 2236416 | tf_op jit(solution)/shard_map/pallas_call | solution.py:40
  21.8 1.9 %collective-permute-start.4 = (f32[144,128]{1,0:T(8,128)S(1)}, f32[144,128]{1,0:T(8,128)S(1)}, u32[]{:S(2)}, u32[]{:S(2)}) collective-permute-start(f32[144,128]{1,0:T(8,128)S(1)} %get-tuple-element.53), channel_id=1, source_target_pairs={{0,64},{64,0},{128,192},{192,128},{1,65},{65,1},{129,193},{193,129... | collective-permute-start | bytes 221192 | tf_op jit(solution)/shard_map/ppermute | solution.py:458
  23.7 0.9 %collective-permute-done.4 = f32[144,128]{1,0:T(8,128)S(1)} collective-permute-done((f32[144,128]{1,0:T(8,128)S(1)}, f32[144,128]{1,0:T(8,128)S(1)}, u32[]{:S(2)}, u32[]{:S(2)}) %collective-permute-start.4) | collective-permute-done | bytes 73760 | tf_op jit(solution)/shard_map/ppermute | solution.py:458
  24.6 2.5 %collective-permute-start.7 = (f32[144,128]{1,0:T(8,128)S(1)}, f32[144,128]{1,0:T(8,128)S(1)}, u32[]{:S(2)}, u32[]{:S(2)}) collective-permute-start(f32[144,128]{1,0:T(8,128)S(1)} %add.33), channel_id=1, source_target_pairs={{0,1},{1,0},{2,3},{3,2},{4,5},{5,4},{6,7},{7,6},{8,9},{9,8},{10,11... | collective-permute-start | bytes 221192 | tf_op jit(solution)/shard_map/ppermute | solution.py:429
  27.2 0.4 collective-permute-start.6
  27.6 0.0 collective-permute-start.5
  27.6 1.8 %collective-permute-done.7 = f32[144,128]{1,0:T(8,128)S(1)} collective-permute-done((f32[144,128]{1,0:T(8,128)S(1)}, f32[144,128]{1,0:T(8,128)S(1)}, u32[]{:S(2)}, u32[]{:S(2)}) %collective-permute-start.7) | collective-permute-done | bytes 73760 | tf_op jit(solution)/shard_map/ppermute | solution.py:429
  29.4 2.2 %collective-permute-done.6 = f32[144,128]{1,0:T(8,128)S(1)} collective-permute-done((f32[144,128]{1,0:T(8,128)S(1)}, f32[144,128]{1,0:T(8,128)S(1)}, u32[]{:S(2)}, u32[]{:S(2)}) %collective-permute-start.6) | collective-permute-done | bytes 73760 | tf_op jit(solution)/shard_map/ppermute | solution.py:429
  31.6 0.0 collective-permute-done.5
  31.6 0.1 collective-permute-start.10
  31.7 2.7 %collective-permute-start.9 = (f32[144,128]{1,0:T(8,128)S(1)}, f32[144,128]{1,0:T(8,128)S(1)}, u32[]{:S(2)}, u32[]{:S(2)}) collective-permute-start(f32[144,128]{1,0:T(8,128)S(1)} %add_add_fusion.2.partial_ref), channel_id=1, source_target_pairs={{0,32},{1,33},{2,34},{3,35},{4,36},{5,37},{6,38},{7,39},{8,40},{9,... | collective-permute-start | bytes 221192 | tf_op jit(solution)/shard_map/ppermute | solution.py:429
  34.4 0.0 collective-permute-start.8
  34.4 1.2 %shard_map.72 = (bf16[3,1088,256]{2,1,0:T(8,128)(2,1)S(1)}, bf16[3,192,256]{2,1,0:T(8,128)(2,1)S(1)}, f32[144,128]{1,0:T(8,128)S(1)}) custom-call(bf16[1024,256]{1,0:T(8,128)(2,1)S(1)} %get-tuple-element.37.x_ref, bf16[1024,256]{1,0:T(8,128)(2,1)S(1)} %get-tuple-element.38.cot_ref, bf16[16,1024]{1,0:T(8,128)(2,1)S(1)} %get-tuple-element.41.core_ref, ...), custom_call_target="tpu_custom_call" | custom-call | flops 1000000000 | bytes 4540416 | tf_op jit(solution)/shard_map/pallas_call | solution.py:40
  35.6 0.9 %collective-permute-done.10 = f32[144,128]{1,0:T(8,128)S(1)} collective-permute-done((f32[144,128]{1,0:T(8,128)S(1)}, f32[144,128]{1,0:T(8,128)S(1)}, u32[]{:S(2)}, u32[]{:S(2)}) %collective-permute-start.10) | collective-permute-done | bytes 73760 | tf_op jit(solution)/shard_map/ppermute | solution.py:429
  36.5 0.5 collective-permute-done.9
  37.0 0.6 %collective-permute-done.8 = f32[144,128]{1,0:T(8,128)S(1)} collective-permute-done((f32[144,128]{1,0:T(8,128)S(1)}, f32[144,128]{1,0:T(8,128)S(1)}, u32[]{:S(2)}, u32[]{:S(2)}) %collective-permute-start.8) | collective-permute-done | bytes 73760 | tf_op jit(solution)/shard_map/ppermute | solution.py:429
  37.6 0.1 collective-permute-start.13
  37.7 0.1 collective-permute-start.12
  37.8 3.4 %collective-permute-start.11 = (f32[144,128]{1,0:T(8,128)S(1)}, f32[144,128]{1,0:T(8,128)S(1)}, u32[]{:S(2)}, u32[]{:S(2)}) collective-permute-start(f32[144,128]{1,0:T(8,128)S(1)} %add_add_fusion.1.partial_ref), channel_id=1, source_target_pairs={{0,32},{1,33},{2,34},{3,35},{4,36},{5,37},{6,38},{7,39},{8,40},{9,... | collective-permute-start | bytes 221192 | tf_op jit(solution)/shard_map/ppermute | solution.py:429
  41.3 2.2 %shard_map.73 = (bf16[32,32,256]{2,1,0:T(8,128)(2,1)}, f32[144,128]{1,0:T(8,128)S(1)}) custom-call(bf16[3,1088,256]{2,1,0:T(8,128)(2,1)S(1)} %get-tuple-element.54.ps, bf16[3,192,256]{2,1,0:T(8,128)(2,1)S(1)} %get-tuple-element.55.last_ref, bf16[4,32,16,256]{3,2,1,0:T(8,128)(2,1)S(1)} %get-tuple-element.32.raw_ref, f32[144,128]{1,0:T(8,128)S(1)} %add_add_fusion.1.partial_ref), custom_call_target="tpu_custom_call" | custom-call | flops 2000000000 | bytes 3686400 | tf_op jit(solution)/shard_map/pallas_call | solution.py:40
  43.4 0.0 collective-permute-done.13
  43.5 0.0 collective-permute-done.12
  43.5 0.3 collective-permute-done.11
  43.8 1.4 %collective-permute-start.14 = (f32[144,128]{1,0:T(8,128)S(1)}, f32[144,128]{1,0:T(8,128)S(1)}, u32[]{:S(2)}, u32[]{:S(2)}) collective-permute-start(f32[144,128]{1,0:T(8,128)S(1)} %add_add_fusion), channel_id=1, source_target_pairs={{0,32},{1,33},{2,34},{3,35},{4,36},{5,37},{6,38},{7,39},{8,40},{9,... | collective-permute-start | bytes 221192 | tf_op jit(solution)/shard_map/ppermute | solution.py:429
  45.3 4.1 %collective-permute-done.14 = f32[144,128]{1,0:T(8,128)S(1)} collective-permute-done((f32[144,128]{1,0:T(8,128)S(1)}, f32[144,128]{1,0:T(8,128)S(1)}, u32[]{:S(2)}, u32[]{:S(2)}) %collective-permute-start.14) | collective-permute-done | bytes 73760 | tf_op jit(solution)/shard_map/ppermute | solution.py:429
  49.3 0.1 collective-permute-start.15
  49.4 1.3 %collective-permute-done.15.given_ref = f32[144,128]{1,0:T(8,128)S(1)} collective-permute-done((f32[144,128]{1,0:T(8,128)S(1)}, f32[144,128]{1,0:T(8,128)S(1)}, u32[]{:S(2)}, u32[]{:S(2)}) %collective-permute-start.15) | collective-permute-done | bytes 73760 | tf_op jit(solution)/shard_map/ppermute | solution.py:458
  50.7 1.0 %shard_map.74 = (f32[3,3,32,32]{3,2,1,0:T(8,128)}, f32[3,3,32,32]{3,2,1,0:T(8,128)}) custom-call(f32[144,128]{1,0:T(8,128)S(1)} %add.43.total_ref, f32[144,128]{1,0:T(8,128)S(1)} %collective-permute-done.15.given_ref), custom_call_target="tpu_custom_call" | custom-call | flops 1000000 | bytes 221184 | tf_op jit(solution)/shard_map/pallas_call | solution.py:40
  (5 shorter events, 0.1 us)
Async XLA Ops:
  2.8 5.6 %collective-permute-start.1 = (bf16[16,256]{1,0:T(8,128)(2,1)S(1)}, bf16[16,256]{1,0:T(8,128)(2,1)S(1)}, u32[]{:S(2)}, u32[]{:S(2)}) collective-permute-start(bf16[16,256]{1,0:T(8,128)(2,1)S(1)} %get-tuple-element.40), channel_id=1, source_target_pairs={{0,192},{64,128},{128,64},{192,0},{1,193},{65,129},{129,65},{193,1... | collective-permute-start | bytes 24584 | tf_op jit(solution)/shard_map/ppermute | solution.py:454
  7.8 1.3 %collective-permute-start = (bf16[16,256]{1,0:T(8,128)(2,1)S(1)}, bf16[16,256]{1,0:T(8,128)(2,1)S(1)}, u32[]{:S(2)}, u32[]{:S(2)}) collective-permute-start(bf16[16,256]{1,0:T(8,128)(2,1)S(1)} %get-tuple-element.39), channel_id=1, source_target_pairs={{0,64},{64,0},{128,192},{192,128},{1,65},{65,1},{129,193},{193,129... | collective-permute-start | bytes 24584 | tf_op jit(solution)/shard_map/ppermute | solution.py:458
  9.2 11.4 %collective-permute-start.2 = (bf16[144,256]{1,0:T(8,128)(2,1)S(1)}, bf16[144,256]{1,0:T(8,128)(2,1)S(1)}, u32[]{:S(2)}, u32[]{:S(2)}) collective-permute-start(bf16[144,256]{1,0:T(8,128)(2,1)S(1)} %get-tuple-element.43), channel_id=1, source_target_pairs={{0,63},{1,2},{2,1},{3,4},{4,3},{5,6},{6,5},{7,8},{8,7},{9,10},{10,... | collective-permute-start | bytes 221192 | tf_op jit(solution)/shard_map/ppermute | solution.py:507
  17.7 3.2 %collective-permute-start.3 = (bf16[144,256]{1,0:T(8,128)(2,1)S(1)}, bf16[144,256]{1,0:T(8,128)(2,1)S(1)}, u32[]{:S(2)}, u32[]{:S(2)}) collective-permute-start(bf16[144,256]{1,0:T(8,128)(2,1)S(1)} %get-tuple-element.44), channel_id=1, source_target_pairs={{0,1},{1,0},{2,3},{3,2},{4,5},{5,4},{6,7},{7,6},{8,9},{9,8},{10,11... | collective-permute-start | bytes 221192 | tf_op jit(solution)/shard_map/ppermute | solution.py:508
  21.8 2.8 %collective-permute-start.4 = (f32[144,128]{1,0:T(8,128)S(1)}, f32[144,128]{1,0:T(8,128)S(1)}, u32[]{:S(2)}, u32[]{:S(2)}) collective-permute-start(f32[144,128]{1,0:T(8,128)S(1)} %get-tuple-element.53), channel_id=1, source_target_pairs={{0,64},{64,0},{128,192},{192,128},{1,65},{65,1},{129,193},{193,129... | collective-permute-start | bytes 221192 | tf_op jit(solution)/shard_map/ppermute | solution.py:458
  24.6 4.8 %collective-permute-start.7 = (f32[144,128]{1,0:T(8,128)S(1)}, f32[144,128]{1,0:T(8,128)S(1)}, u32[]{:S(2)}, u32[]{:S(2)}) collective-permute-start(f32[144,128]{1,0:T(8,128)S(1)} %add.33), channel_id=1, source_target_pairs={{0,1},{1,0},{2,3},{3,2},{4,5},{5,4},{6,7},{7,6},{8,9},{9,8},{10,11... | collective-permute-start | bytes 221192 | tf_op jit(solution)/shard_map/ppermute | solution.py:429
  27.2 4.4 %collective-permute-start.6 = (f32[144,128]{1,0:T(8,128)S(1)}, f32[144,128]{1,0:T(8,128)S(1)}, u32[]{:S(2)}, u32[]{:S(2)}) collective-permute-start(f32[144,128]{1,0:T(8,128)S(1)} %add.33), channel_id=1, source_target_pairs={{0,1},{1,0},{2,3},{3,2},{4,5},{5,4},{6,7},{7,6},{8,9},{9,8},{10,11... | collective-permute-start | bytes 221192 | tf_op jit(solution)/shard_map/ppermute | solution.py:429
  27.6 4.0 %collective-permute-start.5 = (f32[144,128]{1,0:T(8,128)S(1)}, f32[144,128]{1,0:T(8,128)S(1)}, u32[]{:S(2)}, u32[]{:S(2)}) collective-permute-start(f32[144,128]{1,0:T(8,128)S(1)} %add.33), channel_id=1, source_target_pairs={{0,1},{1,0},{2,3},{3,2},{4,5},{5,4},{6,7},{7,6},{8,9},{9,8},{10,11... | collective-permute-start | bytes 221192 | tf_op jit(solution)/shard_map/ppermute | solution.py:429
  31.6 4.9 %collective-permute-start.10 = (f32[144,128]{1,0:T(8,128)S(1)}, f32[144,128]{1,0:T(8,128)S(1)}, u32[]{:S(2)}, u32[]{:S(2)}) collective-permute-start(f32[144,128]{1,0:T(8,128)S(1)} %add_add_fusion.2.partial_ref), channel_id=1, source_target_pairs={{0,32},{1,33},{2,34},{3,35},{4,36},{5,37},{6,38},{7,39},{8,40},{9,... | collective-permute-start | bytes 221192 | tf_op jit(solution)/shard_map/ppermute | solution.py:429
  31.7 5.3 %collective-permute-start.9 = (f32[144,128]{1,0:T(8,128)S(1)}, f32[144,128]{1,0:T(8,128)S(1)}, u32[]{:S(2)}, u32[]{:S(2)}) collective-permute-start(f32[144,128]{1,0:T(8,128)S(1)} %add_add_fusion.2.partial_ref), channel_id=1, source_target_pairs={{0,32},{1,33},{2,34},{3,35},{4,36},{5,37},{6,38},{7,39},{8,40},{9,... | collective-permute-start | bytes 221192 | tf_op jit(solution)/shard_map/ppermute | solution.py:429
  34.4 3.2 %collective-permute-start.8 = (f32[144,128]{1,0:T(8,128)S(1)}, f32[144,128]{1,0:T(8,128)S(1)}, u32[]{:S(2)}, u32[]{:S(2)}) collective-permute-start(f32[144,128]{1,0:T(8,128)S(1)} %add_add_fusion.2.partial_ref), channel_id=1, source_target_pairs={{0,32},{1,33},{2,34},{3,35},{4,36},{5,37},{6,38},{7,39},{8,40},{9,... | collective-permute-start | bytes 221192 | tf_op jit(solution)/shard_map/ppermute | solution.py:429
  37.6 5.8 %collective-permute-start.13 = (f32[144,128]{1,0:T(8,128)S(1)}, f32[144,128]{1,0:T(8,128)S(1)}, u32[]{:S(2)}, u32[]{:S(2)}) collective-permute-start(f32[144,128]{1,0:T(8,128)S(1)} %add_add_fusion.1.partial_ref), channel_id=1, source_target_pairs={{0,32},{1,33},{2,34},{3,35},{4,36},{5,37},{6,38},{7,39},{8,40},{9,... | collective-permute-start | bytes 221192 | tf_op jit(solution)/shard_map/ppermute | solution.py:429
  37.7 5.7 %collective-permute-start.12 = (f32[144,128]{1,0:T(8,128)S(1)}, f32[144,128]{1,0:T(8,128)S(1)}, u32[]{:S(2)}, u32[]{:S(2)}) collective-permute-start(f32[144,128]{1,0:T(8,128)S(1)} %add_add_fusion.1.partial_ref), channel_id=1, source_target_pairs={{0,32},{1,33},{2,34},{3,35},{4,36},{5,37},{6,38},{7,39},{8,40},{9,... | collective-permute-start | bytes 221192 | tf_op jit(solution)/shard_map/ppermute | solution.py:429
  37.8 6.0 %collective-permute-start.11 = (f32[144,128]{1,0:T(8,128)S(1)}, f32[144,128]{1,0:T(8,128)S(1)}, u32[]{:S(2)}, u32[]{:S(2)}) collective-permute-start(f32[144,128]{1,0:T(8,128)S(1)} %add_add_fusion.1.partial_ref), channel_id=1, source_target_pairs={{0,32},{1,33},{2,34},{3,35},{4,36},{5,37},{6,38},{7,39},{8,40},{9,... | collective-permute-start | bytes 221192 | tf_op jit(solution)/shard_map/ppermute | solution.py:429
  43.8 5.5 %collective-permute-start.14 = (f32[144,128]{1,0:T(8,128)S(1)}, f32[144,128]{1,0:T(8,128)S(1)}, u32[]{:S(2)}, u32[]{:S(2)}) collective-permute-start(f32[144,128]{1,0:T(8,128)S(1)} %add_add_fusion), channel_id=1, source_target_pairs={{0,32},{1,33},{2,34},{3,35},{4,36},{5,37},{6,38},{7,39},{8,40},{9,... | collective-permute-start | bytes 221192 | tf_op jit(solution)/shard_map/ppermute | solution.py:429
  49.3 1.4 %collective-permute-start.15 = (f32[144,128]{1,0:T(8,128)S(1)}, f32[144,128]{1,0:T(8,128)S(1)}, u32[]{:S(2)}, u32[]{:S(2)}) collective-permute-start(f32[144,128]{1,0:T(8,128)S(1)} %add.43.total_ref), channel_id=1, source_target_pairs={{0,64},{64,0},{128,192},{192,128},{1,65},{65,1},{129,193},{193,129... | collective-permute-start | bytes 221192 | tf_op jit(solution)/shard_map/ppermute | solution.py:458

commit v7 on v6

--- a/solution.py
+++ b/solution.py
@@ -172,7 +172,7 @@
 
 
 def activate(pre_act, back_grad):
-    sigmoid_value = 0.5 * jnp.tanh(0.5 * pre_act) + 0.5
+    sigmoid_value = 1.0 / (1.0 + jnp.exp(-pre_act))
     activation = pre_act * sigmoid_value
     slope = sigmoid_value + activation * (1.0 - sigmoid_value)
     return activation, back_grad * slope

time: 51.8 us -> 51.8 us (level)
  no operation moved by 1% of the time
where the time goes in v7:
time: 51.8 us; the launch traced here: 51.7 us
  starting transfers between devices  25.6 us (49%)
  waiting for transfers between devices  14 us (27%)
  Pallas kernels  11.2 us (22%)
  between operations  0.78 us (2%)
    pallas_call x8, Pallas kernels, call(): pl.pallas_call(kernel, out_shape=outs, in_specs=[pl.BlockSpec(memory_spac...  11.2 us
    ppermute x10, starting transfers between devices, exchange(): return lax.ppermute(value, ('lat', 'lon'), pairs(counts, partner, idle))  10.8 us
    ppermute x10, waiting for transfers between devices, exchange(): return lax.ppermute(value, ('lat', 'lon'), pairs(counts, partner, idle))  10.4 us
    ppermute x1, starting transfers between devices, on_device(): lax.ppermute(far_out, 'lon', [(i, (i + 1 if i % 2 else i - 1) % count) fo...  8.5 us
    ppermute x1, starting transfers between devices, mid_exchange(): lax.ppermute(edges, 'lat', [(i, (i - 1 if i % 2 == 0 else i + 1) % count)...  4.22 us
    ppermute x3, waiting for transfers between devices, core_exchange(): lax.ppermute(value, 'lat', [(i, i ^ 1) for i in range(lax.axis_size('lat'...  2.92 us
    ppermute x3, starting transfers between devices, core_exchange(): lax.ppermute(value, 'lat', [(i, i ^ 1) for i in range(lax.axis_size('lat'...  2.1 us
  transfers between devices with their start and end apart: 16, of which 12 were waited for; matrix products, arithmetic and copies ran while one was open for 0% of the time, Pallas kernels for 14%

profile of v7, /device:TPU:1, one launch (start us, length us, event | category | flops | bytes accessed | tf_op | source)
XLA Modules:
  0.0 51.7 jit_solution(11960255726526100434)
XLA Ops:
  0.6 2.1 %shard_map.67 = (bf16[4,32,16,256]{3,2,1,0:T(8,128)(2,1)S(1)}, bf16[3,3,32,32]{3,2,1,0:T(8,128)(2,1)S(1)}, bf16[3,3,32,32]{3,2,1,0:T(8,128)(2,1)S(1)}, bf16[512,...) custom-call(bf16[32,32,256]{2,1,0:T(8,128)(2,1)} %x_hbm.1, ...), custom_call_target="tpu_custom_call" | custom-call | flops 100000000 | bytes 2711552 | tf_op jit(solution)/shard_map/pallas_call | solution.py:40
  2.8 4.2 %collective-permute-start.1 = (bf16[16,256]{1,0:T(8,128)(2,1)S(1)}, bf16[16,256]{1,0:T(8,128)(2,1)S(1)}, u32[]{:S(2)}, u32[]{:S(2)}) collective-permute-start(bf16[16,256]{1,0:T(8,128)(2,1)S(1)} %get-tuple-element.40), channel_id=1, source_target_pairs={{0,192},{64,128},{128,64},{192,0},{1,193},{65,129},{129,65},{193,1... | collective-permute-start | bytes 24584 | tf_op jit(solution)/shard_map/ppermute | solution.py:454
  7.0 0.8 %shard_map.68 = (bf16[1024,256]{1,0:T(8,128)(2,1)S(1)}, bf16[1024,256]{1,0:T(8,128)(2,1)S(1)}, bf16[3,192,256]{2,1,0:T(8,128)(2,1)S(1)}, bf16[3,192,256]{2,1,0:T(8,128)(2,1)S(1)}, bf16[16,256]{1,0:T(8,128)(2,1)S(1)}) custom-call(bf16[4,32,16,256]{3,2,1,0:T(8,128)(2,1)S(1)} %get-tuple-element.32.raw_ref, bf16[512,512]{1,0:T(8,128)(2,1)S(1)} %get-tuple-element.33.perm_ref, ...), custom_call_target="tpu_custom_call" | custom-call | flops 1000000000 | bytes 3264512 | tf_op jit(solution)/shard_map/pallas_call | solution.py:40
  7.8 0.1 collective-permute-start
  7.9 0.4 collective-permute-done.1.mid_in
  8.3 0.8 %collective-permute-done.core_in = bf16[16,256]{1,0:T(8,128)(2,1)S(1)} collective-permute-done((bf16[16,256]{1,0:T(8,128)(2,1)S(1)}, bf16[16,256]{1,0:T(8,128)(2,1)S(1)}, u32[]{:S(2)}, u32[]{:S(2)}) %collective-permute-start) | collective-permute-done | bytes 8224 | tf_op jit(solution)/shard_map/ppermute | solution.py:458
  9.1 0.1 shard_map.69
  9.2 8.5 %collective-permute-start.2 = (bf16[144,256]{1,0:T(8,128)(2,1)S(1)}, bf16[144,256]{1,0:T(8,128)(2,1)S(1)}, u32[]{:S(2)}, u32[]{:S(2)}) collective-permute-start(bf16[144,256]{1,0:T(8,128)(2,1)S(1)} %get-tuple-element.43), channel_id=1, source_target_pairs={{0,63},{1,2},{2,1},{3,4},{4,3},{5,6},{6,5},{7,8},{8,7},{9,10},{10,... | collective-permute-start | bytes 221192 | tf_op jit(solution)/shard_map/ppermute | solution.py:507
  17.7 0.0 collective-permute-start.3
  17.7 2.9 %shard_map.70 = (bf16[960,256]{1,0:T(8,128)(2,1)S(1)}, f32[2,3,32,128]{3,2,1,0:T(8,128)S(1)}) custom-call(bf16[1024,256]{1,0:T(8,128)(2,1)S(1)} %get-tuple-element.37.x_ref, bf16[1024,256]{1,0:T(8,128)(2,1)S(1)} %get-tuple-element.38.cot_ref, bf16[16,1024]{1,0:T(8,128)(2,1)S(1)} %get-tuple-element.41.core_ref, ...), custom_call_target="tpu_custom_call" | custom-call | flops 4000000000 | bytes 2293760 | tf_op jit(solution)/shard_map/pallas_call | solution.py:40
  20.6 0.0 collective-permute-done.2.far_ref
  20.6 0.3 collective-permute-done.3.near_ref
  20.9 0.9 %shard_map.71 = (bf16[64,256]{1,0:T(8,128)(2,1)S(1)}, bf16[64,256]{1,0:T(8,128)(2,1)S(1)}, f32[144,128]{1,0:T(8,128)S(1)}, bf16[144,256]{1,0:T(8,128)(2,1)S(1)}, bf16[144,256]{1,0:T(8,128)(2,1)S(1)}) custom-call(bf16[1024,256]{1,0:T(8,128)(2,1)S(1)} %get-tuple-element.37.x_ref, bf16[1024,256]{1,0:T(8,128)(2,1)S(1)} %get-tuple-element.38.cot_ref, ...), custom_call_target="tpu_custom_call" | custom-call | flops 1000000000 | bytes 2236416 | tf_op jit(solution)/shard_map/pallas_call | solution.py:40
  21.8 1.9 %collective-permute-start.4 = (f32[144,128]{1,0:T(8,128)S(1)}, f32[144,128]{1,0:T(8,128)S(1)}, u32[]{:S(2)}, u32[]{:S(2)}) collective-permute-start(f32[144,128]{1,0:T(8,128)S(1)} %get-tuple-element.53), channel_id=1, source_target_pairs={{0,64},{64,0},{128,192},{192,128},{1,65},{65,1},{129,193},{193,129... | collective-permute-start | bytes 221192 | tf_op jit(solution)/shard_map/ppermute | solution.py:458
  23.7 0.9 %collective-permute-done.4 = f32[144,128]{1,0:T(8,128)S(1)} collective-permute-done((f32[144,128]{1,0:T(8,128)S(1)}, f32[144,128]{1,0:T(8,128)S(1)}, u32[]{:S(2)}, u32[]{:S(2)}) %collective-permute-start.4) | collective-permute-done | bytes 73760 | tf_op jit(solution)/shard_map/ppermute | solution.py:458
  24.6 2.5 %collective-permute-start.7 = (f32[144,128]{1,0:T(8,128)S(1)}, f32[144,128]{1,0:T(8,128)S(1)}, u32[]{:S(2)}, u32[]{:S(2)}) collective-permute-start(f32[144,128]{1,0:T(8,128)S(1)} %add.33), channel_id=1, source_target_pairs={{0,1},{1,0},{2,3},{3,2},{4,5},{5,4},{6,7},{7,6},{8,9},{9,8},{10,11... | collective-permute-start | bytes 221192 | tf_op jit(solution)/shard_map/ppermute | solution.py:429
  27.2 0.4 collective-permute-start.6
  27.6 0.0 collective-permute-start.5
  27.6 1.8 %collective-permute-done.7 = f32[144,128]{1,0:T(8,128)S(1)} collective-permute-done((f32[144,128]{1,0:T(8,128)S(1)}, f32[144,128]{1,0:T(8,128)S(1)}, u32[]{:S(2)}, u32[]{:S(2)}) %collective-permute-start.7) | collective-permute-done | bytes 73760 | tf_op jit(solution)/shard_map/ppermute | solution.py:429
  29.4 2.2 %collective-permute-done.6 = f32[144,128]{1,0:T(8,128)S(1)} collective-permute-done((f32[144,128]{1,0:T(8,128)S(1)}, f32[144,128]{1,0:T(8,128)S(1)}, u32[]{:S(2)}, u32[]{:S(2)}) %collective-permute-start.6) | collective-permute-done | bytes 73760 | tf_op jit(solution)/shard_map/ppermute | solution.py:429
  31.6 0.0 collective-permute-done.5
  31.6 0.1 collective-permute-start.10
  31.7 2.7 %collective-permute-start.9 = (f32[144,128]{1,0:T(8,128)S(1)}, f32[144,128]{1,0:T(8,128)S(1)}, u32[]{:S(2)}, u32[]{:S(2)}) collective-permute-start(f32[144,128]{1,0:T(8,128)S(1)} %add_add_fusion.2.partial_ref), channel_id=1, source_target_pairs={{0,32},{1,33},{2,34},{3,35},{4,36},{5,37},{6,38},{7,39},{8,40},{9,... | collective-permute-start | bytes 221192 | tf_op jit(solution)/shard_map/ppermute | solution.py:429
  34.4 0.0 collective-permute-start.8
  34.4 1.2 %shard_map.72 = (bf16[3,1088,256]{2,1,0:T(8,128)(2,1)S(1)}, bf16[3,192,256]{2,1,0:T(8,128)(2,1)S(1)}, f32[144,128]{1,0:T(8,128)S(1)}) custom-call(bf16[1024,256]{1,0:T(8,128)(2,1)S(1)} %get-tuple-element.37.x_ref, bf16[1024,256]{1,0:T(8,128)(2,1)S(1)} %get-tuple-element.38.cot_ref, bf16[16,1024]{1,0:T(8,128)(2,1)S(1)} %get-tuple-element.41.core_ref, ...), custom_call_target="tpu_custom_call" | custom-call | flops 1000000000 | bytes 4540416 | tf_op jit(solution)/shard_map/pallas_call | solution.py:40
  35.6 0.9 %collective-permute-done.10 = f32[144,128]{1,0:T(8,128)S(1)} collective-permute-done((f32[144,128]{1,0:T(8,128)S(1)}, f32[144,128]{1,0:T(8,128)S(1)}, u32[]{:S(2)}, u32[]{:S(2)}) %collective-permute-start.10) | collective-permute-done | bytes 73760 | tf_op jit(solution)/shard_map/ppermute | solution.py:429
  36.5 0.5 collective-permute-done.9
  37.0 0.6 %collective-permute-done.8 = f32[144,128]{1,0:T(8,128)S(1)} collective-permute-done((f32[144,128]{1,0:T(8,128)S(1)}, f32[144,128]{1,0:T(8,128)S(1)}, u32[]{:S(2)}, u32[]{:S(2)}) %collective-permute-start.8) | collective-permute-done | bytes 73760 | tf_op jit(solution)/shard_map/ppermute | solution.py:429
  37.7 0.1 collective-permute-start.13
  37.8 0.1 collective-permute-start.12
  37.9 3.4 %collective-permute-start.11 = (f32[144,128]{1,0:T(8,128)S(1)}, f32[144,128]{1,0:T(8,128)S(1)}, u32[]{:S(2)}, u32[]{:S(2)}) collective-permute-start(f32[144,128]{1,0:T(8,128)S(1)} %add_add_fusion.1.partial_ref), channel_id=1, source_target_pairs={{0,32},{1,33},{2,34},{3,35},{4,36},{5,37},{6,38},{7,39},{8,40},{9,... | collective-permute-start | bytes 221192 | tf_op jit(solution)/shard_map/ppermute | solution.py:429
  41.3 2.2 %shard_map.73 = (bf16[32,32,256]{2,1,0:T(8,128)(2,1)}, f32[144,128]{1,0:T(8,128)S(1)}) custom-call(bf16[3,1088,256]{2,1,0:T(8,128)(2,1)S(1)} %get-tuple-element.54.ps, bf16[3,192,256]{2,1,0:T(8,128)(2,1)S(1)} %get-tuple-element.55.last_ref, bf16[4,32,16,256]{3,2,1,0:T(8,128)(2,1)S(1)} %get-tuple-element.32.raw_ref, f32[144,128]{1,0:T(8,128)S(1)} %add_add_fusion.1.partial_ref), custom_call_target="tpu_custom_call" | custom-call | flops 2000000000 | bytes 3686400 | tf_op jit(solution)/shard_map/pallas_call | solution.py:40
  43.5 0.0 collective-permute-done.13
  43.5 0.0 collective-permute-done.12
  43.5 0.3 collective-permute-done.11
  43.8 1.4 %collective-permute-start.14 = (f32[144,128]{1,0:T(8,128)S(1)}, f32[144,128]{1,0:T(8,128)S(1)}, u32[]{:S(2)}, u32[]{:S(2)}) collective-permute-start(f32[144,128]{1,0:T(8,128)S(1)} %add_add_fusion), channel_id=1, source_target_pairs={{0,32},{1,33},{2,34},{3,35},{4,36},{5,37},{6,38},{7,39},{8,40},{9,... | collective-permute-start | bytes 221192 | tf_op jit(solution)/shard_map/ppermute | solution.py:429
  45.3 4.1 %collective-permute-done.14 = f32[144,128]{1,0:T(8,128)S(1)} collective-permute-done((f32[144,128]{1,0:T(8,128)S(1)}, f32[144,128]{1,0:T(8,128)S(1)}, u32[]{:S(2)}, u32[]{:S(2)}) %collective-permute-start.14) | collective-permute-done | bytes 73760 | tf_op jit(solution)/shard_map/ppermute | solution.py:429
  49.4 0.1 collective-permute-start.15
  49.5 1.3 %collective-permute-done.15.given_ref = f32[144,128]{1,0:T(8,128)S(1)} collective-permute-done((f32[144,128]{1,0:T(8,128)S(1)}, f32[144,128]{1,0:T(8,128)S(1)}, u32[]{:S(2)}, u32[]{:S(2)}) %collective-permute-start.15) | collective-permute-done | bytes 73760 | tf_op jit(solution)/shard_map/ppermute | solution.py:458
  50.7 1.0 %shard_map.74 = (f32[3,3,32,32]{3,2,1,0:T(8,128)}, f32[3,3,32,32]{3,2,1,0:T(8,128)}) custom-call(f32[144,128]{1,0:T(8,128)S(1)} %add.43.total_ref, f32[144,128]{1,0:T(8,128)S(1)} %collective-permute-done.15.given_ref), custom_call_target="tpu_custom_call" | custom-call | flops 1000000 | bytes 221184 | tf_op jit(solution)/shard_map/pallas_call | solution.py:40
  (5 shorter events, 0.1 us)
Async XLA Ops:
  2.8 5.6 %collective-permute-start.1 = (bf16[16,256]{1,0:T(8,128)(2,1)S(1)}, bf16[16,256]{1,0:T(8,128)(2,1)S(1)}, u32[]{:S(2)}, u32[]{:S(2)}) collective-permute-start(bf16[16,256]{1,0:T(8,128)(2,1)S(1)} %get-tuple-element.40), channel_id=1, source_target_pairs={{0,192},{64,128},{128,64},{192,0},{1,193},{65,129},{129,65},{193,1... | collective-permute-start | bytes 24584 | tf_op jit(solution)/shard_map/ppermute | solution.py:454
  7.8 1.3 %collective-permute-start = (bf16[16,256]{1,0:T(8,128)(2,1)S(1)}, bf16[16,256]{1,0:T(8,128)(2,1)S(1)}, u32[]{:S(2)}, u32[]{:S(2)}) collective-permute-start(bf16[16,256]{1,0:T(8,128)(2,1)S(1)} %get-tuple-element.39), channel_id=1, source_target_pairs={{0,64},{64,0},{128,192},{192,128},{1,65},{65,1},{129,193},{193,129... | collective-permute-start | bytes 24584 | tf_op jit(solution)/shard_map/ppermute | solution.py:458
  9.2 11.4 %collective-permute-start.2 = (bf16[144,256]{1,0:T(8,128)(2,1)S(1)}, bf16[144,256]{1,0:T(8,128)(2,1)S(1)}, u32[]{:S(2)}, u32[]{:S(2)}) collective-permute-start(bf16[144,256]{1,0:T(8,128)(2,1)S(1)} %get-tuple-element.43), channel_id=1, source_target_pairs={{0,63},{1,2},{2,1},{3,4},{4,3},{5,6},{6,5},{7,8},{8,7},{9,10},{10,... | collective-permute-start | bytes 221192 | tf_op jit(solution)/shard_map/ppermute | solution.py:507
  17.7 3.2 %collective-permute-start.3 = (bf16[144,256]{1,0:T(8,128)(2,1)S(1)}, bf16[144,256]{1,0:T(8,128)(2,1)S(1)}, u32[]{:S(2)}, u32[]{:S(2)}) collective-permute-start(bf16[144,256]{1,0:T(8,128)(2,1)S(1)} %get-tuple-element.44), channel_id=1, source_target_pairs={{0,1},{1,0},{2,3},{3,2},{4,5},{5,4},{6,7},{7,6},{8,9},{9,8},{10,11... | collective-permute-start | bytes 221192 | tf_op jit(solution)/shard_map/ppermute | solution.py:508
  21.8 2.8 %collective-permute-start.4 = (f32[144,128]{1,0:T(8,128)S(1)}, f32[144,128]{1,0:T(8,128)S(1)}, u32[]{:S(2)}, u32[]{:S(2)}) collective-permute-start(f32[144,128]{1,0:T(8,128)S(1)} %get-tuple-element.53), channel_id=1, source_target_pairs={{0,64},{64,0},{128,192},{192,128},{1,65},{65,1},{129,193},{193,129... | collective-permute-start | bytes 221192 | tf_op jit(solution)/shard_map/ppermute | solution.py:458
  24.6 4.8 %collective-permute-start.7 = (f32[144,128]{1,0:T(8,128)S(1)}, f32[144,128]{1,0:T(8,128)S(1)}, u32[]{:S(2)}, u32[]{:S(2)}) collective-permute-start(f32[144,128]{1,0:T(8,128)S(1)} %add.33), channel_id=1, source_target_pairs={{0,1},{1,0},{2,3},{3,2},{4,5},{5,4},{6,7},{7,6},{8,9},{9,8},{10,11... | collective-permute-start | bytes 221192 | tf_op jit(solution)/shard_map/ppermute | solution.py:429
  27.2 4.4 %collective-permute-start.6 = (f32[144,128]{1,0:T(8,128)S(1)}, f32[144,128]{1,0:T(8,128)S(1)}, u32[]{:S(2)}, u32[]{:S(2)}) collective-permute-start(f32[144,128]{1,0:T(8,128)S(1)} %add.33), channel_id=1, source_target_pairs={{0,1},{1,0},{2,3},{3,2},{4,5},{5,4},{6,7},{7,6},{8,9},{9,8},{10,11... | collective-permute-start | bytes 221192 | tf_op jit(solution)/shard_map/ppermute | solution.py:429
  27.6 4.0 %collective-permute-start.5 = (f32[144,128]{1,0:T(8,128)S(1)}, f32[144,128]{1,0:T(8,128)S(1)}, u32[]{:S(2)}, u32[]{:S(2)}) collective-permute-start(f32[144,128]{1,0:T(8,128)S(1)} %add.33), channel_id=1, source_target_pairs={{0,1},{1,0},{2,3},{3,2},{4,5},{5,4},{6,7},{7,6},{8,9},{9,8},{10,11... | collective-permute-start | bytes 221192 | tf_op jit(solution)/shard_map/ppermute | solution.py:429
  31.6 4.9 %collective-permute-start.10 = (f32[144,128]{1,0:T(8,128)S(1)}, f32[144,128]{1,0:T(8,128)S(1)}, u32[]{:S(2)}, u32[]{:S(2)}) collective-permute-start(f32[144,128]{1,0:T(8,128)S(1)} %add_add_fusion.2.partial_ref), channel_id=1, source_target_pairs={{0,32},{1,33},{2,34},{3,35},{4,36},{5,37},{6,38},{7,39},{8,40},{9,... | collective-permute-start | bytes 221192 | tf_op jit(solution)/shard_map/ppermute | solution.py:429
  31.7 5.3 %collective-permute-start.9 = (f32[144,128]{1,0:T(8,128)S(1)}, f32[144,128]{1,0:T(8,128)S(1)}, u32[]{:S(2)}, u32[]{:S(2)}) collective-permute-start(f32[144,128]{1,0:T(8,128)S(1)} %add_add_fusion.2.partial_ref), channel_id=1, source_target_pairs={{0,32},{1,33},{2,34},{3,35},{4,36},{5,37},{6,38},{7,39},{8,40},{9,... | collective-permute-start | bytes 221192 | tf_op jit(solution)/shard_map/ppermute | solution.py:429
  34.4 3.2 %collective-permute-start.8 = (f32[144,128]{1,0:T(8,128)S(1)}, f32[144,128]{1,0:T(8,128)S(1)}, u32[]{:S(2)}, u32[]{:S(2)}) collective-permute-start(f32[144,128]{1,0:T(8,128)S(1)} %add_add_fusion.2.partial_ref), channel_id=1, source_target_pairs={{0,32},{1,33},{2,34},{3,35},{4,36},{5,37},{6,38},{7,39},{8,40},{9,... | collective-permute-start | bytes 221192 | tf_op jit(solution)/shard_map/ppermute | solution.py:429
  37.7 5.8 %collective-permute-start.13 = (f32[144,128]{1,0:T(8,128)S(1)}, f32[144,128]{1,0:T(8,128)S(1)}, u32[]{:S(2)}, u32[]{:S(2)}) collective-permute-start(f32[144,128]{1,0:T(8,128)S(1)} %add_add_fusion.1.partial_ref), channel_id=1, source_target_pairs={{0,32},{1,33},{2,34},{3,35},{4,36},{5,37},{6,38},{7,39},{8,40},{9,... | collective-permute-start | bytes 221192 | tf_op jit(solution)/shard_map/ppermute | solution.py:429
  37.8 5.7 %collective-permute-start.12 = (f32[144,128]{1,0:T(8,128)S(1)}, f32[144,128]{1,0:T(8,128)S(1)}, u32[]{:S(2)}, u32[]{:S(2)}) collective-permute-start(f32[144,128]{1,0:T(8,128)S(1)} %add_add_fusion.1.partial_ref), channel_id=1, source_target_pairs={{0,32},{1,33},{2,34},{3,35},{4,36},{5,37},{6,38},{7,39},{8,40},{9,... | collective-permute-start | bytes 221192 | tf_op jit(solution)/shard_map/ppermute | solution.py:429
  37.9 6.0 %collective-permute-start.11 = (f32[144,128]{1,0:T(8,128)S(1)}, f32[144,128]{1,0:T(8,128)S(1)}, u32[]{:S(2)}, u32[]{:S(2)}) collective-permute-start(f32[144,128]{1,0:T(8,128)S(1)} %add_add_fusion.1.partial_ref), channel_id=1, source_target_pairs={{0,32},{1,33},{2,34},{3,35},{4,36},{5,37},{6,38},{7,39},{8,40},{9,... | collective-permute-start | bytes 221192 | tf_op jit(solution)/shard_map/ppermute | solution.py:429
  43.8 5.5 %collective-permute-start.14 = (f32[144,128]{1,0:T(8,128)S(1)}, f32[144,128]{1,0:T(8,128)S(1)}, u32[]{:S(2)}, u32[]{:S(2)}) collective-permute-start(f32[144,128]{1,0:T(8,128)S(1)} %add_add_fusion), channel_id=1, source_target_pairs={{0,32},{1,33},{2,34},{3,35},{4,36},{5,37},{6,38},{7,39},{8,40},{9,... | collective-permute-start | bytes 221192 | tf_op jit(solution)/shard_map/ppermute | solution.py:429
  49.4 1.4 %collective-permute-start.15 = (f32[144,128]{1,0:T(8,128)S(1)}, f32[144,128]{1,0:T(8,128)S(1)}, u32[]{:S(2)}, u32[]{:S(2)}) collective-permute-start(f32[144,128]{1,0:T(8,128)S(1)} %add.43.total_ref), channel_id=1, source_target_pairs={{0,64},{64,0},{128,192},{192,128},{1,65},{65,1},{129,193},{193,129... | collective-permute-start | bytes 221192 | tf_op jit(solution)/shard_map/ppermute | solution.py:458

commit v8 on v7

--- a/solution.py
+++ b/solution.py
@@ -219,45 +219,70 @@
             grads_ref[place, q] = summed[:, :128]
 
 
+def sides_of(far, near):
+    far, near = far.astype(F32), near.astype(F32)
+    odd = lon_is_odd()
+    return jnp.where(odd == 1, near, far), jnp.where(odd == 1, far, near)
+
+
+def write_edges(side, sent, sent_halos, own_refs, shifted, two):
+    x_ref, cot_ref, core_ref, mid_ref = own_refs
+    own_rows, lat_cells = x_ref.shape
+    own = slice(0, two) if side == 0 else slice(own_rows - two, own_rows)
+    own_halos = jnp.concatenate([core_ref[:, own], mid_ref[:, own]], 0).astype(F32)
+    order = (sent_halos, own_halos) if side == 0 else (own_halos, sent_halos)
+    halos = jnp.concatenate(order, 1).astype(BF)
+    for place, source in enumerate((x_ref, cot_ref)):
+        order = (sent[place], source[own, :]) if side == 0 else (source[own, :], sent[place])
+        values = jnp.concatenate(order, 0)
+        columns = dot_rows(halos, halo_place(is_odd(), place, lat_cells))
+        write_shifted(values, columns, shifted[place].at[side], slice(0, values.shape[0]))
+
+
 def edge_kernel(x_ref, cot_ref, core_ref, mid_ref, far_ref, near_ref, first_ref, back_ref, grads_ref,
-                low_ref, high_ref, out_ref, left_ref, right_ref, xs_sides, cs_sides):
-    lat_cells = x_ref.shape[1]
+                out_ref, xs_sides, cs_sides):
     channels = grads_ref.shape[2]
-    odd = is_odd()
     two = 2 * channels
-    own_rows = x_ref.shape[0]
     sums = [[grads_ref[place, q][:, : 3 * channels] for q in range(3)] for place in range(2)]
-    far, near = far_ref[...].astype(F32), near_ref[...].astype(F32)
-    left_ref[...] = jnp.where(lon_is_odd() == 1, near, far).astype(BF)
-    right_ref[...] = jnp.where(lon_is_odd() == 1, far, near).astype(BF)
-    sides = ((left_ref, low_ref), (right_ref, high_ref))
-    for side, (message, _) in enumerate(sides):
-        own = slice(0, two) if side == 0 else slice(own_rows - two, own_rows)
-        sent = message[2 * two : 2 * two + HALF, :]
-        sent_halos = jnp.concatenate([sent[:, :two], sent[:, two : 2 * two]], 0).astype(F32)
-        own_halos = jnp.concatenate([core_ref[:, own], mid_ref[:, own]], 0).astype(F32)
-        order = (sent_halos, own_halos) if side == 0 else (own_halos, sent_halos)
-        halos = jnp.concatenate(order, 1).astype(BF)
-        for place, (source, shifted) in enumerate(((x_ref, xs_sides), (cot_ref, cs_sides))):
-            sent_rows = message[place * two : (place + 1) * two, :]
-            order = (sent_rows, source[own, :]) if side == 0 else (source[own, :], sent_rows)
-            columns = dot_rows(halos, halo_place(odd, place, lat_cells))
-            write_shifted(jnp.concatenate(order, 0), columns, shifted.at[side], slice(0, 2 * two))
+    parts = []
+    for first in (0, channels):
+        rows = [far_ref[place * two + first : place * two + first + channels, :] for place in range(2)]
+        more = [near_ref[place * two + first : place * two + first + channels, :] for place in range(2)]
+        parts.append([sides_of(*pair) for pair in zip(rows, more)])
+    halos = sides_of(far_ref[2 * two :, : 2 * two], near_ref[2 * two :, : 2 * two])
+    for side in range(2):
+        sent = [parts[1 - side][place][side].astype(BF) for place in range(2)]
+        lanes = [half * two + (1 - side) * channels for half in range(2)]
+        sent_halos = jnp.concatenate([halos[side][:, lane : lane + channels] for lane in lanes], 0)
+        write_edges(side, sent, sent_halos, (x_ref, cot_ref, core_ref, mid_ref), (xs_sides, cs_sides), two)
+    rows = slice(0, 3 * channels)
+    pre_acts = [conv_rows(first_ref, xs_sides.at[side], rows, channels) for side in range(2)]
+    back_grads = [conv_rows(back_ref, cs_sides.at[side], rows, channels) for side in range(2)]
+    for side in range(2):
+        activation, pre_grad = activate(pre_acts[side], back_grads[side])
+        activation, pre_grad = activation.astype(BF), pre_grad.astype(BF)
+        for q in range(3):
+            sums[0][q] = sums[0][q] + dot_lanes(pre_grad, xs_sides[side, q, :, :])
+            sums[1][q] = sums[1][q] + dot_lanes(activation, cs_sides[side, q, :, :])
+    out_ref[...] = jnp.concatenate([pack_taps(taps) for taps in sums], 0)
+
+
+def rim_kernel(x_ref, cot_ref, core_ref, mid_ref, far_ref, near_ref, first_ref, back_ref,
+               partial_ref, low_ref, high_ref, left_ref, right_ref, passed_ref, xs_sides, cs_sides):
+    passed_ref[...] = partial_ref[...]
+    two = low_ref.shape[0]
+    messages = sides_of(far_ref[...], near_ref[...])
+    for side, target in enumerate((left_ref, right_ref)):
+        target[...] = messages[side].astype(BF)
+        sent = [messages[side][place * two : (place + 1) * two].astype(BF) for place in range(2)]
+        halos = messages[side][2 * two :]
+        sent_halos = jnp.concatenate([halos[:, :two], halos[:, two : 2 * two]], 0)
+        write_edges(side, sent, sent_halos, (x_ref, cot_ref, core_ref, mid_ref), (xs_sides, cs_sides), two)
     rows = slice(0, 2 * two)
-    pre_acts = [conv_rows(first_ref, xs_sides.at[side], rows, two) for side in range(2)]
-    back_grads = [conv_rows(back_ref, cs_sides.at[side], rows, two) for side in range(2)]
-    for side, (_, target) in enumerate(sides):
-        activation, pre_grad = activate(pre_acts[side], back_grads[side])
-        pre_grad = pre_grad.astype(BF)
-        target[...] = pre_grad
-        mine = slice(channels, two) if side == 0 else slice(0, channels)
-        near = slice(channels, 2 * two) if side == 0 else slice(0, 3 * channels)
-        activation = activation[mine].astype(BF)
-        pre_grad = pre_grad[mine]
-        for q in range(3):
-            sums[0][q] = sums[0][q] + dot_lanes(pre_grad, xs_sides[side, q, near, :])
-            sums[1][q] = sums[1][q] + dot_lanes(activation, cs_sides[side, q, near, :])
-    out_ref[...] = jnp.concatenate([pack_taps(taps) for taps in sums], 0)
+    for side, target in enumerate((low_ref, high_ref)):
+        pre_act = conv_rows(first_ref, xs_sides.at[side], rows, two)
+        back_grad = conv_rows(back_ref, cs_sides.at[side], rows, two)
+        target[...] = activate(pre_act, back_grad)[1].astype(BF)
 
 
 def pack_taps(taps):
@@ -429,18 +454,18 @@
     return lax.ppermute(value, ("lat", "lon"), pairs(counts, partner, idle))
 
 
-def sum_of_four(value, partner, masks, idle, beside=None):
+def sum_of_four(value, partner, masks, idle, beside):
     first, second, third = [exchange(value, partner(mask), idle) for mask in masks]
-    result = None
-    if beside is not None:
-        *result, value = beside(value)
+    *result, value = beside(value)
     return (value + first) + (second + third), result
 
 
-def sum_everywhere(mine, widen, finish):
+def sum_everywhere(mine, rim, widen, finish):
     total = mine + core_exchange(mine)
-    total, _ = sum_of_four(total, x_partner, (1, 3, 2), ALONG_Y)
-    total, shifted = sum_of_four(total, y_partner, (1, 3, 2), ALONG_X, widen)
+    total, edges = sum_of_four(total, x_partner, (1, 3, 2), ALONG_Y, rim)
+    total, shifted = sum_of_four(
+        total, y_partner, (1, 3, 2), ALONG_X, lambda value: widen(*edges, value)
+    )
     total, (input_grad,) = sum_of_four(
         total, z_partner, (1, 2, 3), ALONG_X, lambda value: finish(*shifted, value)
     )
@@ -516,16 +541,27 @@
         4 * 10**9,
         x_rows, cot_rows, core_in, mid_in, first, back,
     )
-    edge_shifted = pltpu.VMEM((2, 3, 2 * two, lat_cells), BF)
     partial = shape(2 * 9 * channels * channels // 128, 128, dtype=F32)
-    pre_low, pre_high, grads, from_left, from_right = call(
+    edge_shifted = pltpu.VMEM((2, 3, 3 * channels, lat_cells), BF)
+    (grads,) = call(
         edge_kernel,
-        [shape(two, lat_cells), shape(two, lat_cells), partial, message, message],
+        [partial],
         [edge_shifted, edge_shifted],
         10**9,
         x_rows, cot_rows, core_in, mid_in, far_in, near_in, first, back, inner_grads,
     )
-    def widen(partial):
+
+    def rim(partial):
+        rim_shifted = pltpu.VMEM((2, 3, 2 * two, lat_cells), BF)
+        return call(
+            rim_kernel,
+            [shape(two, lat_cells), shape(two, lat_cells), message, message, shape(*partial.shape, dtype=F32)],
+            [rim_shifted, rim_shifted],
+            10**9,
+            x_rows, cot_rows, core_in, mid_in, far_in, near_in, first, back, partial,
+        )
+
+    def widen(pre_low, pre_high, from_left, from_right, partial):
         return call(
             outer_kernel,
             [shape(3, rows + two, lat_cells), weights, shape(*partial.shape, dtype=F32)],
@@ -552,7 +588,7 @@
             hbm_out=(0,),
         )
 
-    total, given, input_grad = sum_everywhere(grads, widen, finish)
+    total, given, input_grad = sum_everywhere(grads, rim, widen, finish)
     grad_one, grad_two = call(
         functools.partial(result_kernel, 1.0 / math.sqrt(cells)),
         [shape(3, 3, channels, channels, dtype=F32)] * 2,

time: 51.8 us -> 51.9 us (level)
  Pallas kernels: 11.2 us -> 11.8 us
    pallas_call x8 -> x9, Pallas kernels: 11.2 us -> 11.8 us  [call(): pl.pallas_call(kernel, out_shape=outs, in_specs=[pl.BlockSpec(memory_spac...]
  transfers between devices with their start and end apart: 16 -> 16, of which waited for: 12 -> 13; matrix products, arithmetic and copies ran while one was open for 0% -> 0% of each run, Pallas kernels for 14% -> 15%
where the time goes in v8:
time: 51.9 us; the launch traced here: 51.8 us
  starting transfers between devices  25.5 us (49%)
  waiting for transfers between devices  13.6 us (26%)
  Pallas kernels  11.8 us (23%)
  between operations  0.77 us (1%)
    pallas_call x9, Pallas kernels, call(): pl.pallas_call(kernel, out_shape=outs, in_specs=[pl.BlockSpec(memory_spac...  11.8 us
    ppermute x10, starting transfers between devices, exchange(): return lax.ppermute(value, ('lat', 'lon'), pairs(counts, partner, idle))  10.7 us
    ppermute x10, waiting for transfers between devices, exchange(): return lax.ppermute(value, ('lat', 'lon'), pairs(counts, partner, idle))  10 us
    ppermute x1, starting transfers between devices, on_device(): lax.ppermute(far_out, 'lon', [(i, (i + 1 if i % 2 else i - 1) % count) fo...  8.5 us
    ppermute x1, starting transfers between devices, mid_exchange(): lax.ppermute(edges, 'lat', [(i, (i - 1 if i % 2 == 0 else i + 1) % count)...  4.22 us
    ppermute x3, waiting for transfers between devices, core_exchange(): lax.ppermute(value, 'lat', [(i, i ^ 1) for i in range(lax.axis_size('lat'...  2.92 us
    ppermute x3, starting transfers between devices, core_exchange(): lax.ppermute(value, 'lat', [(i, i ^ 1) for i in range(lax.axis_size('lat'...  2.1 us
  transfers between devices with their start and end apart: 16, of which 13 were waited for; matrix products, arithmetic and copies ran while one was open for 0% of the time, Pallas kernels for 15%

profile of v8, /device:TPU:1, one launch (start us, length us, event | category | flops | bytes accessed | tf_op | source)
XLA Modules:
  0.0 51.8 jit_solution(3950465533930924698)
XLA Ops:
  0.6 2.1 %shard_map.67 = (bf16[4,32,16,256]{3,2,1,0:T(8,128)(2,1)S(1)}, bf16[3,3,32,32]{3,2,1,0:T(8,128)(2,1)S(1)}, bf16[3,3,32,32]{3,2,1,0:T(8,128)(2,1)S(1)}, bf16[512,...) custom-call(bf16[32,32,256]{2,1,0:T(8,128)(2,1)} %x_hbm.1, ...), custom_call_target="tpu_custom_call" | custom-call | flops 100000000 | bytes 2711552 | tf_op jit(solution)/shard_map/pallas_call | solution.py:40
  2.8 4.2 %collective-permute-start.1 = (bf16[16,256]{1,0:T(8,128)(2,1)S(1)}, bf16[16,256]{1,0:T(8,128)(2,1)S(1)}, u32[]{:S(2)}, u32[]{:S(2)}) collective-permute-start(bf16[16,256]{1,0:T(8,128)(2,1)S(1)} %get-tuple-element.40), channel_id=1, source_target_pairs={{0,192},{64,128},{128,64},{192,0},{1,193},{65,129},{129,65},{193,1... | collective-permute-start | bytes 24584 | tf_op jit(solution)/shard_map/ppermute | solution.py:479
  7.0 0.8 %shard_map.68 = (bf16[1024,256]{1,0:T(8,128)(2,1)S(1)}, bf16[1024,256]{1,0:T(8,128)(2,1)S(1)}, bf16[3,192,256]{2,1,0:T(8,128)(2,1)S(1)}, bf16[3,192,256]{2,1,0:T(8,128)(2,1)S(1)}, bf16[16,256]{1,0:T(8,128)(2,1)S(1)}) custom-call(bf16[4,32,16,256]{3,2,1,0:T(8,128)(2,1)S(1)} %get-tuple-element.32.raw_ref, bf16[512,512]{1,0:T(8,128)(2,1)S(1)} %get-tuple-element.33.perm_ref, ...), custom_call_target="tpu_custom_call" | custom-call | flops 1000000000 | bytes 3264512 | tf_op jit(solution)/shard_map/pallas_call | solution.py:40
  7.8 0.1 collective-permute-start
  7.9 0.4 collective-permute-done.1.mid_in
  8.3 0.8 %collective-permute-done.core_in = bf16[16,256]{1,0:T(8,128)(2,1)S(1)} collective-permute-done((bf16[16,256]{1,0:T(8,128)(2,1)S(1)}, bf16[16,256]{1,0:T(8,128)(2,1)S(1)}, u32[]{:S(2)}, u32[]{:S(2)}) %collective-permute-start) | collective-permute-done | bytes 8224 | tf_op jit(solution)/shard_map/ppermute | solution.py:483
  9.1 0.1 shard_map.69
  9.2 8.5 %collective-permute-start.2 = (bf16[144,256]{1,0:T(8,128)(2,1)S(1)}, bf16[144,256]{1,0:T(8,128)(2,1)S(1)}, u32[]{:S(2)}, u32[]{:S(2)}) collective-permute-start(bf16[144,256]{1,0:T(8,128)(2,1)S(1)} %get-tuple-element.43), channel_id=1, source_target_pairs={{0,63},{1,2},{2,1},{3,4},{4,3},{5,6},{6,5},{7,8},{8,7},{9,10},{10,... | collective-permute-start | bytes 221192 | tf_op jit(solution)/shard_map/ppermute | solution.py:532
  17.7 0.0 collective-permute-start.3
  17.7 2.9 %shard_map.70 = (bf16[960,256]{1,0:T(8,128)(2,1)S(1)}, f32[2,3,32,128]{3,2,1,0:T(8,128)S(1)}) custom-call(bf16[1024,256]{1,0:T(8,128)(2,1)S(1)} %get-tuple-element.37.x_ref, bf16[1024,256]{1,0:T(8,128)(2,1)S(1)} %get-tuple-element.38.cot_ref, bf16[16,1024]{1,0:T(8,128)(2,1)S(1)} %get-tuple-element.41.core_ref, ...), custom_call_target="tpu_custom_call" | custom-call | flops 4000000000 | bytes 2293760 | tf_op jit(solution)/shard_map/pallas_call | solution.py:40
  20.6 0.0 collective-permute-done.2.far_ref
  20.6 0.3 collective-permute-done.3.near_ref
  20.9 0.9 %shard_map.71 = f32[144,128]{1,0:T(8,128)S(1)} custom-call(bf16[1024,256]{1,0:T(8,128)(2,1)S(1)} %get-tuple-element.37.x_ref, bf16[1024,256]{1,0:T(8,128)(2,1)S(1)} %get-tuple-element.38.cot_ref, bf16[16,1024]{1,0:T(8,128)(2,1)S(1)} %get-tuple-element.41.core_ref, bf16[16,1024]{1,0:T(8,128)(2,1)S(1)} %get-tuple-element.42.mid_ref, ...), custom_call_target="tpu_custom_call" | custom-call | flops 1000000000 | bytes 2023424 | tf_op jit(solution)/shard_map/pallas_call | solution.py:40
  21.8 1.9 %collective-permute-start.4 = (f32[144,128]{1,0:T(8,128)S(1)}, f32[144,128]{1,0:T(8,128)S(1)}, u32[]{:S(2)}, u32[]{:S(2)}) collective-permute-start(f32[144,128]{1,0:T(8,128)S(1)} %shard_map.71), channel_id=1, source_target_pairs={{0,64},{64,0},{128,192},{192,128},{1,65},{65,1},{129,193},{193,129... | collective-permute-start | bytes 221192 | tf_op jit(solution)/shard_map/ppermute | solution.py:483
  23.7 0.9 %collective-permute-done.4 = f32[144,128]{1,0:T(8,128)S(1)} collective-permute-done((f32[144,128]{1,0:T(8,128)S(1)}, f32[144,128]{1,0:T(8,128)S(1)}, u32[]{:S(2)}, u32[]{:S(2)}) %collective-permute-start.4) | collective-permute-done | bytes 73760 | tf_op jit(solution)/shard_map/ppermute | solution.py:483
  24.6 2.5 %collective-permute-start.7 = (f32[144,128]{1,0:T(8,128)S(1)}, f32[144,128]{1,0:T(8,128)S(1)}, u32[]{:S(2)}, u32[]{:S(2)}) collective-permute-start(f32[144,128]{1,0:T(8,128)S(1)} %add.33.partial_ref), channel_id=1, source_target_pairs={{0,1},{1,0},{2,3},{3,2},{4,5},{5,4},{6,7},{7,6},{8,9},{9,8},{10,11... | collective-permute-start | bytes 221192 | tf_op jit(solution)/shard_map/ppermute | solution.py:454
  27.1 0.4 collective-permute-start.6
  27.6 0.0 collective-permute-start.5
  27.6 0.6 %shard_map.72 = (bf16[64,256]{1,0:T(8,128)(2,1)S(1)}, bf16[64,256]{1,0:T(8,128)(2,1)S(1)}, bf16[144,256]{1,0:T(8,128)(2,1)S(1)}, bf16[144,256]{1,0:T(8,128)(2,1)S(1)}, f32[144,128]{1,0:T(8,128)S(1)}) custom-call(bf16[1024,256]{1,0:T(8,128)(2,1)S(1)} %get-tuple-element.37.x_ref, bf16[1024,256]{1,0:T(8,128)(2,1)S(1)} %get-tuple-element.38.cot_ref, ...), custom_call_target="tpu_custom_call" | custom-call | flops 1000000000 | bytes 2211840 | tf_op jit(solution)/shard_map/pallas_call | solution.py:40
  28.2 1.2 %collective-permute-done.7 = f32[144,128]{1,0:T(8,128)S(1)} collective-permute-done((f32[144,128]{1,0:T(8,128)S(1)}, f32[144,128]{1,0:T(8,128)S(1)}, u32[]{:S(2)}, u32[]{:S(2)}) %collective-permute-start.7) | collective-permute-done | bytes 73760 | tf_op jit(solution)/shard_map/ppermute | solution.py:454
  29.4 2.1 %collective-permute-done.6 = f32[144,128]{1,0:T(8,128)S(1)} collective-permute-done((f32[144,128]{1,0:T(8,128)S(1)}, f32[144,128]{1,0:T(8,128)S(1)}, u32[]{:S(2)}, u32[]{:S(2)}) %collective-permute-start.6) | collective-permute-done | bytes 73760 | tf_op jit(solution)/shard_map/ppermute | solution.py:454
  31.6 0.0 collective-permute-done.5
  31.6 0.1 collective-permute-start.10
  31.7 2.7 %collective-permute-start.9 = (f32[144,128]{1,0:T(8,128)S(1)}, f32[144,128]{1,0:T(8,128)S(1)}, u32[]{:S(2)}, u32[]{:S(2)}) collective-permute-start(f32[144,128]{1,0:T(8,128)S(1)} %add_add_fusion.2.partial_ref), channel_id=1, source_target_pairs={{0,32},{1,33},{2,34},{3,35},{4,36},{5,37},{6,38},{7,39},{8,40},{9,... | collective-permute-start | bytes 221192 | tf_op jit(solution)/shard_map/ppermute | solution.py:454
  34.4 0.0 collective-permute-start.8
  34.4 1.2 %shard_map.73 = (bf16[3,1088,256]{2,1,0:T(8,128)(2,1)S(1)}, bf16[3,192,256]{2,1,0:T(8,128)(2,1)S(1)}, f32[144,128]{1,0:T(8,128)S(1)}) custom-call(bf16[1024,256]{1,0:T(8,128)(2,1)S(1)} %get-tuple-element.37.x_ref, bf16[1024,256]{1,0:T(8,128)(2,1)S(1)} %get-tuple-element.38.cot_ref, bf16[16,1024]{1,0:T(8,128)(2,1)S(1)} %get-tuple-element.41.core_ref, ...), custom_call_target="tpu_custom_call" | custom-call | flops 1000000000 | bytes 4540416 | tf_op jit(solution)/shard_map/pallas_call | solution.py:40
  35.6 0.9 %collective-permute-done.10 = f32[144,128]{1,0:T(8,128)S(1)} collective-permute-done((f32[144,128]{1,0:T(8,128)S(1)}, f32[144,128]{1,0:T(8,128)S(1)}, u32[]{:S(2)}, u32[]{:S(2)}) %collective-permute-start.10) | collective-permute-done | bytes 73760 | tf_op jit(solution)/shard_map/ppermute | solution.py:454
  36.5 0.5 collective-permute-done.9
  37.0 0.6 %collective-permute-done.8 = f32[144,128]{1,0:T(8,128)S(1)} collective-permute-done((f32[144,128]{1,0:T(8,128)S(1)}, f32[144,128]{1,0:T(8,128)S(1)}, u32[]{:S(2)}, u32[]{:S(2)}) %collective-permute-start.8) | collective-permute-done | bytes 73760 | tf_op jit(solution)/shard_map/ppermute | solution.py:454
  37.6 0.1 collective-permute-start.13
  37.7 0.3 collective-permute-start.12
  38.0 3.3 %collective-permute-start.11 = (f32[144,128]{1,0:T(8,128)S(1)}, f32[144,128]{1,0:T(8,128)S(1)}, u32[]{:S(2)}, u32[]{:S(2)}) collective-permute-start(f32[144,128]{1,0:T(8,128)S(1)} %add_add_fusion.1.partial_ref), channel_id=1, source_target_pairs={{0,32},{1,33},{2,34},{3,35},{4,36},{5,37},{6,38},{7,39},{8,40},{9,... | collective-permute-start | bytes 221192 | tf_op jit(solution)/shard_map/ppermute | solution.py:454
  41.3 2.2 %shard_map.74 = (bf16[32,32,256]{2,1,0:T(8,128)(2,1)}, f32[144,128]{1,0:T(8,128)S(1)}) custom-call(bf16[3,1088,256]{2,1,0:T(8,128)(2,1)S(1)} %get-tuple-element.54.ps, bf16[3,192,256]{2,1,0:T(8,128)(2,1)S(1)} %get-tuple-element.55.last_ref, bf16[4,32,16,256]{3,2,1,0:T(8,128)(2,1)S(1)} %get-tuple-element.32.raw_ref, f32[144,128]{1,0:T(8,128)S(1)} %add_add_fusion.1.partial_ref), custom_call_target="tpu_custom_call" | custom-call | flops 2000000000 | bytes 3686400 | tf_op jit(solution)/shard_map/pallas_call | solution.py:40
  43.5 0.0 collective-permute-done.13
  43.5 0.2 collective-permute-done.12
  43.7 0.2 collective-permute-done.11
  43.9 1.3 %collective-permute-start.14 = (f32[144,128]{1,0:T(8,128)S(1)}, f32[144,128]{1,0:T(8,128)S(1)}, u32[]{:S(2)}, u32[]{:S(2)}) collective-permute-start(f32[144,128]{1,0:T(8,128)S(1)} %add_add_fusion), channel_id=1, source_target_pairs={{0,32},{1,33},{2,34},{3,35},{4,36},{5,37},{6,38},{7,39},{8,40},{9,... | collective-permute-start | bytes 221192 | tf_op jit(solution)/shard_map/ppermute | solution.py:454
  45.3 4.2 %collective-permute-done.14 = f32[144,128]{1,0:T(8,128)S(1)} collective-permute-done((f32[144,128]{1,0:T(8,128)S(1)}, f32[144,128]{1,0:T(8,128)S(1)}, u32[]{:S(2)}, u32[]{:S(2)}) %collective-permute-start.14) | collective-permute-done | bytes 73760 | tf_op jit(solution)/shard_map/ppermute | solution.py:454
  49.5 0.1 collective-permute-start.15
  49.6 1.3 %collective-permute-done.15.given_ref = f32[144,128]{1,0:T(8,128)S(1)} collective-permute-done((f32[144,128]{1,0:T(8,128)S(1)}, f32[144,128]{1,0:T(8,128)S(1)}, u32[]{:S(2)}, u32[]{:S(2)}) %collective-permute-start.15) | collective-permute-done | bytes 73760 | tf_op jit(solution)/shard_map/ppermute | solution.py:483
  50.8 1.0 %shard_map.75 = (f32[3,3,32,32]{3,2,1,0:T(8,128)}, f32[3,3,32,32]{3,2,1,0:T(8,128)}) custom-call(f32[144,128]{1,0:T(8,128)S(1)} %add.43.total_ref, f32[144,128]{1,0:T(8,128)S(1)} %collective-permute-done.15.given_ref), custom_call_target="tpu_custom_call" | custom-call | flops 1000000 | bytes 221184 | tf_op jit(solution)/shard_map/pallas_call | solution.py:40
  (5 shorter events, 0.1 us)
Async XLA Ops:
  2.8 5.6 %collective-permute-start.1 = (bf16[16,256]{1,0:T(8,128)(2,1)S(1)}, bf16[16,256]{1,0:T(8,128)(2,1)S(1)}, u32[]{:S(2)}, u32[]{:S(2)}) collective-permute-start(bf16[16,256]{1,0:T(8,128)(2,1)S(1)} %get-tuple-element.40), channel_id=1, source_target_pairs={{0,192},{64,128},{128,64},{192,0},{1,193},{65,129},{129,65},{193,1... | collective-permute-start | bytes 24584 | tf_op jit(solution)/shard_map/ppermute | solution.py:479
  7.8 1.3 %collective-permute-start = (bf16[16,256]{1,0:T(8,128)(2,1)S(1)}, bf16[16,256]{1,0:T(8,128)(2,1)S(1)}, u32[]{:S(2)}, u32[]{:S(2)}) collective-permute-start(bf16[16,256]{1,0:T(8,128)(2,1)S(1)} %get-tuple-element.39), channel_id=1, source_target_pairs={{0,64},{64,0},{128,192},{192,128},{1,65},{65,1},{129,193},{193,129... | collective-permute-start | bytes 24584 | tf_op jit(solution)/shard_map/ppermute | solution.py:483
  9.2 11.4 %collective-permute-start.2 = (bf16[144,256]{1,0:T(8,128)(2,1)S(1)}, bf16[144,256]{1,0:T(8,128)(2,1)S(1)}, u32[]{:S(2)}, u32[]{:S(2)}) collective-permute-start(bf16[144,256]{1,0:T(8,128)(2,1)S(1)} %get-tuple-element.43), channel_id=1, source_target_pairs={{0,63},{1,2},{2,1},{3,4},{4,3},{5,6},{6,5},{7,8},{8,7},{9,10},{10,... | collective-permute-start | bytes 221192 | tf_op jit(solution)/shard_map/ppermute | solution.py:532
  17.7 3.2 %collective-permute-start.3 = (bf16[144,256]{1,0:T(8,128)(2,1)S(1)}, bf16[144,256]{1,0:T(8,128)(2,1)S(1)}, u32[]{:S(2)}, u32[]{:S(2)}) collective-permute-start(bf16[144,256]{1,0:T(8,128)(2,1)S(1)} %get-tuple-element.44), channel_id=1, source_target_pairs={{0,1},{1,0},{2,3},{3,2},{4,5},{5,4},{6,7},{7,6},{8,9},{9,8},{10,11... | collective-permute-start | bytes 221192 | tf_op jit(solution)/shard_map/ppermute | solution.py:533
  21.8 2.8 %collective-permute-start.4 = (f32[144,128]{1,0:T(8,128)S(1)}, f32[144,128]{1,0:T(8,128)S(1)}, u32[]{:S(2)}, u32[]{:S(2)}) collective-permute-start(f32[144,128]{1,0:T(8,128)S(1)} %shard_map.71), channel_id=1, source_target_pairs={{0,64},{64,0},{128,192},{192,128},{1,65},{65,1},{129,193},{193,129... | collective-permute-start | bytes 221192 | tf_op jit(solution)/shard_map/ppermute | solution.py:483
  24.6 4.8 %collective-permute-start.7 = (f32[144,128]{1,0:T(8,128)S(1)}, f32[144,128]{1,0:T(8,128)S(1)}, u32[]{:S(2)}, u32[]{:S(2)}) collective-permute-start(f32[144,128]{1,0:T(8,128)S(1)} %add.33.partial_ref), channel_id=1, source_target_pairs={{0,1},{1,0},{2,3},{3,2},{4,5},{5,4},{6,7},{7,6},{8,9},{9,8},{10,11... | collective-permute-start | bytes 221192 | tf_op jit(solution)/shard_map/ppermute | solution.py:454
  27.1 4.4 %collective-permute-start.6 = (f32[144,128]{1,0:T(8,128)S(1)}, f32[144,128]{1,0:T(8,128)S(1)}, u32[]{:S(2)}, u32[]{:S(2)}) collective-permute-start(f32[144,128]{1,0:T(8,128)S(1)} %add.33.partial_ref), channel_id=1, source_target_pairs={{0,1},{1,0},{2,3},{3,2},{4,5},{5,4},{6,7},{7,6},{8,9},{9,8},{10,11... | collective-permute-start | bytes 221192 | tf_op jit(solution)/shard_map/ppermute | solution.py:454
  27.6 4.0 %collective-permute-start.5 = (f32[144,128]{1,0:T(8,128)S(1)}, f32[144,128]{1,0:T(8,128)S(1)}, u32[]{:S(2)}, u32[]{:S(2)}) collective-permute-start(f32[144,128]{1,0:T(8,128)S(1)} %add.33.partial_ref), channel_id=1, source_target_pairs={{0,1},{1,0},{2,3},{3,2},{4,5},{5,4},{6,7},{7,6},{8,9},{9,8},{10,11... | collective-permute-start | bytes 221192 | tf_op jit(solution)/shard_map/ppermute | solution.py:454
  31.6 4.9 %collective-permute-start.10 = (f32[144,128]{1,0:T(8,128)S(1)}, f32[144,128]{1,0:T(8,128)S(1)}, u32[]{:S(2)}, u32[]{:S(2)}) collective-permute-start(f32[144,128]{1,0:T(8,128)S(1)} %add_add_fusion.2.partial_ref), channel_id=1, source_target_pairs={{0,32},{1,33},{2,34},{3,35},{4,36},{5,37},{6,38},{7,39},{8,40},{9,... | collective-permute-start | bytes 221192 | tf_op jit(solution)/shard_map/ppermute | solution.py:454
  31.7 5.3 %collective-permute-start.9 = (f32[144,128]{1,0:T(8,128)S(1)}, f32[144,128]{1,0:T(8,128)S(1)}, u32[]{:S(2)}, u32[]{:S(2)}) collective-permute-start(f32[144,128]{1,0:T(8,128)S(1)} %add_add_fusion.2.partial_ref), channel_id=1, source_target_pairs={{0,32},{1,33},{2,34},{3,35},{4,36},{5,37},{6,38},{7,39},{8,40},{9,... | collective-permute-start | bytes 221192 | tf_op jit(solution)/shard_map/ppermute | solution.py:454
  34.4 3.2 %collective-permute-start.8 = (f32[144,128]{1,0:T(8,128)S(1)}, f32[144,128]{1,0:T(8,128)S(1)}, u32[]{:S(2)}, u32[]{:S(2)}) collective-permute-start(f32[144,128]{1,0:T(8,128)S(1)} %add_add_fusion.2.partial_ref), channel_id=1, source_target_pairs={{0,32},{1,33},{2,34},{3,35},{4,36},{5,37},{6,38},{7,39},{8,40},{9,... | collective-permute-start | bytes 221192 | tf_op jit(solution)/shard_map/ppermute | solution.py:454
  37.6 5.8 %collective-permute-start.13 = (f32[144,128]{1,0:T(8,128)S(1)}, f32[144,128]{1,0:T(8,128)S(1)}, u32[]{:S(2)}, u32[]{:S(2)}) collective-permute-start(f32[144,128]{1,0:T(8,128)S(1)} %add_add_fusion.1.partial_ref), channel_id=1, source_target_pairs={{0,32},{1,33},{2,34},{3,35},{4,36},{5,37},{6,38},{7,39},{8,40},{9,... | collective-permute-start | bytes 221192 | tf_op jit(solution)/shard_map/ppermute | solution.py:454
  37.7 6.0 %collective-permute-start.12 = (f32[144,128]{1,0:T(8,128)S(1)}, f32[144,128]{1,0:T(8,128)S(1)}, u32[]{:S(2)}, u32[]{:S(2)}) collective-permute-start(f32[144,128]{1,0:T(8,128)S(1)} %add_add_fusion.1.partial_ref), channel_id=1, source_target_pairs={{0,32},{1,33},{2,34},{3,35},{4,36},{5,37},{6,38},{7,39},{8,40},{9,... | collective-permute-start | bytes 221192 | tf_op jit(solution)/shard_map/ppermute | solution.py:454
  38.0 5.9 %collective-permute-start.11 = (f32[144,128]{1,0:T(8,128)S(1)}, f32[144,128]{1,0:T(8,128)S(1)}, u32[]{:S(2)}, u32[]{:S(2)}) collective-permute-start(f32[144,128]{1,0:T(8,128)S(1)} %add_add_fusion.1.partial_ref), channel_id=1, source_target_pairs={{0,32},{1,33},{2,34},{3,35},{4,36},{5,37},{6,38},{7,39},{8,40},{9,... | collective-permute-start | bytes 221192 | tf_op jit(solution)/shard_map/ppermute | solution.py:454
  43.9 5.5 %collective-permute-start.14 = (f32[144,128]{1,0:T(8,128)S(1)}, f32[144,128]{1,0:T(8,128)S(1)}, u32[]{:S(2)}, u32[]{:S(2)}) collective-permute-start(f32[144,128]{1,0:T(8,128)S(1)} %add_add_fusion), channel_id=1, source_target_pairs={{0,32},{1,33},{2,34},{3,35},{4,36},{5,37},{6,38},{7,39},{8,40},{9,... | collective-permute-start | bytes 221192 | tf_op jit(solution)/shard_map/ppermute | solution.py:454
  49.5 1.4 %collective-permute-start.15 = (f32[144,128]{1,0:T(8,128)S(1)}, f32[144,128]{1,0:T(8,128)S(1)}, u32[]{:S(2)}, u32[]{:S(2)}) collective-permute-start(f32[144,128]{1,0:T(8,128)S(1)} %add.43.total_ref), channel_id=1, source_target_pairs={{0,64},{64,0},{128,192},{192,128},{1,65},{65,1},{129,193},{193,129... | collective-permute-start | bytes 221192 | tf_op jit(solution)/shard_map/ppermute | solution.py:483

commit v9 on v7

--- a/solution.py
+++ b/solution.py
@@ -439,12 +439,12 @@
 
 def sum_everywhere(mine, widen, finish):
     total = mine + core_exchange(mine)
-    total, _ = sum_of_four(total, x_partner, (1, 3, 2), ALONG_Y)
-    total, shifted = sum_of_four(total, y_partner, (1, 3, 2), ALONG_X, widen)
+    total, _ = sum_of_four(total, z_partner, (1, 2, 3), ALONG_X)
+    total = total + exchange(total, z_partner(6), ALONG_X)
+    total, shifted = sum_of_four(total, x_partner, (1, 3, 2), ALONG_Y, widen)
     total, (input_grad,) = sum_of_four(
-        total, z_partner, (1, 2, 3), ALONG_X, lambda value: finish(*shifted, value)
-    )
-    total = total + exchange(total, z_partner(6), ALONG_X)
+        total, y_partner, (1, 3, 2), ALONG_X, lambda value: finish(*shifted, value)
+    )
     given = core_exchange(total)
     return total, given, input_grad
 

time: 51.8 us -> 51.8 us (level)
  waiting for transfers between devices: 14 us -> 14.7 us
  starting transfers between devices: 25.6 us -> 25 us
    ppermute x10, waiting for transfers between devices: 10.4 us -> 11.1 us  [exchange(): return lax.ppermute(value, ('lat', 'lon'), pairs(counts, partner, idle))]
    ppermute x10, starting transfers between devices: 10.8 us -> 10.2 us  [exchange(): return lax.ppermute(value, ('lat', 'lon'), pairs(counts, partner, idle))]
where the time goes in v9:
time: 51.8 us; the launch traced here: 51.7 us
  starting transfers between devices  25 us (48%)
  waiting for transfers between devices  14.7 us (28%)
  Pallas kernels  11.2 us (22%)
  between operations  0.77 us (1%)
    pallas_call x8, Pallas kernels, call(): pl.pallas_call(kernel, out_shape=outs, in_specs=[pl.BlockSpec(memory_spac...  11.2 us
    ppermute x10, waiting for transfers between devices, exchange(): return lax.ppermute(value, ('lat', 'lon'), pairs(counts, partner, idle))  11.1 us
    ppermute x10, starting transfers between devices, exchange(): return lax.ppermute(value, ('lat', 'lon'), pairs(counts, partner, idle))  10.2 us
    ppermute x1, starting transfers between devices, on_device(): lax.ppermute(far_out, 'lon', [(i, (i + 1 if i % 2 else i - 1) % count) fo...  8.5 us
    ppermute x1, starting transfers between devices, mid_exchange(): lax.ppermute(edges, 'lat', [(i, (i - 1 if i % 2 == 0 else i + 1) % count)...  4.22 us
    ppermute x3, waiting for transfers between devices, core_exchange(): lax.ppermute(value, 'lat', [(i, i ^ 1) for i in range(lax.axis_size('lat'...  2.92 us
    ppermute x3, starting transfers between devices, core_exchange(): lax.ppermute(value, 'lat', [(i, i ^ 1) for i in range(lax.axis_size('lat'...  2.1 us
  transfers between devices with their start and end apart: 16, of which 12 were waited for; matrix products, arithmetic and copies ran while one was open for 0% of the time, Pallas kernels for 14%

profile of v9, /device:TPU:1, one launch (start us, length us, event | category | flops | bytes accessed | tf_op | source)
XLA Modules:
  0.0 51.7 jit_solution(11088183932775107875)
XLA Ops:
  0.6 2.1 %shard_map.67 = (bf16[4,32,16,256]{3,2,1,0:T(8,128)(2,1)S(1)}, bf16[3,3,32,32]{3,2,1,0:T(8,128)(2,1)S(1)}, bf16[3,3,32,32]{3,2,1,0:T(8,128)(2,1)S(1)}, bf16[512,...) custom-call(bf16[32,32,256]{2,1,0:T(8,128)(2,1)} %x_hbm.1, ...), custom_call_target="tpu_custom_call" | custom-call | flops 100000000 | bytes 2711552 | tf_op jit(solution)/shard_map/pallas_call | solution.py:40
  2.8 4.2 %collective-permute-start.1 = (bf16[16,256]{1,0:T(8,128)(2,1)S(1)}, bf16[16,256]{1,0:T(8,128)(2,1)S(1)}, u32[]{:S(2)}, u32[]{:S(2)}) collective-permute-start(bf16[16,256]{1,0:T(8,128)(2,1)S(1)} %get-tuple-element.40), channel_id=1, source_target_pairs={{0,192},{64,128},{128,64},{192,0},{1,193},{65,129},{129,65},{193,1... | collective-permute-start | bytes 24584 | tf_op jit(solution)/shard_map/ppermute | solution.py:454
  7.0 0.8 %shard_map.68 = (bf16[1024,256]{1,0:T(8,128)(2,1)S(1)}, bf16[1024,256]{1,0:T(8,128)(2,1)S(1)}, bf16[3,192,256]{2,1,0:T(8,128)(2,1)S(1)}, bf16[3,192,256]{2,1,0:T(8,128)(2,1)S(1)}, bf16[16,256]{1,0:T(8,128)(2,1)S(1)}) custom-call(bf16[4,32,16,256]{3,2,1,0:T(8,128)(2,1)S(1)} %get-tuple-element.32.raw_ref, bf16[512,512]{1,0:T(8,128)(2,1)S(1)} %get-tuple-element.33.perm_ref, ...), custom_call_target="tpu_custom_call" | custom-call | flops 1000000000 | bytes 3264512 | tf_op jit(solution)/shard_map/pallas_call | solution.py:40
  7.8 0.1 collective-permute-start
  7.9 0.4 collective-permute-done.1.mid_in
  8.3 0.8 %collective-permute-done.core_in = bf16[16,256]{1,0:T(8,128)(2,1)S(1)} collective-permute-done((bf16[16,256]{1,0:T(8,128)(2,1)S(1)}, bf16[16,256]{1,0:T(8,128)(2,1)S(1)}, u32[]{:S(2)}, u32[]{:S(2)}) %collective-permute-start) | collective-permute-done | bytes 8224 | tf_op jit(solution)/shard_map/ppermute | solution.py:458
  9.1 0.1 shard_map.69
  9.2 8.5 %collective-permute-start.2 = (bf16[144,256]{1,0:T(8,128)(2,1)S(1)}, bf16[144,256]{1,0:T(8,128)(2,1)S(1)}, u32[]{:S(2)}, u32[]{:S(2)}) collective-permute-start(bf16[144,256]{1,0:T(8,128)(2,1)S(1)} %get-tuple-element.43), channel_id=1, source_target_pairs={{0,63},{1,2},{2,1},{3,4},{4,3},{5,6},{6,5},{7,8},{8,7},{9,10},{10,... | collective-permute-start | bytes 221192 | tf_op jit(solution)/shard_map/ppermute | solution.py:507
  17.7 0.0 collective-permute-start.3
  17.7 2.9 %shard_map.70 = (bf16[960,256]{1,0:T(8,128)(2,1)S(1)}, f32[2,3,32,128]{3,2,1,0:T(8,128)S(1)}) custom-call(bf16[1024,256]{1,0:T(8,128)(2,1)S(1)} %get-tuple-element.37.x_ref, bf16[1024,256]{1,0:T(8,128)(2,1)S(1)} %get-tuple-element.38.cot_ref, bf16[16,1024]{1,0:T(8,128)(2,1)S(1)} %get-tuple-element.41.core_ref, ...), custom_call_target="tpu_custom_call" | custom-call | flops 4000000000 | bytes 2293760 | tf_op jit(solution)/shard_map/pallas_call | solution.py:40
  20.6 0.0 collective-permute-done.2.far_ref
  20.6 0.3 collective-permute-done.3.near_ref
  20.9 0.9 %shard_map.71 = (bf16[64,256]{1,0:T(8,128)(2,1)S(1)}, bf16[64,256]{1,0:T(8,128)(2,1)S(1)}, f32[144,128]{1,0:T(8,128)S(1)}, bf16[144,256]{1,0:T(8,128)(2,1)S(1)}, bf16[144,256]{1,0:T(8,128)(2,1)S(1)}) custom-call(bf16[1024,256]{1,0:T(8,128)(2,1)S(1)} %get-tuple-element.37.x_ref, bf16[1024,256]{1,0:T(8,128)(2,1)S(1)} %get-tuple-element.38.cot_ref, ...), custom_call_target="tpu_custom_call" | custom-call | flops 1000000000 | bytes 2236416 | tf_op jit(solution)/shard_map/pallas_call | solution.py:40
  21.8 1.9 %collective-permute-start.4 = (f32[144,128]{1,0:T(8,128)S(1)}, f32[144,128]{1,0:T(8,128)S(1)}, u32[]{:S(2)}, u32[]{:S(2)}) collective-permute-start(f32[144,128]{1,0:T(8,128)S(1)} %get-tuple-element.53), channel_id=1, source_target_pairs={{0,64},{64,0},{128,192},{192,128},{1,65},{65,1},{129,193},{193,129... | collective-permute-start | bytes 221192 | tf_op jit(solution)/shard_map/ppermute | solution.py:458
  23.7 0.9 %collective-permute-done.4 = f32[144,128]{1,0:T(8,128)S(1)} collective-permute-done((f32[144,128]{1,0:T(8,128)S(1)}, f32[144,128]{1,0:T(8,128)S(1)}, u32[]{:S(2)}, u32[]{:S(2)}) %collective-permute-start.4) | collective-permute-done | bytes 73760 | tf_op jit(solution)/shard_map/ppermute | solution.py:458
  24.6 0.1 collective-permute-start.7
  24.7 0.1 collective-permute-start.6
  24.8 3.4 %collective-permute-start.5 = (f32[144,128]{1,0:T(8,128)S(1)}, f32[144,128]{1,0:T(8,128)S(1)}, u32[]{:S(2)}, u32[]{:S(2)}) collective-permute-start(f32[144,128]{1,0:T(8,128)S(1)} %add.33), channel_id=1, source_target_pairs={{0,32},{1,33},{2,34},{3,35},{4,36},{5,37},{6,38},{7,39},{8,40},{9,... | collective-permute-start | bytes 221192 | tf_op jit(solution)/shard_map/ppermute | solution.py:429
  28.3 1.5 %collective-permute-done.7 = f32[144,128]{1,0:T(8,128)S(1)} collective-permute-done((f32[144,128]{1,0:T(8,128)S(1)}, f32[144,128]{1,0:T(8,128)S(1)}, u32[]{:S(2)}, u32[]{:S(2)}) %collective-permute-start.7) | collective-permute-done | bytes 73760 | tf_op jit(solution)/shard_map/ppermute | solution.py:429
  29.8 0.0 collective-permute-done.6
  29.8 1.0 %collective-permute-done.5 = f32[144,128]{1,0:T(8,128)S(1)} collective-permute-done((f32[144,128]{1,0:T(8,128)S(1)}, f32[144,128]{1,0:T(8,128)S(1)}, u32[]{:S(2)}, u32[]{:S(2)}) %collective-permute-start.5) | collective-permute-done | bytes 73760 | tf_op jit(solution)/shard_map/ppermute | solution.py:429
  30.8 0.8 %collective-permute-start.8 = (f32[144,128]{1,0:T(8,128)S(1)}, f32[144,128]{1,0:T(8,128)S(1)}, u32[]{:S(2)}, u32[]{:S(2)}) collective-permute-start(f32[144,128]{1,0:T(8,128)S(1)} %add_add_fusion.2), channel_id=1, source_target_pairs={{0,32},{1,33},{2,34},{3,35},{4,36},{5,37},{6,38},{7,39},{8,40},{9,... | collective-permute-start | bytes 221192 | tf_op jit(solution)/shard_map/ppermute | solution.py:429
  31.6 4.7 %collective-permute-done.8 = f32[144,128]{1,0:T(8,128)S(1)} collective-permute-done((f32[144,128]{1,0:T(8,128)S(1)}, f32[144,128]{1,0:T(8,128)S(1)}, u32[]{:S(2)}, u32[]{:S(2)}) %collective-permute-start.8) | collective-permute-done | bytes 73760 | tf_op jit(solution)/shard_map/ppermute | solution.py:429
  36.3 2.5 %collective-permute-start.11 = (f32[144,128]{1,0:T(8,128)S(1)}, f32[144,128]{1,0:T(8,128)S(1)}, u32[]{:S(2)}, u32[]{:S(2)}) collective-permute-start(f32[144,128]{1,0:T(8,128)S(1)} %add.37.partial_ref), channel_id=1, source_target_pairs={{0,1},{1,0},{2,3},{3,2},{4,5},{5,4},{6,7},{7,6},{8,9},{9,8},{10,11... | collective-permute-start | bytes 221192 | tf_op jit(solution)/shard_map/ppermute | solution.py:429
  38.9 0.4 collective-permute-start.10
  39.3 0.0 collective-permute-start.9
  39.3 1.2 %shard_map.72 = (bf16[3,1088,256]{2,1,0:T(8,128)(2,1)S(1)}, bf16[3,192,256]{2,1,0:T(8,128)(2,1)S(1)}, f32[144,128]{1,0:T(8,128)S(1)}) custom-call(bf16[1024,256]{1,0:T(8,128)(2,1)S(1)} %get-tuple-element.37.x_ref, bf16[1024,256]{1,0:T(8,128)(2,1)S(1)} %get-tuple-element.38.cot_ref, bf16[16,1024]{1,0:T(8,128)(2,1)S(1)} %get-tuple-element.41.core_ref, ...), custom_call_target="tpu_custom_call" | custom-call | flops 1000000000 | bytes 4540416 | tf_op jit(solution)/shard_map/pallas_call | solution.py:40
  40.5 0.6 %collective-permute-done.11 = f32[144,128]{1,0:T(8,128)S(1)} collective-permute-done((f32[144,128]{1,0:T(8,128)S(1)}, f32[144,128]{1,0:T(8,128)S(1)}, u32[]{:S(2)}, u32[]{:S(2)}) %collective-permute-start.11) | collective-permute-done | bytes 73760 | tf_op jit(solution)/shard_map/ppermute | solution.py:429
  41.1 2.2 %collective-permute-done.10 = f32[144,128]{1,0:T(8,128)S(1)} collective-permute-done((f32[144,128]{1,0:T(8,128)S(1)}, f32[144,128]{1,0:T(8,128)S(1)}, u32[]{:S(2)}, u32[]{:S(2)}) %collective-permute-start.10) | collective-permute-done | bytes 73760 | tf_op jit(solution)/shard_map/ppermute | solution.py:429
  43.3 0.0 collective-permute-done.9
  43.3 0.1 collective-permute-start.14
  43.4 2.7 %collective-permute-start.13 = (f32[144,128]{1,0:T(8,128)S(1)}, f32[144,128]{1,0:T(8,128)S(1)}, u32[]{:S(2)}, u32[]{:S(2)}) collective-permute-start(f32[144,128]{1,0:T(8,128)S(1)} %add_add_fusion.1.partial_ref), channel_id=1, source_target_pairs={{0,32},{1,33},{2,34},{3,35},{4,36},{5,37},{6,38},{7,39},{8,40},{9,... | collective-permute-start | bytes 221192 | tf_op jit(solution)/shard_map/ppermute | solution.py:429
  46.1 0.0 collective-permute-start.12
  46.1 2.2 %shard_map.73 = (bf16[32,32,256]{2,1,0:T(8,128)(2,1)}, f32[144,128]{1,0:T(8,128)S(1)}) custom-call(bf16[3,1088,256]{2,1,0:T(8,128)(2,1)S(1)} %get-tuple-element.54.ps, bf16[3,192,256]{2,1,0:T(8,128)(2,1)S(1)} %get-tuple-element.55.last_ref, bf16[4,32,16,256]{3,2,1,0:T(8,128)(2,1)S(1)} %get-tuple-element.32.raw_ref, f32[144,128]{1,0:T(8,128)S(1)} %add_add_fusion.1.partial_ref), custom_call_target="tpu_custom_call" | custom-call | flops 2000000000 | bytes 3686400 | tf_op jit(solution)/shard_map/pallas_call | solution.py:40
  48.3 0.0 collective-permute-done.14
  48.3 0.6 %collective-permute-done.13 = f32[144,128]{1,0:T(8,128)S(1)} collective-permute-done((f32[144,128]{1,0:T(8,128)S(1)}, f32[144,128]{1,0:T(8,128)S(1)}, u32[]{:S(2)}, u32[]{:S(2)}) %collective-permute-start.13) | collective-permute-done | bytes 73760 | tf_op jit(solution)/shard_map/ppermute | solution.py:429
  48.9 0.5 collective-permute-done.12
  49.4 0.1 collective-permute-start.15
  49.5 1.3 %collective-permute-done.15.given_ref = f32[144,128]{1,0:T(8,128)S(1)} collective-permute-done((f32[144,128]{1,0:T(8,128)S(1)}, f32[144,128]{1,0:T(8,128)S(1)}, u32[]{:S(2)}, u32[]{:S(2)}) %collective-permute-start.15) | collective-permute-done | bytes 73760 | tf_op jit(solution)/shard_map/ppermute | solution.py:458
  50.7 1.0 %shard_map.74 = (f32[3,3,32,32]{3,2,1,0:T(8,128)}, f32[3,3,32,32]{3,2,1,0:T(8,128)}) custom-call(f32[144,128]{1,0:T(8,128)S(1)} %add_add_fusion.total_ref, f32[144,128]{1,0:T(8,128)S(1)} %collective-permute-done.15.given_ref), custom_call_target="tpu_custom_call" | custom-call | flops 1000000 | bytes 221184 | tf_op jit(solution)/shard_map/pallas_call | solution.py:40
  (5 shorter events, 0.1 us)
Async XLA Ops:
  2.8 5.6 %collective-permute-start.1 = (bf16[16,256]{1,0:T(8,128)(2,1)S(1)}, bf16[16,256]{1,0:T(8,128)(2,1)S(1)}, u32[]{:S(2)}, u32[]{:S(2)}) collective-permute-start(bf16[16,256]{1,0:T(8,128)(2,1)S(1)} %get-tuple-element.40), channel_id=1, source_target_pairs={{0,192},{64,128},{128,64},{192,0},{1,193},{65,129},{129,65},{193,1... | collective-permute-start | bytes 24584 | tf_op jit(solution)/shard_map/ppermute | solution.py:454
  7.8 1.3 %collective-permute-start = (bf16[16,256]{1,0:T(8,128)(2,1)S(1)}, bf16[16,256]{1,0:T(8,128)(2,1)S(1)}, u32[]{:S(2)}, u32[]{:S(2)}) collective-permute-start(bf16[16,256]{1,0:T(8,128)(2,1)S(1)} %get-tuple-element.39), channel_id=1, source_target_pairs={{0,64},{64,0},{128,192},{192,128},{1,65},{65,1},{129,193},{193,129... | collective-permute-start | bytes 24584 | tf_op jit(solution)/shard_map/ppermute | solution.py:458
  9.2 11.4 %collective-permute-start.2 = (bf16[144,256]{1,0:T(8,128)(2,1)S(1)}, bf16[144,256]{1,0:T(8,128)(2,1)S(1)}, u32[]{:S(2)}, u32[]{:S(2)}) collective-permute-start(bf16[144,256]{1,0:T(8,128)(2,1)S(1)} %get-tuple-element.43), channel_id=1, source_target_pairs={{0,63},{1,2},{2,1},{3,4},{4,3},{5,6},{6,5},{7,8},{8,7},{9,10},{10,... | collective-permute-start | bytes 221192 | tf_op jit(solution)/shard_map/ppermute | solution.py:507
  17.7 3.2 %collective-permute-start.3 = (bf16[144,256]{1,0:T(8,128)(2,1)S(1)}, bf16[144,256]{1,0:T(8,128)(2,1)S(1)}, u32[]{:S(2)}, u32[]{:S(2)}) collective-permute-start(bf16[144,256]{1,0:T(8,128)(2,1)S(1)} %get-tuple-element.44), channel_id=1, source_target_pairs={{0,1},{1,0},{2,3},{3,2},{4,5},{5,4},{6,7},{7,6},{8,9},{9,8},{10,11... | collective-permute-start | bytes 221192 | tf_op jit(solution)/shard_map/ppermute | solution.py:508
  21.8 2.8 %collective-permute-start.4 = (f32[144,128]{1,0:T(8,128)S(1)}, f32[144,128]{1,0:T(8,128)S(1)}, u32[]{:S(2)}, u32[]{:S(2)}) collective-permute-start(f32[144,128]{1,0:T(8,128)S(1)} %get-tuple-element.53), channel_id=1, source_target_pairs={{0,64},{64,0},{128,192},{192,128},{1,65},{65,1},{129,193},{193,129... | collective-permute-start | bytes 221192 | tf_op jit(solution)/shard_map/ppermute | solution.py:458
  24.6 5.1 %collective-permute-start.7 = (f32[144,128]{1,0:T(8,128)S(1)}, f32[144,128]{1,0:T(8,128)S(1)}, u32[]{:S(2)}, u32[]{:S(2)}) collective-permute-start(f32[144,128]{1,0:T(8,128)S(1)} %add.33), channel_id=1, source_target_pairs={{0,32},{1,33},{2,34},{3,35},{4,36},{5,37},{6,38},{7,39},{8,40},{9,... | collective-permute-start | bytes 221192 | tf_op jit(solution)/shard_map/ppermute | solution.py:429
  24.7 5.0 %collective-permute-start.6 = (f32[144,128]{1,0:T(8,128)S(1)}, f32[144,128]{1,0:T(8,128)S(1)}, u32[]{:S(2)}, u32[]{:S(2)}) collective-permute-start(f32[144,128]{1,0:T(8,128)S(1)} %add.33), channel_id=1, source_target_pairs={{0,32},{1,33},{2,34},{3,35},{4,36},{5,37},{6,38},{7,39},{8,40},{9,... | collective-permute-start | bytes 221192 | tf_op jit(solution)/shard_map/ppermute | solution.py:429
  24.8 6.0 %collective-permute-start.5 = (f32[144,128]{1,0:T(8,128)S(1)}, f32[144,128]{1,0:T(8,128)S(1)}, u32[]{:S(2)}, u32[]{:S(2)}) collective-permute-start(f32[144,128]{1,0:T(8,128)S(1)} %add.33), channel_id=1, source_target_pairs={{0,32},{1,33},{2,34},{3,35},{4,36},{5,37},{6,38},{7,39},{8,40},{9,... | collective-permute-start | bytes 221192 | tf_op jit(solution)/shard_map/ppermute | solution.py:429
  30.8 5.5 %collective-permute-start.8 = (f32[144,128]{1,0:T(8,128)S(1)}, f32[144,128]{1,0:T(8,128)S(1)}, u32[]{:S(2)}, u32[]{:S(2)}) collective-permute-start(f32[144,128]{1,0:T(8,128)S(1)} %add_add_fusion.2), channel_id=1, source_target_pairs={{0,32},{1,33},{2,34},{3,35},{4,36},{5,37},{6,38},{7,39},{8,40},{9,... | collective-permute-start | bytes 221192 | tf_op jit(solution)/shard_map/ppermute | solution.py:429
  36.3 4.8 %collective-permute-start.11 = (f32[144,128]{1,0:T(8,128)S(1)}, f32[144,128]{1,0:T(8,128)S(1)}, u32[]{:S(2)}, u32[]{:S(2)}) collective-permute-start(f32[144,128]{1,0:T(8,128)S(1)} %add.37.partial_ref), channel_id=1, source_target_pairs={{0,1},{1,0},{2,3},{3,2},{4,5},{5,4},{6,7},{7,6},{8,9},{9,8},{10,11... | collective-permute-start | bytes 221192 | tf_op jit(solution)/shard_map/ppermute | solution.py:429
  38.9 4.4 %collective-permute-start.10 = (f32[144,128]{1,0:T(8,128)S(1)}, f32[144,128]{1,0:T(8,128)S(1)}, u32[]{:S(2)}, u32[]{:S(2)}) collective-permute-start(f32[144,128]{1,0:T(8,128)S(1)} %add.37.partial_ref), channel_id=1, source_target_pairs={{0,1},{1,0},{2,3},{3,2},{4,5},{5,4},{6,7},{7,6},{8,9},{9,8},{10,11... | collective-permute-start | bytes 221192 | tf_op jit(solution)/shard_map/ppermute | solution.py:429
  39.3 4.0 %collective-permute-start.9 = (f32[144,128]{1,0:T(8,128)S(1)}, f32[144,128]{1,0:T(8,128)S(1)}, u32[]{:S(2)}, u32[]{:S(2)}) collective-permute-start(f32[144,128]{1,0:T(8,128)S(1)} %add.37.partial_ref), channel_id=1, source_target_pairs={{0,1},{1,0},{2,3},{3,2},{4,5},{5,4},{6,7},{7,6},{8,9},{9,8},{10,11... | collective-permute-start | bytes 221192 | tf_op jit(solution)/shard_map/ppermute | solution.py:429
  43.3 5.0 %collective-permute-start.14 = (f32[144,128]{1,0:T(8,128)S(1)}, f32[144,128]{1,0:T(8,128)S(1)}, u32[]{:S(2)}, u32[]{:S(2)}) collective-permute-start(f32[144,128]{1,0:T(8,128)S(1)} %add_add_fusion.1.partial_ref), channel_id=1, source_target_pairs={{0,32},{1,33},{2,34},{3,35},{4,36},{5,37},{6,38},{7,39},{8,40},{9,... | collective-permute-start | bytes 221192 | tf_op jit(solution)/shard_map/ppermute | solution.py:429
  43.4 5.5 %collective-permute-start.13 = (f32[144,128]{1,0:T(8,128)S(1)}, f32[144,128]{1,0:T(8,128)S(1)}, u32[]{:S(2)}, u32[]{:S(2)}) collective-permute-start(f32[144,128]{1,0:T(8,128)S(1)} %add_add_fusion.1.partial_ref), channel_id=1, source_target_pairs={{0,32},{1,33},{2,34},{3,35},{4,36},{5,37},{6,38},{7,39},{8,40},{9,... | collective-permute-start | bytes 221192 | tf_op jit(solution)/shard_map/ppermute | solution.py:429
  46.1 3.2 %collective-permute-start.12 = (f32[144,128]{1,0:T(8,128)S(1)}, f32[144,128]{1,0:T(8,128)S(1)}, u32[]{:S(2)}, u32[]{:S(2)}) collective-permute-start(f32[144,128]{1,0:T(8,128)S(1)} %add_add_fusion.1.partial_ref), channel_id=1, source_target_pairs={{0,32},{1,33},{2,34},{3,35},{4,36},{5,37},{6,38},{7,39},{8,40},{9,... | collective-permute-start | bytes 221192 | tf_op jit(solution)/shard_map/ppermute | solution.py:429
  49.4 1.4 %collective-permute-start.15 = (f32[144,128]{1,0:T(8,128)S(1)}, f32[144,128]{1,0:T(8,128)S(1)}, u32[]{:S(2)}, u32[]{:S(2)}) collective-permute-start(f32[144,128]{1,0:T(8,128)S(1)} %add_add_fusion.total_ref), channel_id=1, source_target_pairs={{0,64},{64,0},{128,192},{192,128},{1,65},{65,1},{129,193},{193,129... | collective-permute-start | bytes 221192 | tf_op jit(solution)/shard_map/ppermute | solution.py:458

commit v10 on v7

--- a/solution.py
+++ b/solution.py
@@ -162,6 +162,10 @@
     return ((row % HALF == wanted_row) & (lane == wanted_lane) & (inside > 0)).astype(F32).astype(BF)
 
 
+def halo_places(odd, lat_cells):
+    return jnp.concatenate([halo_place(odd, place, lat_cells) for place in range(2)], 1)
+
+
 def write_shifted(values, edge_columns, target, rows):
     lat_cells = values.shape[1]
     lane = iota(values.shape, 1)
@@ -189,9 +193,9 @@
     odd = is_odd()
     halos = jnp.concatenate([core_ref[...], mid_ref[...]], 0)
     everything = slice(0, x_ref.shape[0])
+    columns = dot_rows(halos, halo_places(odd, lat_cells))
     for place, (source, target) in enumerate(((x_ref, xs), (cot_ref, cs))):
-        columns = dot_rows(halos, halo_place(odd, place, lat_cells))
-        write_shifted(source[...], columns, target, everything)
+        write_shifted(source[...], columns[:, place * lat_cells : (place + 1) * lat_cells], target, everything)
     group_rows = GROUP * channels
     for k in range(pre_ref.shape[0] // group_rows):
         rows = slice(k * group_rows, k * group_rows + WINDOW * channels)
@@ -231,6 +235,7 @@
     left_ref[...] = jnp.where(lon_is_odd() == 1, near, far).astype(BF)
     right_ref[...] = jnp.where(lon_is_odd() == 1, far, near).astype(BF)
     sides = ((left_ref, low_ref), (right_ref, high_ref))
+    places = halo_places(odd, lat_cells)
     for side, (message, _) in enumerate(sides):
         own = slice(0, two) if side == 0 else slice(own_rows - two, own_rows)
         sent = message[2 * two : 2 * two + HALF, :]
@@ -238,10 +243,11 @@
         own_halos = jnp.concatenate([core_ref[:, own], mid_ref[:, own]], 0).astype(F32)
         order = (sent_halos, own_halos) if side == 0 else (own_halos, sent_halos)
         halos = jnp.concatenate(order, 1).astype(BF)
+        both = dot_rows(halos, places)
         for place, (source, shifted) in enumerate(((x_ref, xs_sides), (cot_ref, cs_sides))):
             sent_rows = message[place * two : (place + 1) * two, :]
             order = (sent_rows, source[own, :]) if side == 0 else (source[own, :], sent_rows)
-            columns = dot_rows(halos, halo_place(odd, place, lat_cells))
+            columns = both[:, place * lat_cells : (place + 1) * lat_cells]
             write_shifted(jnp.concatenate(order, 0), columns, shifted.at[side], slice(0, 2 * two))
     rows = slice(0, 2 * two)
     pre_acts = [conv_rows(first_ref, xs_sides.at[side], rows, two) for side in range(2)]

time: 51.8 us -> 51.8 us (level)
  no operation moved by 1% of the time
where the time goes in v10:
time: 51.8 us; the launch traced here: 51.7 us
  starting transfers between devices  25.6 us (49%)
  waiting for transfers between devices  14 us (27%)
  Pallas kernels  11.2 us (22%)
  between operations  0.78 us (2%)
    pallas_call x8, Pallas kernels, call(): pl.pallas_call(kernel, out_shape=outs, in_specs=[pl.BlockSpec(memory_spac...  11.2 us
    ppermute x10, starting transfers between devices, exchange(): return lax.ppermute(value, ('lat', 'lon'), pairs(counts, partner, idle))  10.8 us
    ppermute x10, waiting for transfers between devices, exchange(): return lax.ppermute(value, ('lat', 'lon'), pairs(counts, partner, idle))  10.4 us
    ppermute x1, starting transfers between devices, on_device(): lax.ppermute(far_out, 'lon', [(i, (i + 1 if i % 2 else i - 1) % count) fo...  8.5 us
    ppermute x1, starting transfers between devices, mid_exchange(): lax.ppermute(edges, 'lat', [(i, (i - 1 if i % 2 == 0 else i + 1) % count)...  4.22 us
    ppermute x3, waiting for transfers between devices, core_exchange(): lax.ppermute(value, 'lat', [(i, i ^ 1) for i in range(lax.axis_size('lat'...  2.92 us
    ppermute x3, starting transfers between devices, core_exchange(): lax.ppermute(value, 'lat', [(i, i ^ 1) for i in range(lax.axis_size('lat'...  2.1 us
  transfers between devices with their start and end apart: 16, of which 12 were waited for; matrix products, arithmetic and copies ran while one was open for 0% of the time, Pallas kernels for 14%

profile of v10, /device:TPU:1, one launch (start us, length us, event | category | flops | bytes accessed | tf_op | source)
XLA Modules:
  0.0 51.7 jit_solution(2910400709975018779)
XLA Ops:
  0.6 2.1 %shard_map.67 = (bf16[4,32,16,256]{3,2,1,0:T(8,128)(2,1)S(1)}, bf16[3,3,32,32]{3,2,1,0:T(8,128)(2,1)S(1)}, bf16[3,3,32,32]{3,2,1,0:T(8,128)(2,1)S(1)}, bf16[512,...) custom-call(bf16[32,32,256]{2,1,0:T(8,128)(2,1)} %x_hbm.1, ...), custom_call_target="tpu_custom_call" | custom-call | flops 100000000 | bytes 2711552 | tf_op jit(solution)/shard_map/pallas_call | solution.py:40
  2.8 4.2 %collective-permute-start.1 = (bf16[16,256]{1,0:T(8,128)(2,1)S(1)}, bf16[16,256]{1,0:T(8,128)(2,1)S(1)}, u32[]{:S(2)}, u32[]{:S(2)}) collective-permute-start(bf16[16,256]{1,0:T(8,128)(2,1)S(1)} %get-tuple-element.40), channel_id=1, source_target_pairs={{0,192},{64,128},{128,64},{192,0},{1,193},{65,129},{129,65},{193,1... | collective-permute-start | bytes 24584 | tf_op jit(solution)/shard_map/ppermute | solution.py:460
  7.0 0.8 %shard_map.68 = (bf16[1024,256]{1,0:T(8,128)(2,1)S(1)}, bf16[1024,256]{1,0:T(8,128)(2,1)S(1)}, bf16[3,192,256]{2,1,0:T(8,128)(2,1)S(1)}, bf16[3,192,256]{2,1,0:T(8,128)(2,1)S(1)}, bf16[16,256]{1,0:T(8,128)(2,1)S(1)}) custom-call(bf16[4,32,16,256]{3,2,1,0:T(8,128)(2,1)S(1)} %get-tuple-element.32.raw_ref, bf16[512,512]{1,0:T(8,128)(2,1)S(1)} %get-tuple-element.33.perm_ref, ...), custom_call_target="tpu_custom_call" | custom-call | flops 1000000000 | bytes 3264512 | tf_op jit(solution)/shard_map/pallas_call | solution.py:40
  7.8 0.1 collective-permute-start
  7.9 0.4 collective-permute-done.1.mid_in
  8.3 0.8 %collective-permute-done.core_in = bf16[16,256]{1,0:T(8,128)(2,1)S(1)} collective-permute-done((bf16[16,256]{1,0:T(8,128)(2,1)S(1)}, bf16[16,256]{1,0:T(8,128)(2,1)S(1)}, u32[]{:S(2)}, u32[]{:S(2)}) %collective-permute-start) | collective-permute-done | bytes 8224 | tf_op jit(solution)/shard_map/ppermute | solution.py:464
  9.1 0.1 shard_map.69
  9.2 8.5 %collective-permute-start.2 = (bf16[144,256]{1,0:T(8,128)(2,1)S(1)}, bf16[144,256]{1,0:T(8,128)(2,1)S(1)}, u32[]{:S(2)}, u32[]{:S(2)}) collective-permute-start(bf16[144,256]{1,0:T(8,128)(2,1)S(1)} %get-tuple-element.43), channel_id=1, source_target_pairs={{0,63},{1,2},{2,1},{3,4},{4,3},{5,6},{6,5},{7,8},{8,7},{9,10},{10,... | collective-permute-start | bytes 221192 | tf_op jit(solution)/shard_map/ppermute | solution.py:513
  17.7 0.0 collective-permute-start.3
  17.7 2.9 %shard_map.70 = (bf16[960,256]{1,0:T(8,128)(2,1)S(1)}, f32[2,3,32,128]{3,2,1,0:T(8,128)S(1)}) custom-call(bf16[1024,256]{1,0:T(8,128)(2,1)S(1)} %get-tuple-element.37.x_ref, bf16[1024,256]{1,0:T(8,128)(2,1)S(1)} %get-tuple-element.38.cot_ref, bf16[16,1024]{1,0:T(8,128)(2,1)S(1)} %get-tuple-element.41.core_ref, ...), custom_call_target="tpu_custom_call" | custom-call | flops 4000000000 | bytes 2293760 | tf_op jit(solution)/shard_map/pallas_call | solution.py:40
  20.6 0.0 collective-permute-done.2.far_ref
  20.6 0.3 collective-permute-done.3.near_ref
  20.9 0.9 %shard_map.71 = (bf16[64,256]{1,0:T(8,128)(2,1)S(1)}, bf16[64,256]{1,0:T(8,128)(2,1)S(1)}, f32[144,128]{1,0:T(8,128)S(1)}, bf16[144,256]{1,0:T(8,128)(2,1)S(1)}, bf16[144,256]{1,0:T(8,128)(2,1)S(1)}) custom-call(bf16[1024,256]{1,0:T(8,128)(2,1)S(1)} %get-tuple-element.37.x_ref, bf16[1024,256]{1,0:T(8,128)(2,1)S(1)} %get-tuple-element.38.cot_ref, ...), custom_call_target="tpu_custom_call" | custom-call | flops 1000000000 | bytes 2236416 | tf_op jit(solution)/shard_map/pallas_call | solution.py:40
  21.8 1.9 %collective-permute-start.4 = (f32[144,128]{1,0:T(8,128)S(1)}, f32[144,128]{1,0:T(8,128)S(1)}, u32[]{:S(2)}, u32[]{:S(2)}) collective-permute-start(f32[144,128]{1,0:T(8,128)S(1)} %get-tuple-element.53), channel_id=1, source_target_pairs={{0,64},{64,0},{128,192},{192,128},{1,65},{65,1},{129,193},{193,129... | collective-permute-start | bytes 221192 | tf_op jit(solution)/shard_map/ppermute | solution.py:464
  23.7 0.9 %collective-permute-done.4 = f32[144,128]{1,0:T(8,128)S(1)} collective-permute-done((f32[144,128]{1,0:T(8,128)S(1)}, f32[144,128]{1,0:T(8,128)S(1)}, u32[]{:S(2)}, u32[]{:S(2)}) %collective-permute-start.4) | collective-permute-done | bytes 73760 | tf_op jit(solution)/shard_map/ppermute | solution.py:464
  24.6 2.5 %collective-permute-start.7 = (f32[144,128]{1,0:T(8,128)S(1)}, f32[144,128]{1,0:T(8,128)S(1)}, u32[]{:S(2)}, u32[]{:S(2)}) collective-permute-start(f32[144,128]{1,0:T(8,128)S(1)} %add.33), channel_id=1, source_target_pairs={{0,1},{1,0},{2,3},{3,2},{4,5},{5,4},{6,7},{7,6},{8,9},{9,8},{10,11... | collective-permute-start | bytes 221192 | tf_op jit(solution)/shard_map/ppermute | solution.py:435
  27.2 0.4 collective-permute-start.6
  27.6 0.0 collective-permute-start.5
  27.6 1.8 %collective-permute-done.7 = f32[144,128]{1,0:T(8,128)S(1)} collective-permute-done((f32[144,128]{1,0:T(8,128)S(1)}, f32[144,128]{1,0:T(8,128)S(1)}, u32[]{:S(2)}, u32[]{:S(2)}) %collective-permute-start.7) | collective-permute-done | bytes 73760 | tf_op jit(solution)/shard_map/ppermute | solution.py:435
  29.4 2.2 %collective-permute-done.6 = f32[144,128]{1,0:T(8,128)S(1)} collective-permute-done((f32[144,128]{1,0:T(8,128)S(1)}, f32[144,128]{1,0:T(8,128)S(1)}, u32[]{:S(2)}, u32[]{:S(2)}) %collective-permute-start.6) | collective-permute-done | bytes 73760 | tf_op jit(solution)/shard_map/ppermute | solution.py:435
  31.6 0.0 collective-permute-done.5
  31.6 0.1 collective-permute-start.10
  31.7 2.7 %collective-permute-start.9 = (f32[144,128]{1,0:T(8,128)S(1)}, f32[144,128]{1,0:T(8,128)S(1)}, u32[]{:S(2)}, u32[]{:S(2)}) collective-permute-start(f32[144,128]{1,0:T(8,128)S(1)} %add_add_fusion.2.partial_ref), channel_id=1, source_target_pairs={{0,32},{1,33},{2,34},{3,35},{4,36},{5,37},{6,38},{7,39},{8,40},{9,... | collective-permute-start | bytes 221192 | tf_op jit(solution)/shard_map/ppermute | solution.py:435
  34.4 0.0 collective-permute-start.8
  34.4 1.2 %shard_map.72 = (bf16[3,1088,256]{2,1,0:T(8,128)(2,1)S(1)}, bf16[3,192,256]{2,1,0:T(8,128)(2,1)S(1)}, f32[144,128]{1,0:T(8,128)S(1)}) custom-call(bf16[1024,256]{1,0:T(8,128)(2,1)S(1)} %get-tuple-element.37.x_ref, bf16[1024,256]{1,0:T(8,128)(2,1)S(1)} %get-tuple-element.38.cot_ref, bf16[16,1024]{1,0:T(8,128)(2,1)S(1)} %get-tuple-element.41.core_ref, ...), custom_call_target="tpu_custom_call" | custom-call | flops 1000000000 | bytes 4540416 | tf_op jit(solution)/shard_map/pallas_call | solution.py:40
  35.6 0.9 %collective-permute-done.10 = f32[144,128]{1,0:T(8,128)S(1)} collective-permute-done((f32[144,128]{1,0:T(8,128)S(1)}, f32[144,128]{1,0:T(8,128)S(1)}, u32[]{:S(2)}, u32[]{:S(2)}) %collective-permute-start.10) | collective-permute-done | bytes 73760 | tf_op jit(solution)/shard_map/ppermute | solution.py:435
  36.5 0.5 collective-permute-done.9
  37.0 0.6 %collective-permute-done.8 = f32[144,128]{1,0:T(8,128)S(1)} collective-permute-done((f32[144,128]{1,0:T(8,128)S(1)}, f32[144,128]{1,0:T(8,128)S(1)}, u32[]{:S(2)}, u32[]{:S(2)}) %collective-permute-start.8) | collective-permute-done | bytes 73760 | tf_op jit(solution)/shard_map/ppermute | solution.py:435
  37.7 0.1 collective-permute-start.13
  37.8 0.1 collective-permute-start.12
  37.9 3.4 %collective-permute-start.11 = (f32[144,128]{1,0:T(8,128)S(1)}, f32[144,128]{1,0:T(8,128)S(1)}, u32[]{:S(2)}, u32[]{:S(2)}) collective-permute-start(f32[144,128]{1,0:T(8,128)S(1)} %add_add_fusion.1.partial_ref), channel_id=1, source_target_pairs={{0,32},{1,33},{2,34},{3,35},{4,36},{5,37},{6,38},{7,39},{8,40},{9,... | collective-permute-start | bytes 221192 | tf_op jit(solution)/shard_map/ppermute | solution.py:435
  41.3 2.2 %shard_map.73 = (bf16[32,32,256]{2,1,0:T(8,128)(2,1)}, f32[144,128]{1,0:T(8,128)S(1)}) custom-call(bf16[3,1088,256]{2,1,0:T(8,128)(2,1)S(1)} %get-tuple-element.54.ps, bf16[3,192,256]{2,1,0:T(8,128)(2,1)S(1)} %get-tuple-element.55.last_ref, bf16[4,32,16,256]{3,2,1,0:T(8,128)(2,1)S(1)} %get-tuple-element.32.raw_ref, f32[144,128]{1,0:T(8,128)S(1)} %add_add_fusion.1.partial_ref), custom_call_target="tpu_custom_call" | custom-call | flops 2000000000 | bytes 3686400 | tf_op jit(solution)/shard_map/pallas_call | solution.py:40
  43.5 0.0 collective-permute-done.13
  43.5 0.0 collective-permute-done.12
  43.5 0.3 collective-permute-done.11
  43.8 1.4 %collective-permute-start.14 = (f32[144,128]{1,0:T(8,128)S(1)}, f32[144,128]{1,0:T(8,128)S(1)}, u32[]{:S(2)}, u32[]{:S(2)}) collective-permute-start(f32[144,128]{1,0:T(8,128)S(1)} %add_add_fusion), channel_id=1, source_target_pairs={{0,32},{1,33},{2,34},{3,35},{4,36},{5,37},{6,38},{7,39},{8,40},{9,... | collective-permute-start | bytes 221192 | tf_op jit(solution)/shard_map/ppermute | solution.py:435
  45.3 4.1 %collective-permute-done.14 = f32[144,128]{1,0:T(8,128)S(1)} collective-permute-done((f32[144,128]{1,0:T(8,128)S(1)}, f32[144,128]{1,0:T(8,128)S(1)}, u32[]{:S(2)}, u32[]{:S(2)}) %collective-permute-start.14) | collective-permute-done | bytes 73760 | tf_op jit(solution)/shard_map/ppermute | solution.py:435
  49.4 0.1 collective-permute-start.15
  49.5 1.3 %collective-permute-done.15.given_ref = f32[144,128]{1,0:T(8,128)S(1)} collective-permute-done((f32[144,128]{1,0:T(8,128)S(1)}, f32[144,128]{1,0:T(8,128)S(1)}, u32[]{:S(2)}, u32[]{:S(2)}) %collective-permute-start.15) | collective-permute-done | bytes 73760 | tf_op jit(solution)/shard_map/ppermute | solution.py:464
  50.7 1.0 %shard_map.74 = (f32[3,3,32,32]{3,2,1,0:T(8,128)}, f32[3,3,32,32]{3,2,1,0:T(8,128)}) custom-call(f32[144,128]{1,0:T(8,128)S(1)} %add.43.total_ref, f32[144,128]{1,0:T(8,128)S(1)} %collective-permute-done.15.given_ref), custom_call_target="tpu_custom_call" | custom-call | flops 1000000 | bytes 221184 | tf_op jit(solution)/shard_map/pallas_call | solution.py:40
  (5 shorter events, 0.1 us)
Async XLA Ops:
  2.8 5.6 %collective-permute-start.1 = (bf16[16,256]{1,0:T(8,128)(2,1)S(1)}, bf16[16,256]{1,0:T(8,128)(2,1)S(1)}, u32[]{:S(2)}, u32[]{:S(2)}) collective-permute-start(bf16[16,256]{1,0:T(8,128)(2,1)S(1)} %get-tuple-element.40), channel_id=1, source_target_pairs={{0,192},{64,128},{128,64},{192,0},{1,193},{65,129},{129,65},{193,1... | collective-permute-start | bytes 24584 | tf_op jit(solution)/shard_map/ppermute | solution.py:460
  7.8 1.3 %collective-permute-start = (bf16[16,256]{1,0:T(8,128)(2,1)S(1)}, bf16[16,256]{1,0:T(8,128)(2,1)S(1)}, u32[]{:S(2)}, u32[]{:S(2)}) collective-permute-start(bf16[16,256]{1,0:T(8,128)(2,1)S(1)} %get-tuple-element.39), channel_id=1, source_target_pairs={{0,64},{64,0},{128,192},{192,128},{1,65},{65,1},{129,193},{193,129... | collective-permute-start | bytes 24584 | tf_op jit(solution)/shard_map/ppermute | solution.py:464
  9.2 11.4 %collective-permute-start.2 = (bf16[144,256]{1,0:T(8,128)(2,1)S(1)}, bf16[144,256]{1,0:T(8,128)(2,1)S(1)}, u32[]{:S(2)}, u32[]{:S(2)}) collective-permute-start(bf16[144,256]{1,0:T(8,128)(2,1)S(1)} %get-tuple-element.43), channel_id=1, source_target_pairs={{0,63},{1,2},{2,1},{3,4},{4,3},{5,6},{6,5},{7,8},{8,7},{9,10},{10,... | collective-permute-start | bytes 221192 | tf_op jit(solution)/shard_map/ppermute | solution.py:513
  17.7 3.2 %collective-permute-start.3 = (bf16[144,256]{1,0:T(8,128)(2,1)S(1)}, bf16[144,256]{1,0:T(8,128)(2,1)S(1)}, u32[]{:S(2)}, u32[]{:S(2)}) collective-permute-start(bf16[144,256]{1,0:T(8,128)(2,1)S(1)} %get-tuple-element.44), channel_id=1, source_target_pairs={{0,1},{1,0},{2,3},{3,2},{4,5},{5,4},{6,7},{7,6},{8,9},{9,8},{10,11... | collective-permute-start | bytes 221192 | tf_op jit(solution)/shard_map/ppermute | solution.py:514
  21.8 2.8 %collective-permute-start.4 = (f32[144,128]{1,0:T(8,128)S(1)}, f32[144,128]{1,0:T(8,128)S(1)}, u32[]{:S(2)}, u32[]{:S(2)}) collective-permute-start(f32[144,128]{1,0:T(8,128)S(1)} %get-tuple-element.53), channel_id=1, source_target_pairs={{0,64},{64,0},{128,192},{192,128},{1,65},{65,1},{129,193},{193,129... | collective-permute-start | bytes 221192 | tf_op jit(solution)/shard_map/ppermute | solution.py:464
  24.6 4.8 %collective-permute-start.7 = (f32[144,128]{1,0:T(8,128)S(1)}, f32[144,128]{1,0:T(8,128)S(1)}, u32[]{:S(2)}, u32[]{:S(2)}) collective-permute-start(f32[144,128]{1,0:T(8,128)S(1)} %add.33), channel_id=1, source_target_pairs={{0,1},{1,0},{2,3},{3,2},{4,5},{5,4},{6,7},{7,6},{8,9},{9,8},{10,11... | collective-permute-start | bytes 221192 | tf_op jit(solution)/shard_map/ppermute | solution.py:435
  27.2 4.4 %collective-permute-start.6 = (f32[144,128]{1,0:T(8,128)S(1)}, f32[144,128]{1,0:T(8,128)S(1)}, u32[]{:S(2)}, u32[]{:S(2)}) collective-permute-start(f32[144,128]{1,0:T(8,128)S(1)} %add.33), channel_id=1, source_target_pairs={{0,1},{1,0},{2,3},{3,2},{4,5},{5,4},{6,7},{7,6},{8,9},{9,8},{10,11... | collective-permute-start | bytes 221192 | tf_op jit(solution)/shard_map/ppermute | solution.py:435
  27.6 4.0 %collective-permute-start.5 = (f32[144,128]{1,0:T(8,128)S(1)}, f32[144,128]{1,0:T(8,128)S(1)}, u32[]{:S(2)}, u32[]{:S(2)}) collective-permute-start(f32[144,128]{1,0:T(8,128)S(1)} %add.33), channel_id=1, source_target_pairs={{0,1},{1,0},{2,3},{3,2},{4,5},{5,4},{6,7},{7,6},{8,9},{9,8},{10,11... | collective-permute-start | bytes 221192 | tf_op jit(solution)/shard_map/ppermute | solution.py:435
  31.6 4.9 %collective-permute-start.10 = (f32[144,128]{1,0:T(8,128)S(1)}, f32[144,128]{1,0:T(8,128)S(1)}, u32[]{:S(2)}, u32[]{:S(2)}) collective-permute-start(f32[144,128]{1,0:T(8,128)S(1)} %add_add_fusion.2.partial_ref), channel_id=1, source_target_pairs={{0,32},{1,33},{2,34},{3,35},{4,36},{5,37},{6,38},{7,39},{8,40},{9,... | collective-permute-start | bytes 221192 | tf_op jit(solution)/shard_map/ppermute | solution.py:435
  31.7 5.3 %collective-permute-start.9 = (f32[144,128]{1,0:T(8,128)S(1)}, f32[144,128]{1,0:T(8,128)S(1)}, u32[]{:S(2)}, u32[]{:S(2)}) collective-permute-start(f32[144,128]{1,0:T(8,128)S(1)} %add_add_fusion.2.partial_ref), channel_id=1, source_target_pairs={{0,32},{1,33},{2,34},{3,35},{4,36},{5,37},{6,38},{7,39},{8,40},{9,... | collective-permute-start | bytes 221192 | tf_op jit(solution)/shard_map/ppermute | solution.py:435
  34.4 3.2 %collective-permute-start.8 = (f32[144,128]{1,0:T(8,128)S(1)}, f32[144,128]{1,0:T(8,128)S(1)}, u32[]{:S(2)}, u32[]{:S(2)}) collective-permute-start(f32[144,128]{1,0:T(8,128)S(1)} %add_add_fusion.2.partial_ref), channel_id=1, source_target_pairs={{0,32},{1,33},{2,34},{3,35},{4,36},{5,37},{6,38},{7,39},{8,40},{9,... | collective-permute-start | bytes 221192 | tf_op jit(solution)/shard_map/ppermute | solution.py:435
  37.7 5.8 %collective-permute-start.13 = (f32[144,128]{1,0:T(8,128)S(1)}, f32[144,128]{1,0:T(8,128)S(1)}, u32[]{:S(2)}, u32[]{:S(2)}) collective-permute-start(f32[144,128]{1,0:T(8,128)S(1)} %add_add_fusion.1.partial_ref), channel_id=1, source_target_pairs={{0,32},{1,33},{2,34},{3,35},{4,36},{5,37},{6,38},{7,39},{8,40},{9,... | collective-permute-start | bytes 221192 | tf_op jit(solution)/shard_map/ppermute | solution.py:435
  37.8 5.7 %collective-permute-start.12 = (f32[144,128]{1,0:T(8,128)S(1)}, f32[144,128]{1,0:T(8,128)S(1)}, u32[]{:S(2)}, u32[]{:S(2)}) collective-permute-start(f32[144,128]{1,0:T(8,128)S(1)} %add_add_fusion.1.partial_ref), channel_id=1, source_target_pairs={{0,32},{1,33},{2,34},{3,35},{4,36},{5,37},{6,38},{7,39},{8,40},{9,... | collective-permute-start | bytes 221192 | tf_op jit(solution)/shard_map/ppermute | solution.py:435
  37.9 6.0 %collective-permute-start.11 = (f32[144,128]{1,0:T(8,128)S(1)}, f32[144,128]{1,0:T(8,128)S(1)}, u32[]{:S(2)}, u32[]{:S(2)}) collective-permute-start(f32[144,128]{1,0:T(8,128)S(1)} %add_add_fusion.1.partial_ref), channel_id=1, source_target_pairs={{0,32},{1,33},{2,34},{3,35},{4,36},{5,37},{6,38},{7,39},{8,40},{9,... | collective-permute-start | bytes 221192 | tf_op jit(solution)/shard_map/ppermute | solution.py:435
  43.8 5.5 %collective-permute-start.14 = (f32[144,128]{1,0:T(8,128)S(1)}, f32[144,128]{1,0:T(8,128)S(1)}, u32[]{:S(2)}, u32[]{:S(2)}) collective-permute-start(f32[144,128]{1,0:T(8,128)S(1)} %add_add_fusion), channel_id=1, source_target_pairs={{0,32},{1,33},{2,34},{3,35},{4,36},{5,37},{6,38},{7,39},{8,40},{9,... | collective-permute-start | bytes 221192 | tf_op jit(solution)/shard_map/ppermute | solution.py:435
  49.4 1.4 %collective-permute-start.15 = (f32[144,128]{1,0:T(8,128)S(1)}, f32[144,128]{1,0:T(8,128)S(1)}, u32[]{:S(2)}, u32[]{:S(2)}) collective-permute-start(f32[144,128]{1,0:T(8,128)S(1)} %add.43.total_ref), channel_id=1, source_target_pairs={{0,64},{64,0},{128,192},{192,128},{1,65},{65,1},{129,193},{193,129... | collective-permute-start | bytes 221192 | tf_op jit(solution)/shard_map/ppermute | solution.py:464

commit v11 on v10

--- a/solution.py
+++ b/solution.py
@@ -231,9 +231,9 @@
     two = 2 * channels
     own_rows = x_ref.shape[0]
     sums = [[grads_ref[place, q][:, : 3 * channels] for q in range(3)] for place in range(2)]
-    far, near = far_ref[...].astype(F32), near_ref[...].astype(F32)
-    left_ref[...] = jnp.where(lon_is_odd() == 1, near, far).astype(BF)
-    right_ref[...] = jnp.where(lon_is_odd() == 1, far, near).astype(BF)
+    far, near = far_ref[...], near_ref[...]
+    left_ref[...] = jnp.where(lon_is_odd() == 1, near, far)
+    right_ref[...] = jnp.where(lon_is_odd() == 1, far, near)
     sides = ((left_ref, low_ref), (right_ref, high_ref))
     places = halo_places(odd, lat_cells)
     for side, (message, _) in enumerate(sides):

time: 51.8 us -> 51.8 us (level)
  no operation moved by 1% of the time
where the time goes in v11:
time: 51.8 us; the launch traced here: 51.7 us
  starting transfers between devices  25.6 us (49%)
  waiting for transfers between devices  14 us (27%)
  Pallas kernels  11.1 us (21%)
  between operations  0.78 us (2%)
    pallas_call x8, Pallas kernels, call(): pl.pallas_call(kernel, out_shape=outs, in_specs=[pl.BlockSpec(memory_spac...  11.1 us
    ppermute x10, starting transfers between devices, exchange(): return lax.ppermute(value, ('lat', 'lon'), pairs(counts, partner, idle))  10.8 us
    ppermute x10, waiting for transfers between devices, exchange(): return lax.ppermute(value, ('lat', 'lon'), pairs(counts, partner, idle))  10.4 us
    ppermute x1, starting transfers between devices, on_device(): lax.ppermute(far_out, 'lon', [(i, (i + 1 if i % 2 else i - 1) % count) fo...  8.5 us
    ppermute x1, starting transfers between devices, mid_exchange(): lax.ppermute(edges, 'lat', [(i, (i - 1 if i % 2 == 0 else i + 1) % count)...  4.22 us
    ppermute x3, waiting for transfers between devices, core_exchange(): lax.ppermute(value, 'lat', [(i, i ^ 1) for i in range(lax.axis_size('lat'...  2.92 us
    ppermute x3, starting transfers between devices, core_exchange(): lax.ppermute(value, 'lat', [(i, i ^ 1) for i in range(lax.axis_size('lat'...  2.1 us
  transfers between devices with their start and end apart: 16, of which 12 were waited for; matrix products, arithmetic and copies ran while one was open for 0% of the time, Pallas kernels for 14%

profile of v11, /device:TPU:1, one launch (start us, length us, event | category | flops | bytes accessed | tf_op | source)
XLA Modules:
  0.0 51.7 jit_solution(4042133977321429278)
XLA Ops:
  0.6 2.1 %shard_map.67 = (bf16[4,32,16,256]{3,2,1,0:T(8,128)(2,1)S(1)}, bf16[3,3,32,32]{3,2,1,0:T(8,128)(2,1)S(1)}, bf16[3,3,32,32]{3,2,1,0:T(8,128)(2,1)S(1)}, bf16[512,...) custom-call(bf16[32,32,256]{2,1,0:T(8,128)(2,1)} %x_hbm.1, ...), custom_call_target="tpu_custom_call" | custom-call | flops 100000000 | bytes 2711552 | tf_op jit(solution)/shard_map/pallas_call | solution.py:40
  2.8 4.2 %collective-permute-start.1 = (bf16[16,256]{1,0:T(8,128)(2,1)S(1)}, bf16[16,256]{1,0:T(8,128)(2,1)S(1)}, u32[]{:S(2)}, u32[]{:S(2)}) collective-permute-start(bf16[16,256]{1,0:T(8,128)(2,1)S(1)} %get-tuple-element.40), channel_id=1, source_target_pairs={{0,192},{64,128},{128,64},{192,0},{1,193},{65,129},{129,65},{193,1... | collective-permute-start | bytes 24584 | tf_op jit(solution)/shard_map/ppermute | solution.py:460
  7.0 0.8 %shard_map.68 = (bf16[1024,256]{1,0:T(8,128)(2,1)S(1)}, bf16[1024,256]{1,0:T(8,128)(2,1)S(1)}, bf16[3,192,256]{2,1,0:T(8,128)(2,1)S(1)}, bf16[3,192,256]{2,1,0:T(8,128)(2,1)S(1)}, bf16[16,256]{1,0:T(8,128)(2,1)S(1)}) custom-call(bf16[4,32,16,256]{3,2,1,0:T(8,128)(2,1)S(1)} %get-tuple-element.32.raw_ref, bf16[512,512]{1,0:T(8,128)(2,1)S(1)} %get-tuple-element.33.perm_ref, ...), custom_call_target="tpu_custom_call" | custom-call | flops 1000000000 | bytes 3264512 | tf_op jit(solution)/shard_map/pallas_call | solution.py:40
  7.8 0.1 collective-permute-start
  7.9 0.4 collective-permute-done.1.mid_in
  8.3 0.8 %collective-permute-done.core_in = bf16[16,256]{1,0:T(8,128)(2,1)S(1)} collective-permute-done((bf16[16,256]{1,0:T(8,128)(2,1)S(1)}, bf16[16,256]{1,0:T(8,128)(2,1)S(1)}, u32[]{:S(2)}, u32[]{:S(2)}) %collective-permute-start) | collective-permute-done | bytes 8224 | tf_op jit(solution)/shard_map/ppermute | solution.py:464
  9.1 0.1 shard_map.69
  9.2 8.5 %collective-permute-start.2 = (bf16[144,256]{1,0:T(8,128)(2,1)S(1)}, bf16[144,256]{1,0:T(8,128)(2,1)S(1)}, u32[]{:S(2)}, u32[]{:S(2)}) collective-permute-start(bf16[144,256]{1,0:T(8,128)(2,1)S(1)} %get-tuple-element.43), channel_id=1, source_target_pairs={{0,63},{1,2},{2,1},{3,4},{4,3},{5,6},{6,5},{7,8},{8,7},{9,10},{10,... | collective-permute-start | bytes 221192 | tf_op jit(solution)/shard_map/ppermute | solution.py:513
  17.7 0.0 collective-permute-start.3
  17.7 2.9 %shard_map.70 = (bf16[960,256]{1,0:T(8,128)(2,1)S(1)}, f32[2,3,32,128]{3,2,1,0:T(8,128)S(1)}) custom-call(bf16[1024,256]{1,0:T(8,128)(2,1)S(1)} %get-tuple-element.37.x_ref, bf16[1024,256]{1,0:T(8,128)(2,1)S(1)} %get-tuple-element.38.cot_ref, bf16[16,1024]{1,0:T(8,128)(2,1)S(1)} %get-tuple-element.41.core_ref, ...), custom_call_target="tpu_custom_call" | custom-call | flops 4000000000 | bytes 2293760 | tf_op jit(solution)/shard_map/pallas_call | solution.py:40
  20.6 0.0 collective-permute-done.2.far_ref
  20.6 0.3 collective-permute-done.3.near_ref
  20.9 0.8 %shard_map.71 = (bf16[64,256]{1,0:T(8,128)(2,1)S(1)}, bf16[64,256]{1,0:T(8,128)(2,1)S(1)}, f32[144,128]{1,0:T(8,128)S(1)}, bf16[144,256]{1,0:T(8,128)(2,1)S(1)}, bf16[144,256]{1,0:T(8,128)(2,1)S(1)}) custom-call(bf16[1024,256]{1,0:T(8,128)(2,1)S(1)} %get-tuple-element.37.x_ref, bf16[1024,256]{1,0:T(8,128)(2,1)S(1)} %get-tuple-element.38.cot_ref, ...), custom_call_target="tpu_custom_call" | custom-call | flops 1000000000 | bytes 2236416 | tf_op jit(solution)/shard_map/pallas_call | solution.py:40
  21.8 1.9 %collective-permute-start.4 = (f32[144,128]{1,0:T(8,128)S(1)}, f32[144,128]{1,0:T(8,128)S(1)}, u32[]{:S(2)}, u32[]{:S(2)}) collective-permute-start(f32[144,128]{1,0:T(8,128)S(1)} %get-tuple-element.53), channel_id=1, source_target_pairs={{0,64},{64,0},{128,192},{192,128},{1,65},{65,1},{129,193},{193,129... | collective-permute-start | bytes 221192 | tf_op jit(solution)/shard_map/ppermute | solution.py:464
  23.7 0.9 %collective-permute-done.4 = f32[144,128]{1,0:T(8,128)S(1)} collective-permute-done((f32[144,128]{1,0:T(8,128)S(1)}, f32[144,128]{1,0:T(8,128)S(1)}, u32[]{:S(2)}, u32[]{:S(2)}) %collective-permute-start.4) | collective-permute-done | bytes 73760 | tf_op jit(solution)/shard_map/ppermute | solution.py:464
  24.6 2.5 %collective-permute-start.7 = (f32[144,128]{1,0:T(8,128)S(1)}, f32[144,128]{1,0:T(8,128)S(1)}, u32[]{:S(2)}, u32[]{:S(2)}) collective-permute-start(f32[144,128]{1,0:T(8,128)S(1)} %add.33), channel_id=1, source_target_pairs={{0,1},{1,0},{2,3},{3,2},{4,5},{5,4},{6,7},{7,6},{8,9},{9,8},{10,11... | collective-permute-start | bytes 221192 | tf_op jit(solution)/shard_map/ppermute | solution.py:435
  27.2 0.4 collective-permute-start.6
  27.6 0.0 collective-permute-start.5
  27.6 1.8 %collective-permute-done.7 = f32[144,128]{1,0:T(8,128)S(1)} collective-permute-done((f32[144,128]{1,0:T(8,128)S(1)}, f32[144,128]{1,0:T(8,128)S(1)}, u32[]{:S(2)}, u32[]{:S(2)}) %collective-permute-start.7) | collective-permute-done | bytes 73760 | tf_op jit(solution)/shard_map/ppermute | solution.py:435
  29.4 2.2 %collective-permute-done.6 = f32[144,128]{1,0:T(8,128)S(1)} collective-permute-done((f32[144,128]{1,0:T(8,128)S(1)}, f32[144,128]{1,0:T(8,128)S(1)}, u32[]{:S(2)}, u32[]{:S(2)}) %collective-permute-start.6) | collective-permute-done | bytes 73760 | tf_op jit(solution)/shard_map/ppermute | solution.py:435
  31.6 0.0 collective-permute-done.5
  31.6 0.1 collective-permute-start.10
  31.7 2.7 %collective-permute-start.9 = (f32[144,128]{1,0:T(8,128)S(1)}, f32[144,128]{1,0:T(8,128)S(1)}, u32[]{:S(2)}, u32[]{:S(2)}) collective-permute-start(f32[144,128]{1,0:T(8,128)S(1)} %add_add_fusion.2.partial_ref), channel_id=1, source_target_pairs={{0,32},{1,33},{2,34},{3,35},{4,36},{5,37},{6,38},{7,39},{8,40},{9,... | collective-permute-start | bytes 221192 | tf_op jit(solution)/shard_map/ppermute | solution.py:435
  34.4 0.0 collective-permute-start.8
  34.4 1.2 %shard_map.72 = (bf16[3,1088,256]{2,1,0:T(8,128)(2,1)S(1)}, bf16[3,192,256]{2,1,0:T(8,128)(2,1)S(1)}, f32[144,128]{1,0:T(8,128)S(1)}) custom-call(bf16[1024,256]{1,0:T(8,128)(2,1)S(1)} %get-tuple-element.37.x_ref, bf16[1024,256]{1,0:T(8,128)(2,1)S(1)} %get-tuple-element.38.cot_ref, bf16[16,1024]{1,0:T(8,128)(2,1)S(1)} %get-tuple-element.41.core_ref, ...), custom_call_target="tpu_custom_call" | custom-call | flops 1000000000 | bytes 4540416 | tf_op jit(solution)/shard_map/pallas_call | solution.py:40
  35.6 0.9 %collective-permute-done.10 = f32[144,128]{1,0:T(8,128)S(1)} collective-permute-done((f32[144,128]{1,0:T(8,128)S(1)}, f32[144,128]{1,0:T(8,128)S(1)}, u32[]{:S(2)}, u32[]{:S(2)}) %collective-permute-start.10) | collective-permute-done | bytes 73760 | tf_op jit(solution)/shard_map/ppermute | solution.py:435
  36.5 0.5 collective-permute-done.9
  37.0 0.6 %collective-permute-done.8 = f32[144,128]{1,0:T(8,128)S(1)} collective-permute-done((f32[144,128]{1,0:T(8,128)S(1)}, f32[144,128]{1,0:T(8,128)S(1)}, u32[]{:S(2)}, u32[]{:S(2)}) %collective-permute-start.8) | collective-permute-done | bytes 73760 | tf_op jit(solution)/shard_map/ppermute | solution.py:435
  37.6 0.1 collective-permute-start.13
  37.7 0.1 collective-permute-start.12
  37.8 3.4 %collective-permute-start.11 = (f32[144,128]{1,0:T(8,128)S(1)}, f32[144,128]{1,0:T(8,128)S(1)}, u32[]{:S(2)}, u32[]{:S(2)}) collective-permute-start(f32[144,128]{1,0:T(8,128)S(1)} %add_add_fusion.1.partial_ref), channel_id=1, source_target_pairs={{0,32},{1,33},{2,34},{3,35},{4,36},{5,37},{6,38},{7,39},{8,40},{9,... | collective-permute-start | bytes 221192 | tf_op jit(solution)/shard_map/ppermute | solution.py:435
  41.3 2.2 %shard_map.73 = (bf16[32,32,256]{2,1,0:T(8,128)(2,1)}, f32[144,128]{1,0:T(8,128)S(1)}) custom-call(bf16[3,1088,256]{2,1,0:T(8,128)(2,1)S(1)} %get-tuple-element.54.ps, bf16[3,192,256]{2,1,0:T(8,128)(2,1)S(1)} %get-tuple-element.55.last_ref, bf16[4,32,16,256]{3,2,1,0:T(8,128)(2,1)S(1)} %get-tuple-element.32.raw_ref, f32[144,128]{1,0:T(8,128)S(1)} %add_add_fusion.1.partial_ref), custom_call_target="tpu_custom_call" | custom-call | flops 2000000000 | bytes 3686400 | tf_op jit(solution)/shard_map/pallas_call | solution.py:40
  43.5 0.0 collective-permute-done.13
  43.5 0.0 collective-permute-done.12
  43.5 0.3 collective-permute-done.11
  43.8 1.4 %collective-permute-start.14 = (f32[144,128]{1,0:T(8,128)S(1)}, f32[144,128]{1,0:T(8,128)S(1)}, u32[]{:S(2)}, u32[]{:S(2)}) collective-permute-start(f32[144,128]{1,0:T(8,128)S(1)} %add_add_fusion), channel_id=1, source_target_pairs={{0,32},{1,33},{2,34},{3,35},{4,36},{5,37},{6,38},{7,39},{8,40},{9,... | collective-permute-start | bytes 221192 | tf_op jit(solution)/shard_map/ppermute | solution.py:435
  45.3 4.1 %collective-permute-done.14 = f32[144,128]{1,0:T(8,128)S(1)} collective-permute-done((f32[144,128]{1,0:T(8,128)S(1)}, f32[144,128]{1,0:T(8,128)S(1)}, u32[]{:S(2)}, u32[]{:S(2)}) %collective-permute-start.14) | collective-permute-done | bytes 73760 | tf_op jit(solution)/shard_map/ppermute | solution.py:435
  49.4 0.1 collective-permute-start.15
  49.5 1.3 %collective-permute-done.15.given_ref = f32[144,128]{1,0:T(8,128)S(1)} collective-permute-done((f32[144,128]{1,0:T(8,128)S(1)}, f32[144,128]{1,0:T(8,128)S(1)}, u32[]{:S(2)}, u32[]{:S(2)}) %collective-permute-start.15) | collective-permute-done | bytes 73760 | tf_op jit(solution)/shard_map/ppermute | solution.py:464
  50.7 1.0 %shard_map.74 = (f32[3,3,32,32]{3,2,1,0:T(8,128)}, f32[3,3,32,32]{3,2,1,0:T(8,128)}) custom-call(f32[144,128]{1,0:T(8,128)S(1)} %add.43.total_ref, f32[144,128]{1,0:T(8,128)S(1)} %collective-permute-done.15.given_ref), custom_call_target="tpu_custom_call" | custom-call | flops 1000000 | bytes 221184 | tf_op jit(solution)/shard_map/pallas_call | solution.py:40
  (5 shorter events, 0.1 us)
Async XLA Ops:
  2.8 5.6 %collective-permute-start.1 = (bf16[16,256]{1,0:T(8,128)(2,1)S(1)}, bf16[16,256]{1,0:T(8,128)(2,1)S(1)}, u32[]{:S(2)}, u32[]{:S(2)}) collective-permute-start(bf16[16,256]{1,0:T(8,128)(2,1)S(1)} %get-tuple-element.40), channel_id=1, source_target_pairs={{0,192},{64,128},{128,64},{192,0},{1,193},{65,129},{129,65},{193,1... | collective-permute-start | bytes 24584 | tf_op jit(solution)/shard_map/ppermute | solution.py:460
  7.8 1.3 %collective-permute-start = (bf16[16,256]{1,0:T(8,128)(2,1)S(1)}, bf16[16,256]{1,0:T(8,128)(2,1)S(1)}, u32[]{:S(2)}, u32[]{:S(2)}) collective-permute-start(bf16[16,256]{1,0:T(8,128)(2,1)S(1)} %get-tuple-element.39), channel_id=1, source_target_pairs={{0,64},{64,0},{128,192},{192,128},{1,65},{65,1},{129,193},{193,129... | collective-permute-start | bytes 24584 | tf_op jit(solution)/shard_map/ppermute | solution.py:464
  9.2 11.4 %collective-permute-start.2 = (bf16[144,256]{1,0:T(8,128)(2,1)S(1)}, bf16[144,256]{1,0:T(8,128)(2,1)S(1)}, u32[]{:S(2)}, u32[]{:S(2)}) collective-permute-start(bf16[144,256]{1,0:T(8,128)(2,1)S(1)} %get-tuple-element.43), channel_id=1, source_target_pairs={{0,63},{1,2},{2,1},{3,4},{4,3},{5,6},{6,5},{7,8},{8,7},{9,10},{10,... | collective-permute-start | bytes 221192 | tf_op jit(solution)/shard_map/ppermute | solution.py:513
  17.7 3.2 %collective-permute-start.3 = (bf16[144,256]{1,0:T(8,128)(2,1)S(1)}, bf16[144,256]{1,0:T(8,128)(2,1)S(1)}, u32[]{:S(2)}, u32[]{:S(2)}) collective-permute-start(bf16[144,256]{1,0:T(8,128)(2,1)S(1)} %get-tuple-element.44), channel_id=1, source_target_pairs={{0,1},{1,0},{2,3},{3,2},{4,5},{5,4},{6,7},{7,6},{8,9},{9,8},{10,11... | collective-permute-start | bytes 221192 | tf_op jit(solution)/shard_map/ppermute | solution.py:514
  21.8 2.8 %collective-permute-start.4 = (f32[144,128]{1,0:T(8,128)S(1)}, f32[144,128]{1,0:T(8,128)S(1)}, u32[]{:S(2)}, u32[]{:S(2)}) collective-permute-start(f32[144,128]{1,0:T(8,128)S(1)} %get-tuple-element.53), channel_id=1, source_target_pairs={{0,64},{64,0},{128,192},{192,128},{1,65},{65,1},{129,193},{193,129... | collective-permute-start | bytes 221192 | tf_op jit(solution)/shard_map/ppermute | solution.py:464
  24.6 4.8 %collective-permute-start.7 = (f32[144,128]{1,0:T(8,128)S(1)}, f32[144,128]{1,0:T(8,128)S(1)}, u32[]{:S(2)}, u32[]{:S(2)}) collective-permute-start(f32[144,128]{1,0:T(8,128)S(1)} %add.33), channel_id=1, source_target_pairs={{0,1},{1,0},{2,3},{3,2},{4,5},{5,4},{6,7},{7,6},{8,9},{9,8},{10,11... | collective-permute-start | bytes 221192 | tf_op jit(solution)/shard_map/ppermute | solution.py:435
  27.2 4.4 %collective-permute-start.6 = (f32[144,128]{1,0:T(8,128)S(1)}, f32[144,128]{1,0:T(8,128)S(1)}, u32[]{:S(2)}, u32[]{:S(2)}) collective-permute-start(f32[144,128]{1,0:T(8,128)S(1)} %add.33), channel_id=1, source_target_pairs={{0,1},{1,0},{2,3},{3,2},{4,5},{5,4},{6,7},{7,6},{8,9},{9,8},{10,11... | collective-permute-start | bytes 221192 | tf_op jit(solution)/shard_map/ppermute | solution.py:435
  27.6 4.0 %collective-permute-start.5 = (f32[144,128]{1,0:T(8,128)S(1)}, f32[144,128]{1,0:T(8,128)S(1)}, u32[]{:S(2)}, u32[]{:S(2)}) collective-permute-start(f32[144,128]{1,0:T(8,128)S(1)} %add.33), channel_id=1, source_target_pairs={{0,1},{1,0},{2,3},{3,2},{4,5},{5,4},{6,7},{7,6},{8,9},{9,8},{10,11... | collective-permute-start | bytes 221192 | tf_op jit(solution)/shard_map/ppermute | solution.py:435
  31.6 4.9 %collective-permute-start.10 = (f32[144,128]{1,0:T(8,128)S(1)}, f32[144,128]{1,0:T(8,128)S(1)}, u32[]{:S(2)}, u32[]{:S(2)}) collective-permute-start(f32[144,128]{1,0:T(8,128)S(1)} %add_add_fusion.2.partial_ref), channel_id=1, source_target_pairs={{0,32},{1,33},{2,34},{3,35},{4,36},{5,37},{6,38},{7,39},{8,40},{9,... | collective-permute-start | bytes 221192 | tf_op jit(solution)/shard_map/ppermute | solution.py:435
  31.7 5.3 %collective-permute-start.9 = (f32[144,128]{1,0:T(8,128)S(1)}, f32[144,128]{1,0:T(8,128)S(1)}, u32[]{:S(2)}, u32[]{:S(2)}) collective-permute-start(f32[144,128]{1,0:T(8,128)S(1)} %add_add_fusion.2.partial_ref), channel_id=1, source_target_pairs={{0,32},{1,33},{2,34},{3,35},{4,36},{5,37},{6,38},{7,39},{8,40},{9,... | collective-permute-start | bytes 221192 | tf_op jit(solution)/shard_map/ppermute | solution.py:435
  34.4 3.2 %collective-permute-start.8 = (f32[144,128]{1,0:T(8,128)S(1)}, f32[144,128]{1,0:T(8,128)S(1)}, u32[]{:S(2)}, u32[]{:S(2)}) collective-permute-start(f32[144,128]{1,0:T(8,128)S(1)} %add_add_fusion.2.partial_ref), channel_id=1, source_target_pairs={{0,32},{1,33},{2,34},{3,35},{4,36},{5,37},{6,38},{7,39},{8,40},{9,... | collective-permute-start | bytes 221192 | tf_op jit(solution)/shard_map/ppermute | solution.py:435
  37.6 5.8 %collective-permute-start.13 = (f32[144,128]{1,0:T(8,128)S(1)}, f32[144,128]{1,0:T(8,128)S(1)}, u32[]{:S(2)}, u32[]{:S(2)}) collective-permute-start(f32[144,128]{1,0:T(8,128)S(1)} %add_add_fusion.1.partial_ref), channel_id=1, source_target_pairs={{0,32},{1,33},{2,34},{3,35},{4,36},{5,37},{6,38},{7,39},{8,40},{9,... | collective-permute-start | bytes 221192 | tf_op jit(solution)/shard_map/ppermute | solution.py:435
  37.7 5.7 %collective-permute-start.12 = (f32[144,128]{1,0:T(8,128)S(1)}, f32[144,128]{1,0:T(8,128)S(1)}, u32[]{:S(2)}, u32[]{:S(2)}) collective-permute-start(f32[144,128]{1,0:T(8,128)S(1)} %add_add_fusion.1.partial_ref), channel_id=1, source_target_pairs={{0,32},{1,33},{2,34},{3,35},{4,36},{5,37},{6,38},{7,39},{8,40},{9,... | collective-permute-start | bytes 221192 | tf_op jit(solution)/shard_map/ppermute | solution.py:435
  37.8 6.0 %collective-permute-start.11 = (f32[144,128]{1,0:T(8,128)S(1)}, f32[144,128]{1,0:T(8,128)S(1)}, u32[]{:S(2)}, u32[]{:S(2)}) collective-permute-start(f32[144,128]{1,0:T(8,128)S(1)} %add_add_fusion.1.partial_ref), channel_id=1, source_target_pairs={{0,32},{1,33},{2,34},{3,35},{4,36},{5,37},{6,38},{7,39},{8,40},{9,... | collective-permute-start | bytes 221192 | tf_op jit(solution)/shard_map/ppermute | solution.py:435
  43.8 5.5 %collective-permute-start.14 = (f32[144,128]{1,0:T(8,128)S(1)}, f32[144,128]{1,0:T(8,128)S(1)}, u32[]{:S(2)}, u32[]{:S(2)}) collective-permute-start(f32[144,128]{1,0:T(8,128)S(1)} %add_add_fusion), channel_id=1, source_target_pairs={{0,32},{1,33},{2,34},{3,35},{4,36},{5,37},{6,38},{7,39},{8,40},{9,... | collective-permute-start | bytes 221192 | tf_op jit(solution)/shard_map/ppermute | solution.py:435
  49.4 1.4 %collective-permute-start.15 = (f32[144,128]{1,0:T(8,128)S(1)}, f32[144,128]{1,0:T(8,128)S(1)}, u32[]{:S(2)}, u32[]{:S(2)}) collective-permute-start(f32[144,128]{1,0:T(8,128)S(1)} %add.43.total_ref), channel_id=1, source_target_pairs={{0,64},{64,0},{128,192},{192,128},{1,65},{65,1},{129,193},{193,129... | collective-permute-start | bytes 221192 | tf_op jit(solution)/shard_map/ppermute | solution.py:464
